TPU v7x, 256 devices: a whole 4x4x8 slice. The times are simulated.
256 devices in a mesh: seq: 32 (over z, x), head: 8 (over y, core).
Axes of the slice: x: 4, y: 4, z: 8, core: 2. Of those that a mesh axis runs over, the one named last changes fastest.
Arguments:
- tokens: bfloat16 [32768, 1024], P(('seq', 'head')), may hold values from -6 to 6
- win_first: int32 [32768], P('seq'), may hold values from 0 to 32767, as said below
- win_count: int32 [32768], P('seq'), may hold values from 1 to 64, as said below
- norm1_gain: float32 [1024], replicated, may hold values from 0.25 to 1.75
- qkv_weight: bfloat16 [1024, 3, 1024], P('seq', None, 'head'), may hold values from -0.1875 to 0.1875
- qk_gain: float32 [2, 16, 64], P(None, 'head'), may hold values from 0.25 to 1.75
- out_weight: bfloat16 [1024, 1024], P('head', 'seq'), may hold values from -0.1875 to 0.1875
- norm2_gain: float32 [1024], replicated, may hold values from 0.25 to 1.75
- up_weight: bfloat16 [1024, 4096], P('seq', 'head'), may hold values from -0.1875 to 0.1875
- down_weight: bfloat16 [4096, 1024], P('head', 'seq'), may hold values from -0.09375 to 0.09375
Outputs:
- block_out: bfloat16 [32768, 1024], P(('seq', 'head'))
Inputs may be any that keep to these rules, and one draw needn't show every extreme that they name: Each token's window block is the run of consecutive tokens from win_first to win_first + win_count - 1, which contains the token; window blocks tile the tokens in order, and some window block has exactly 64 tokens. `win_count`: all tokens of one window block carry the same count.
All inputs are finite; a program needn't handle non-finite values.
Results may differ from a plain program's by a relative error of at most 0.008.
Values may be sent and summed in bfloat16 or wider, within the bound.
No kernel may reach another device: no remote copies, remote signals or barrier semaphores. Data moves between devices by JAX's collectives and lax.ppermute only.
A program may use at most 64 MiB of HBM per device.

v0:
```python
import functools

import jax
import jax.numpy as jnp
from jax import lax
from jax.experimental import pallas as pl
from jax.experimental.pallas import tpu as pltpu
from jax.sharding import Mesh, PartitionSpec as P

WIN = 64
F32, BF16 = jnp.float32, jnp.bfloat16
NT = (((1,), (1,)), ((), ()))
VMEM = pl.BlockSpec(memory_space=pltpu.VMEM)
SMEM = pl.BlockSpec(memory_space=pltpu.SMEM)


def params(mib):
    return pltpu.CompilerParams(vmem_limit_bytes=mib * 2**20)


def layer_norm(values, gain):
    center = values - jnp.mean(values, axis=-1, keepdims=True)
    spread = jnp.mean(center * center, axis=-1, keepdims=True)
    return (center * lax.rsqrt(spread + 1e-06) * gain).astype(BF16)


def head_norm(values, gain, half):
    square = values * values
    low = jnp.sum(jnp.where(half, square, 0.0), axis=-1, keepdims=True)
    high = jnp.sum(jnp.where(half, 0.0, square), axis=-1, keepdims=True)
    scale = lax.rsqrt(jnp.where(half, low, high) * (1.0 / 64) + 1e-06)
    return (values * scale * gain).astype(BF16)


def first_half(rows):
    return lax.broadcasted_iota(jnp.int32, (rows, 128), 1) < 64


def start_kernel(tok, gain, qkv, out_w, up, down, normed, front, back):
    normed[...] = layer_norm(tok[...].astype(F32), gain[...])
    pack = jnp.concatenate(
        [qkv[:, 0], qkv[:, 1], qkv[:, 2], out_w[...].astype(F32).T.astype(BF16)], axis=1
    )
    for i in range(front.shape[0]):
        front[i] = pack
    back[:, :512] = up[...]
    back[:, 512:] = down[...].astype(F32).T.astype(BF16)


def edge_kernel(at, *refs):
    own, peer = refs[:4], refs[4:8]
    weight, gain, head_kv, tail_kv, rows = refs[8:]
    y, core = at[0], at[1]
    for k in range(4):

        @pl.when(lax.rem(y + k, 4) == 0)
        def _():
            rows[:WIN] = jnp.where(core == 0, own[k][:WIN], peer[k][:WIN])

        @pl.when(lax.rem(y + k, 4) == 3)
        def _():
            rows[WIN:] = jnp.where(core == 1, own[k][128 - WIN :], peer[k][128 - WIN :])

    kv = jnp.dot(rows[...], weight[:, 128:384], preferred_element_type=F32)
    key = head_norm(kv[:, :128], gain[1:2], first_half(128))
    both = jnp.concatenate([key, kv[:, 128:].astype(BF16)], axis=1)
    head_kv[...] = both[:WIN]
    tail_kv[...] = both[WIN:]


def attend(query, kv, first, count, key_start):
    lower = jnp.broadcast_to(first, (128, 128)).T
    upper = lower + jnp.broadcast_to(count, (128, 128)).T
    index = key_start + lax.broadcasted_iota(jnp.int32, (128, 256), 1)
    lower = jnp.concatenate([lower, lower], axis=1)
    upper = jnp.concatenate([upper, upper], axis=1)
    allowed = (index >= lower) & (index < upper)
    outs = []
    for h in range(2):
        lanes = slice(h * 64, h * 64 + 64)
        score = lax.dot_general(query[:, lanes], kv[:, lanes], NT, preferred_element_type=F32)
        weight = jnp.where(allowed, jnp.exp(score * 0.125), 0.0)
        total = jnp.sum(weight, axis=-1, keepdims=True)
        prob = (weight / total).astype(BF16)
        value = kv[:, 128 + h * 64 : 192 + h * 64]
        outs.append(jnp.dot(prob, value, preferred_element_type=F32))
    return jnp.concatenate(outs, axis=1).astype(BF16)


def main_kernel(at, *refs):
    own, peer = refs[:4], refs[4:8]
    weight, gain, first, count, att, q_edge, kv_edge, q_s, kv_s = refs[8:]
    y, core, anchor = at[0], at[1], at[2]
    half = first_half(256)
    for k in range(4):
        rows = jnp.concatenate([own[k][...], peer[k][...]], axis=0)
        qkv = jnp.dot(rows, weight[:, :384], preferred_element_type=F32)
        query = head_norm(qkv[:, :128], gain[0:1], half)
        key = head_norm(qkv[:, 128:256], gain[1:2], half)
        kv = jnp.concatenate([key, qkv[:, 256:].astype(BF16)], axis=1)
        base = lax.rem(y + k, 4) * 256
        mine = pl.multiple_of(base + core * 128, 128)
        theirs = pl.multiple_of(base + (1 - core) * 128, 128)
        q_s[pl.ds(mine, 128)] = query[:128]
        q_s[pl.ds(theirs, 128)] = query[128:]
        kv_s[pl.ds(mine, 128)] = kv[:128]
        kv_s[pl.ds(theirs, 128)] = kv[128:]
    for b in range(1, 7):
        start = b * 128 - WIN
        att[lax.rem(core + b, 2), b // 2] = attend(
            q_s[b * 128 : b * 128 + 128],
            kv_s[start : start + 256],
            first[b : b + 1],
            count[b : b + 1],
            anchor + start,
        )
    zero = jnp.zeros((128, 128), BF16)
    att[core, 0] = zero
    att[lax.rem(core + 1, 2), 3] = zero
    q_edge[0] = q_s[:128]
    q_edge[1] = q_s[896:]
    kv_edge[0] = kv_s[:192]
    kv_edge[1] = kv_s[832:]


def last_kernel(at, att, q_edge, kv_edge, before, after, first, count, out):
    core, anchor = at[1], at[2]
    out[...] = att[...]
    top = jnp.concatenate([before[...], kv_edge[0]], axis=0)
    out[core, 0] = attend(q_edge[0], top, first[0:1], count[0:1], anchor - WIN)
    bottom = jnp.concatenate([kv_edge[1], after[...]], axis=0)
    out[lax.rem(core + 1, 2), 3] = attend(
        q_edge[1], bottom, first[7:8], count[7:8], anchor + 896 - WIN
    )


def project_kernel(at, att, got, weight, other, mine, away):
    y = at[0]
    for k in (2, 1, 3, 0):
        t = lax.rem(y + k, 4)
        part = lax.dot_general(
            att[0, t], weight[:, 384:], NT, preferred_element_type=F32
        ) + lax.dot_general(got[t], other[...], NT, preferred_element_type=F32)
        if k == 0:
            mine[...] = part
        else:
            away[k - 1] = part.astype(BF16)


def middle_kernel(tok, mine, a, b, c, gain, middle, normed):
    total = mine[...] + a[...].astype(F32) + b[...].astype(F32) + c[...].astype(F32)
    mid = (tok[...].astype(F32) + total).astype(BF16)
    middle[...] = mid
    normed[...] = layer_norm(mid.astype(F32), gain[...])


def mlp_kernel(rows, up_own, down_own, up_peer, down_peer, out, total):
    step = pl.program_id(0)
    up = jnp.concatenate([up_own[...], up_peer[...]], axis=1)
    down = jnp.concatenate([down_own[...], down_peer[...]], axis=1)
    hidden = jax.nn.gelu(
        jnp.dot(rows[...], up, preferred_element_type=F32), approximate=True
    ).astype(BF16)
    part = lax.dot_general(hidden, down, NT, preferred_element_type=F32)

    @pl.when(step == 0)
    def _():
        total[...] = part

    @pl.when(step == 1)
    def _():
        out[...] = (total[...] + part).astype(out.dtype)


def mlp(rows, own, peer, dtype):
    block = lambda at: pl.BlockSpec((1024, 256), lambda i, at=at: (0, at + i))
    whole = pl.BlockSpec((128, 1024), lambda i: (0, 0))
    return pl.pallas_call(
        mlp_kernel,
        grid=(2,),
        out_shape=jax.ShapeDtypeStruct((128, 1024), dtype),
        in_specs=[whole, block(0), block(2), block(0), block(2)],
        out_specs=whole,
        scratch_shapes=[pltpu.VMEM((128, 1024), F32)],
        compiler_params=params(24),
        cost_estimate=pl.CostEstimate(flops=4 * 128 * 2**20, bytes_accessed=5 * 2**20, transcendentals=2**17),
        name="mlp",
    )(rows, own, own, peer, peer)


def end_kernel(middle, mine, a, b, c, out):
    total = middle[...].astype(F32) + mine[...]
    total += a[...].astype(F32) + b[...].astype(F32) + c[...].astype(F32)
    out[...] = total.astype(BF16)


def call(kernel, outs, specs, name, mib=24, scratch=(), flops=2**20, **more):
    return pl.pallas_call(
        kernel,
        out_shape=[jax.ShapeDtypeStruct(s, d) for s, d in outs],
        in_specs=specs,
        out_specs=[VMEM] * len(outs),
        scratch_shapes=list(scratch),
        compiler_params=params(mib),
        cost_estimate=pl.CostEstimate(flops=flops, bytes_accessed=2**21, transcendentals=0),
        name=name,
        **more,
    )


def fetch(value, axis, step):
    n = lax.axis_size(axis)
    return lax.ppermute(value, axis, [((i + step) % n, i) for i in range(n)])


def local(
    tokens,
    win_first,
    win_count,
    norm1_gain,
    qkv_weight,
    qk_gain,
    out_weight,
    norm2_gain,
    up_weight,
    down_weight,
):
    y, core = lax.axis_index("y"), lax.axis_index("core")
    seq = lax.axis_index("z") * lax.axis_size("x") + lax.axis_index("x")
    at = jnp.stack([y, core, seq * 1024]).astype(jnp.int32)
    first, count = win_first.reshape(8, 128), win_count.reshape(8, 128)
    gain = qk_gain.reshape(2, 128)

    normed, front, back = call(
        start_kernel,
        [((128, 1024), BF16), ((32, 32, 512), BF16), ((32, 1024), BF16)],
        [VMEM] * 6,
        "start",
    )(tokens, norm1_gain.reshape(1, 1024), qkv_weight, out_weight, up_weight, down_weight)

    mlp_own = lax.all_gather(back, ("z", "x"), axis=0, tiled=True)
    far = {k: fetch(normed, "y", k) for k in (2, 1, 3)}
    own = [normed, far[1], far[2], far[3]]
    peer = [fetch(rows, "core", 1) for rows in own]
    weight = lax.all_to_all(front, ("z", "x"), 0, 0, tiled=True).reshape(1024, 512)
    out_peer = fetch(weight[:, 384:], "core", 1)

    head_kv, tail_kv = call(
        edge_kernel,
        [((WIN, 256), BF16)] * 2,
        [SMEM] + [VMEM] * 10,
        "edge",
        scratch=[pltpu.VMEM((2 * WIN, 1024), BF16)],
    )(at, *own, *peer, weight, gain)
    n_seq = lax.axis_size("z") * lax.axis_size("x")
    before = lax.ppermute(tail_kv, ("z", "x"), [(i, (i + 1) % n_seq) for i in range(n_seq)])
    after = lax.ppermute(head_kv, ("z", "x"), [((i + 1) % n_seq, i) for i in range(n_seq)])
    att, q_edge, kv_edge = call(
        main_kernel,
        [((2, 4, 128, 128), BF16), ((2, 128, 128), BF16), ((2, 192, 256), BF16)],
        [SMEM] + [VMEM] * 12,
        "attention",
        scratch=[pltpu.VMEM((1024, 128), BF16), pltpu.VMEM((1024, 256), BF16)],
        flops=5 * 2**30,
    )(at, *own, *peer, weight, gain, first, count)
    (att,) = call(
        last_kernel,
        [((2, 4, 128, 128), BF16)],
        [SMEM] + [VMEM] * 7,
        "attention_edge",
    )(at, att, q_edge, kv_edge, before, after, first, count)

    got = fetch(att[1], "core", 1)
    mine, away = call(
        project_kernel,
        [((128, 1024), F32), ((3, 128, 1024), BF16)],
        [SMEM] + [VMEM] * 4,
        "project",
    )(at, att, got, weight, out_peer)
    parts = [fetch(away[k - 1], "y", 4 - k) for k in (2, 1, 3)]
    middle, normed_two = call(
        middle_kernel,
        [((128, 1024), BF16)] * 2,
        [VMEM] * 6,
        "middle",
    )(tokens, mine, *parts, norm2_gain.reshape(1, 1024))

    mlp_own, _ = lax.optimization_barrier((mlp_own, normed_two))
    mlp_peer = fetch(mlp_own, "core", 1)
    far = {k: fetch(normed_two, "y", k) for k in (2, 1, 3)}
    mine = mlp(normed_two, mlp_own, mlp_peer, F32)
    parts = [fetch(mlp(far[k], mlp_own, mlp_peer, BF16), "y", 4 - k) for k in (3, 2, 1)]
    (out,) = call(end_kernel, [((128, 1024), BF16)], [VMEM] * 5, "end")(middle, mine, *parts)
    return out


def solution(mesh):
    fine = Mesh(mesh.devices.reshape(8, 4, 4, 2), ("z", "x", "y", "core"))
    seq, head = ("z", "x"), ("y", "core")
    return jax.shard_map(
        local,
        mesh=fine,
        in_specs=(
            P(seq + head, None),
            P(seq),
            P(seq),
            P(),
            P(seq, None, head),
            P(None, head, None),
            P(head, seq),
            P(),
            P(seq, head),
            P(head, seq),
        ),
        out_specs=P(seq + head, None),
        check_vma=False,
    )
```

profile of v0, /device:TPU:1, one launch (start us, length us, event | category | flops | bytes accessed | tf_op | source)
XLA Modules:
  0.0 140.3 jit_solution(7055044534133274044)
XLA Ops:
  12.8 11.9 %all-to-all-start = ((bf16[32,32,512]{2,1,0:T(8,128)(2,1)}), bf16[32,32,512]{2,1,0:T(8,128)(2,1)S(1)}, u32[]{:S(2)}, u32[]{:S(2)}) async-start(bf16[32,32,512]{2,1,0:T(8,128)(2,1)} %get-tuple-element.19), calls=%async_computation | async-start | bytes 2097152 | tf_op jit(solution)/shard_map/all_to_all | solution.py:245
  24.7 2.8 %collective-permute-start = (bf16[128,1024]{1,0:T(8,128)(2,1)S(1)}, bf16[128,1024]{1,0:T(8,128)(2,1)S(1)}, u32[]{:S(2)}, u32[]{:S(2)}) collective-permute-start(bf16[128,1024]{1,0:T(8,128)(2,1)S(1)} %get-tuple-element.18.refs_0_), channel_id=1, source_target_pairs={{2,0},{4,2},{6,4},{0,6},{3,1},{5,3},{7,5},{1,7},{10,8},{12,10},{14... | collective-permute-start | bytes 786440 | tf_op jit(solution)/shard_map/ppermute | solution.py:213
  30.4 2.8 %collective-permute-done.refs_1_ = bf16[128,1024]{1,0:T(8,128)(2,1)S(1)} collective-permute-done((bf16[128,1024]{1,0:T(8,128)(2,1)S(1)}, bf16[128,1024]{1,0:T(8,128)(2,1)S(1)}, u32[]{:S(2)}, u32[]{:S(2)}) %collective-permute-start) | collective-permute-done | bytes 262176 | tf_op jit(solution)/shard_map/ppermute | solution.py:213
  33.2 6.5 %collective-permute-start.4 = (bf16[128,1024]{1,0:T(8,128)(2,1)S(1)}, bf16[128,1024]{1,0:T(8,128)(2,1)S(1)}, u32[]{:S(2)}, u32[]{:S(2)}) collective-permute-start(bf16[128,1024]{1,0:T(8,128)(2,1)S(1)} %collective-permute-done.refs_1_), channel_id=1, source_target_pairs={{1,0},{0,1},{3,2},{2,3},{5,4},{4,5},{7,6},{6,7},{9,8},{8,9},{11,10... | collective-permute-start | bytes 786440 | tf_op jit(solution)/shard_map/ppermute | solution.py:213
  39.7 3.2 %collective-permute-done.2.refs_3_ = bf16[128,1024]{1,0:T(8,128)(2,1)S(1)} collective-permute-done((bf16[128,1024]{1,0:T(8,128)(2,1)S(1)}, bf16[128,1024]{1,0:T(8,128)(2,1)S(1)}, u32[]{:S(2)}, u32[]{:S(2)}) %collective-permute-start.2) | collective-permute-done | bytes 262176 | tf_op jit(solution)/shard_map/ppermute | solution.py:213
  43.5 8.9 %all-to-all-done = bf16[32,32,512]{2,1,0:T(8,128)(2,1)S(1)} async-done(((bf16[32,32,512]{2,1,0:T(8,128)(2,1)}), bf16[32,32,512]{2,1,0:T(8,128)(2,1)S(1)}, u32[]{:S(2)}, u32[]{:S(2)}) %all-to-all-start) | async-done | bytes 1048608 | tf_op jit(solution)/shard_map/all_to_all | solution.py:245
  53.5 2.1 %collective-permute-start.7 = (bf16[64,256]{1,0:T(8,128)(2,1)S(1)}, bf16[64,256]{1,0:T(8,128)(2,1)S(1)}, u32[]{:S(2)}, u32[]{:S(2)}) collective-permute-start(bf16[64,256]{1,0:T(8,128)(2,1)S(1)} %get-tuple-element.23), channel_id=1, source_target_pairs={{0,8},{8,16},{16,24},{24,32},{32,40},{40,48},{48,56},{56,64},{64,7... | collective-permute-start | bytes 98312 | tf_op jit(solution)/shard_map/ppermute | solution.py:256
  55.6 2.8 %collective-permute-start.8 = (bf16[64,256]{1,0:T(8,128)(2,1)S(1)}, bf16[64,256]{1,0:T(8,128)(2,1)S(1)}, u32[]{:S(2)}, u32[]{:S(2)}) collective-permute-start(bf16[64,256]{1,0:T(8,128)(2,1)S(1)} %get-tuple-element.24), channel_id=1, source_target_pairs={{8,0},{16,8},{24,16},{32,24},{40,32},{48,40},{56,48},{64,56},{72,6... | collective-permute-start | bytes 98312 | tf_op jit(solution)/shard_map/ppermute | solution.py:257
  58.3 4.1 %collective-permute-start.10 = (bf16[1024,128]{1,0:T(8,128)(2,1)S(1)}, bf16[1024,128]{1,0:T(8,128)(2,1)S(1)}, u32[]{:S(2)}, u32[]{:S(2)}) collective-permute-start(bf16[1024,128]{1,0:T(8,128)(2,1)S(1)} %slice.21), channel_id=1, source_target_pairs={{1,0},{0,1},{3,2},{2,3},{5,4},{4,5},{7,6},{6,7},{9,8},{8,9},{11,10... | collective-permute-start | bytes 786440 | tf_op jit(solution)/shard_map/ppermute | solution.py:213
  62.4 3.8 %attention.1 = (bf16[2,4,128,128]{3,2,1,0:T(8,128)(2,1)S(1)}, bf16[2,128,128]{2,1,0:T(8,128)(2,1)S(1)}, bf16[2,192,256]{2,1,0:T(8,128)(2,1)S(1)}) custom-call(s32[3]{0:T(128)S(1)} %pad_add_fusion.at, bf16[128,1024]{1,0:T(8,128)(2,1)S(1)} %get-tuple-element.18.refs_0_, bf16[128,1024]{1,0:T(8,128)(2,1)S(1)} %collective-permute-done.refs_1_, ...), custom_call_target="tpu_custom_call" | custom-call | flops 5368709120 | bytes 2097152 | tf_op jit(solution)/shard_map/attention/pallas_call | solution.py:258
  70.8 3.1 %collective-permute-start.11 = (bf16[128,1024]{1,0:T(8,128)(2,1)S(1)}, bf16[128,1024]{1,0:T(8,128)(2,1)S(1)}, u32[]{:S(2)}, u32[]{:S(2)}) collective-permute-start(bf16[128,1024]{1,0:T(8,128)(2,1)S(1)} %get-tuple-element.33), channel_id=1, source_target_pairs={{4,0},{6,2},{0,4},{2,6},{5,1},{7,3},{1,5},{3,7},{12,8},{14,10},{8,... | collective-permute-start | bytes 786440 | tf_op jit(solution)/shard_map/ppermute | solution.py:213
  74.3 2.3 %collective-permute-start.13 = (bf16[128,1024]{1,0:T(8,128)(2,1)S(1)}, bf16[128,1024]{1,0:T(8,128)(2,1)S(1)}, u32[]{:S(2)}, u32[]{:S(2)}) collective-permute-start(bf16[128,1024]{1,0:T(8,128)(2,1)S(1)} %get-tuple-element.31), channel_id=1, source_target_pairs={{2,0},{4,2},{6,4},{0,6},{3,1},{5,3},{7,5},{1,7},{10,8},{12,10},{14... | collective-permute-start | bytes 786440 | tf_op jit(solution)/shard_map/ppermute | solution.py:213
  76.6 3.7 %collective-permute-done.11.a = bf16[128,1024]{1,0:T(8,128)(2,1)S(1)} collective-permute-done((bf16[128,1024]{1,0:T(8,128)(2,1)S(1)}, bf16[128,1024]{1,0:T(8,128)(2,1)S(1)}, u32[]{:S(2)}, u32[]{:S(2)}) %collective-permute-start.11) | collective-permute-done | bytes 262176 | tf_op jit(solution)/shard_map/ppermute | solution.py:213
  80.3 6.1 %collective-permute-done.12.b = bf16[128,1024]{1,0:T(8,128)(2,1)S(1)} collective-permute-done((bf16[128,1024]{1,0:T(8,128)(2,1)S(1)}, bf16[128,1024]{1,0:T(8,128)(2,1)S(1)}, u32[]{:S(2)}, u32[]{:S(2)}) %collective-permute-start.12) | collective-permute-done | bytes 262176 | tf_op jit(solution)/shard_map/ppermute | solution.py:213
  86.8 5.9 %all-gather.2.cloned.1.call-done.up_own.down_own = bf16[1024,1024]{1,0:T(8,128)(2,1)} async-done(((bf16[32,1024]{1,0:T(8,128)(2,1)}), bf16[1024,1024]{1,0:T(8,128)(2,1)}) %all-gather.2.cloned.1.call-update) | async-done | bytes 2097168 | tf_op jit(solution)/shard_map/all_gather | solution.py:241
  92.7 4.6 %collective-permute-start.14 = (bf16[1024,1024]{1,0:T(8,128)(2,1)}, bf16[1024,1024]{1,0:T(8,128)(2,1)S(1)}, u32[]{:S(2)}, u32[]{:S(2)}) collective-permute-start(bf16[1024,1024]{1,0:T(8,128)(2,1)} %all-gather.2.cloned.1.call-done.up_own.down_own), channel_id=1, source_target_pairs={{1,0},{0,1},{3,2},{2,3},{5,4},{4,5},{7,6},{6,7},{9,8},{8,9},{11,10... | collective-permute-start | bytes 6291464 | tf_op jit(solution)/shard_map/ppermute | solution.py:213
  97.3 2.5 %collective-permute-start.19 = (bf16[128,1024]{1,0:T(8,128)(2,1)S(1)}, bf16[128,1024]{1,0:T(8,128)(2,1)S(1)}, u32[]{:S(2)}, u32[]{:S(2)}) collective-permute-start(bf16[128,1024]{1,0:T(8,128)(2,1)S(1)} %get-tuple-element.28.rows), channel_id=1, source_target_pairs={{2,0},{4,2},{6,4},{0,6},{3,1},{5,3},{7,5},{1,7},{10,8},{12,10},{14... | collective-permute-start | bytes 786440 | tf_op jit(solution)/shard_map/ppermute | solution.py:213
  100.8 10.2 %collective-permute-done.19.rows = bf16[128,1024]{1,0:T(8,128)(2,1)S(1)} collective-permute-done((bf16[128,1024]{1,0:T(8,128)(2,1)S(1)}, bf16[128,1024]{1,0:T(8,128)(2,1)S(1)}, u32[]{:S(2)}, u32[]{:S(2)}) %collective-permute-start.19) | collective-permute-done | bytes 262176 | tf_op jit(solution)/shard_map/ppermute | solution.py:213
  112.7 2.1 %mlp.7 = bf16[128,1024]{1,0:T(8,128)(2,1)S(1)} custom-call(bf16[128,1024]{1,0:T(8,128)(2,1)S(1)} %collective-permute-done.19.rows, bf16[1024,1024]{1,0:T(8,128)(2,1)S(1)} %copy-done, bf16[1024,1024]{1,0:T(8,128)(2,1)S(1)} %copy-done, bf16[1024,1024]{1,0:T(8,128)(2,1)S(1)} %collective-permute-done.14.up_peer.down_peer, ...), custom_call_target="tpu_custom_call" | custom-call | flops 536870912 | bytes 5242880 | tf_op jit(solution)/shard_map/mlp/pallas_call | solution.py:178
  114.9 2.1 %mlp.6 = bf16[128,1024]{1,0:T(8,128)(2,1)S(1)} custom-call(bf16[128,1024]{1,0:T(8,128)(2,1)S(1)} %collective-permute-done.17.rows, bf16[1024,1024]{1,0:T(8,128)(2,1)S(1)} %copy-done, bf16[1024,1024]{1,0:T(8,128)(2,1)S(1)} %copy-done, bf16[1024,1024]{1,0:T(8,128)(2,1)S(1)} %collective-permute-done.14.up_peer.down_peer, ...), custom_call_target="tpu_custom_call" | custom-call | flops 536870912 | bytes 5242880 | tf_op jit(solution)/shard_map/mlp/pallas_call | solution.py:178
  117.0 4.8 %collective-permute-start.18 = (bf16[128,1024]{1,0:T(8,128)(2,1)S(1)}, bf16[128,1024]{1,0:T(8,128)(2,1)S(1)}, u32[]{:S(2)}, u32[]{:S(2)}) collective-permute-start(bf16[128,1024]{1,0:T(8,128)(2,1)S(1)} %mlp.6), channel_id=1, source_target_pairs={{4,0},{6,2},{0,4},{2,6},{5,1},{7,3},{1,5},{3,7},{12,8},{14,10},{8,... | collective-permute-start | bytes 786440 | tf_op jit(solution)/shard_map/ppermute | solution.py:213
  121.8 2.1 %mlp.5 = bf16[128,1024]{1,0:T(8,128)(2,1)S(1)} custom-call(bf16[128,1024]{1,0:T(8,128)(2,1)S(1)} %collective-permute-done.15.rows, bf16[1024,1024]{1,0:T(8,128)(2,1)S(1)} %copy-done, bf16[1024,1024]{1,0:T(8,128)(2,1)S(1)} %copy-done, bf16[1024,1024]{1,0:T(8,128)(2,1)S(1)} %collective-permute-done.14.up_peer.down_peer, ...), custom_call_target="tpu_custom_call" | custom-call | flops 536870912 | bytes 5242880 | tf_op jit(solution)/shard_map/mlp/pallas_call | solution.py:178
  124.0 2.1 %mlp.4.mine = f32[128,1024]{1,0:T(8,128)S(1)} custom-call(bf16[128,1024]{1,0:T(8,128)(2,1)S(1)} %get-tuple-element.28.rows, bf16[1024,1024]{1,0:T(8,128)(2,1)S(1)} %copy-done.1, bf16[1024,1024]{1,0:T(8,128)(2,1)S(1)} %copy-done.1, bf16[1024,1024]{1,0:T(8,128)(2,1)S(1)} %collective-permute-done.14.up_peer.down_peer, ...), custom_call_target="tpu_custom_call" | custom-call | flops 536870912 | bytes 5242880 | tf_op jit(solution)/shard_map/mlp/pallas_call | solution.py:178
  126.1 4.6 %collective-permute-done.18.b = bf16[128,1024]{1,0:T(8,128)(2,1)S(1)} collective-permute-done((bf16[128,1024]{1,0:T(8,128)(2,1)S(1)}, bf16[128,1024]{1,0:T(8,128)(2,1)S(1)}, u32[]{:S(2)}, u32[]{:S(2)}) %collective-permute-start.18) | collective-permute-done | bytes 262176 | tf_op jit(solution)/shard_map/ppermute | solution.py:213
  (62 shorter events, 21.4 us)
Async XLA Ops:
  6.5 86.1 %all-gather.2.cloned.1.call-start = ((), (), s32[]{:S(2)}) async-start(), calls=%async_computation.1 | async-start | bytes 2162688 | tf_op jit(solution)/shard_map/all_gather | solution.py:241
  12.8 39.6 %all-to-all-start = ((bf16[32,32,512]{2,1,0:T(8,128)(2,1)}), bf16[32,32,512]{2,1,0:T(8,128)(2,1)S(1)}, u32[]{:S(2)}, u32[]{:S(2)}) async-start(bf16[32,32,512]{2,1,0:T(8,128)(2,1)} %get-tuple-element.19), calls=%async_computation | async-start | bytes 2097152 | tf_op jit(solution)/shard_map/all_to_all | solution.py:245
  24.7 37.7 %copy-start.6 = (s32[1024]{0:T(1024)S(1)}, s32[1024]{0:T(1024)}, u32[]{:S(2)}) copy-start(s32[1024]{0:T(1024)} %param.11) | copy-start | bytes 12292
  24.7 8.5 %collective-permute-start = (bf16[128,1024]{1,0:T(8,128)(2,1)S(1)}, bf16[128,1024]{1,0:T(8,128)(2,1)S(1)}, u32[]{:S(2)}, u32[]{:S(2)}) collective-permute-start(bf16[128,1024]{1,0:T(8,128)(2,1)S(1)} %get-tuple-element.18.refs_0_), channel_id=1, source_target_pairs={{2,0},{4,2},{6,4},{0,6},{3,1},{5,3},{7,5},{1,7},{10,8},{12,10},{14... | collective-permute-start | bytes 786440 | tf_op jit(solution)/shard_map/ppermute | solution.py:213
  27.5 12.1 %collective-permute-start.1 = (bf16[128,1024]{1,0:T(8,128)(2,1)S(1)}, bf16[128,1024]{1,0:T(8,128)(2,1)S(1)}, u32[]{:S(2)}, u32[]{:S(2)}) collective-permute-start(bf16[128,1024]{1,0:T(8,128)(2,1)S(1)} %get-tuple-element.18.refs_0_), channel_id=1, source_target_pairs={{4,0},{6,2},{0,4},{2,6},{5,1},{7,3},{1,5},{3,7},{12,8},{14,10},{8,... | collective-permute-start | bytes 786440 | tf_op jit(solution)/shard_map/ppermute | solution.py:213
  27.9 15.0 %collective-permute-start.2 = (bf16[128,1024]{1,0:T(8,128)(2,1)S(1)}, bf16[128,1024]{1,0:T(8,128)(2,1)S(1)}, u32[]{:S(2)}, u32[]{:S(2)}) collective-permute-start(bf16[128,1024]{1,0:T(8,128)(2,1)S(1)} %get-tuple-element.18.refs_0_), channel_id=1, source_target_pairs={{6,0},{0,2},{2,4},{4,6},{7,1},{1,3},{3,5},{5,7},{14,8},{8,10},{10,... | collective-permute-start | bytes 786440 | tf_op jit(solution)/shard_map/ppermute | solution.py:213
  28.6 23.9 %collective-permute-start.3 = (bf16[128,1024]{1,0:T(8,128)(2,1)S(1)}, bf16[128,1024]{1,0:T(8,128)(2,1)S(1)}, u32[]{:S(2)}, u32[]{:S(2)}) collective-permute-start(bf16[128,1024]{1,0:T(8,128)(2,1)S(1)} %get-tuple-element.18.refs_0_), channel_id=1, source_target_pairs={{1,0},{0,1},{3,2},{2,3},{5,4},{4,5},{7,6},{6,7},{9,8},{8,9},{11,10... | collective-permute-start | bytes 786440 | tf_op jit(solution)/shard_map/ppermute | solution.py:213
  33.2 19.3 %collective-permute-start.4 = (bf16[128,1024]{1,0:T(8,128)(2,1)S(1)}, bf16[128,1024]{1,0:T(8,128)(2,1)S(1)}, u32[]{:S(2)}, u32[]{:S(2)}) collective-permute-start(bf16[128,1024]{1,0:T(8,128)(2,1)S(1)} %collective-permute-done.refs_1_), channel_id=1, source_target_pairs={{1,0},{0,1},{3,2},{2,3},{5,4},{4,5},{7,6},{6,7},{9,8},{8,9},{11,10... | collective-permute-start | bytes 786440 | tf_op jit(solution)/shard_map/ppermute | solution.py:213
  39.7 12.8 %collective-permute-start.5 = (bf16[128,1024]{1,0:T(8,128)(2,1)S(1)}, bf16[128,1024]{1,0:T(8,128)(2,1)S(1)}, u32[]{:S(2)}, u32[]{:S(2)}) collective-permute-start(bf16[128,1024]{1,0:T(8,128)(2,1)S(1)} %collective-permute-done.1.refs_2_), channel_id=1, source_target_pairs={{1,0},{0,1},{3,2},{2,3},{5,4},{4,5},{7,6},{6,7},{9,8},{8,9},{11,10... | collective-permute-start | bytes 786440 | tf_op jit(solution)/shard_map/ppermute | solution.py:213
  42.9 9.6 %collective-permute-start.6 = (bf16[128,1024]{1,0:T(8,128)(2,1)S(1)}, bf16[128,1024]{1,0:T(8,128)(2,1)S(1)}, u32[]{:S(2)}, u32[]{:S(2)}) collective-permute-start(bf16[128,1024]{1,0:T(8,128)(2,1)S(1)} %collective-permute-done.2.refs_3_), channel_id=1, source_target_pairs={{1,0},{0,1},{3,2},{2,3},{5,4},{4,5},{7,6},{6,7},{9,8},{8,9},{11,10... | collective-permute-start | bytes 786440 | tf_op jit(solution)/shard_map/ppermute | solution.py:213
  53.5 12.7 %collective-permute-start.7 = (bf16[64,256]{1,0:T(8,128)(2,1)S(1)}, bf16[64,256]{1,0:T(8,128)(2,1)S(1)}, u32[]{:S(2)}, u32[]{:S(2)}) collective-permute-start(bf16[64,256]{1,0:T(8,128)(2,1)S(1)} %get-tuple-element.23), channel_id=1, source_target_pairs={{0,8},{8,16},{16,24},{24,32},{32,40},{40,48},{48,56},{56,64},{64,7... | collective-permute-start | bytes 98312 | tf_op jit(solution)/shard_map/ppermute | solution.py:256
  55.6 10.6 %collective-permute-start.8 = (bf16[64,256]{1,0:T(8,128)(2,1)S(1)}, bf16[64,256]{1,0:T(8,128)(2,1)S(1)}, u32[]{:S(2)}, u32[]{:S(2)}) collective-permute-start(bf16[64,256]{1,0:T(8,128)(2,1)S(1)} %get-tuple-element.24), channel_id=1, source_target_pairs={{8,0},{16,8},{24,16},{32,24},{40,32},{48,40},{56,48},{64,56},{72,6... | collective-permute-start | bytes 98312 | tf_op jit(solution)/shard_map/ppermute | solution.py:257
  58.3 11.1 %collective-permute-start.10 = (bf16[1024,128]{1,0:T(8,128)(2,1)S(1)}, bf16[1024,128]{1,0:T(8,128)(2,1)S(1)}, u32[]{:S(2)}, u32[]{:S(2)}) collective-permute-start(bf16[1024,128]{1,0:T(8,128)(2,1)S(1)} %slice.21), channel_id=1, source_target_pairs={{1,0},{0,1},{3,2},{2,3},{5,4},{4,5},{7,6},{6,7},{9,8},{8,9},{11,10... | collective-permute-start | bytes 786440 | tf_op jit(solution)/shard_map/ppermute | solution.py:213
  67.9 1.6 %collective-permute-start.9 = (bf16[4,128,128]{2,1,0:T(8,128)(2,1)S(1)}, bf16[4,128,128]{2,1,0:T(8,128)(2,1)S(1)}, u32[]{:S(2)}, u32[]{:S(2)}) collective-permute-start(bf16[4,128,128]{2,1,0:T(8,128)(2,1)S(1)} %slice_bitcast_fusion.3), channel_id=1, source_target_pairs={{1,0},{0,1},{3,2},{2,3},{5,4},{4,5},{7,6},{6,7},{9,8},{8,9},{11,10... | collective-permute-start | bytes 393224 | tf_op jit(solution)/shard_map/ppermute | solution.py:213
  70.8 9.5 %collective-permute-start.11 = (bf16[128,1024]{1,0:T(8,128)(2,1)S(1)}, bf16[128,1024]{1,0:T(8,128)(2,1)S(1)}, u32[]{:S(2)}, u32[]{:S(2)}) collective-permute-start(bf16[128,1024]{1,0:T(8,128)(2,1)S(1)} %get-tuple-element.33), channel_id=1, source_target_pairs={{4,0},{6,2},{0,4},{2,6},{5,1},{7,3},{1,5},{3,7},{12,8},{14,10},{8,... | collective-permute-start | bytes 786440 | tf_op jit(solution)/shard_map/ppermute | solution.py:213
  73.9 12.5 %collective-permute-start.12 = (bf16[128,1024]{1,0:T(8,128)(2,1)S(1)}, bf16[128,1024]{1,0:T(8,128)(2,1)S(1)}, u32[]{:S(2)}, u32[]{:S(2)}) collective-permute-start(bf16[128,1024]{1,0:T(8,128)(2,1)S(1)} %get-tuple-element.32), channel_id=1, source_target_pairs={{6,0},{0,2},{2,4},{4,6},{7,1},{1,3},{3,5},{5,7},{14,8},{8,10},{10,... | collective-permute-start | bytes 786440 | tf_op jit(solution)/shard_map/ppermute | solution.py:213
  74.3 12.1 %collective-permute-start.13 = (bf16[128,1024]{1,0:T(8,128)(2,1)S(1)}, bf16[128,1024]{1,0:T(8,128)(2,1)S(1)}, u32[]{:S(2)}, u32[]{:S(2)}) collective-permute-start(bf16[128,1024]{1,0:T(8,128)(2,1)S(1)} %get-tuple-element.31), channel_id=1, source_target_pairs={{2,0},{4,2},{6,4},{0,6},{3,1},{5,3},{7,5},{1,7},{10,8},{12,10},{14... | collective-permute-start | bytes 786440 | tf_op jit(solution)/shard_map/ppermute | solution.py:213
  92.7 18.4 %collective-permute-start.14 = (bf16[1024,1024]{1,0:T(8,128)(2,1)}, bf16[1024,1024]{1,0:T(8,128)(2,1)S(1)}, u32[]{:S(2)}, u32[]{:S(2)}) collective-permute-start(bf16[1024,1024]{1,0:T(8,128)(2,1)} %all-gather.2.cloned.1.call-done.up_own.down_own), channel_id=1, source_target_pairs={{1,0},{0,1},{3,2},{2,3},{5,4},{4,5},{7,6},{6,7},{9,8},{8,9},{11,10... | collective-permute-start | bytes 6291464 | tf_op jit(solution)/shard_map/ppermute | solution.py:213
  97.3 13.7 %collective-permute-start.19 = (bf16[128,1024]{1,0:T(8,128)(2,1)S(1)}, bf16[128,1024]{1,0:T(8,128)(2,1)S(1)}, u32[]{:S(2)}, u32[]{:S(2)}) collective-permute-start(bf16[128,1024]{1,0:T(8,128)(2,1)S(1)} %get-tuple-element.28.rows), channel_id=1, source_target_pairs={{2,0},{4,2},{6,4},{0,6},{3,1},{5,3},{7,5},{1,7},{10,8},{12,10},{14... | collective-permute-start | bytes 786440 | tf_op jit(solution)/shard_map/ppermute | solution.py:213
  99.8 15.0 %collective-permute-start.17 = (bf16[128,1024]{1,0:T(8,128)(2,1)S(1)}, bf16[128,1024]{1,0:T(8,128)(2,1)S(1)}, u32[]{:S(2)}, u32[]{:S(2)}) collective-permute-start(bf16[128,1024]{1,0:T(8,128)(2,1)S(1)} %get-tuple-element.28.rows), channel_id=1, source_target_pairs={{4,0},{6,2},{0,4},{2,6},{5,1},{7,3},{1,5},{3,7},{12,8},{14,10},{8,... | collective-permute-start | bytes 786440 | tf_op jit(solution)/shard_map/ppermute | solution.py:213
  100.2 21.5 %collective-permute-start.15 = (bf16[128,1024]{1,0:T(8,128)(2,1)S(1)}, bf16[128,1024]{1,0:T(8,128)(2,1)S(1)}, u32[]{:S(2)}, u32[]{:S(2)}) collective-permute-start(bf16[128,1024]{1,0:T(8,128)(2,1)S(1)} %get-tuple-element.28.rows), channel_id=1, source_target_pairs={{6,0},{0,2},{2,4},{4,6},{7,1},{1,3},{3,5},{5,7},{14,8},{8,10},{10,... | collective-permute-start | bytes 786440 | tf_op jit(solution)/shard_map/ppermute | solution.py:213
  114.8 11.4 %collective-permute-start.20 = (bf16[128,1024]{1,0:T(8,128)(2,1)S(1)}, bf16[128,1024]{1,0:T(8,128)(2,1)S(1)}, u32[]{:S(2)}, u32[]{:S(2)}) collective-permute-start(bf16[128,1024]{1,0:T(8,128)(2,1)S(1)} %mlp.7), channel_id=1, source_target_pairs={{6,0},{0,2},{2,4},{4,6},{7,1},{1,3},{3,5},{5,7},{14,8},{8,10},{10,... | collective-permute-start | bytes 786440 | tf_op jit(solution)/shard_map/ppermute | solution.py:213
  117.0 13.8 %collective-permute-start.18 = (bf16[128,1024]{1,0:T(8,128)(2,1)S(1)}, bf16[128,1024]{1,0:T(8,128)(2,1)S(1)}, u32[]{:S(2)}, u32[]{:S(2)}) collective-permute-start(bf16[128,1024]{1,0:T(8,128)(2,1)S(1)} %mlp.6), channel_id=1, source_target_pairs={{4,0},{6,2},{0,4},{2,6},{5,1},{7,3},{1,5},{3,7},{12,8},{14,10},{8,... | collective-permute-start | bytes 786440 | tf_op jit(solution)/shard_map/ppermute | solution.py:213
  123.9 8.7 %collective-permute-start.16 = (bf16[128,1024]{1,0:T(8,128)(2,1)S(1)}, bf16[128,1024]{1,0:T(8,128)(2,1)S(1)}, u32[]{:S(2)}, u32[]{:S(2)}) collective-permute-start(bf16[128,1024]{1,0:T(8,128)(2,1)S(1)} %mlp.5), channel_id=1, source_target_pairs={{2,0},{4,2},{6,4},{0,6},{3,1},{5,3},{7,5},{1,7},{10,8},{12,10},{14... | collective-permute-start | bytes 786440 | tf_op jit(solution)/shard_map/ppermute | solution.py:213
  (9 other events, 125.9 us)
Sparse Core Ops, SparseCore 0:
  12.9 79.7 all-gather.1
where the time goes:
time: 141 us; the launch traced here: 140 us
  starting transfers between devices  52.6 us (37%)
  waiting for transfers between devices  48.7 us (35%)
  Pallas kernels  18.6 us (13%)
  between operations  13.7 us (10%)
  local copies, waits for them, and re-layouts  6.66 us (5%)
    ppermute x19, starting transfers between devices, fetch(): return lax.ppermute(value, axis, [((i + step) % n, i) for i in range(n)])  35.9 us
    ppermute x19, waiting for transfers between devices, fetch(): return lax.ppermute(value, axis, [((i + step) % n, i) for i in range(n)])  33.9 us
    all_to_all x1, starting transfers between devices, local(): lax.all_to_all(front, ('z', 'x'), 0, 0, tiled=True).reshape(1024, 512)  11.9 us
    all_to_all x1, waiting for transfers between devices, local(): lax.all_to_all(front, ('z', 'x'), 0, 0, tiled=True).reshape(1024, 512)  8.92 us
    pallas_call x4, Pallas kernels, mlp(): pl.pallas_call(mlp_kernel, grid=(2,), out_shape=jax.ShapeDtypeStruct((128...  8.44 us
    unnamed x23, local copies, waits for them, and re-layouts  6.48 us
    all_gather x1, waiting for transfers between devices, local(): mlp_own = lax.all_gather(back, ('z', 'x'), axis=0, tiled=True)  5.89 us
    pallas_call x1, Pallas kernels, local(): call(main_kernel, [((2, 4, 128, 128), BF16), ((2, 128, 128), BF16), ((2,...  3.77 us
  transfers between devices with their start and end apart: 23, of which 10 were waited for; matrix products, arithmetic and copies ran while one was open for 0% of the time, Pallas kernels for 12%

commit v1 on v0

v1 whole, which is shorter than its diff:
```python
import functools

import jax
import jax.numpy as jnp
from jax import lax
from jax.experimental import pallas as pl
from jax.experimental.pallas import tpu as pltpu
from jax.sharding import Mesh, PartitionSpec as P

WIN = 64
F32, BF16 = jnp.float32, jnp.bfloat16
NT = (((1,), (1,)), ((), ()))
VMEM = pl.BlockSpec(memory_space=pltpu.VMEM)
SMEM = pl.BlockSpec(memory_space=pltpu.SMEM)


def params(mib):
    return pltpu.CompilerParams(vmem_limit_bytes=mib * 2**20)


def layer_norm(values, gain):
    center = values - jnp.mean(values, axis=-1, keepdims=True)
    spread = jnp.mean(center * center, axis=-1, keepdims=True)
    return (center * lax.rsqrt(spread + 1e-06) * gain).astype(BF16)


def head_norm(values, gain, half):
    square = values * values
    low = jnp.sum(jnp.where(half, square, 0.0), axis=-1, keepdims=True)
    high = jnp.sum(jnp.where(half, 0.0, square), axis=-1, keepdims=True)
    scale = lax.rsqrt(jnp.where(half, low, high) * (1.0 / 64) + 1e-06)
    return (values * scale * gain).astype(BF16)


def first_half(rows):
    return lax.broadcasted_iota(jnp.int32, (rows, 128), 1) < 64


def start_kernel(tok, gain, qkv, out_t, normed, front):
    normed[...] = layer_norm(tok[...].astype(F32), gain[...])
    pack = jnp.concatenate([qkv[0], qkv[1], qkv[2], out_t[...]], axis=1)
    for i in range(8):
        front[i] = pack


def mlp_pack_kernel(up, down_t, back):
    pack = jnp.concatenate([up[...], down_t[...]], axis=1)
    for i in range(8):
        back[i] = pack


def collect_kernel(at, *refs):
    blocks, own, border = refs[:4], refs[4], refs[5]
    y, core = at[0], at[1]
    for k in range(4):
        t = lax.rem(y + k, 4)
        own[t] = blocks[k][...]

        @pl.when((core == 0) & (t == 0))
        def _():
            border[...] = blocks[k][:WIN]

        @pl.when((core == 1) & (t == 3))
        def _():
            border[...] = blocks[k][128 - WIN :]


def lay_kernel(at, *refs):
    blocks, out = refs[:4], refs[4]
    for k in range(4):
        base = lax.rem(at[2] + k, 4) * 32
        for z in range(8):
            out[pl.ds(pl.multiple_of(z * 128 + base, 32), 32)] = blocks[k][z]


def attend(query, kv, first, count, key_start):
    lower = jnp.broadcast_to(first, (128, 128)).T
    upper = lower + jnp.broadcast_to(count, (128, 128)).T
    index = key_start + lax.broadcasted_iota(jnp.int32, (128, 256), 1)
    lower = jnp.concatenate([lower, lower], axis=1)
    upper = jnp.concatenate([upper, upper], axis=1)
    allowed = (index >= lower) & (index < upper)
    outs = []
    for h in range(2):
        lanes = slice(h * 64, h * 64 + 64)
        score = lax.dot_general(query[:, lanes], kv[:, lanes], NT, preferred_element_type=F32)
        weight = jnp.where(allowed, jnp.exp(score * 0.125), 0.0)
        total = jnp.sum(weight, axis=-1, keepdims=True)
        prob = (weight / total).astype(BF16)
        value = kv[:, 128 + h * 64 : 192 + h * 64]
        outs.append(jnp.dot(prob, value, preferred_element_type=F32))
    return jnp.concatenate(outs, axis=1).astype(BF16)


def attention_kernel(at, *refs):
    own, peer, blocks = refs[0], refs[1], refs[2:6]
    near_own, near_peer, gain, first, count, att, weight, q_s, kv_s = refs[6:]
    core, anchor = at[1], at[3]
    for k in range(4):
        base = lax.rem(at[2] + k, 4) * 32
        for z in range(8):
            weight[pl.ds(pl.multiple_of(z * 128 + base, 32), 32)] = blocks[k][z]

    rows = jnp.concatenate([near_own[...], near_peer[...]], axis=0)
    part = jnp.dot(rows, weight[:, 128:], preferred_element_type=F32)
    key = head_norm(part[:, :128], gain[1:2], first_half(2 * WIN))
    kv = jnp.concatenate([key, part[:, 128:].astype(BF16)], axis=1)
    end = WIN + 1024
    kv_s[pl.ds(pl.multiple_of((1 - core) * end, WIN), WIN)] = kv[:WIN]
    kv_s[pl.ds(pl.multiple_of(core * end, WIN), WIN)] = kv[WIN:]

    half = first_half(256)
    for t in range(4):
        rows = jnp.concatenate([own[t], peer[t]], axis=0)
        qkv = jnp.dot(rows, weight[...], preferred_element_type=F32)
        query = head_norm(qkv[:, :128], gain[0:1], half)
        key = head_norm(qkv[:, 128:256], gain[1:2], half)
        kv = jnp.concatenate([key, qkv[:, 256:].astype(BF16)], axis=1)
        mine = pl.multiple_of(t * 256 + core * 128, 128)
        theirs = pl.multiple_of(t * 256 + (1 - core) * 128, 128)
        q_s[pl.ds(mine, 128)] = query[:128]
        q_s[pl.ds(theirs, 128)] = query[128:]
        kv_s[pl.ds(pl.multiple_of(mine + WIN, WIN), 128)] = kv[:128]
        kv_s[pl.ds(pl.multiple_of(theirs + WIN, WIN), 128)] = kv[128:]
    for b in range(8):
        att[lax.rem(core + b, 2), b // 2] = attend(
            q_s[b * 128 : b * 128 + 128],
            kv_s[b * 128 : b * 128 + 256],
            first[b : b + 1],
            count[b : b + 1],
            anchor + (b * 128 - WIN),
        )


def project_kernel(at, att, got, weight, other, mine, away):
    y = at[0]
    for k in (2, 1, 3, 0):
        t = lax.rem(y + k, 4)
        part = lax.dot_general(
            att[0, t], weight[...], NT, preferred_element_type=F32
        ) + lax.dot_general(got[t], other[...], NT, preferred_element_type=F32)
        if k == 0:
            mine[...] = part
        else:
            away[k - 1] = part.astype(BF16)


def middle_kernel(tok, mine, a, b, c, gain, middle, normed):
    total = mine[...] + a[...].astype(F32) + b[...].astype(F32) + c[...].astype(F32)
    mid = (tok[...].astype(F32) + total).astype(BF16)
    middle[...] = mid
    normed[...] = layer_norm(mid.astype(F32), gain[...])


def mlp_kernel(rows, up_own, down_own, up_peer, down_peer, out, total):
    step = pl.program_id(0)
    up = jnp.concatenate([up_own[...], up_peer[...]], axis=1)
    down = jnp.concatenate([down_own[...], down_peer[...]], axis=1)
    hidden = jax.nn.gelu(
        jnp.dot(rows[...], up, preferred_element_type=F32), approximate=True
    ).astype(BF16)
    part = lax.dot_general(hidden, down, NT, preferred_element_type=F32)

    @pl.when(step == 0)
    def _():
        total[...] = part

    @pl.when(step == 1)
    def _():
        out[...] = (total[...] + part).astype(out.dtype)


def mlp(rows, own, peer, dtype):
    block = lambda at: pl.BlockSpec((1024, 256), lambda i, at=at: (0, at + i))
    whole = pl.BlockSpec((128, 1024), lambda i: (0, 0))
    return pl.pallas_call(
        mlp_kernel,
        grid=(2,),
        out_shape=jax.ShapeDtypeStruct((128, 1024), dtype),
        in_specs=[whole, block(0), block(2), block(0), block(2)],
        out_specs=whole,
        scratch_shapes=[pltpu.VMEM((128, 1024), F32)],
        compiler_params=params(8),
        cost_estimate=pl.CostEstimate(flops=4 * 128 * 2**20, bytes_accessed=5 * 2**20, transcendentals=2**17),
        name="mlp",
    )(rows, own, own, peer, peer)


def end_kernel(middle, mine, a, b, c, out):
    total = middle[...].astype(F32) + mine[...]
    total += a[...].astype(F32) + b[...].astype(F32) + c[...].astype(F32)
    out[...] = total.astype(BF16)


def call(kernel, outs, specs, name, mib=8, scratch=(), flops=2**20, **more):
    return pl.pallas_call(
        kernel,
        out_shape=[jax.ShapeDtypeStruct(s, d) for s, d in outs],
        in_specs=specs,
        out_specs=[VMEM] * len(outs),
        scratch_shapes=list(scratch),
        compiler_params=params(mib),
        cost_estimate=pl.CostEstimate(flops=flops, bytes_accessed=2**21, transcendentals=0),
        name=name,
        **more,
    )


def fetch(value, axis, step):
    n = lax.axis_size(axis)
    return lax.ppermute(value, axis, [((i + step) % n, i) for i in range(n)])


def local(
    tokens,
    win_first,
    win_count,
    norm1_gain,
    qkv_weight,
    qk_gain,
    out_weight,
    norm2_gain,
    up_weight,
    down_weight,
):
    y, core = lax.axis_index("y"), lax.axis_index("core")
    seq = lax.axis_index("z") * lax.axis_size("x") + lax.axis_index("x")
    at = jnp.stack([y, core, lax.axis_index("x"), seq * 1024]).astype(jnp.int32)
    first, count = win_first.reshape(8, 128), win_count.reshape(8, 128)
    gain = qk_gain.reshape(2, 128)

    normed, front = call(
        start_kernel,
        [((128, 1024), BF16), ((8, 32, 512), BF16)],
        [VMEM] * 4,
        "start",
    )(
        tokens,
        norm1_gain.reshape(1, 1024),
        jnp.transpose(qkv_weight, (1, 0, 2)),
        out_weight.T,
    )
    (back,) = call(mlp_pack_kernel, [((8, 32, 1024), BF16)], [VMEM] * 2, "mlp_pack")(
        up_weight, down_weight.T
    )
    front = lax.all_to_all(front, "z", 0, 0, tiled=True)
    front, out_block = front[:, :, :384], front[:, :, 384:]
    far = {k: fetch(normed, "y", k) for k in (2, 1, 3)}
    blocks = [front] + [fetch(front, "x", k) for k in (1, 2, 3)]
    back, _ = lax.optimization_barrier((back, front))
    back = lax.all_to_all(back, "z", 0, 0, tiled=True)
    far, _ = lax.optimization_barrier((far, (blocks[1], blocks[3])))
    own, border = call(
        collect_kernel,
        [((4, 128, 1024), BF16), ((WIN, 1024), BF16)],
        [SMEM] + [VMEM] * 4,
        "collect",
    )(at, normed, far[1], far[2], far[3])
    peer = fetch(own, "core", 1)
    out_block, _ = lax.optimization_barrier((out_block, blocks))
    out_blocks = [out_block] + [fetch(out_block, "x", k) for k in (1, 2, 3)]
    spot = lambda z, x, y, core: ((z * 4 + x) * 4 + y) * 2 + core
    shift = lambda s, by: divmod((s + by) % 32, 4)
    near_own = lax.ppermute(
        border,
        ("z", "x", "y", "core"),
        [
            (spot(*divmod(s, 4), j, c), spot(*shift(s, 2 * c - 1), j, c))
            for s in range(32)
            for j in range(4)
            for c in range(2)
        ],
    )
    near_peer = fetch(near_own, "core", 1)
    (att,) = call(
        attention_kernel,
        [((2, 4, 128, 128), BF16)],
        [SMEM] + [VMEM] * 11,
        "attention",
        scratch=[
            pltpu.VMEM((1024, 384), BF16),
            pltpu.VMEM((1024, 128), BF16),
            pltpu.VMEM((1024 + 2 * WIN, 256), BF16),
        ],
        flops=5 * 2**30,
    )(at, own, peer, *blocks, near_own, near_peer, gain, first, count)

    mlp_block, _ = lax.optimization_barrier((back, (att, out_blocks)))
    mlp_blocks = [mlp_block] + [fetch(mlp_block, "x", k) for k in (1, 2, 3)]

    def laid(blocks, width, after, name):
        blocks, _ = lax.optimization_barrier((blocks, after))
        (out,) = call(lay_kernel, [((1024, width), BF16)], [SMEM] + [VMEM] * 4, name)(at, *blocks)
        return out

    weight = laid(out_blocks, 128, att, "out_lay")
    out_peer = fetch(weight, "core", 1)
    got = fetch(att[1], "core", 1)
    mine_attended, away = call(
        project_kernel,
        [((128, 1024), F32), ((3, 128, 1024), BF16)],
        [SMEM] + [VMEM] * 4,
        "project",
    )(at, att, got, weight, out_peer)
    parts = [fetch(away[k - 1], "y", 4 - k) for k in (2, 1, 3)]
    middle, normed_two = call(
        middle_kernel,
        [((128, 1024), BF16)] * 2,
        [VMEM] * 6,
        "middle",
    )(tokens, mine_attended, *parts, norm2_gain.reshape(1, 1024))

    far = {k: fetch(normed_two, "y", k) for k in (2, 1, 3)}
    mlp_own = laid(mlp_blocks, 1024, far, "mlp_lay")
    mlp_peer = fetch(mlp_own, "core", 1)
    mine = mlp(normed_two, mlp_own, mlp_peer, F32)
    parts = [fetch(mlp(far[k], mlp_own, mlp_peer, BF16), "y", 4 - k) for k in (3, 2, 1)]
    (out,) = call(end_kernel, [((128, 1024), BF16)], [VMEM] * 5, "end")(middle, mine, *parts)
    return out


def solution(mesh):
    fine = Mesh(mesh.devices.reshape(8, 4, 4, 2), ("z", "x", "y", "core"))
    seq, head = ("z", "x"), ("y", "core")
    return jax.shard_map(
        local,
        mesh=fine,
        in_specs=(
            P(seq + head, None),
            P(seq),
            P(seq),
            P(),
            P(seq, None, head),
            P(None, head, None),
            P(head, seq),
            P(),
            P(seq, head),
            P(head, seq),
        ),
        out_specs=P(seq + head, None),
        check_vma=False,
    )
```

time: 141 us -> 128 us (0.908)
  between operations: 13.7 us -> 0.25 us
  starting transfers between devices: 52.6 us -> 59.6 us
  waiting for transfers between devices: 48.7 us -> 44.9 us
  local copies, waits for them, and re-layouts: 6.66 us -> 3.29 us
    ppermute x19 -> x26, starting transfers between devices: 35.9 us -> 45.9 us  [fetch(): return lax.ppermute(value, axis, [((i + step) % n, i) for i in range(n)])]
    all_gather x1 -> x0, waiting for transfers between devices: 5.89 us -> none  [local(): mlp_own = lax.all_gather(back, ('z', 'x'), axis=0, tiled=True)]
    ppermute x19 -> x26, waiting for transfers between devices: 33.9 us -> 28.2 us  [fetch(): return lax.ppermute(value, axis, [((i + step) % n, i) for i in range(n)])]
    ppermute x2 -> x1, waiting for transfers between devices: 0.01 us -> 4.21 us  [local(): lax.ppermute(border, ('z', 'x', 'y', 'core'), [(spot(*divmod(s, 4), j, c)...]
    ppermute x2 -> x1, starting transfers between devices: 4.86 us -> 1.21 us  [local(): lax.ppermute(border, ('z', 'x', 'y', 'core'), [(spot(*divmod(s, 4), j, c)...]
    all_to_all x1 -> x2, waiting for transfers between devices: 8.92 us -> 12.4 us  [the longest x1 7.04 us: local(): back = lax.all_to_all(back, 'z', 0, 0, tiled=True)]
    unnamed x23 -> x22, local copies, waits for them, and re-layouts: 6.48 us -> 3.11 us
    pallas_call x4 -> x6, Pallas kernels: 7.67 us -> 8.56 us  [the longest x1 4.91 us: local(): call(attention_kernel, [((2, 4, 128, 128), BF16)], [SMEM] + [VMEM] * 11,...]
  transfers between devices with their start and end apart: 23 -> 29, of which waited for: 10 -> 12; matrix products, arithmetic and copies ran while one was open for 0% -> 0% of each run, Pallas kernels for 12% -> 10%
where the time goes in v1:
time: 128 us
  starting transfers between devices  59.6 us (47%)
  waiting for transfers between devices  44.9 us (35%)
  Pallas kernels  19.5 us (15%)
  local copies, waits for them, and re-layouts  3.29 us (3%)
    ppermute x26, starting transfers between devices, fetch(): return lax.ppermute(value, axis, [((i + step) % n, i) for i in range(n)])  45.9 us
    ppermute x26, waiting for transfers between devices, fetch(): return lax.ppermute(value, axis, [((i + step) % n, i) for i in range(n)])  28.2 us
    all_to_all x1, starting transfers between devices, local(): front = lax.all_to_all(front, 'z', 0, 0, tiled=True)  9.01 us
    pallas_call x4, Pallas kernels, mlp(): pl.pallas_call(mlp_kernel, grid=(2,), out_shape=jax.ShapeDtypeStruct((128...  8.46 us
    all_to_all x1, waiting for transfers between devices, local(): back = lax.all_to_all(back, 'z', 0, 0, tiled=True)  7.04 us
    all_to_all x1, waiting for transfers between devices, local(): front = lax.all_to_all(front, 'z', 0, 0, tiled=True)  5.38 us
    pallas_call x1, Pallas kernels, local(): call(attention_kernel, [((2, 4, 128, 128), BF16)], [SMEM] + [VMEM] * 11,...  4.91 us
    ppermute x1, waiting for transfers between devices, local(): lax.ppermute(border, ('z', 'x', 'y', 'core'), [(spot(*divmod(s, 4), j, c)...  4.21 us
  transfers between devices with their start and end apart: 29, of which 12 were waited for; matrix products, arithmetic and copies ran while one was open for 0% of the time, Pallas kernels for 10%

profile of v1, /device:TPU:1, one launch (start us, length us, event | category | flops | bytes accessed | tf_op | source)
XLA Modules:
  0.0 127.6 jit_solution(8030957826373828155)
XLA Ops:
  4.0 9.0 %all-to-all-start = ((bf16[8,32,512]{2,1,0:T(8,128)(2,1)}), bf16[8,32,512]{2,1,0:T(8,128)(2,1)S(1)}, u32[]{:S(2)}, u32[]{:S(2)}) async-start(bf16[8,32,512]{2,1,0:T(8,128)(2,1)} %get-tuple-element.28), calls=%async_computation | async-start | bytes 524288 | tf_op jit(solution)/shard_map/all_to_all | solution.py:246
  14.3 2.6 %collective-permute-start.1 = (bf16[128,1024]{1,0:T(8,128)(2,1)S(1)}, bf16[128,1024]{1,0:T(8,128)(2,1)S(1)}, u32[]{:S(2)}, u32[]{:S(2)}) collective-permute-start(bf16[128,1024]{1,0:T(8,128)(2,1)S(1)} %get-tuple-element.27.refs_0_), channel_id=1, source_target_pairs={{4,0},{6,2},{0,4},{2,6},{5,1},{7,3},{1,5},{3,7},{12,8},{14,10},{8,... | collective-permute-start | bytes 786440 | tf_op jit(solution)/shard_map/ppermute | solution.py:211
  18.0 5.4 %all-to-all-done = bf16[8,32,512]{2,1,0:T(8,128)(2,1)S(1)} async-done(((bf16[8,32,512]{2,1,0:T(8,128)(2,1)}), bf16[8,32,512]{2,1,0:T(8,128)(2,1)S(1)}, u32[]{:S(2)}, u32[]{:S(2)}) %all-to-all-start) | async-done | bytes 262176 | tf_op jit(solution)/shard_map/all_to_all | solution.py:246
  30.1 3.8 %collective-permute-start.5 = (bf16[4,128,1024]{2,1,0:T(8,128)(2,1)S(1)}, bf16[4,128,1024]{2,1,0:T(8,128)(2,1)}, u32[]{:S(2)}, u32[]{:S(2)}) collective-permute-start(bf16[4,128,1024]{2,1,0:T(8,128)(2,1)S(1)} %get-tuple-element.32.refs_0_), channel_id=1, source_target_pairs={{1,0},{0,1},{3,2},{2,3},{5,4},{4,5},{7,6},{6,7},{9,8},{8,9},{11,10... | collective-permute-start | bytes 3145736 | tf_op jit(solution)/shard_map/ppermute | solution.py:211
  35.1 2.6 %collective-permute-start.6 = (bf16[8,32,384]{2,1,0:T(8,128)(2,1)S(1)}, bf16[8,32,384]{2,1,0:T(8,128)(2,1)S(1)}, u32[]{:S(2)}, u32[]{:S(2)}) collective-permute-start(bf16[8,32,384]{2,1,0:T(8,128)(2,1)S(1)} %slice.24.refs_2_), channel_id=1, source_target_pairs={{16,0},{24,8},{0,16},{8,24},{17,1},{25,9},{1,17},{9,25},{18,2},{26... | collective-permute-start | bytes 589832 | tf_op jit(solution)/shard_map/ppermute | solution.py:211
  37.7 4.2 %collective-permute-done.7.refs_6_ = bf16[64,1024]{1,0:T(8,128)(2,1)S(1)} collective-permute-done((bf16[64,1024]{1,0:T(8,128)(2,1)S(1)}, bf16[64,1024]{1,0:T(8,128)(2,1)S(1)}, u32[]{:S(2)}, u32[]{:S(2)}) %collective-permute-start.7) | collective-permute-done | bytes 131104 | tf_op jit(solution)/shard_map/ppermute | solution.py:264
  42.8 3.5 %all-to-all-start.1 = ((bf16[8,32,1024]{2,1,0:T(8,128)(2,1)}), bf16[8,32,1024]{2,1,0:T(8,128)(2,1)S(1)}, u32[]{:S(2)}, u32[]{:S(2)}) async-start(bf16[8,32,1024]{2,1,0:T(8,128)(2,1)} %mlp_pack.1), calls=%async_computation.1 | async-start | bytes 1048576 | tf_op jit(solution)/shard_map/all_to_all | solution.py:251
  46.5 4.3 %collective-permute-start.11 = (bf16[8,32,128]{2,1,0:T(8,128)(2,1)S(1)}, bf16[8,32,128]{2,1,0:T(8,128)(2,1)S(1)}, u32[]{:S(2)}, u32[]{:S(2)}) collective-permute-start(bf16[8,32,128]{2,1,0:T(8,128)(2,1)S(1)} %slice.26.refs_0_), channel_id=1, source_target_pairs={{16,0},{24,8},{0,16},{8,24},{17,1},{25,9},{1,17},{9,25},{18,2},{26... | collective-permute-start | bytes 196616 | tf_op jit(solution)/shard_map/ppermute | solution.py:211
  50.9 4.9 %attention.1.att = bf16[2,4,128,128]{3,2,1,0:T(8,128)(2,1)S(1)} custom-call(s32[4]{0:T(128)S(1)} %pad_add_fusion.at, bf16[4,128,1024]{2,1,0:T(8,128)(2,1)S(1)} %get-tuple-element.32.refs_0_, bf16[4,128,1024]{2,1,0:T(8,128)(2,1)} %collective-permute-done.5.refs_1_, bf16[8,32,384]{2,1,0:T(8,128)(2,1)S(1)} %slice.24.refs_2_, ...), custom_call_target="tpu_custom_call" | custom-call | flops 5368709120 | bytes 2097152 | tf_op jit(solution)/shard_map/attention/pallas_call | solution.py:275
  57.2 7.0 %all-to-all-done.1.refs_0_ = bf16[8,32,1024]{2,1,0:T(8,128)(2,1)S(1)} async-done(((bf16[8,32,1024]{2,1,0:T(8,128)(2,1)}), bf16[8,32,1024]{2,1,0:T(8,128)(2,1)S(1)}, u32[]{:S(2)}, u32[]{:S(2)}) %all-to-all-start.1) | async-done | bytes 524320 | tf_op jit(solution)/shard_map/all_to_all | solution.py:251
  65.5 2.5 %collective-permute-start.16 = (bf16[128,1024]{1,0:T(8,128)(2,1)S(1)}, bf16[128,1024]{1,0:T(8,128)(2,1)S(1)}, u32[]{:S(2)}, u32[]{:S(2)}) collective-permute-start(bf16[128,1024]{1,0:T(8,128)(2,1)S(1)} %get-tuple-element.49), channel_id=1, source_target_pairs={{2,0},{4,2},{6,4},{0,6},{3,1},{5,3},{7,5},{1,7},{10,8},{12,10},{14... | collective-permute-start | bytes 786440 | tf_op jit(solution)/shard_map/ppermute | solution.py:211
  69.9 4.5 %collective-permute-start.18 = (bf16[8,32,1024]{2,1,0:T(8,128)(2,1)S(1)}, bf16[8,32,1024]{2,1,0:T(8,128)(2,1)S(1)}, u32[]{:S(2)}, u32[]{:S(2)}) collective-permute-start(bf16[8,32,1024]{2,1,0:T(8,128)(2,1)S(1)} %all-to-all-done.1.refs_0_), channel_id=1, source_target_pairs={{16,0},{24,8},{0,16},{8,24},{17,1},{25,9},{1,17},{9,25},{18,2},{26... | collective-permute-start | bytes 1572872 | tf_op jit(solution)/shard_map/ppermute | solution.py:211
  74.4 7.9 %collective-permute-start.17 = (bf16[8,32,1024]{2,1,0:T(8,128)(2,1)S(1)}, bf16[8,32,1024]{2,1,0:T(8,128)(2,1)S(1)}, u32[]{:S(2)}, u32[]{:S(2)}) collective-permute-start(bf16[8,32,1024]{2,1,0:T(8,128)(2,1)S(1)} %all-to-all-done.1.refs_0_), channel_id=1, source_target_pairs={{8,0},{16,8},{24,16},{0,24},{9,1},{17,9},{25,17},{1,25},{10,2},{18... | collective-permute-start | bytes 1572872 | tf_op jit(solution)/shard_map/ppermute | solution.py:211
  82.7 4.7 %collective-permute-start.21 = (bf16[128,1024]{1,0:T(8,128)(2,1)S(1)}, bf16[128,1024]{1,0:T(8,128)(2,1)S(1)}, u32[]{:S(2)}, u32[]{:S(2)}) collective-permute-start(bf16[128,1024]{1,0:T(8,128)(2,1)S(1)} %get-tuple-element.42.rows), channel_id=1, source_target_pairs={{4,0},{6,2},{0,4},{2,6},{5,1},{7,3},{1,5},{3,7},{12,8},{14,10},{8,... | collective-permute-start | bytes 786440 | tf_op jit(solution)/shard_map/ppermute | solution.py:211
  87.5 7.8 %collective-permute-done.18.refs_2_ = bf16[8,32,1024]{2,1,0:T(8,128)(2,1)S(1)} collective-permute-done((bf16[8,32,1024]{2,1,0:T(8,128)(2,1)S(1)}, bf16[8,32,1024]{2,1,0:T(8,128)(2,1)S(1)}, u32[]{:S(2)}, u32[]{:S(2)}) %collective-permute-start.18) | collective-permute-done | bytes 524320 | tf_op jit(solution)/shard_map/ppermute | solution.py:211
  95.8 2.1 %collective-permute-done.21.rows = bf16[128,1024]{1,0:T(8,128)(2,1)S(1)} collective-permute-done((bf16[128,1024]{1,0:T(8,128)(2,1)S(1)}, bf16[128,1024]{1,0:T(8,128)(2,1)S(1)}, u32[]{:S(2)}, u32[]{:S(2)}) %collective-permute-start.21) | collective-permute-done | bytes 262176 | tf_op jit(solution)/shard_map/ppermute | solution.py:211
  99.0 2.3 %collective-permute-start.23 = (bf16[1024,1024]{1,0:T(8,128)(2,1)S(1)}, bf16[1024,1024]{1,0:T(8,128)(2,1)S(1)}, u32[]{:S(2)}, u32[]{:S(2)}) collective-permute-start(bf16[1024,1024]{1,0:T(8,128)(2,1)S(1)} %mlp_lay.1.up_own.down_own), channel_id=1, source_target_pairs={{1,0},{0,1},{3,2},{2,3},{5,4},{4,5},{7,6},{6,7},{9,8},{8,9},{11,10... | collective-permute-start | bytes 6291464 | tf_op jit(solution)/shard_map/ppermute | solution.py:211
  101.3 3.8 %collective-permute-done.23.up_peer.down_peer = bf16[1024,1024]{1,0:T(8,128)(2,1)S(1)} collective-permute-done((bf16[1024,1024]{1,0:T(8,128)(2,1)S(1)}, bf16[1024,1024]{1,0:T(8,128)(2,1)S(1)}, u32[]{:S(2)}, u32[]{:S(2)}) %collective-permute-start.23) | collective-permute-done | bytes 2097184 | tf_op jit(solution)/shard_map/ppermute | solution.py:211
  105.1 2.1 %mlp.5 = bf16[128,1024]{1,0:T(8,128)(2,1)S(1)} custom-call(bf16[128,1024]{1,0:T(8,128)(2,1)S(1)} %collective-permute-done.22.rows, bf16[1024,1024]{1,0:T(8,128)(2,1)S(1)} %mlp_lay.1.up_own.down_own, bf16[1024,1024]{1,0:T(8,128)(2,1)S(1)} %mlp_lay.1.up_own.down_own, bf16[1024,1024]{1,0:T(8,128)(2,1)S(1)} %collective-permute-done.23.up_peer.down_peer, ...), custom_call_target="tpu_custom_call" | custom-call | flops 536870912 | bytes 5242880 | tf_op jit(solution)/shard_map/mlp/pallas_call | solution.py:176
  109.2 2.1 %mlp.6 = bf16[128,1024]{1,0:T(8,128)(2,1)S(1)} custom-call(bf16[128,1024]{1,0:T(8,128)(2,1)S(1)} %collective-permute-done.21.rows, bf16[1024,1024]{1,0:T(8,128)(2,1)S(1)} %mlp_lay.1.up_own.down_own, bf16[1024,1024]{1,0:T(8,128)(2,1)S(1)} %mlp_lay.1.up_own.down_own, bf16[1024,1024]{1,0:T(8,128)(2,1)S(1)} %collective-permute-done.23.up_peer.down_peer, ...), custom_call_target="tpu_custom_call" | custom-call | flops 536870912 | bytes 5242880 | tf_op jit(solution)/shard_map/mlp/pallas_call | solution.py:176
  111.4 2.1 %mlp.7 = bf16[128,1024]{1,0:T(8,128)(2,1)S(1)} custom-call(bf16[128,1024]{1,0:T(8,128)(2,1)S(1)} %collective-permute-done.20.rows, bf16[1024,1024]{1,0:T(8,128)(2,1)S(1)} %mlp_lay.1.up_own.down_own, bf16[1024,1024]{1,0:T(8,128)(2,1)S(1)} %mlp_lay.1.up_own.down_own, bf16[1024,1024]{1,0:T(8,128)(2,1)S(1)} %collective-permute-done.23.up_peer.down_peer, ...), custom_call_target="tpu_custom_call" | custom-call | flops 536870912 | bytes 5242880 | tf_op jit(solution)/shard_map/mlp/pallas_call | solution.py:176
  114.2 2.1 %mlp.4.mine = f32[128,1024]{1,0:T(8,128)S(1)} custom-call(bf16[128,1024]{1,0:T(8,128)(2,1)S(1)} %get-tuple-element.42.rows, bf16[1024,1024]{1,0:T(8,128)(2,1)S(1)} %mlp_lay.1.up_own.down_own, bf16[1024,1024]{1,0:T(8,128)(2,1)S(1)} %mlp_lay.1.up_own.down_own, bf16[1024,1024]{1,0:T(8,128)(2,1)S(1)} %collective-permute-done.23.up_peer.down_peer, ...), custom_call_target="tpu_custom_call" | custom-call | flops 536870912 | bytes 5242880 | tf_op jit(solution)/shard_map/mlp/pallas_call | solution.py:176
  116.3 3.8 %collective-permute-done.25.b = bf16[128,1024]{1,0:T(8,128)(2,1)S(1)} collective-permute-done((bf16[128,1024]{1,0:T(8,128)(2,1)S(1)}, bf16[128,1024]{1,0:T(8,128)(2,1)S(1)}, u32[]{:S(2)}, u32[]{:S(2)}) %collective-permute-start.25) | collective-permute-done | bytes 262176 | tf_op jit(solution)/shard_map/ppermute | solution.py:211
  120.1 6.6 %collective-permute-done.26.c = bf16[128,1024]{1,0:T(8,128)(2,1)S(1)} collective-permute-done((bf16[128,1024]{1,0:T(8,128)(2,1)S(1)}, bf16[128,1024]{1,0:T(8,128)(2,1)S(1)}, u32[]{:S(2)}, u32[]{:S(2)}) %collective-permute-start.26) | collective-permute-done | bytes 262176 | tf_op jit(solution)/shard_map/ppermute | solution.py:211
  (75 shorter events, 25.5 us)
Async XLA Ops:
  4.0 19.4 %all-to-all-start = ((bf16[8,32,512]{2,1,0:T(8,128)(2,1)}), bf16[8,32,512]{2,1,0:T(8,128)(2,1)S(1)}, u32[]{:S(2)}, u32[]{:S(2)}) async-start(bf16[8,32,512]{2,1,0:T(8,128)(2,1)} %get-tuple-element.28), calls=%async_computation | async-start | bytes 524288 | tf_op jit(solution)/shard_map/all_to_all | solution.py:246
  13.0 13.2 %collective-permute-start.2 = (bf16[128,1024]{1,0:T(8,128)(2,1)S(1)}, bf16[128,1024]{1,0:T(8,128)(2,1)S(1)}, u32[]{:S(2)}, u32[]{:S(2)}) collective-permute-start(bf16[128,1024]{1,0:T(8,128)(2,1)S(1)} %get-tuple-element.27.refs_0_), channel_id=1, source_target_pairs={{6,0},{0,2},{2,4},{4,6},{7,1},{1,3},{3,5},{5,7},{14,8},{8,10},{10,... | collective-permute-start | bytes 786440 | tf_op jit(solution)/shard_map/ppermute | solution.py:211
  14.3 13.6 %collective-permute-start.1 = (bf16[128,1024]{1,0:T(8,128)(2,1)S(1)}, bf16[128,1024]{1,0:T(8,128)(2,1)S(1)}, u32[]{:S(2)}, u32[]{:S(2)}) collective-permute-start(bf16[128,1024]{1,0:T(8,128)(2,1)S(1)} %get-tuple-element.27.refs_0_), channel_id=1, source_target_pairs={{4,0},{6,2},{0,4},{2,6},{5,1},{7,3},{1,5},{3,7},{12,8},{14,10},{8,... | collective-permute-start | bytes 786440 | tf_op jit(solution)/shard_map/ppermute | solution.py:211
  16.9 11.0 %collective-permute-start = (bf16[128,1024]{1,0:T(8,128)(2,1)S(1)}, bf16[128,1024]{1,0:T(8,128)(2,1)S(1)}, u32[]{:S(2)}, u32[]{:S(2)}) collective-permute-start(bf16[128,1024]{1,0:T(8,128)(2,1)S(1)} %get-tuple-element.27.refs_0_), channel_id=1, source_target_pairs={{2,0},{4,2},{6,4},{0,6},{3,1},{5,3},{7,5},{1,7},{10,8},{12,10},{14... | collective-permute-start | bytes 786440 | tf_op jit(solution)/shard_map/ppermute | solution.py:211
  30.1 20.8 %collective-permute-start.5 = (bf16[4,128,1024]{2,1,0:T(8,128)(2,1)S(1)}, bf16[4,128,1024]{2,1,0:T(8,128)(2,1)}, u32[]{:S(2)}, u32[]{:S(2)}) collective-permute-start(bf16[4,128,1024]{2,1,0:T(8,128)(2,1)S(1)} %get-tuple-element.32.refs_0_), channel_id=1, source_target_pairs={{1,0},{0,1},{3,2},{2,3},{5,4},{4,5},{7,6},{6,7},{9,8},{8,9},{11,10... | collective-permute-start | bytes 3145736 | tf_op jit(solution)/shard_map/ppermute | solution.py:211
  33.9 8.1 %collective-permute-start.7 = (bf16[64,1024]{1,0:T(8,128)(2,1)S(1)}, bf16[64,1024]{1,0:T(8,128)(2,1)S(1)}, u32[]{:S(2)}, u32[]{:S(2)}) collective-permute-start(bf16[64,1024]{1,0:T(8,128)(2,1)S(1)} %get-tuple-element.33), channel_id=1, source_target_pairs={{0,248},{1,9},{2,250},{3,11},{4,252},{5,13},{6,254},{7,15},{8,0},{... | collective-permute-start | bytes 393224 | tf_op jit(solution)/shard_map/ppermute | solution.py:264
  35.1 11.3 %collective-permute-start.6 = (bf16[8,32,384]{2,1,0:T(8,128)(2,1)S(1)}, bf16[8,32,384]{2,1,0:T(8,128)(2,1)S(1)}, u32[]{:S(2)}, u32[]{:S(2)}) collective-permute-start(bf16[8,32,384]{2,1,0:T(8,128)(2,1)S(1)} %slice.24.refs_2_), channel_id=1, source_target_pairs={{16,0},{24,8},{0,16},{8,24},{17,1},{25,9},{1,17},{9,25},{18,2},{26... | collective-permute-start | bytes 589832 | tf_op jit(solution)/shard_map/ppermute | solution.py:211
  41.9 8.9 %collective-permute-start.8 = (bf16[64,1024]{1,0:T(8,128)(2,1)S(1)}, bf16[64,1024]{1,0:T(8,128)(2,1)S(1)}, u32[]{:S(2)}, u32[]{:S(2)}) collective-permute-start(bf16[64,1024]{1,0:T(8,128)(2,1)S(1)} %collective-permute-done.7.refs_6_), channel_id=1, source_target_pairs={{1,0},{0,1},{3,2},{2,3},{5,4},{4,5},{7,6},{6,7},{9,8},{8,9},{11,10... | collective-permute-start | bytes 393224 | tf_op jit(solution)/shard_map/ppermute | solution.py:211
  42.8 21.5 %all-to-all-start.1 = ((bf16[8,32,1024]{2,1,0:T(8,128)(2,1)}), bf16[8,32,1024]{2,1,0:T(8,128)(2,1)S(1)}, u32[]{:S(2)}, u32[]{:S(2)}) async-start(bf16[8,32,1024]{2,1,0:T(8,128)(2,1)} %mlp_pack.1), calls=%async_computation.1 | async-start | bytes 1048576 | tf_op jit(solution)/shard_map/all_to_all | solution.py:251
  46.4 9.4 %collective-permute-start.12 = (bf16[8,32,128]{2,1,0:T(8,128)(2,1)S(1)}, bf16[8,32,128]{2,1,0:T(8,128)(2,1)S(1)}, u32[]{:S(2)}, u32[]{:S(2)}) collective-permute-start(bf16[8,32,128]{2,1,0:T(8,128)(2,1)S(1)} %slice.26.refs_0_), channel_id=1, source_target_pairs={{24,0},{0,8},{8,16},{16,24},{25,1},{1,9},{9,17},{17,25},{26,2},{2,... | collective-permute-start | bytes 196616 | tf_op jit(solution)/shard_map/ppermute | solution.py:211
  46.5 9.3 %collective-permute-start.11 = (bf16[8,32,128]{2,1,0:T(8,128)(2,1)S(1)}, bf16[8,32,128]{2,1,0:T(8,128)(2,1)S(1)}, u32[]{:S(2)}, u32[]{:S(2)}) collective-permute-start(bf16[8,32,128]{2,1,0:T(8,128)(2,1)S(1)} %slice.26.refs_0_), channel_id=1, source_target_pairs={{16,0},{24,8},{0,16},{8,24},{17,1},{25,9},{1,17},{9,25},{18,2},{26... | collective-permute-start | bytes 196616 | tf_op jit(solution)/shard_map/ppermute | solution.py:211
  56.4 7.8 %collective-permute-start.13 = (bf16[1024,128]{1,0:T(8,128)(2,1)S(1)}, bf16[1024,128]{1,0:T(8,128)(2,1)S(1)}, u32[]{:S(2)}, u32[]{:S(2)}) collective-permute-start(bf16[1024,128]{1,0:T(8,128)(2,1)S(1)} %out_lay.1.weight), channel_id=1, source_target_pairs={{1,0},{0,1},{3,2},{2,3},{5,4},{4,5},{7,6},{6,7},{9,8},{8,9},{11,10... | collective-permute-start | bytes 786440 | tf_op jit(solution)/shard_map/ppermute | solution.py:211
  65.5 8.8 %collective-permute-start.16 = (bf16[128,1024]{1,0:T(8,128)(2,1)S(1)}, bf16[128,1024]{1,0:T(8,128)(2,1)S(1)}, u32[]{:S(2)}, u32[]{:S(2)}) collective-permute-start(bf16[128,1024]{1,0:T(8,128)(2,1)S(1)} %get-tuple-element.49), channel_id=1, source_target_pairs={{2,0},{4,2},{6,4},{0,6},{3,1},{5,3},{7,5},{1,7},{10,8},{12,10},{14... | collective-permute-start | bytes 786440 | tf_op jit(solution)/shard_map/ppermute | solution.py:211
  68.1 19.4 %collective-permute-start.19 = (bf16[8,32,1024]{2,1,0:T(8,128)(2,1)S(1)}, bf16[8,32,1024]{2,1,0:T(8,128)(2,1)S(1)}, u32[]{:S(2)}, u32[]{:S(2)}) collective-permute-start(bf16[8,32,1024]{2,1,0:T(8,128)(2,1)S(1)} %all-to-all-done.1.refs_0_), channel_id=1, source_target_pairs={{24,0},{0,8},{8,16},{16,24},{25,1},{1,9},{9,17},{17,25},{26,2},{2,... | collective-permute-start | bytes 1572872 | tf_op jit(solution)/shard_map/ppermute | solution.py:211
  68.1 14.2 %collective-permute-start.15 = (bf16[128,1024]{1,0:T(8,128)(2,1)S(1)}, bf16[128,1024]{1,0:T(8,128)(2,1)S(1)}, u32[]{:S(2)}, u32[]{:S(2)}) collective-permute-start(bf16[128,1024]{1,0:T(8,128)(2,1)S(1)} %get-tuple-element.50), channel_id=1, source_target_pairs={{6,0},{0,2},{2,4},{4,6},{7,1},{1,3},{3,5},{5,7},{14,8},{8,10},{10,... | collective-permute-start | bytes 786440 | tf_op jit(solution)/shard_map/ppermute | solution.py:211
  68.1 14.2 %collective-permute-start.14 = (bf16[128,1024]{1,0:T(8,128)(2,1)S(1)}, bf16[128,1024]{1,0:T(8,128)(2,1)S(1)}, u32[]{:S(2)}, u32[]{:S(2)}) collective-permute-start(bf16[128,1024]{1,0:T(8,128)(2,1)S(1)} %get-tuple-element.51), channel_id=1, source_target_pairs={{4,0},{6,2},{0,4},{2,6},{5,1},{7,3},{1,5},{3,7},{12,8},{14,10},{8,... | collective-permute-start | bytes 786440 | tf_op jit(solution)/shard_map/ppermute | solution.py:211
  69.9 25.3 %collective-permute-start.18 = (bf16[8,32,1024]{2,1,0:T(8,128)(2,1)S(1)}, bf16[8,32,1024]{2,1,0:T(8,128)(2,1)S(1)}, u32[]{:S(2)}, u32[]{:S(2)}) collective-permute-start(bf16[8,32,1024]{2,1,0:T(8,128)(2,1)S(1)} %all-to-all-done.1.refs_0_), channel_id=1, source_target_pairs={{16,0},{24,8},{0,16},{8,24},{17,1},{25,9},{1,17},{9,25},{18,2},{26... | collective-permute-start | bytes 1572872 | tf_op jit(solution)/shard_map/ppermute | solution.py:211
  74.4 21.4 %collective-permute-start.17 = (bf16[8,32,1024]{2,1,0:T(8,128)(2,1)S(1)}, bf16[8,32,1024]{2,1,0:T(8,128)(2,1)S(1)}, u32[]{:S(2)}, u32[]{:S(2)}) collective-permute-start(bf16[8,32,1024]{2,1,0:T(8,128)(2,1)S(1)} %all-to-all-done.1.refs_0_), channel_id=1, source_target_pairs={{8,0},{16,8},{24,16},{0,24},{9,1},{17,9},{25,17},{1,25},{10,2},{18... | collective-permute-start | bytes 1572872 | tf_op jit(solution)/shard_map/ppermute | solution.py:211
  82.6 13.1 %collective-permute-start.22 = (bf16[128,1024]{1,0:T(8,128)(2,1)S(1)}, bf16[128,1024]{1,0:T(8,128)(2,1)S(1)}, u32[]{:S(2)}, u32[]{:S(2)}) collective-permute-start(bf16[128,1024]{1,0:T(8,128)(2,1)S(1)} %get-tuple-element.42.rows), channel_id=1, source_target_pairs={{6,0},{0,2},{2,4},{4,6},{7,1},{1,3},{3,5},{5,7},{14,8},{8,10},{10,... | collective-permute-start | bytes 786440 | tf_op jit(solution)/shard_map/ppermute | solution.py:211
  82.7 15.1 %collective-permute-start.21 = (bf16[128,1024]{1,0:T(8,128)(2,1)S(1)}, bf16[128,1024]{1,0:T(8,128)(2,1)S(1)}, u32[]{:S(2)}, u32[]{:S(2)}) collective-permute-start(bf16[128,1024]{1,0:T(8,128)(2,1)S(1)} %get-tuple-element.42.rows), channel_id=1, source_target_pairs={{4,0},{6,2},{0,4},{2,6},{5,1},{7,3},{1,5},{3,7},{12,8},{14,10},{8,... | collective-permute-start | bytes 786440 | tf_op jit(solution)/shard_map/ppermute | solution.py:211
  87.5 10.9 %collective-permute-start.20 = (bf16[128,1024]{1,0:T(8,128)(2,1)S(1)}, bf16[128,1024]{1,0:T(8,128)(2,1)S(1)}, u32[]{:S(2)}, u32[]{:S(2)}) collective-permute-start(bf16[128,1024]{1,0:T(8,128)(2,1)S(1)} %get-tuple-element.42.rows), channel_id=1, source_target_pairs={{2,0},{4,2},{6,4},{0,6},{3,1},{5,3},{7,5},{1,7},{10,8},{12,10},{14... | collective-permute-start | bytes 786440 | tf_op jit(solution)/shard_map/ppermute | solution.py:211
  107.2 9.1 %collective-permute-start.24 = (bf16[128,1024]{1,0:T(8,128)(2,1)S(1)}, bf16[128,1024]{1,0:T(8,128)(2,1)S(1)}, u32[]{:S(2)}, u32[]{:S(2)}) collective-permute-start(bf16[128,1024]{1,0:T(8,128)(2,1)S(1)} %mlp.5), channel_id=1, source_target_pairs={{2,0},{4,2},{6,4},{0,6},{3,1},{5,3},{7,5},{1,7},{10,8},{12,10},{14... | collective-permute-start | bytes 786440 | tf_op jit(solution)/shard_map/ppermute | solution.py:211
  111.3 8.8 %collective-permute-start.25 = (bf16[128,1024]{1,0:T(8,128)(2,1)S(1)}, bf16[128,1024]{1,0:T(8,128)(2,1)S(1)}, u32[]{:S(2)}, u32[]{:S(2)}) collective-permute-start(bf16[128,1024]{1,0:T(8,128)(2,1)S(1)} %mlp.6), channel_id=1, source_target_pairs={{4,0},{6,2},{0,4},{2,6},{5,1},{7,3},{1,5},{3,7},{12,8},{14,10},{8,... | collective-permute-start | bytes 786440 | tf_op jit(solution)/shard_map/ppermute | solution.py:211
  113.6 13.2 %collective-permute-start.26 = (bf16[128,1024]{1,0:T(8,128)(2,1)S(1)}, bf16[128,1024]{1,0:T(8,128)(2,1)S(1)}, u32[]{:S(2)}, u32[]{:S(2)}) collective-permute-start(bf16[128,1024]{1,0:T(8,128)(2,1)S(1)} %mlp.7), channel_id=1, source_target_pairs={{6,0},{0,2},{2,4},{4,6},{7,1},{1,3},{3,5},{5,7},{14,8},{8,10},{10,... | collective-permute-start | bytes 786440 | tf_op jit(solution)/shard_map/ppermute | solution.py:211
  (16 other events, 304.5 us)

commit v2 on v1

--- a/solution.py
+++ b/solution.py
@@ -11,6 +11,7 @@
 F32, BF16 = jnp.float32, jnp.bfloat16
 NT = (((1,), (1,)), ((), ()))
 VMEM = pl.BlockSpec(memory_space=pltpu.VMEM)
+HBM = pl.BlockSpec(memory_space=pltpu.HBM)
 SMEM = pl.BlockSpec(memory_space=pltpu.SMEM)
 
 
@@ -36,14 +37,24 @@
     return lax.broadcasted_iota(jnp.int32, (rows, 128), 1) < 64
 
 
-def start_kernel(tok, gain, qkv, out_t, normed, front):
-    normed[...] = layer_norm(tok[...].astype(F32), gain[...])
+def start_kernel(*refs):
+    held, (normed, front, back), here, sems = refs[:6], refs[6:9], refs[9:15], refs[15]
+    copies = [
+        pltpu.make_async_copy(a, b, sems.at[i]) for i, (a, b) in enumerate(zip(held, here))
+    ]
+    for copy in copies:
+        copy.start()
+    qkv, out_t, tok, gain, up, down_t = here
+    copies[0].wait()
+    copies[1].wait()
     pack = jnp.concatenate([qkv[0], qkv[1], qkv[2], out_t[...]], axis=1)
     for i in range(8):
         front[i] = pack
-
-
-def mlp_pack_kernel(up, down_t, back):
+    copies[2].wait()
+    copies[3].wait()
+    normed[...] = layer_norm(tok[...].astype(F32), gain[...])
+    copies[4].wait()
+    copies[5].wait()
     pack = jnp.concatenate([up[...], down_t[...]], axis=1)
     for i in range(8):
         back[i] = pack
@@ -65,12 +76,16 @@
             border[...] = blocks[k][128 - WIN :]
 
 
-def lay_kernel(at, *refs):
-    blocks, out = refs[:4], refs[4]
-    for k in range(4):
+def lay_kernel(at, here, right, up_far, down_far, left, out):
+    for k, block in enumerate((here, right, None, left)):
         base = lax.rem(at[2] + k, 4) * 32
         for z in range(8):
-            out[pl.ds(pl.multiple_of(z * 128 + base, 32), 32)] = blocks[k][z]
+            rows = pl.ds(pl.multiple_of(z * 128 + base, 32), 32)
+            if block is None:
+                out[rows, :512] = up_far[z]
+                out[rows, 512:] = down_far[z]
+            else:
+                out[rows] = block[z]
 
 
 def attend(query, kv, first, count, key_start):
@@ -94,12 +109,14 @@
 
 def attention_kernel(at, *refs):
     own, peer, blocks = refs[0], refs[1], refs[2:6]
-    near_own, near_peer, gain, first, count, att, weight, q_s, kv_s = refs[6:]
+    near_own, near_peer, gain, first, count, att, out_w, weight, q_s, kv_s = refs[6:]
     core, anchor = at[1], at[3]
     for k in range(4):
         base = lax.rem(at[2] + k, 4) * 32
         for z in range(8):
-            weight[pl.ds(pl.multiple_of(z * 128 + base, 32), 32)] = blocks[k][z]
+            rows = pl.ds(pl.multiple_of(z * 128 + base, 32), 32)
+            weight[rows] = blocks[k][z, :, :384]
+            out_w[rows] = blocks[k][z, :, 384:]
 
     rows = jnp.concatenate([near_own[...], near_peer[...]], axis=0)
     part = jnp.dot(rows, weight[:, 128:], preferred_element_type=F32)
@@ -152,38 +169,30 @@
     normed[...] = layer_norm(mid.astype(F32), gain[...])
 
 
-def mlp_kernel(rows, up_own, down_own, up_peer, down_peer, out, total):
-    step = pl.program_id(0)
-    up = jnp.concatenate([up_own[...], up_peer[...]], axis=1)
-    down = jnp.concatenate([down_own[...], down_peer[...]], axis=1)
+def hidden_share(rows, weight):
     hidden = jax.nn.gelu(
-        jnp.dot(rows[...], up, preferred_element_type=F32), approximate=True
+        jnp.dot(rows, weight[:, :512], preferred_element_type=F32), approximate=True
     ).astype(BF16)
-    part = lax.dot_general(hidden, down, NT, preferred_element_type=F32)
-
-    @pl.when(step == 0)
-    def _():
-        total[...] = part
-
-    @pl.when(step == 1)
-    def _():
-        out[...] = (total[...] + part).astype(out.dtype)
-
-
-def mlp(rows, own, peer, dtype):
-    block = lambda at: pl.BlockSpec((1024, 256), lambda i, at=at: (0, at + i))
-    whole = pl.BlockSpec((128, 1024), lambda i: (0, 0))
-    return pl.pallas_call(
-        mlp_kernel,
-        grid=(2,),
-        out_shape=jax.ShapeDtypeStruct((128, 1024), dtype),
-        in_specs=[whole, block(0), block(2), block(0), block(2)],
-        out_specs=whole,
-        scratch_shapes=[pltpu.VMEM((128, 1024), F32)],
-        compiler_params=params(8),
-        cost_estimate=pl.CostEstimate(flops=4 * 128 * 2**20, bytes_accessed=5 * 2**20, transcendentals=2**17),
-        name="mlp",
-    )(rows, own, own, peer, peer)
+    return lax.dot_general(hidden, weight[:, 512:], NT, preferred_element_type=F32)
+
+
+def mlp_first_kernel(a, b, c, d, weight, out):
+    rows = jnp.concatenate([a[...], b[...], c[...], d[...]], axis=0)
+    out[...] = hidden_share(rows, weight)
+
+
+def mlp_second_kernel(rows, weight, part, out, *, at):
+    total = part[at * 128 : at * 128 + 128] + hidden_share(rows[...], weight)
+    out[...] = total.astype(out.dtype)
+
+
+def mlp_second(rows, weight, part, at):
+    return call(
+        functools.partial(mlp_second_kernel, at=at),
+        [((128, 1024), F32 if at == 0 else BF16)],
+        [VMEM] * 3,
+        "mlp_second",
+    )(rows, weight, part)[0]
 
 
 def end_kernel(middle, mine, a, b, c, out):
@@ -229,22 +238,23 @@
     first, count = win_first.reshape(8, 128), win_count.reshape(8, 128)
     gain = qk_gain.reshape(2, 128)
 
-    normed, front = call(
-        start_kernel,
-        [((128, 1024), BF16), ((8, 32, 512), BF16)],
-        [VMEM] * 4,
-        "start",
-    )(
+    given = [
+        jnp.transpose(qkv_weight, (1, 0, 2)),
+        out_weight.T,
         tokens,
         norm1_gain.reshape(1, 1024),
-        jnp.transpose(qkv_weight, (1, 0, 2)),
-        out_weight.T,
-    )
-    (back,) = call(mlp_pack_kernel, [((8, 32, 1024), BF16)], [VMEM] * 2, "mlp_pack")(
-        up_weight, down_weight.T
-    )
+        up_weight,
+        down_weight.T,
+    ]
+    normed, front, back = call(
+        start_kernel,
+        [((128, 1024), BF16), ((8, 32, 512), BF16), ((8, 32, 1024), BF16)],
+        [HBM] * 6,
+        "start",
+        scratch=[pltpu.VMEM(v.shape, v.dtype) for v in given]
+        + [pltpu.SemaphoreType.DMA((6,))],
+    )(*[pltpu.with_memory_space_constraint(v, pltpu.HBM) for v in given])
     front = lax.all_to_all(front, "z", 0, 0, tiled=True)
-    front, out_block = front[:, :, :384], front[:, :, 384:]
     far = {k: fetch(normed, "y", k) for k in (2, 1, 3)}
     blocks = [front] + [fetch(front, "x", k) for k in (1, 2, 3)]
     back, _ = lax.optimization_barrier((back, front))
@@ -257,8 +267,6 @@
         "collect",
     )(at, normed, far[1], far[2], far[3])
     peer = fetch(own, "core", 1)
-    out_block, _ = lax.optimization_barrier((out_block, blocks))
-    out_blocks = [out_block] + [fetch(out_block, "x", k) for k in (1, 2, 3)]
     spot = lambda z, x, y, core: ((z * 4 + x) * 4 + y) * 2 + core
     shift = lambda s, by: divmod((s + by) % 32, 4)
     near_own = lax.ppermute(
@@ -272,9 +280,10 @@
         ],
     )
     near_peer = fetch(near_own, "core", 1)
-    (att,) = call(
+    own, back = lax.optimization_barrier((own, back))
+    att, weight = call(
         attention_kernel,
-        [((2, 4, 128, 128), BF16)],
+        [((2, 4, 128, 128), BF16), ((1024, 128), BF16)],
         [SMEM] + [VMEM] * 11,
         "attention",
         scratch=[
@@ -282,18 +291,12 @@
             pltpu.VMEM((1024, 128), BF16),
             pltpu.VMEM((1024 + 2 * WIN, 256), BF16),
         ],
-        flops=5 * 2**30,
     )(at, own, peer, *blocks, near_own, near_peer, gain, first, count)
 
-    mlp_block, _ = lax.optimization_barrier((back, (att, out_blocks)))
-    mlp_blocks = [mlp_block] + [fetch(mlp_block, "x", k) for k in (1, 2, 3)]
-
-    def laid(blocks, width, after, name):
-        blocks, _ = lax.optimization_barrier((blocks, after))
-        (out,) = call(lay_kernel, [((1024, width), BF16)], [SMEM] + [VMEM] * 4, name)(at, *blocks)
-        return out
-
-    weight = laid(out_blocks, 128, att, "out_lay")
+    right, left = fetch(back, "x", 1), fetch(back, "x", 3)
+    up_far = fetch(right[:, :, :512], "x", 1)
+    down_far = fetch(left[:, :, 512:], "x", 3)
+
     out_peer = fetch(weight, "core", 1)
     got = fetch(att[1], "core", 1)
     mine_attended, away = call(
@@ -311,10 +314,16 @@
     )(tokens, mine_attended, *parts, norm2_gain.reshape(1, 1024))
 
     far = {k: fetch(normed_two, "y", k) for k in (2, 1, 3)}
-    mlp_own = laid(mlp_blocks, 1024, far, "mlp_lay")
+    laid, far = lax.optimization_barrier(((back, right, up_far, down_far, left), far))
+    (mlp_own,) = call(lay_kernel, [((1024, 1024), BF16)], [SMEM] + [VMEM] * 5, "mlp_lay")(
+        at, *laid
+    )
     mlp_peer = fetch(mlp_own, "core", 1)
-    mine = mlp(normed_two, mlp_own, mlp_peer, F32)
-    parts = [fetch(mlp(far[k], mlp_own, mlp_peer, BF16), "y", 4 - k) for k in (3, 2, 1)]
+    (part,) = call(mlp_first_kernel, [((512, 1024), F32)], [VMEM] * 5, "mlp_first", mib=16)(
+        normed_two, far[1], far[2], far[3], mlp_own
+    )
+    parts = [fetch(mlp_second(far[k], mlp_peer, part, k), "y", 4 - k) for k in (2, 1, 3)]
+    mine = mlp_second(normed_two, mlp_peer, part, 0)
     (out,) = call(end_kernel, [((128, 1024), BF16)], [VMEM] * 5, "end")(middle, mine, *parts)
     return out
 

time: 128 us -> 121 us (0.945)
  waiting for transfers between devices: 44.9 us -> 62.3 us
  starting transfers between devices: 59.6 us -> 42.4 us
  Pallas kernels: 19.5 us -> 15 us
  local copies, waits for them, and re-layouts: 3.29 us -> 0.89 us
    ppermute x26 -> x24, starting transfers between devices: 45.9 us -> 29.5 us  [fetch(): return lax.ppermute(value, axis, [((i + step) % n, i) for i in range(n)])]
    ppermute x26 -> x24, waiting for transfers between devices: 28.2 us -> 40.1 us  [fetch(): return lax.ppermute(value, axis, [((i + step) % n, i) for i in range(n)])]
    ppermute x1, waiting for transfers between devices: 4.21 us -> 14.2 us  [local(): lax.ppermute(border, ('z', 'x', 'y', 'core'), [(spot(*divmod(s, 4), j, c)...]
    all_to_all x1, waiting for transfers between devices: 7.04 us -> 1.36 us  [local(): back = lax.all_to_all(back, 'z', 0, 0, tiled=True)]
    pallas_call x9 -> x8, Pallas kernels: 16.4 us -> 11.9 us  [the longest x1 4.67 us: local(): call(attention_kernel, [((2, 4, 128, 128), BF16), ((1024, 128), BF16)], [...]
    unnamed x22 -> x10, local copies, waits for them, and re-layouts: 3.11 us -> 0.03 us
  transfers between devices with their start and end apart: 29 -> 27, of which waited for: 12 -> 14; matrix products, arithmetic and copies ran while one was open for 0% -> 1% of each run, Pallas kernels for 10% -> 4%
where the time goes in v2:
time: 121 us
  waiting for transfers between devices  62.3 us (51%)
  starting transfers between devices  42.4 us (35%)
  Pallas kernels  15 us (12%)
    ppermute x24, waiting for transfers between devices, fetch(): return lax.ppermute(value, axis, [((i + step) % n, i) for i in range(n)])  40.1 us
    ppermute x24, starting transfers between devices, fetch(): return lax.ppermute(value, axis, [((i + step) % n, i) for i in range(n)])  29.5 us
    ppermute x1, waiting for transfers between devices, local(): lax.ppermute(border, ('z', 'x', 'y', 'core'), [(spot(*divmod(s, 4), j, c)...  14.2 us
    all_to_all x1, starting transfers between devices, local(): front = lax.all_to_all(front, 'z', 0, 0, tiled=True)  9.03 us
    all_to_all x1, waiting for transfers between devices, local(): front = lax.all_to_all(front, 'z', 0, 0, tiled=True)  6.59 us
    pallas_call x1, Pallas kernels, local(): call(attention_kernel, [((2, 4, 128, 128), BF16), ((1024, 128), BF16)], [...  4.67 us
    all_to_all x1, starting transfers between devices, local(): back = lax.all_to_all(back, 'z', 0, 0, tiled=True)  3.49 us
    pallas_call x4, Pallas kernels, mlp_second(): call(functools.partial(mlp_second_kernel, at=at), [((128, 1024), F32 if a...  2.99 us
  transfers between devices with their start and end apart: 27, of which 14 were waited for; matrix products, arithmetic and copies ran while one was open for 1% of the time, Pallas kernels for 4%

profile of v2, /device:TPU:1, one launch (start us, length us, event | category | flops | bytes accessed | tf_op | source)
XLA Modules:
  0.0 120.8 jit_solution(1475409603600079978)
XLA Ops:
  0.0 2.2 %start.1 = (bf16[128,1024]{1,0:T(8,128)(2,1)S(1)}, bf16[8,32,512]{2,1,0:T(8,128)(2,1)}, bf16[8,32,1024]{2,1,0:T(8,128)(2,1)}) custom-call(bf16[3,32,128]{2,1,0:T(8,128)(2,1)} %bitcast.23, bf16[32,128]{1,0:T(8,128)(2,1)} %bitcast.24, bf16[128,1024]{1,0:T(8,128)(2,1)} %tok.1, f32[1,1024]{1,0:T(1,128)} %bitcast.25, bf16[32,512]{1,0:T(8,128)(2,1)} %refs_4_.1, ...), custom_call_target="tpu_custom_call" | custom-call | flops 1048576 | bytes 2097152 | tf_op jit(solution)/shard_map/start/pallas_call | solution.py:249
  2.2 9.0 %all-to-all-start = ((bf16[8,32,512]{2,1,0:T(8,128)(2,1)}), bf16[8,32,512]{2,1,0:T(8,128)(2,1)S(1)}, u32[]{:S(2)}, u32[]{:S(2)}) async-start(bf16[8,32,512]{2,1,0:T(8,128)(2,1)} %get-tuple-element.31), calls=%async_computation | async-start | bytes 524288 | tf_op jit(solution)/shard_map/all_to_all | solution.py:257
  11.2 2.7 %collective-permute-start = (bf16[128,1024]{1,0:T(8,128)(2,1)S(1)}, bf16[128,1024]{1,0:T(8,128)(2,1)S(1)}, u32[]{:S(2)}, u32[]{:S(2)}) collective-permute-start(bf16[128,1024]{1,0:T(8,128)(2,1)S(1)} %get-tuple-element.30.refs_0_), channel_id=1, source_target_pairs={{2,0},{4,2},{6,4},{0,6},{3,1},{5,3},{7,5},{1,7},{10,8},{12,10},{14... | collective-permute-start | bytes 786440 | tf_op jit(solution)/shard_map/ppermute | solution.py:220
  15.0 6.6 %all-to-all-done.refs_2_ = bf16[8,32,512]{2,1,0:T(8,128)(2,1)S(1)} async-done(((bf16[8,32,512]{2,1,0:T(8,128)(2,1)}), bf16[8,32,512]{2,1,0:T(8,128)(2,1)S(1)}, u32[]{:S(2)}, u32[]{:S(2)}) %all-to-all-start) | async-done | bytes 262176 | tf_op jit(solution)/shard_map/all_to_all | solution.py:257
  21.6 2.5 %collective-permute-start.3 = (bf16[8,32,512]{2,1,0:T(8,128)(2,1)S(1)}, bf16[8,32,512]{2,1,0:T(8,128)(2,1)S(1)}, u32[]{:S(2)}, u32[]{:S(2)}) collective-permute-start(bf16[8,32,512]{2,1,0:T(8,128)(2,1)S(1)} %all-to-all-done.refs_2_), channel_id=1, source_target_pairs={{8,0},{16,8},{24,16},{0,24},{9,1},{17,9},{25,17},{1,25},{10,2},{18... | collective-permute-start | bytes 786440 | tf_op jit(solution)/shard_map/ppermute | solution.py:220
  24.2 5.1 %collective-permute-done.2.refs_3_ = bf16[128,1024]{1,0:T(8,128)(2,1)S(1)} collective-permute-done((bf16[128,1024]{1,0:T(8,128)(2,1)S(1)}, bf16[128,1024]{1,0:T(8,128)(2,1)S(1)}, u32[]{:S(2)}, u32[]{:S(2)}) %collective-permute-start.2) | collective-permute-done | bytes 262176 | tf_op jit(solution)/shard_map/ppermute | solution.py:220
  31.2 4.0 %collective-permute-start.5 = (bf16[4,128,1024]{2,1,0:T(8,128)(2,1)S(1)}, bf16[4,128,1024]{2,1,0:T(8,128)(2,1)S(1)}, u32[]{:S(2)}, u32[]{:S(2)}) collective-permute-start(bf16[4,128,1024]{2,1,0:T(8,128)(2,1)S(1)} %get-tuple-element.38.refs_0_), channel_id=1, source_target_pairs={{1,0},{0,1},{3,2},{2,3},{5,4},{4,5},{7,6},{6,7},{9,8},{8,9},{11,10... | collective-permute-start | bytes 3145736 | tf_op jit(solution)/shard_map/ppermute | solution.py:220
  35.2 3.5 %all-to-all-start.1 = ((bf16[8,32,1024]{2,1,0:T(8,128)(2,1)}), bf16[8,32,1024]{2,1,0:T(8,128)(2,1)S(1)}, u32[]{:S(2)}, u32[]{:S(2)}) async-start(bf16[8,32,1024]{2,1,0:T(8,128)(2,1)} %get-tuple-element.37), calls=%async_computation.1 | async-start | bytes 1048576 | tf_op jit(solution)/shard_map/all_to_all | solution.py:261
  40.3 14.2 %collective-permute-done.7.refs_6_ = bf16[64,1024]{1,0:T(8,128)(2,1)S(1)} collective-permute-done((bf16[64,1024]{1,0:T(8,128)(2,1)}, bf16[64,1024]{1,0:T(8,128)(2,1)S(1)}, u32[]{:S(2)}, u32[]{:S(2)}) %collective-permute-start.7) | collective-permute-done | bytes 131104 | tf_op jit(solution)/shard_map/ppermute | solution.py:272
  56.7 4.7 %attention.1 = (bf16[2,4,128,128]{3,2,1,0:T(8,128)(2,1)S(1)}, bf16[1024,128]{1,0:T(8,128)(2,1)S(1)}) custom-call(s32[4]{0:T(128)S(1)} %pad_add_fusion.at, bf16[4,128,1024]{2,1,0:T(8,128)(2,1)S(1)} %get-tuple-element.38.refs_0_, bf16[4,128,1024]{2,1,0:T(8,128)(2,1)S(1)} %collective-permute-done.5.refs_1_, bf16[8,32,512]{2,1,0:T(8,128)(2,1)S(1)} %all-to-all-done.refs_2_, ...), custom_call_target="tpu_custom_call" | custom-call | flops 1048576 | bytes 2097152 | tf_op jit(solution)/shard_map/attention/pallas_call | solution.py:284
  64.9 3.0 %collective-permute-start.11 = (bf16[128,1024]{1,0:T(8,128)(2,1)S(1)}, bf16[128,1024]{1,0:T(8,128)(2,1)S(1)}, u32[]{:S(2)}, u32[]{:S(2)}) collective-permute-start(bf16[128,1024]{1,0:T(8,128)(2,1)S(1)} %get-tuple-element.57), channel_id=1, source_target_pairs={{4,0},{6,2},{0,4},{2,6},{5,1},{7,3},{1,5},{3,7},{12,8},{14,10},{8,... | collective-permute-start | bytes 786440 | tf_op jit(solution)/shard_map/ppermute | solution.py:220
  68.3 2.3 %collective-permute-start.13 = (bf16[128,1024]{1,0:T(8,128)(2,1)S(1)}, bf16[128,1024]{1,0:T(8,128)(2,1)S(1)}, u32[]{:S(2)}, u32[]{:S(2)}) collective-permute-start(bf16[128,1024]{1,0:T(8,128)(2,1)S(1)} %get-tuple-element.55), channel_id=1, source_target_pairs={{2,0},{4,2},{6,4},{0,6},{3,1},{5,3},{7,5},{1,7},{10,8},{12,10},{14... | collective-permute-start | bytes 786440 | tf_op jit(solution)/shard_map/ppermute | solution.py:220
  70.6 4.6 %collective-permute-done.14.right = bf16[8,32,1024]{2,1,0:T(8,128)(2,1)S(1)} collective-permute-done((bf16[8,32,1024]{2,1,0:T(8,128)(2,1)S(1)}, bf16[8,32,1024]{2,1,0:T(8,128)(2,1)S(1)}, u32[]{:S(2)}, u32[]{:S(2)}) %collective-permute-start.14) | collective-permute-done | bytes 524320 | tf_op jit(solution)/shard_map/ppermute | solution.py:220
  75.2 2.7 %collective-permute-start.15 = (bf16[8,32,512]{2,1,0:T(8,128)(2,1)S(1)}, bf16[8,32,512]{2,1,0:T(8,128)(2,1)S(1)}, u32[]{:S(2)}, u32[]{:S(2)}) collective-permute-start(bf16[8,32,512]{2,1,0:T(8,128)(2,1)S(1)} %slice.24), channel_id=1, source_target_pairs={{8,0},{16,8},{24,16},{0,24},{9,1},{17,9},{25,17},{1,25},{10,2},{18... | collective-permute-start | bytes 786440 | tf_op jit(solution)/shard_map/ppermute | solution.py:220
  78.0 2.3 %collective-permute-done.12.b = bf16[128,1024]{1,0:T(8,128)(2,1)S(1)} collective-permute-done((bf16[128,1024]{1,0:T(8,128)(2,1)S(1)}, bf16[128,1024]{1,0:T(8,128)(2,1)S(1)}, u32[]{:S(2)}, u32[]{:S(2)}) %collective-permute-start.12) | collective-permute-done | bytes 262176 | tf_op jit(solution)/shard_map/ppermute | solution.py:220
  80.7 2.7 %collective-permute-start.18 = (bf16[128,1024]{1,0:T(8,128)(2,1)S(1)}, bf16[128,1024]{1,0:T(8,128)(2,1)S(1)}, u32[]{:S(2)}, u32[]{:S(2)}) collective-permute-start(bf16[128,1024]{1,0:T(8,128)(2,1)S(1)} %get-tuple-element.45.a.rows), channel_id=1, source_target_pairs={{2,0},{4,2},{6,4},{0,6},{3,1},{5,3},{7,5},{1,7},{10,8},{12,10},{14... | collective-permute-start | bytes 786440 | tf_op jit(solution)/shard_map/ppermute | solution.py:220
  84.0 1.5 %collective-permute-done.17.down_far = bf16[8,32,512]{2,1,0:T(8,128)(2,1)S(1)} collective-permute-done((bf16[8,32,512]{2,1,0:T(8,128)(2,1)S(1)}, bf16[8,32,512]{2,1,0:T(8,128)(2,1)S(1)}, u32[]{:S(2)}, u32[]{:S(2)}) %collective-permute-start.17) | collective-permute-done | bytes 262176 | tf_op jit(solution)/shard_map/ppermute | solution.py:220
  85.5 4.1 %collective-permute-done.18.b.rows = bf16[128,1024]{1,0:T(8,128)(2,1)S(1)} collective-permute-done((bf16[128,1024]{1,0:T(8,128)(2,1)S(1)}, bf16[128,1024]{1,0:T(8,128)(2,1)S(1)}, u32[]{:S(2)}, u32[]{:S(2)}) %collective-permute-start.18) | collective-permute-done | bytes 262176 | tf_op jit(solution)/shard_map/ppermute | solution.py:220
  89.6 2.2 %collective-permute-done.19.c.rows = bf16[128,1024]{1,0:T(8,128)(2,1)S(1)} collective-permute-done((bf16[128,1024]{1,0:T(8,128)(2,1)S(1)}, bf16[128,1024]{1,0:T(8,128)(2,1)S(1)}, u32[]{:S(2)}, u32[]{:S(2)}) %collective-permute-start.19) | collective-permute-done | bytes 262176 | tf_op jit(solution)/shard_map/ppermute | solution.py:220
  91.8 6.9 %collective-permute-done.20.d.rows = bf16[128,1024]{1,0:T(8,128)(2,1)S(1)} collective-permute-done((bf16[128,1024]{1,0:T(8,128)(2,1)S(1)}, bf16[128,1024]{1,0:T(8,128)(2,1)S(1)}, u32[]{:S(2)}, u32[]{:S(2)}) %collective-permute-start.20) | collective-permute-done | bytes 262176 | tf_op jit(solution)/shard_map/ppermute | solution.py:220
  101.4 2.4 %collective-permute-done.21.weight = bf16[1024,1024]{1,0:T(8,128)(2,1)S(1)} collective-permute-done((bf16[1024,1024]{1,0:T(8,128)(2,1)S(1)}, bf16[1024,1024]{1,0:T(8,128)(2,1)S(1)}, u32[]{:S(2)}, u32[]{:S(2)}) %collective-permute-start.21) | collective-permute-done | bytes 2097184 | tf_op jit(solution)/shard_map/ppermute | solution.py:220
  107.1 2.3 %collective-permute-start.24 = (bf16[128,1024]{1,0:T(8,128)(2,1)S(1)}, bf16[128,1024]{1,0:T(8,128)(2,1)S(1)}, u32[]{:S(2)}, u32[]{:S(2)}) collective-permute-start(bf16[128,1024]{1,0:T(8,128)(2,1)S(1)} %mlp_second.7), channel_id=1, source_target_pairs={{2,0},{4,2},{6,4},{0,6},{3,1},{5,3},{7,5},{1,7},{10,8},{12,10},{14... | collective-permute-start | bytes 786440 | tf_op jit(solution)/shard_map/ppermute | solution.py:220
  110.2 3.5 %collective-permute-done.22.a = bf16[128,1024]{1,0:T(8,128)(2,1)S(1)} collective-permute-done((bf16[128,1024]{1,0:T(8,128)(2,1)S(1)}, bf16[128,1024]{1,0:T(8,128)(2,1)S(1)}, u32[]{:S(2)}, u32[]{:S(2)}) %collective-permute-start.22) | collective-permute-done | bytes 262176 | tf_op jit(solution)/shard_map/ppermute | solution.py:220
  113.7 6.3 %collective-permute-done.23.b = bf16[128,1024]{1,0:T(8,128)(2,1)S(1)} collective-permute-done((bf16[128,1024]{1,0:T(8,128)(2,1)S(1)}, bf16[128,1024]{1,0:T(8,128)(2,1)S(1)}, u32[]{:S(2)}, u32[]{:S(2)}) %collective-permute-start.23) | collective-permute-done | bytes 262176 | tf_op jit(solution)/shard_map/ppermute | solution.py:220
  (58 shorter events, 19.4 us)
Async XLA Ops:
  2.2 19.4 %all-to-all-start = ((bf16[8,32,512]{2,1,0:T(8,128)(2,1)}), bf16[8,32,512]{2,1,0:T(8,128)(2,1)S(1)}, u32[]{:S(2)}, u32[]{:S(2)}) async-start(bf16[8,32,512]{2,1,0:T(8,128)(2,1)} %get-tuple-element.31), calls=%async_computation | async-start | bytes 524288 | tf_op jit(solution)/shard_map/all_to_all | solution.py:257
  11.2 12.9 %collective-permute-start = (bf16[128,1024]{1,0:T(8,128)(2,1)S(1)}, bf16[128,1024]{1,0:T(8,128)(2,1)S(1)}, u32[]{:S(2)}, u32[]{:S(2)}) collective-permute-start(bf16[128,1024]{1,0:T(8,128)(2,1)S(1)} %get-tuple-element.30.refs_0_), channel_id=1, source_target_pairs={{2,0},{4,2},{6,4},{0,6},{3,1},{5,3},{7,5},{1,7},{10,8},{12,10},{14... | collective-permute-start | bytes 786440 | tf_op jit(solution)/shard_map/ppermute | solution.py:220
  14.0 10.2 %collective-permute-start.1 = (bf16[128,1024]{1,0:T(8,128)(2,1)S(1)}, bf16[128,1024]{1,0:T(8,128)(2,1)S(1)}, u32[]{:S(2)}, u32[]{:S(2)}) collective-permute-start(bf16[128,1024]{1,0:T(8,128)(2,1)S(1)} %get-tuple-element.30.refs_0_), channel_id=1, source_target_pairs={{4,0},{6,2},{0,4},{2,6},{5,1},{7,3},{1,5},{3,7},{12,8},{14,10},{8,... | collective-permute-start | bytes 786440 | tf_op jit(solution)/shard_map/ppermute | solution.py:220
  14.3 15.0 %collective-permute-start.2 = (bf16[128,1024]{1,0:T(8,128)(2,1)S(1)}, bf16[128,1024]{1,0:T(8,128)(2,1)S(1)}, u32[]{:S(2)}, u32[]{:S(2)}) collective-permute-start(bf16[128,1024]{1,0:T(8,128)(2,1)S(1)} %get-tuple-element.30.refs_0_), channel_id=1, source_target_pairs={{6,0},{0,2},{2,4},{4,6},{7,1},{1,3},{3,5},{5,7},{14,8},{8,10},{10,... | collective-permute-start | bytes 786440 | tf_op jit(solution)/shard_map/ppermute | solution.py:220
  21.6 7.7 %collective-permute-start.3 = (bf16[8,32,512]{2,1,0:T(8,128)(2,1)S(1)}, bf16[8,32,512]{2,1,0:T(8,128)(2,1)S(1)}, u32[]{:S(2)}, u32[]{:S(2)}) collective-permute-start(bf16[8,32,512]{2,1,0:T(8,128)(2,1)S(1)} %all-to-all-done.refs_2_), channel_id=1, source_target_pairs={{8,0},{16,8},{24,16},{0,24},{9,1},{17,9},{25,17},{1,25},{10,2},{18... | collective-permute-start | bytes 786440 | tf_op jit(solution)/shard_map/ppermute | solution.py:220
  24.1 6.4 %collective-permute-start.4 = (bf16[8,32,512]{2,1,0:T(8,128)(2,1)S(1)}, bf16[8,32,512]{2,1,0:T(8,128)(2,1)S(1)}, u32[]{:S(2)}, u32[]{:S(2)}) collective-permute-start(bf16[8,32,512]{2,1,0:T(8,128)(2,1)S(1)} %all-to-all-done.refs_2_), channel_id=1, source_target_pairs={{24,0},{0,8},{8,16},{16,24},{25,1},{1,9},{9,17},{17,25},{26,2},{2,... | collective-permute-start | bytes 786440 | tf_op jit(solution)/shard_map/ppermute | solution.py:220
  31.2 25.5 %collective-permute-start.5 = (bf16[4,128,1024]{2,1,0:T(8,128)(2,1)S(1)}, bf16[4,128,1024]{2,1,0:T(8,128)(2,1)S(1)}, u32[]{:S(2)}, u32[]{:S(2)}) collective-permute-start(bf16[4,128,1024]{2,1,0:T(8,128)(2,1)S(1)} %get-tuple-element.38.refs_0_), channel_id=1, source_target_pairs={{1,0},{0,1},{3,2},{2,3},{5,4},{4,5},{7,6},{6,7},{9,8},{8,9},{11,10... | collective-permute-start | bytes 3145736 | tf_op jit(solution)/shard_map/ppermute | solution.py:220
  35.2 21.5 %all-to-all-start.1 = ((bf16[8,32,1024]{2,1,0:T(8,128)(2,1)}), bf16[8,32,1024]{2,1,0:T(8,128)(2,1)S(1)}, u32[]{:S(2)}, u32[]{:S(2)}) async-start(bf16[8,32,1024]{2,1,0:T(8,128)(2,1)} %get-tuple-element.37), calls=%async_computation.1 | async-start | bytes 1048576 | tf_op jit(solution)/shard_map/all_to_all | solution.py:261
  38.7 18.0 %collective-permute-start.6 = (bf16[8,32,512]{2,1,0:T(8,128)(2,1)S(1)}, bf16[8,32,512]{2,1,0:T(8,128)(2,1)}, u32[]{:S(2)}, u32[]{:S(2)}) collective-permute-start(bf16[8,32,512]{2,1,0:T(8,128)(2,1)S(1)} %all-to-all-done.refs_2_), channel_id=1, source_target_pairs={{16,0},{24,8},{0,16},{8,24},{17,1},{25,9},{1,17},{9,25},{18,2},{26... | collective-permute-start | bytes 786440 | tf_op jit(solution)/shard_map/ppermute | solution.py:220
  40.0 14.5 %collective-permute-start.7 = (bf16[64,1024]{1,0:T(8,128)(2,1)}, bf16[64,1024]{1,0:T(8,128)(2,1)S(1)}, u32[]{:S(2)}, u32[]{:S(2)}) collective-permute-start(bf16[64,1024]{1,0:T(8,128)(2,1)} %copy-done.4), channel_id=1, source_target_pairs={{0,248},{1,9},{2,250},{3,11},{4,252},{5,13},{6,254},{7,15},{8,0},{... | collective-permute-start | bytes 393224 | tf_op jit(solution)/shard_map/ppermute | solution.py:272
  62.1 13.1 %collective-permute-start.14 = (bf16[8,32,1024]{2,1,0:T(8,128)(2,1)S(1)}, bf16[8,32,1024]{2,1,0:T(8,128)(2,1)S(1)}, u32[]{:S(2)}, u32[]{:S(2)}) collective-permute-start(bf16[8,32,1024]{2,1,0:T(8,128)(2,1)S(1)} %all-to-all-done.1.here), channel_id=1, source_target_pairs={{8,0},{16,8},{24,16},{0,24},{9,1},{17,9},{25,17},{1,25},{10,2},{18... | collective-permute-start | bytes 1572872 | tf_op jit(solution)/shard_map/ppermute | solution.py:220
  63.4 14.5 %collective-permute-start.16 = (bf16[8,32,1024]{2,1,0:T(8,128)(2,1)S(1)}, bf16[8,32,1024]{2,1,0:T(8,128)(2,1)S(1)}, u32[]{:S(2)}, u32[]{:S(2)}) collective-permute-start(bf16[8,32,1024]{2,1,0:T(8,128)(2,1)S(1)} %all-to-all-done.1.here), channel_id=1, source_target_pairs={{24,0},{0,8},{8,16},{16,24},{25,1},{1,9},{9,17},{17,25},{26,2},{2,... | collective-permute-start | bytes 1572872 | tf_op jit(solution)/shard_map/ppermute | solution.py:220
  64.9 13.1 %collective-permute-start.11 = (bf16[128,1024]{1,0:T(8,128)(2,1)S(1)}, bf16[128,1024]{1,0:T(8,128)(2,1)S(1)}, u32[]{:S(2)}, u32[]{:S(2)}) collective-permute-start(bf16[128,1024]{1,0:T(8,128)(2,1)S(1)} %get-tuple-element.57), channel_id=1, source_target_pairs={{4,0},{6,2},{0,4},{2,6},{5,1},{7,3},{1,5},{3,7},{12,8},{14,10},{8,... | collective-permute-start | bytes 786440 | tf_op jit(solution)/shard_map/ppermute | solution.py:220
  67.9 12.4 %collective-permute-start.12 = (bf16[128,1024]{1,0:T(8,128)(2,1)S(1)}, bf16[128,1024]{1,0:T(8,128)(2,1)S(1)}, u32[]{:S(2)}, u32[]{:S(2)}) collective-permute-start(bf16[128,1024]{1,0:T(8,128)(2,1)S(1)} %get-tuple-element.56), channel_id=1, source_target_pairs={{6,0},{0,2},{2,4},{4,6},{7,1},{1,3},{3,5},{5,7},{14,8},{8,10},{10,... | collective-permute-start | bytes 786440 | tf_op jit(solution)/shard_map/ppermute | solution.py:220
  68.3 12.0 %collective-permute-start.13 = (bf16[128,1024]{1,0:T(8,128)(2,1)S(1)}, bf16[128,1024]{1,0:T(8,128)(2,1)S(1)}, u32[]{:S(2)}, u32[]{:S(2)}) collective-permute-start(bf16[128,1024]{1,0:T(8,128)(2,1)S(1)} %get-tuple-element.55), channel_id=1, source_target_pairs={{2,0},{4,2},{6,4},{0,6},{3,1},{5,3},{7,5},{1,7},{10,8},{12,10},{14... | collective-permute-start | bytes 786440 | tf_op jit(solution)/shard_map/ppermute | solution.py:220
  75.2 8.9 %collective-permute-start.15 = (bf16[8,32,512]{2,1,0:T(8,128)(2,1)S(1)}, bf16[8,32,512]{2,1,0:T(8,128)(2,1)S(1)}, u32[]{:S(2)}, u32[]{:S(2)}) collective-permute-start(bf16[8,32,512]{2,1,0:T(8,128)(2,1)S(1)} %slice.24), channel_id=1, source_target_pairs={{8,0},{16,8},{24,16},{0,24},{9,1},{17,9},{25,17},{1,25},{10,2},{18... | collective-permute-start | bytes 786440 | tf_op jit(solution)/shard_map/ppermute | solution.py:220
  77.9 7.6 %collective-permute-start.17 = (bf16[8,32,512]{2,1,0:T(8,128)(2,1)S(1)}, bf16[8,32,512]{2,1,0:T(8,128)(2,1)S(1)}, u32[]{:S(2)}, u32[]{:S(2)}) collective-permute-start(bf16[8,32,512]{2,1,0:T(8,128)(2,1)S(1)} %slice.25), channel_id=1, source_target_pairs={{24,0},{0,8},{8,16},{16,24},{25,1},{1,9},{9,17},{17,25},{26,2},{2,... | collective-permute-start | bytes 786440 | tf_op jit(solution)/shard_map/ppermute | solution.py:220
  80.7 8.9 %collective-permute-start.18 = (bf16[128,1024]{1,0:T(8,128)(2,1)S(1)}, bf16[128,1024]{1,0:T(8,128)(2,1)S(1)}, u32[]{:S(2)}, u32[]{:S(2)}) collective-permute-start(bf16[128,1024]{1,0:T(8,128)(2,1)S(1)} %get-tuple-element.45.a.rows), channel_id=1, source_target_pairs={{2,0},{4,2},{6,4},{0,6},{3,1},{5,3},{7,5},{1,7},{10,8},{12,10},{14... | collective-permute-start | bytes 786440 | tf_op jit(solution)/shard_map/ppermute | solution.py:220
  83.4 8.5 %collective-permute-start.19 = (bf16[128,1024]{1,0:T(8,128)(2,1)S(1)}, bf16[128,1024]{1,0:T(8,128)(2,1)S(1)}, u32[]{:S(2)}, u32[]{:S(2)}) collective-permute-start(bf16[128,1024]{1,0:T(8,128)(2,1)S(1)} %get-tuple-element.45.a.rows), channel_id=1, source_target_pairs={{4,0},{6,2},{0,4},{2,6},{5,1},{7,3},{1,5},{3,7},{12,8},{14,10},{8,... | collective-permute-start | bytes 786440 | tf_op jit(solution)/shard_map/ppermute | solution.py:220
  83.8 14.9 %collective-permute-start.20 = (bf16[128,1024]{1,0:T(8,128)(2,1)S(1)}, bf16[128,1024]{1,0:T(8,128)(2,1)S(1)}, u32[]{:S(2)}, u32[]{:S(2)}) collective-permute-start(bf16[128,1024]{1,0:T(8,128)(2,1)S(1)} %get-tuple-element.45.a.rows), channel_id=1, source_target_pairs={{6,0},{0,2},{2,4},{4,6},{7,1},{1,3},{3,5},{5,7},{14,8},{8,10},{10,... | collective-permute-start | bytes 786440 | tf_op jit(solution)/shard_map/ppermute | solution.py:220
  99.4 4.4 %collective-permute-start.21 = (bf16[1024,1024]{1,0:T(8,128)(2,1)S(1)}, bf16[1024,1024]{1,0:T(8,128)(2,1)S(1)}, u32[]{:S(2)}, u32[]{:S(2)}) collective-permute-start(bf16[1024,1024]{1,0:T(8,128)(2,1)S(1)} %mlp_lay.1.weight), channel_id=1, source_target_pairs={{1,0},{0,1},{3,2},{2,3},{5,4},{4,5},{7,6},{6,7},{9,8},{8,9},{11,10... | collective-permute-start | bytes 6291464 | tf_op jit(solution)/shard_map/ppermute | solution.py:220
  104.5 9.2 %collective-permute-start.22 = (bf16[128,1024]{1,0:T(8,128)(2,1)S(1)}, bf16[128,1024]{1,0:T(8,128)(2,1)S(1)}, u32[]{:S(2)}, u32[]{:S(2)}) collective-permute-start(bf16[128,1024]{1,0:T(8,128)(2,1)S(1)} %mlp_second.5), channel_id=1, source_target_pairs={{4,0},{6,2},{0,4},{2,6},{5,1},{7,3},{1,5},{3,7},{12,8},{14,10},{8,... | collective-permute-start | bytes 786440 | tf_op jit(solution)/shard_map/ppermute | solution.py:220
  105.9 14.1 %collective-permute-start.23 = (bf16[128,1024]{1,0:T(8,128)(2,1)S(1)}, bf16[128,1024]{1,0:T(8,128)(2,1)S(1)}, u32[]{:S(2)}, u32[]{:S(2)}) collective-permute-start(bf16[128,1024]{1,0:T(8,128)(2,1)S(1)} %mlp_second.6), channel_id=1, source_target_pairs={{6,0},{0,2},{2,4},{4,6},{7,1},{1,3},{3,5},{5,7},{14,8},{8,10},{10,... | collective-permute-start | bytes 786440 | tf_op jit(solution)/shard_map/ppermute | solution.py:220
  107.1 12.9 %collective-permute-start.24 = (bf16[128,1024]{1,0:T(8,128)(2,1)S(1)}, bf16[128,1024]{1,0:T(8,128)(2,1)S(1)}, u32[]{:S(2)}, u32[]{:S(2)}) collective-permute-start(bf16[128,1024]{1,0:T(8,128)(2,1)S(1)} %mlp_second.7), channel_id=1, source_target_pairs={{2,0},{4,2},{6,4},{0,6},{3,1},{5,3},{7,5},{1,7},{10,8},{12,10},{14... | collective-permute-start | bytes 786440 | tf_op jit(solution)/shard_map/ppermute | solution.py:220
  (8 other events, 166.0 us)

commit v3 on v2

--- a/solution.py
+++ b/solution.py
@@ -48,7 +48,7 @@
     copies[0].wait()
     copies[1].wait()
     pack = jnp.concatenate([qkv[0], qkv[1], qkv[2], out_t[...]], axis=1)
-    for i in range(8):
+    for i in range(32):
         front[i] = pack
     copies[2].wait()
     copies[3].wait()
@@ -107,19 +107,17 @@
     return jnp.concatenate(outs, axis=1).astype(BF16)
 
 
-def attention_kernel(at, *refs):
-    own, peer, blocks = refs[0], refs[1], refs[2:6]
-    near_own, near_peer, gain, first, count, att, out_w, weight, q_s, kv_s = refs[6:]
+def attention_kernel(
+    at, own, peer, weight, near_own, near_peer, gains, first, count,
+    keep, give, out_w, q_s, kv_s, att,
+):
     core, anchor = at[1], at[3]
-    for k in range(4):
-        base = lax.rem(at[2] + k, 4) * 32
-        for z in range(8):
-            rows = pl.ds(pl.multiple_of(z * 128 + base, 32), 32)
-            weight[rows] = blocks[k][z, :, :384]
-            out_w[rows] = blocks[k][z, :, 384:]
+    gain = gains[...]
+    gain = jnp.concatenate([gain[:, 0], gain[:, 1]], axis=1)
+    out_w[...] = weight[:, 384:]
 
     rows = jnp.concatenate([near_own[...], near_peer[...]], axis=0)
-    part = jnp.dot(rows, weight[:, 128:], preferred_element_type=F32)
+    part = jnp.dot(rows, weight[:, 128:384], preferred_element_type=F32)
     key = head_norm(part[:, :128], gain[1:2], first_half(2 * WIN))
     kv = jnp.concatenate([key, part[:, 128:].astype(BF16)], axis=1)
     end = WIN + 1024
@@ -129,7 +127,7 @@
     half = first_half(256)
     for t in range(4):
         rows = jnp.concatenate([own[t], peer[t]], axis=0)
-        qkv = jnp.dot(rows, weight[...], preferred_element_type=F32)
+        qkv = jnp.dot(rows, weight[:, :384], preferred_element_type=F32)
         query = head_norm(qkv[:, :128], gain[0:1], half)
         key = head_norm(qkv[:, 128:256], gain[1:2], half)
         kv = jnp.concatenate([key, qkv[:, 256:].astype(BF16)], axis=1)
@@ -147,19 +145,27 @@
             count[b : b + 1],
             anchor + (b * 128 - WIN),
         )
-
-
-def project_kernel(at, att, got, weight, other, mine, away):
+    keep[...] = att[0]
+    give[...] = att[1]
+
+
+def project_kernel(at, keep, got, weight, other, mine, away):
     y = at[0]
-    for k in (2, 1, 3, 0):
-        t = lax.rem(y + k, 4)
-        part = lax.dot_general(
-            att[0, t], weight[...], NT, preferred_element_type=F32
-        ) + lax.dot_general(got[t], other[...], NT, preferred_element_type=F32)
-        if k == 0:
-            mine[...] = part
-        else:
-            away[k - 1] = part.astype(BF16)
+    rows = jnp.concatenate(
+        [keep[...].reshape(512, 128), got[...].reshape(512, 128)], axis=1
+    )
+    both = jnp.concatenate([weight[...], other[...]], axis=1)
+    part = lax.dot_general(rows, both, NT, preferred_element_type=F32)
+    for t in range(4):
+        block = part[t * 128 : t * 128 + 128]
+
+        @pl.when(y == t)
+        def _():
+            mine[...] = block
+
+        @pl.when(y != t)
+        def _():
+            away[lax.rem(t + 3 - y, 4)] = block.astype(BF16)
 
 
 def middle_kernel(tok, mine, a, b, c, gain, middle, normed):
@@ -236,7 +242,6 @@
     seq = lax.axis_index("z") * lax.axis_size("x") + lax.axis_index("x")
     at = jnp.stack([y, core, lax.axis_index("x"), seq * 1024]).astype(jnp.int32)
     first, count = win_first.reshape(8, 128), win_count.reshape(8, 128)
-    gain = qk_gain.reshape(2, 128)
 
     given = [
         jnp.transpose(qkv_weight, (1, 0, 2)),
@@ -248,18 +253,14 @@
     ]
     normed, front, back = call(
         start_kernel,
-        [((128, 1024), BF16), ((8, 32, 512), BF16), ((8, 32, 1024), BF16)],
+        [((128, 1024), BF16), ((32, 32, 512), BF16), ((8, 32, 1024), BF16)],
         [HBM] * 6,
         "start",
         scratch=[pltpu.VMEM(v.shape, v.dtype) for v in given]
         + [pltpu.SemaphoreType.DMA((6,))],
     )(*[pltpu.with_memory_space_constraint(v, pltpu.HBM) for v in given])
-    front = lax.all_to_all(front, "z", 0, 0, tiled=True)
+    weight = lax.all_to_all(front, ("z", "x"), 0, 0, tiled=True).reshape(1024, 512)
     far = {k: fetch(normed, "y", k) for k in (2, 1, 3)}
-    blocks = [front] + [fetch(front, "x", k) for k in (1, 2, 3)]
-    back, _ = lax.optimization_barrier((back, front))
-    back = lax.all_to_all(back, "z", 0, 0, tiled=True)
-    far, _ = lax.optimization_barrier((far, (blocks[1], blocks[3])))
     own, border = call(
         collect_kernel,
         [((4, 128, 1024), BF16), ((WIN, 1024), BF16)],
@@ -280,31 +281,32 @@
         ],
     )
     near_peer = fetch(near_own, "core", 1)
-    own, back = lax.optimization_barrier((own, back))
-    att, weight = call(
+    back, _ = lax.optimization_barrier((back, (weight, border)))
+    back = lax.all_to_all(back, "z", 0, 0, tiled=True)
+    keep, give, weight = call(
         attention_kernel,
-        [((2, 4, 128, 128), BF16), ((1024, 128), BF16)],
-        [SMEM] + [VMEM] * 11,
+        [((4, 128, 128), BF16), ((4, 128, 128), BF16), ((1024, 128), BF16)],
+        [SMEM] + [VMEM] * 8,
         "attention",
         scratch=[
-            pltpu.VMEM((1024, 384), BF16),
             pltpu.VMEM((1024, 128), BF16),
             pltpu.VMEM((1024 + 2 * WIN, 256), BF16),
+            pltpu.VMEM((2, 4, 128, 128), BF16),
         ],
-    )(at, own, peer, *blocks, near_own, near_peer, gain, first, count)
+    )(at, own, peer, weight, near_own, near_peer, qk_gain, first, count)
 
     right, left = fetch(back, "x", 1), fetch(back, "x", 3)
     up_far = fetch(right[:, :, :512], "x", 1)
     down_far = fetch(left[:, :, 512:], "x", 3)
 
     out_peer = fetch(weight, "core", 1)
-    got = fetch(att[1], "core", 1)
+    got = fetch(give, "core", 1)
     mine_attended, away = call(
         project_kernel,
         [((128, 1024), F32), ((3, 128, 1024), BF16)],
         [SMEM] + [VMEM] * 4,
         "project",
-    )(at, att, got, weight, out_peer)
+    )(at, keep, got, weight, out_peer)
     parts = [fetch(away[k - 1], "y", 4 - k) for k in (2, 1, 3)]
     middle, normed_two = call(
         middle_kernel,

time: 121 us -> 129 us (1.066)
  waiting for transfers between devices: 62.3 us -> 73.4 us
  starting transfers between devices: 42.4 us -> 39.1 us
    ppermute x24 -> x21, waiting for transfers between devices: 40.1 us -> 50.6 us  [fetch(): return lax.ppermute(value, axis, [((i + step) % n, i) for i in range(n)])]
    ppermute x24 -> x21, starting transfers between devices: 29.5 us -> 21.4 us  [fetch(): return lax.ppermute(value, axis, [((i + step) % n, i) for i in range(n)])]
    all_to_all x1, starting transfers between devices: 9.03 us -> 12 us  [local(): lax.all_to_all(front, ('z', 'x'), 0, 0, tiled=True).reshape(1024, 512)]
    ppermute x1, waiting for transfers between devices: 14.2 us -> 16.1 us  [local(): lax.ppermute(border, ('z', 'x', 'y', 'core'), [(spot(*divmod(s, 4), j, c)...]
    all_to_all x1, waiting for transfers between devices: 1.36 us -> 0.01 us  [local(): back = lax.all_to_all(back, 'z', 0, 0, tiled=True)]
  transfers between devices with their start and end apart: 27 -> 24, of which waited for: 14 -> 13; matrix products, arithmetic and copies ran while one was open for 1% -> 0% of each run, Pallas kernels for 4% -> 8%
where the time goes in v3:
time: 129 us; the launch traced here: 128 us
  waiting for transfers between devices  73.4 us (57%)
  starting transfers between devices  39.1 us (30%)
  Pallas kernels  15.5 us (12%)
    ppermute x21, waiting for transfers between devices, fetch(): return lax.ppermute(value, axis, [((i + step) % n, i) for i in range(n)])  50.6 us
    ppermute x21, starting transfers between devices, fetch(): return lax.ppermute(value, axis, [((i + step) % n, i) for i in range(n)])  21.4 us
    ppermute x1, waiting for transfers between devices, local(): lax.ppermute(border, ('z', 'x', 'y', 'core'), [(spot(*divmod(s, 4), j, c)...  16.1 us
    all_to_all x1, starting transfers between devices, local(): lax.all_to_all(front, ('z', 'x'), 0, 0, tiled=True).reshape(1024, 512)  12 us
    all_to_all x1, waiting for transfers between devices, local(): lax.all_to_all(front, ('z', 'x'), 0, 0, tiled=True).reshape(1024, 512)  6.8 us
    pallas_call x1, Pallas kernels, local(): call(attention_kernel, [((4, 128, 128), BF16), ((4, 128, 128), BF16), ((1...  4.96 us
    all_to_all x1, starting transfers between devices, local(): back = lax.all_to_all(back, 'z', 0, 0, tiled=True)  4.16 us
    pallas_call x4, Pallas kernels, mlp_second(): call(functools.partial(mlp_second_kernel, at=at), [((128, 1024), F32 if a...  2.99 us
  transfers between devices with their start and end apart: 24, of which 13 were waited for; matrix products, arithmetic and copies ran while one was open for 0% of the time, Pallas kernels for 8%

profile of v3, /device:TPU:1, one launch (start us, length us, event | category | flops | bytes accessed | tf_op | source)
XLA Modules:
  0.0 128.3 jit_solution(7484076283309052595)
XLA Ops:
  0.0 2.4 %start.1 = (bf16[128,1024]{1,0:T(8,128)(2,1)S(1)}, bf16[32,32,512]{2,1,0:T(8,128)(2,1)}, bf16[8,32,1024]{2,1,0:T(8,128)(2,1)}) custom-call(bf16[3,32,128]{2,1,0:T(8,128)(2,1)} %bitcast.23, bf16[32,128]{1,0:T(8,128)(2,1)} %bitcast.24, bf16[128,1024]{1,0:T(8,128)(2,1)} %tok.1, f32[1,1024]{1,0:T(1,128)} %bitcast.25, bf16[32,512]{1,0:T(8,128)(2,1)} %refs_4_.1, ...), custom_call_target="tpu_custom_call" | custom-call | flops 1048576 | bytes 2097152 | tf_op jit(solution)/shard_map/start/pallas_call | solution.py:254
  2.5 12.0 %all-to-all-start = ((bf16[32,32,512]{2,1,0:T(8,128)(2,1)}), bf16[32,32,512]{2,1,0:T(8,128)(2,1)S(1)}, u32[]{:S(2)}, u32[]{:S(2)}) async-start(bf16[32,32,512]{2,1,0:T(8,128)(2,1)} %get-tuple-element.28), calls=%async_computation | async-start | bytes 2097152 | tf_op jit(solution)/shard_map/all_to_all | solution.py:262
  14.5 2.8 %collective-permute-start = (bf16[128,1024]{1,0:T(8,128)(2,1)S(1)}, bf16[128,1024]{1,0:T(8,128)(2,1)S(1)}, u32[]{:S(2)}, u32[]{:S(2)}) collective-permute-start(bf16[128,1024]{1,0:T(8,128)(2,1)S(1)} %get-tuple-element.26.refs_0_), channel_id=1, source_target_pairs={{2,0},{4,2},{6,4},{0,6},{3,1},{5,3},{7,5},{1,7},{10,8},{12,10},{14... | collective-permute-start | bytes 786440 | tf_op jit(solution)/shard_map/ppermute | solution.py:226
  18.4 4.6 %collective-permute-done.refs_1_ = bf16[128,1024]{1,0:T(8,128)(2,1)S(1)} collective-permute-done((bf16[128,1024]{1,0:T(8,128)(2,1)S(1)}, bf16[128,1024]{1,0:T(8,128)(2,1)S(1)}, u32[]{:S(2)}, u32[]{:S(2)}) %collective-permute-start) | collective-permute-done | bytes 262176 | tf_op jit(solution)/shard_map/ppermute | solution.py:226
  23.0 2.4 %collective-permute-done.1.refs_2_ = bf16[128,1024]{1,0:T(8,128)(2,1)S(1)} collective-permute-done((bf16[128,1024]{1,0:T(8,128)(2,1)S(1)}, bf16[128,1024]{1,0:T(8,128)(2,1)S(1)}, u32[]{:S(2)}, u32[]{:S(2)}) %collective-permute-start.1) | collective-permute-done | bytes 262176 | tf_op jit(solution)/shard_map/ppermute | solution.py:226
  25.4 7.2 %collective-permute-done.2.refs_3_ = bf16[128,1024]{1,0:T(8,128)(2,1)S(1)} collective-permute-done((bf16[128,1024]{1,0:T(8,128)(2,1)S(1)}, bf16[128,1024]{1,0:T(8,128)(2,1)S(1)}, u32[]{:S(2)}, u32[]{:S(2)}) %collective-permute-start.2) | collective-permute-done | bytes 262176 | tf_op jit(solution)/shard_map/ppermute | solution.py:226
  33.9 6.8 %all-to-all-done = bf16[32,32,512]{2,1,0:T(8,128)(2,1)S(1)} async-done(((bf16[32,32,512]{2,1,0:T(8,128)(2,1)}), bf16[32,32,512]{2,1,0:T(8,128)(2,1)S(1)}, u32[]{:S(2)}, u32[]{:S(2)}) %all-to-all-start) | async-done | bytes 1048608 | tf_op jit(solution)/shard_map/all_to_all | solution.py:262
  40.7 4.2 %all-to-all-start.1 = ((bf16[8,32,1024]{2,1,0:T(8,128)(2,1)}), bf16[8,32,1024]{2,1,0:T(8,128)(2,1)S(1)}, u32[]{:S(2)}, u32[]{:S(2)}) async-start(bf16[8,32,1024]{2,1,0:T(8,128)(2,1)} %get-tuple-element.38), calls=%async_computation.1 | async-start | bytes 1048576 | tf_op jit(solution)/shard_map/all_to_all | solution.py:285
  44.9 1.5 %collective-permute-start.4 = (bf16[64,1024]{1,0:T(8,128)(2,1)S(1)}, bf16[64,1024]{1,0:T(8,128)(2,1)S(1)}, u32[]{:S(2)}, u32[]{:S(2)}) collective-permute-start(bf16[64,1024]{1,0:T(8,128)(2,1)S(1)} %get-tuple-element.29), channel_id=1, source_target_pairs={{0,248},{1,9},{2,250},{3,11},{4,252},{5,13},{6,254},{7,15},{8,0},{... | collective-permute-start | bytes 393224 | tf_op jit(solution)/shard_map/ppermute | solution.py:273
  46.4 16.1 %collective-permute-done.4.near_own = bf16[64,1024]{1,0:T(8,128)(2,1)S(1)} collective-permute-done((bf16[64,1024]{1,0:T(8,128)(2,1)S(1)}, bf16[64,1024]{1,0:T(8,128)(2,1)S(1)}, u32[]{:S(2)}, u32[]{:S(2)}) %collective-permute-start.4) | collective-permute-done | bytes 131104 | tf_op jit(solution)/shard_map/ppermute | solution.py:273
  63.8 5.0 %attention.1 = (bf16[4,128,128]{2,1,0:T(8,128)(2,1)S(1)}, bf16[4,128,128]{2,1,0:T(8,128)(2,1)S(1)}, bf16[1024,128]{1,0:T(8,128)(2,1)S(1)}) custom-call(s32[4]{0:T(128)S(1)} %pad_add_fusion.at, bf16[4,128,1024]{2,1,0:T(8,128)(2,1)S(1)} %get-tuple-element.27.own, bf16[4,128,1024]{2,1,0:T(8,128)(2,1)} %collective-permute-done.3.peer, ...), custom_call_target="tpu_custom_call" | custom-call | flops 1048576 | bytes 2097152 | tf_op jit(solution)/shard_map/attention/pallas_call | solution.py:286
  72.1 3.2 %collective-permute-start.8 = (bf16[128,1024]{1,0:T(8,128)(2,1)S(1)}, bf16[128,1024]{1,0:T(8,128)(2,1)S(1)}, u32[]{:S(2)}, u32[]{:S(2)}) collective-permute-start(bf16[128,1024]{1,0:T(8,128)(2,1)S(1)} %get-tuple-element.49), channel_id=1, source_target_pairs={{4,0},{6,2},{0,4},{2,6},{5,1},{7,3},{1,5},{3,7},{12,8},{14,10},{8,... | collective-permute-start | bytes 786440 | tf_op jit(solution)/shard_map/ppermute | solution.py:226
  75.6 2.3 %collective-permute-start.10 = (bf16[128,1024]{1,0:T(8,128)(2,1)S(1)}, bf16[128,1024]{1,0:T(8,128)(2,1)S(1)}, u32[]{:S(2)}, u32[]{:S(2)}) collective-permute-start(bf16[128,1024]{1,0:T(8,128)(2,1)S(1)} %get-tuple-element.47), channel_id=1, source_target_pairs={{2,0},{4,2},{6,4},{0,6},{3,1},{5,3},{7,5},{1,7},{10,8},{12,10},{14... | collective-permute-start | bytes 786440 | tf_op jit(solution)/shard_map/ppermute | solution.py:226
  77.9 3.1 %collective-permute-done.8.a = bf16[128,1024]{1,0:T(8,128)(2,1)S(1)} collective-permute-done((bf16[128,1024]{1,0:T(8,128)(2,1)S(1)}, bf16[128,1024]{1,0:T(8,128)(2,1)S(1)}, u32[]{:S(2)}, u32[]{:S(2)}) %collective-permute-start.8) | collective-permute-done | bytes 262176 | tf_op jit(solution)/shard_map/ppermute | solution.py:226
  81.0 6.7 %collective-permute-done.9.b = bf16[128,1024]{1,0:T(8,128)(2,1)S(1)} collective-permute-done((bf16[128,1024]{1,0:T(8,128)(2,1)S(1)}, bf16[128,1024]{1,0:T(8,128)(2,1)S(1)}, u32[]{:S(2)}, u32[]{:S(2)}) %collective-permute-start.9) | collective-permute-done | bytes 262176 | tf_op jit(solution)/shard_map/ppermute | solution.py:226
  88.1 2.8 %collective-permute-start.15 = (bf16[128,1024]{1,0:T(8,128)(2,1)S(1)}, bf16[128,1024]{1,0:T(8,128)(2,1)S(1)}, u32[]{:S(2)}, u32[]{:S(2)}) collective-permute-start(bf16[128,1024]{1,0:T(8,128)(2,1)S(1)} %get-tuple-element.36.a.rows), channel_id=1, source_target_pairs={{2,0},{4,2},{6,4},{0,6},{3,1},{5,3},{7,5},{1,7},{10,8},{12,10},{14... | collective-permute-start | bytes 786440 | tf_op jit(solution)/shard_map/ppermute | solution.py:226
  91.6 1.6 %collective-permute-start.12 = (bf16[8,32,512]{2,1,0:T(8,128)(2,1)S(1)}, bf16[8,32,512]{2,1,0:T(8,128)(2,1)S(1)}, u32[]{:S(2)}, u32[]{:S(2)}) collective-permute-start(bf16[8,32,512]{2,1,0:T(8,128)(2,1)S(1)} %slice.20), channel_id=1, source_target_pairs={{8,0},{16,8},{24,16},{0,24},{9,1},{17,9},{25,17},{1,25},{10,2},{18... | collective-permute-start | bytes 786440 | tf_op jit(solution)/shard_map/ppermute | solution.py:226
  93.3 8.2 %collective-permute-done.15.b.rows = bf16[128,1024]{1,0:T(8,128)(2,1)S(1)} collective-permute-done((bf16[128,1024]{1,0:T(8,128)(2,1)S(1)}, bf16[128,1024]{1,0:T(8,128)(2,1)S(1)}, u32[]{:S(2)}, u32[]{:S(2)}) %collective-permute-start.15) | collective-permute-done | bytes 262176 | tf_op jit(solution)/shard_map/ppermute | solution.py:226
  101.5 4.7 %collective-permute-done.17.d.rows = bf16[128,1024]{1,0:T(8,128)(2,1)S(1)} collective-permute-done((bf16[128,1024]{1,0:T(8,128)(2,1)S(1)}, bf16[128,1024]{1,0:T(8,128)(2,1)S(1)}, u32[]{:S(2)}, u32[]{:S(2)}) %collective-permute-start.17) | collective-permute-done | bytes 262176 | tf_op jit(solution)/shard_map/ppermute | solution.py:226
  107.5 1.4 %mlp_first.1.part = f32[512,1024]{1,0:T(8,128)S(1)} custom-call(bf16[128,1024]{1,0:T(8,128)(2,1)S(1)} %get-tuple-element.36.a.rows, bf16[128,1024]{1,0:T(8,128)(2,1)S(1)} %collective-permute-done.15.b.rows, bf16[128,1024]{1,0:T(8,128)(2,1)S(1)} %collective-permute-done.16.c.rows, bf16[128,1024]{1,0:T(8,128)(2,1)S(1)} %collective-permute-done.17.d.rows, ...), custom_call_target="tpu_custom_call" | custom-call | flops 1048576 | bytes 2097152 | tf_op jit(solution)/shard_map/mlp_first/pallas_call | solution.py:324
  108.9 2.4 %collective-permute-done.18.weight = bf16[1024,1024]{1,0:T(8,128)(2,1)S(1)} collective-permute-done((bf16[1024,1024]{1,0:T(8,128)(2,1)S(1)}, bf16[1024,1024]{1,0:T(8,128)(2,1)S(1)}, u32[]{:S(2)}, u32[]{:S(2)}) %collective-permute-start.18) | collective-permute-done | bytes 2097184 | tf_op jit(solution)/shard_map/ppermute | solution.py:226
  114.6 2.2 %collective-permute-start.21 = (bf16[128,1024]{1,0:T(8,128)(2,1)S(1)}, bf16[128,1024]{1,0:T(8,128)(2,1)S(1)}, u32[]{:S(2)}, u32[]{:S(2)}) collective-permute-start(bf16[128,1024]{1,0:T(8,128)(2,1)S(1)} %mlp_second.7), channel_id=1, source_target_pairs={{2,0},{4,2},{6,4},{0,6},{3,1},{5,3},{7,5},{1,7},{10,8},{12,10},{14... | collective-permute-start | bytes 786440 | tf_op jit(solution)/shard_map/ppermute | solution.py:226
  117.6 3.6 %collective-permute-done.19.a = bf16[128,1024]{1,0:T(8,128)(2,1)S(1)} collective-permute-done((bf16[128,1024]{1,0:T(8,128)(2,1)S(1)}, bf16[128,1024]{1,0:T(8,128)(2,1)S(1)}, u32[]{:S(2)}, u32[]{:S(2)}) %collective-permute-start.19) | collective-permute-done | bytes 262176 | tf_op jit(solution)/shard_map/ppermute | solution.py:226
  121.2 6.3 %collective-permute-done.20.b = bf16[128,1024]{1,0:T(8,128)(2,1)S(1)} collective-permute-done((bf16[128,1024]{1,0:T(8,128)(2,1)S(1)}, bf16[128,1024]{1,0:T(8,128)(2,1)S(1)}, u32[]{:S(2)}, u32[]{:S(2)}) %collective-permute-start.20) | collective-permute-done | bytes 262176 | tf_op jit(solution)/shard_map/ppermute | solution.py:226
  (50 shorter events, 14.7 us)
Async XLA Ops:
  2.5 38.2 %all-to-all-start = ((bf16[32,32,512]{2,1,0:T(8,128)(2,1)}), bf16[32,32,512]{2,1,0:T(8,128)(2,1)S(1)}, u32[]{:S(2)}, u32[]{:S(2)}) async-start(bf16[32,32,512]{2,1,0:T(8,128)(2,1)} %get-tuple-element.28), calls=%async_computation | async-start | bytes 2097152 | tf_op jit(solution)/shard_map/all_to_all | solution.py:262
  14.5 8.5 %collective-permute-start = (bf16[128,1024]{1,0:T(8,128)(2,1)S(1)}, bf16[128,1024]{1,0:T(8,128)(2,1)S(1)}, u32[]{:S(2)}, u32[]{:S(2)}) collective-permute-start(bf16[128,1024]{1,0:T(8,128)(2,1)S(1)} %get-tuple-element.26.refs_0_), channel_id=1, source_target_pairs={{2,0},{4,2},{6,4},{0,6},{3,1},{5,3},{7,5},{1,7},{10,8},{12,10},{14... | collective-permute-start | bytes 786440 | tf_op jit(solution)/shard_map/ppermute | solution.py:226
  17.3 8.1 %collective-permute-start.1 = (bf16[128,1024]{1,0:T(8,128)(2,1)S(1)}, bf16[128,1024]{1,0:T(8,128)(2,1)S(1)}, u32[]{:S(2)}, u32[]{:S(2)}) collective-permute-start(bf16[128,1024]{1,0:T(8,128)(2,1)S(1)} %get-tuple-element.26.refs_0_), channel_id=1, source_target_pairs={{4,0},{6,2},{0,4},{2,6},{5,1},{7,3},{1,5},{3,7},{12,8},{14,10},{8,... | collective-permute-start | bytes 786440 | tf_op jit(solution)/shard_map/ppermute | solution.py:226
  17.7 15.0 %collective-permute-start.2 = (bf16[128,1024]{1,0:T(8,128)(2,1)S(1)}, bf16[128,1024]{1,0:T(8,128)(2,1)S(1)}, u32[]{:S(2)}, u32[]{:S(2)}) collective-permute-start(bf16[128,1024]{1,0:T(8,128)(2,1)S(1)} %get-tuple-element.26.refs_0_), channel_id=1, source_target_pairs={{6,0},{0,2},{2,4},{4,6},{7,1},{1,3},{3,5},{5,7},{14,8},{8,10},{10,... | collective-permute-start | bytes 786440 | tf_op jit(solution)/shard_map/ppermute | solution.py:226
  33.3 30.5 %collective-permute-start.3 = (bf16[4,128,1024]{2,1,0:T(8,128)(2,1)S(1)}, bf16[4,128,1024]{2,1,0:T(8,128)(2,1)}, u32[]{:S(2)}, u32[]{:S(2)}) collective-permute-start(bf16[4,128,1024]{2,1,0:T(8,128)(2,1)S(1)} %get-tuple-element.27.own), channel_id=1, source_target_pairs={{1,0},{0,1},{3,2},{2,3},{5,4},{4,5},{7,6},{6,7},{9,8},{8,9},{11,10... | collective-permute-start | bytes 3145736 | tf_op jit(solution)/shard_map/ppermute | solution.py:226
  40.7 28.7 %all-to-all-start.1 = ((bf16[8,32,1024]{2,1,0:T(8,128)(2,1)}), bf16[8,32,1024]{2,1,0:T(8,128)(2,1)S(1)}, u32[]{:S(2)}, u32[]{:S(2)}) async-start(bf16[8,32,1024]{2,1,0:T(8,128)(2,1)} %get-tuple-element.38), calls=%async_computation.1 | async-start | bytes 1048576 | tf_op jit(solution)/shard_map/all_to_all | solution.py:285
  44.9 17.6 %collective-permute-start.4 = (bf16[64,1024]{1,0:T(8,128)(2,1)S(1)}, bf16[64,1024]{1,0:T(8,128)(2,1)S(1)}, u32[]{:S(2)}, u32[]{:S(2)}) collective-permute-start(bf16[64,1024]{1,0:T(8,128)(2,1)S(1)} %get-tuple-element.29), channel_id=1, source_target_pairs={{0,248},{1,9},{2,250},{3,11},{4,252},{5,13},{6,254},{7,15},{8,0},{... | collective-permute-start | bytes 393224 | tf_op jit(solution)/shard_map/ppermute | solution.py:273
  62.4 1.3 %collective-permute-start.5 = (bf16[64,1024]{1,0:T(8,128)(2,1)S(1)}, bf16[64,1024]{1,0:T(8,128)(2,1)S(1)}, u32[]{:S(2)}, u32[]{:S(2)}) collective-permute-start(bf16[64,1024]{1,0:T(8,128)(2,1)S(1)} %collective-permute-done.4.near_own), channel_id=1, source_target_pairs={{1,0},{0,1},{3,2},{2,3},{5,4},{4,5},{7,6},{6,7},{9,8},{8,9},{11,10... | collective-permute-start | bytes 393224 | tf_op jit(solution)/shard_map/ppermute | solution.py:226
  68.8 2.1 %collective-permute-start.7 = (bf16[1024,128]{1,0:T(8,128)(2,1)S(1)}, bf16[1024,128]{1,0:T(8,128)(2,1)S(1)}, u32[]{:S(2)}, u32[]{:S(2)}) collective-permute-start(bf16[1024,128]{1,0:T(8,128)(2,1)S(1)} %get-tuple-element.32.weight), channel_id=1, source_target_pairs={{1,0},{0,1},{3,2},{2,3},{5,4},{4,5},{7,6},{6,7},{9,8},{8,9},{11,10... | collective-permute-start | bytes 786440 | tf_op jit(solution)/shard_map/ppermute | solution.py:226
  69.0 1.8 %collective-permute-start.6 = (bf16[4,128,128]{2,1,0:T(8,128)(2,1)S(1)}, bf16[4,128,128]{2,1,0:T(8,128)(2,1)S(1)}, u32[]{:S(2)}, u32[]{:S(2)}) collective-permute-start(bf16[4,128,128]{2,1,0:T(8,128)(2,1)S(1)} %get-tuple-element.31), channel_id=1, source_target_pairs={{1,0},{0,1},{3,2},{2,3},{5,4},{4,5},{7,6},{6,7},{9,8},{8,9},{11,10... | collective-permute-start | bytes 393224 | tf_op jit(solution)/shard_map/ppermute | solution.py:226
  69.4 22.2 %collective-permute-start.11 = (bf16[8,32,1024]{2,1,0:T(8,128)(2,1)S(1)}, bf16[8,32,1024]{2,1,0:T(8,128)(2,1)S(1)}, u32[]{:S(2)}, u32[]{:S(2)}) collective-permute-start(bf16[8,32,1024]{2,1,0:T(8,128)(2,1)S(1)} %all-to-all-done.1.here), channel_id=1, source_target_pairs={{8,0},{16,8},{24,16},{0,24},{9,1},{17,9},{25,17},{1,25},{10,2},{18... | collective-permute-start | bytes 1572872 | tf_op jit(solution)/shard_map/ppermute | solution.py:226
  69.8 23.4 %collective-permute-start.13 = (bf16[8,32,1024]{2,1,0:T(8,128)(2,1)S(1)}, bf16[8,32,1024]{2,1,0:T(8,128)(2,1)S(1)}, u32[]{:S(2)}, u32[]{:S(2)}) collective-permute-start(bf16[8,32,1024]{2,1,0:T(8,128)(2,1)S(1)} %all-to-all-done.1.here), channel_id=1, source_target_pairs={{24,0},{0,8},{8,16},{16,24},{25,1},{1,9},{9,17},{17,25},{26,2},{2,... | collective-permute-start | bytes 1572872 | tf_op jit(solution)/shard_map/ppermute | solution.py:226
  72.1 8.9 %collective-permute-start.8 = (bf16[128,1024]{1,0:T(8,128)(2,1)S(1)}, bf16[128,1024]{1,0:T(8,128)(2,1)S(1)}, u32[]{:S(2)}, u32[]{:S(2)}) collective-permute-start(bf16[128,1024]{1,0:T(8,128)(2,1)S(1)} %get-tuple-element.49), channel_id=1, source_target_pairs={{4,0},{6,2},{0,4},{2,6},{5,1},{7,3},{1,5},{3,7},{12,8},{14,10},{8,... | collective-permute-start | bytes 786440 | tf_op jit(solution)/shard_map/ppermute | solution.py:226
  75.2 12.4 %collective-permute-start.9 = (bf16[128,1024]{1,0:T(8,128)(2,1)S(1)}, bf16[128,1024]{1,0:T(8,128)(2,1)S(1)}, u32[]{:S(2)}, u32[]{:S(2)}) collective-permute-start(bf16[128,1024]{1,0:T(8,128)(2,1)S(1)} %get-tuple-element.48), channel_id=1, source_target_pairs={{6,0},{0,2},{2,4},{4,6},{7,1},{1,3},{3,5},{5,7},{14,8},{8,10},{10,... | collective-permute-start | bytes 786440 | tf_op jit(solution)/shard_map/ppermute | solution.py:226
  75.6 12.0 %collective-permute-start.10 = (bf16[128,1024]{1,0:T(8,128)(2,1)S(1)}, bf16[128,1024]{1,0:T(8,128)(2,1)S(1)}, u32[]{:S(2)}, u32[]{:S(2)}) collective-permute-start(bf16[128,1024]{1,0:T(8,128)(2,1)S(1)} %get-tuple-element.47), channel_id=1, source_target_pairs={{2,0},{4,2},{6,4},{0,6},{3,1},{5,3},{7,5},{1,7},{10,8},{12,10},{14... | collective-permute-start | bytes 786440 | tf_op jit(solution)/shard_map/ppermute | solution.py:226
  88.1 13.5 %collective-permute-start.15 = (bf16[128,1024]{1,0:T(8,128)(2,1)S(1)}, bf16[128,1024]{1,0:T(8,128)(2,1)S(1)}, u32[]{:S(2)}, u32[]{:S(2)}) collective-permute-start(bf16[128,1024]{1,0:T(8,128)(2,1)S(1)} %get-tuple-element.36.a.rows), channel_id=1, source_target_pairs={{2,0},{4,2},{6,4},{0,6},{3,1},{5,3},{7,5},{1,7},{10,8},{12,10},{14... | collective-permute-start | bytes 786440 | tf_op jit(solution)/shard_map/ppermute | solution.py:226
  90.9 10.7 %collective-permute-start.16 = (bf16[128,1024]{1,0:T(8,128)(2,1)S(1)}, bf16[128,1024]{1,0:T(8,128)(2,1)S(1)}, u32[]{:S(2)}, u32[]{:S(2)}) collective-permute-start(bf16[128,1024]{1,0:T(8,128)(2,1)S(1)} %get-tuple-element.36.a.rows), channel_id=1, source_target_pairs={{4,0},{6,2},{0,4},{2,6},{5,1},{7,3},{1,5},{3,7},{12,8},{14,10},{8,... | collective-permute-start | bytes 786440 | tf_op jit(solution)/shard_map/ppermute | solution.py:226
  91.2 15.0 %collective-permute-start.17 = (bf16[128,1024]{1,0:T(8,128)(2,1)S(1)}, bf16[128,1024]{1,0:T(8,128)(2,1)S(1)}, u32[]{:S(2)}, u32[]{:S(2)}) collective-permute-start(bf16[128,1024]{1,0:T(8,128)(2,1)S(1)} %get-tuple-element.36.a.rows), channel_id=1, source_target_pairs={{6,0},{0,2},{2,4},{4,6},{7,1},{1,3},{3,5},{5,7},{14,8},{8,10},{10,... | collective-permute-start | bytes 786440 | tf_op jit(solution)/shard_map/ppermute | solution.py:226
  91.6 14.6 %collective-permute-start.12 = (bf16[8,32,512]{2,1,0:T(8,128)(2,1)S(1)}, bf16[8,32,512]{2,1,0:T(8,128)(2,1)S(1)}, u32[]{:S(2)}, u32[]{:S(2)}) collective-permute-start(bf16[8,32,512]{2,1,0:T(8,128)(2,1)S(1)} %slice.20), channel_id=1, source_target_pairs={{8,0},{16,8},{24,16},{0,24},{9,1},{17,9},{25,17},{1,25},{10,2},{18... | collective-permute-start | bytes 786440 | tf_op jit(solution)/shard_map/ppermute | solution.py:226
  93.2 13.0 %collective-permute-start.14 = (bf16[8,32,512]{2,1,0:T(8,128)(2,1)S(1)}, bf16[8,32,512]{2,1,0:T(8,128)(2,1)S(1)}, u32[]{:S(2)}, u32[]{:S(2)}) collective-permute-start(bf16[8,32,512]{2,1,0:T(8,128)(2,1)S(1)} %slice.21), channel_id=1, source_target_pairs={{24,0},{0,8},{8,16},{16,24},{25,1},{1,9},{9,17},{17,25},{26,2},{2,... | collective-permute-start | bytes 786440 | tf_op jit(solution)/shard_map/ppermute | solution.py:226
  106.9 4.4 %collective-permute-start.18 = (bf16[1024,1024]{1,0:T(8,128)(2,1)S(1)}, bf16[1024,1024]{1,0:T(8,128)(2,1)S(1)}, u32[]{:S(2)}, u32[]{:S(2)}) collective-permute-start(bf16[1024,1024]{1,0:T(8,128)(2,1)S(1)} %mlp_lay.1.weight), channel_id=1, source_target_pairs={{1,0},{0,1},{3,2},{2,3},{5,4},{4,5},{7,6},{6,7},{9,8},{8,9},{11,10... | collective-permute-start | bytes 6291464 | tf_op jit(solution)/shard_map/ppermute | solution.py:226
  112.0 9.2 %collective-permute-start.19 = (bf16[128,1024]{1,0:T(8,128)(2,1)S(1)}, bf16[128,1024]{1,0:T(8,128)(2,1)S(1)}, u32[]{:S(2)}, u32[]{:S(2)}) collective-permute-start(bf16[128,1024]{1,0:T(8,128)(2,1)S(1)} %mlp_second.5), channel_id=1, source_target_pairs={{4,0},{6,2},{0,4},{2,6},{5,1},{7,3},{1,5},{3,7},{12,8},{14,10},{8,... | collective-permute-start | bytes 786440 | tf_op jit(solution)/shard_map/ppermute | solution.py:226
  113.2 14.2 %collective-permute-start.20 = (bf16[128,1024]{1,0:T(8,128)(2,1)S(1)}, bf16[128,1024]{1,0:T(8,128)(2,1)S(1)}, u32[]{:S(2)}, u32[]{:S(2)}) collective-permute-start(bf16[128,1024]{1,0:T(8,128)(2,1)S(1)} %mlp_second.6), channel_id=1, source_target_pairs={{6,0},{0,2},{2,4},{4,6},{7,1},{1,3},{3,5},{5,7},{14,8},{8,10},{10,... | collective-permute-start | bytes 786440 | tf_op jit(solution)/shard_map/ppermute | solution.py:226
  114.6 12.9 %collective-permute-start.21 = (bf16[128,1024]{1,0:T(8,128)(2,1)S(1)}, bf16[128,1024]{1,0:T(8,128)(2,1)S(1)}, u32[]{:S(2)}, u32[]{:S(2)}) collective-permute-start(bf16[128,1024]{1,0:T(8,128)(2,1)S(1)} %mlp_second.7), channel_id=1, source_target_pairs={{2,0},{4,2},{6,4},{0,6},{3,1},{5,3},{7,5},{1,7},{10,8},{12,10},{14... | collective-permute-start | bytes 786440 | tf_op jit(solution)/shard_map/ppermute | solution.py:226
  (5 other events, 231.8 us)

commit v4 on v3

--- a/solution.py
+++ b/solution.py
@@ -48,7 +48,7 @@
     copies[0].wait()
     copies[1].wait()
     pack = jnp.concatenate([qkv[0], qkv[1], qkv[2], out_t[...]], axis=1)
-    for i in range(32):
+    for i in range(8):
         front[i] = pack
     copies[2].wait()
     copies[3].wait()
@@ -61,11 +61,15 @@
 
 
 def collect_kernel(at, *refs):
-    blocks, own, border = refs[:4], refs[4], refs[5]
+    blocks, own, border = refs[:4], refs[4:6], refs[6]
     y, core = at[0], at[1]
     for k in range(4):
         t = lax.rem(y + k, 4)
-        own[t] = blocks[k][...]
+        for low in range(2):
+
+            @pl.when(t // 2 == low)
+            def _():
+                own[low][lax.rem(t, 2)] = blocks[k][...]
 
         @pl.when((core == 0) & (t == 0))
         def _():
@@ -76,16 +80,21 @@
             border[...] = blocks[k][128 - WIN :]
 
 
-def lay_kernel(at, here, right, up_far, down_far, left, out):
+def lay(x, here, right, far_low, far_high, left, out):
+    half = out.shape[1] // 2
     for k, block in enumerate((here, right, None, left)):
-        base = lax.rem(at[2] + k, 4) * 32
+        base = lax.rem(x + k, 4) * 32
         for z in range(8):
             rows = pl.ds(pl.multiple_of(z * 128 + base, 32), 32)
             if block is None:
-                out[rows, :512] = up_far[z]
-                out[rows, 512:] = down_far[z]
+                out[rows, :half] = far_low[z]
+                out[rows, half:] = far_high[z]
             else:
                 out[rows] = block[z]
+
+
+def lay_kernel(at, *refs):
+    lay(at[2], *refs)
 
 
 def attend(query, kv, first, count, key_start):
@@ -108,9 +117,10 @@
 
 
 def attention_kernel(
-    at, own, peer, weight, near_own, near_peer, gains, first, count,
-    keep, give, out_w, q_s, kv_s, att,
+    at, own_low, own_high, peer_low, peer_high, here, right, far_low, far_high, left,
+    near_own, near_peer, gains, first, count, keep, give, out_w, weight, q_s, kv_s, att,
 ):
+    lay(at[2], here, right, far_low, far_high, left, weight)
     core, anchor = at[1], at[3]
     gain = gains[...]
     gain = jnp.concatenate([gain[:, 0], gain[:, 1]], axis=1)
@@ -126,7 +136,8 @@
 
     half = first_half(256)
     for t in range(4):
-        rows = jnp.concatenate([own[t], peer[t]], axis=0)
+        other = peer_low[t] if t < 2 else peer_high[t - 2]
+        rows = jnp.concatenate([own_low[t] if t < 2 else own_high[t - 2], other], axis=0)
         qkv = jnp.dot(rows, weight[:, :384], preferred_element_type=F32)
         query = head_norm(qkv[:, :128], gain[0:1], half)
         key = head_norm(qkv[:, 128:256], gain[1:2], half)
@@ -226,6 +237,13 @@
     return lax.ppermute(value, axis, [((i + step) % n, i) for i in range(n)])
 
 
+def relay(block):
+    half = block.shape[2] // 2
+    right, left = fetch(block, "x", 1), fetch(block, "x", 3)
+    far_low, far_high = fetch(right[:, :, :half], "x", 1), fetch(left[:, :, half:], "x", 3)
+    return block, right, far_low, far_high, left
+
+
 def local(
     tokens,
     win_first,
@@ -253,21 +271,25 @@
     ]
     normed, front, back = call(
         start_kernel,
-        [((128, 1024), BF16), ((32, 32, 512), BF16), ((8, 32, 1024), BF16)],
+        [((128, 1024), BF16), ((8, 32, 512), BF16), ((8, 32, 1024), BF16)],
         [HBM] * 6,
         "start",
         scratch=[pltpu.VMEM(v.shape, v.dtype) for v in given]
         + [pltpu.SemaphoreType.DMA((6,))],
     )(*[pltpu.with_memory_space_constraint(v, pltpu.HBM) for v in given])
-    weight = lax.all_to_all(front, ("z", "x"), 0, 0, tiled=True).reshape(1024, 512)
+    front = lax.all_to_all(front, "z", 0, 0, tiled=True)
     far = {k: fetch(normed, "y", k) for k in (2, 1, 3)}
-    own, border = call(
+    weights = relay(front)
+    back, _ = lax.optimization_barrier((back, front))
+    back = lax.all_to_all(back, "z", 0, 0, tiled=True)
+    far, _ = lax.optimization_barrier((far, (weights[1], weights[4])))
+    own_low, own_high, border = call(
         collect_kernel,
-        [((4, 128, 1024), BF16), ((WIN, 1024), BF16)],
+        [((2, 128, 1024), BF16), ((2, 128, 1024), BF16), ((WIN, 1024), BF16)],
         [SMEM] + [VMEM] * 4,
         "collect",
     )(at, normed, far[1], far[2], far[3])
-    peer = fetch(own, "core", 1)
+    peer_low, peer_high = fetch(own_low, "core", 1), fetch(own_high, "core", 1)
     spot = lambda z, x, y, core: ((z * 4 + x) * 4 + y) * 2 + core
     shift = lambda s, by: divmod((s + by) % 32, 4)
     near_own = lax.ppermute(
@@ -281,24 +303,20 @@
         ],
     )
     near_peer = fetch(near_own, "core", 1)
-    back, _ = lax.optimization_barrier((back, (weight, border)))
-    back = lax.all_to_all(back, "z", 0, 0, tiled=True)
     keep, give, weight = call(
         attention_kernel,
         [((4, 128, 128), BF16), ((4, 128, 128), BF16), ((1024, 128), BF16)],
-        [SMEM] + [VMEM] * 8,
+        [SMEM] + [VMEM] * 14,
         "attention",
         scratch=[
+            pltpu.VMEM((1024, 512), BF16),
             pltpu.VMEM((1024, 128), BF16),
             pltpu.VMEM((1024 + 2 * WIN, 256), BF16),
             pltpu.VMEM((2, 4, 128, 128), BF16),
         ],
-    )(at, own, peer, weight, near_own, near_peer, qk_gain, first, count)
-
-    right, left = fetch(back, "x", 1), fetch(back, "x", 3)
-    up_far = fetch(right[:, :, :512], "x", 1)
-    down_far = fetch(left[:, :, 512:], "x", 3)
-
+    )(at, own_low, own_high, peer_low, peer_high, *weights, near_own, near_peer, qk_gain, first, count)
+
+    mlp_weights = relay(back)
     out_peer = fetch(weight, "core", 1)
     got = fetch(give, "core", 1)
     mine_attended, away = call(
@@ -316,7 +334,7 @@
     )(tokens, mine_attended, *parts, norm2_gain.reshape(1, 1024))
 
     far = {k: fetch(normed_two, "y", k) for k in (2, 1, 3)}
-    laid, far = lax.optimization_barrier(((back, right, up_far, down_far, left), far))
+    laid, far = lax.optimization_barrier((mlp_weights, far))
     (mlp_own,) = call(lay_kernel, [((1024, 1024), BF16)], [SMEM] + [VMEM] * 5, "mlp_lay")(
         at, *laid
     )

time: 129 us -> 111 us (0.86)
  waiting for transfers between devices: 73.4 us -> 52.9 us
  starting transfers between devices: 39.1 us -> 42.8 us
    ppermute x21 -> x26, waiting for transfers between devices: 50.6 us -> 39.3 us  [fetch(): return lax.ppermute(value, axis, [((i + step) % n, i) for i in range(n)])]
    ppermute x1, waiting for transfers between devices: 16.1 us -> 7.08 us  [local(): lax.ppermute(border, ('z', 'x', 'y', 'core'), [(spot(*divmod(s, 4), j, c)...]
    ppermute x21 -> x26, starting transfers between devices: 21.4 us -> 30.3 us  [fetch(): return lax.ppermute(value, axis, [((i + step) % n, i) for i in range(n)])]
    all_to_all x1, starting transfers between devices: 12 us -> 9.03 us  [local(): front = lax.all_to_all(front, 'z', 0, 0, tiled=True)]
    ppermute x1, starting transfers between devices: 1.51 us -> 0.01 us  [local(): lax.ppermute(border, ('z', 'x', 'y', 'core'), [(spot(*divmod(s, 4), j, c)...]
  transfers between devices with their start and end apart: 24 -> 29, of which waited for: 13 -> 13; matrix products, arithmetic and copies ran while one was open for 0% -> 0% of each run, Pallas kernels for 8% -> 9%
where the time goes in v4:
time: 111 us
  waiting for transfers between devices  52.9 us (48%)
  starting transfers between devices  42.8 us (39%)
  Pallas kernels  14.7 us (13%)
    ppermute x26, waiting for transfers between devices, fetch(): return lax.ppermute(value, axis, [((i + step) % n, i) for i in range(n)])  39.3 us
    ppermute x26, starting transfers between devices, fetch(): return lax.ppermute(value, axis, [((i + step) % n, i) for i in range(n)])  30.3 us
    all_to_all x1, starting transfers between devices, local(): front = lax.all_to_all(front, 'z', 0, 0, tiled=True)  9.03 us
    ppermute x1, waiting for transfers between devices, local(): lax.ppermute(border, ('z', 'x', 'y', 'core'), [(spot(*divmod(s, 4), j, c)...  7.08 us
    all_to_all x1, waiting for transfers between devices, local(): front = lax.all_to_all(front, 'z', 0, 0, tiled=True)  6.59 us
    pallas_call x1, Pallas kernels, local(): call(attention_kernel, [((4, 128, 128), BF16), ((4, 128, 128), BF16), ((1...  4.34 us
    all_to_all x1, starting transfers between devices, local(): back = lax.all_to_all(back, 'z', 0, 0, tiled=True)  3.49 us
    pallas_call x4, Pallas kernels, mlp_second(): call(functools.partial(mlp_second_kernel, at=at), [((128, 1024), F32 if a...  3 us
  transfers between devices with their start and end apart: 29, of which 13 were waited for; matrix products, arithmetic and copies ran while one was open for 0% of the time, Pallas kernels for 9%

profile of v4, /device:TPU:1, one launch (start us, length us, event | category | flops | bytes accessed | tf_op | source)
XLA Modules:
  0.0 110.8 jit_solution(6995990760470951467)
XLA Ops:
  0.0 2.2 %start.1 = (bf16[128,1024]{1,0:T(8,128)(2,1)S(1)}, bf16[8,32,512]{2,1,0:T(8,128)(2,1)}, bf16[8,32,1024]{2,1,0:T(8,128)(2,1)}) custom-call(bf16[3,32,128]{2,1,0:T(8,128)(2,1)} %bitcast.21, bf16[32,128]{1,0:T(8,128)(2,1)} %bitcast.22, bf16[128,1024]{1,0:T(8,128)(2,1)} %tok.1, f32[1,1024]{1,0:T(1,128)} %bitcast.23, bf16[32,512]{1,0:T(8,128)(2,1)} %refs_4_.1, ...), custom_call_target="tpu_custom_call" | custom-call | flops 1048576 | bytes 2097152 | tf_op jit(solution)/shard_map/start/pallas_call | solution.py:272
  2.2 9.0 %all-to-all-start = ((bf16[8,32,512]{2,1,0:T(8,128)(2,1)}), bf16[8,32,512]{2,1,0:T(8,128)(2,1)S(1)}, u32[]{:S(2)}, u32[]{:S(2)}) async-start(bf16[8,32,512]{2,1,0:T(8,128)(2,1)} %get-tuple-element.31), calls=%async_computation | async-start | bytes 524288 | tf_op jit(solution)/shard_map/all_to_all | solution.py:280
  11.2 2.7 %collective-permute-start = (bf16[128,1024]{1,0:T(8,128)(2,1)S(1)}, bf16[128,1024]{1,0:T(8,128)(2,1)S(1)}, u32[]{:S(2)}, u32[]{:S(2)}) collective-permute-start(bf16[128,1024]{1,0:T(8,128)(2,1)S(1)} %get-tuple-element.30.refs_0_), channel_id=1, source_target_pairs={{2,0},{4,2},{6,4},{0,6},{3,1},{5,3},{7,5},{1,7},{10,8},{12,10},{14... | collective-permute-start | bytes 786440 | tf_op jit(solution)/shard_map/ppermute | solution.py:237
  15.0 6.6 %all-to-all-done.here = bf16[8,32,512]{2,1,0:T(8,128)(2,1)S(1)} async-done(((bf16[8,32,512]{2,1,0:T(8,128)(2,1)}), bf16[8,32,512]{2,1,0:T(8,128)(2,1)S(1)}, u32[]{:S(2)}, u32[]{:S(2)}) %all-to-all-start) | async-done | bytes 262176 | tf_op jit(solution)/shard_map/all_to_all | solution.py:280
  21.6 2.5 %collective-permute-start.3 = (bf16[8,32,512]{2,1,0:T(8,128)(2,1)S(1)}, bf16[8,32,512]{2,1,0:T(8,128)(2,1)S(1)}, u32[]{:S(2)}, u32[]{:S(2)}) collective-permute-start(bf16[8,32,512]{2,1,0:T(8,128)(2,1)S(1)} %all-to-all-done.here), channel_id=1, source_target_pairs={{8,0},{16,8},{24,16},{0,24},{9,1},{17,9},{25,17},{1,25},{10,2},{18... | collective-permute-start | bytes 786440 | tf_op jit(solution)/shard_map/ppermute | solution.py:237
  24.1 3.5 %all-to-all-start.1 = ((bf16[8,32,1024]{2,1,0:T(8,128)(2,1)}), bf16[8,32,1024]{2,1,0:T(8,128)(2,1)S(1)}, u32[]{:S(2)}, u32[]{:S(2)}) async-start(bf16[8,32,1024]{2,1,0:T(8,128)(2,1)} %get-tuple-element.46), calls=%async_computation.1 | async-start | bytes 1048576 | tf_op jit(solution)/shard_map/all_to_all | solution.py:284
  27.7 1.6 %collective-permute-done.2.refs_3_ = bf16[128,1024]{1,0:T(8,128)(2,1)S(1)} collective-permute-done((bf16[128,1024]{1,0:T(8,128)(2,1)S(1)}, bf16[128,1024]{1,0:T(8,128)(2,1)S(1)}, u32[]{:S(2)}, u32[]{:S(2)}) %collective-permute-start.2) | collective-permute-done | bytes 262176 | tf_op jit(solution)/shard_map/ppermute | solution.py:237
  31.2 4.0 %collective-permute-start.5 = (bf16[2,128,1024]{2,1,0:T(8,128)(2,1)S(1)}, bf16[2,128,1024]{2,1,0:T(8,128)(2,1)S(1)}, u32[]{:S(2)}, u32[]{:S(2)}) collective-permute-start(bf16[2,128,1024]{2,1,0:T(8,128)(2,1)S(1)} %get-tuple-element.35.own_low), channel_id=1, source_target_pairs={{1,0},{0,1},{3,2},{2,3},{5,4},{4,5},{7,6},{6,7},{9,8},{8,9},{11,10... | collective-permute-start | bytes 1572872 | tf_op jit(solution)/shard_map/ppermute | solution.py:237
  35.3 2.8 %collective-permute-start.7 = (bf16[8,32,256]{2,1,0:T(8,128)(2,1)S(1)}, bf16[8,32,256]{2,1,0:T(8,128)(2,1)S(1)}, u32[]{:S(2)}, u32[]{:S(2)}) collective-permute-start(bf16[8,32,256]{2,1,0:T(8,128)(2,1)S(1)} %slice.28), channel_id=1, source_target_pairs={{8,0},{16,8},{24,16},{0,24},{9,1},{17,9},{25,17},{1,25},{10,2},{18... | collective-permute-start | bytes 393224 | tf_op jit(solution)/shard_map/ppermute | solution.py:237
  38.2 7.1 %collective-permute-done.9.near_own = bf16[64,1024]{1,0:T(8,128)(2,1)S(1)} collective-permute-done((bf16[64,1024]{1,0:T(8,128)(2,1)S(1)}, bf16[64,1024]{1,0:T(8,128)(2,1)S(1)}, u32[]{:S(2)}, u32[]{:S(2)}) %collective-permute-start.9) | collective-permute-done | bytes 131104 | tf_op jit(solution)/shard_map/ppermute | solution.py:295
  46.7 4.3 %attention.1 = (bf16[4,128,128]{2,1,0:T(8,128)(2,1)S(1)}, bf16[4,128,128]{2,1,0:T(8,128)(2,1)S(1)}, bf16[1024,128]{1,0:T(8,128)(2,1)S(1)}) custom-call(s32[4]{0:T(128)S(1)} %pad_add_fusion.at, bf16[2,128,1024]{2,1,0:T(8,128)(2,1)S(1)} %get-tuple-element.35.own_low, bf16[2,128,1024]{2,1,0:T(8,128)(2,1)S(1)} %get-tuple-element.36.own_high, ...), custom_call_target="tpu_custom_call" | custom-call | flops 1048576 | bytes 2097152 | tf_op jit(solution)/shard_map/attention/pallas_call | solution.py:306
  54.5 3.0 %collective-permute-start.13 = (bf16[128,1024]{1,0:T(8,128)(2,1)S(1)}, bf16[128,1024]{1,0:T(8,128)(2,1)S(1)}, u32[]{:S(2)}, u32[]{:S(2)}) collective-permute-start(bf16[128,1024]{1,0:T(8,128)(2,1)S(1)} %get-tuple-element.57), channel_id=1, source_target_pairs={{4,0},{6,2},{0,4},{2,6},{5,1},{7,3},{1,5},{3,7},{12,8},{14,10},{8,... | collective-permute-start | bytes 786440 | tf_op jit(solution)/shard_map/ppermute | solution.py:237
  57.9 2.3 %collective-permute-start.15 = (bf16[128,1024]{1,0:T(8,128)(2,1)S(1)}, bf16[128,1024]{1,0:T(8,128)(2,1)S(1)}, u32[]{:S(2)}, u32[]{:S(2)}) collective-permute-start(bf16[128,1024]{1,0:T(8,128)(2,1)S(1)} %get-tuple-element.55), channel_id=1, source_target_pairs={{2,0},{4,2},{6,4},{0,6},{3,1},{5,3},{7,5},{1,7},{10,8},{12,10},{14... | collective-permute-start | bytes 786440 | tf_op jit(solution)/shard_map/ppermute | solution.py:237
  60.2 3.1 %collective-permute-done.13.a = bf16[128,1024]{1,0:T(8,128)(2,1)S(1)} collective-permute-done((bf16[128,1024]{1,0:T(8,128)(2,1)S(1)}, bf16[128,1024]{1,0:T(8,128)(2,1)S(1)}, u32[]{:S(2)}, u32[]{:S(2)}) %collective-permute-start.13) | collective-permute-done | bytes 262176 | tf_op jit(solution)/shard_map/ppermute | solution.py:237
  63.2 6.7 %collective-permute-done.14.b = bf16[128,1024]{1,0:T(8,128)(2,1)S(1)} collective-permute-done((bf16[128,1024]{1,0:T(8,128)(2,1)S(1)}, bf16[128,1024]{1,0:T(8,128)(2,1)S(1)}, u32[]{:S(2)}, u32[]{:S(2)}) %collective-permute-start.14) | collective-permute-done | bytes 262176 | tf_op jit(solution)/shard_map/ppermute | solution.py:237
  70.3 2.8 %collective-permute-start.20 = (bf16[128,1024]{1,0:T(8,128)(2,1)S(1)}, bf16[128,1024]{1,0:T(8,128)(2,1)S(1)}, u32[]{:S(2)}, u32[]{:S(2)}) collective-permute-start(bf16[128,1024]{1,0:T(8,128)(2,1)S(1)} %get-tuple-element.44.a.rows), channel_id=1, source_target_pairs={{2,0},{4,2},{6,4},{0,6},{3,1},{5,3},{7,5},{1,7},{10,8},{12,10},{14... | collective-permute-start | bytes 786440 | tf_op jit(solution)/shard_map/ppermute | solution.py:237
  73.8 1.5 %collective-permute-start.17 = (bf16[8,32,512]{2,1,0:T(8,128)(2,1)S(1)}, bf16[8,32,512]{2,1,0:T(8,128)(2,1)S(1)}, u32[]{:S(2)}, u32[]{:S(2)}) collective-permute-start(bf16[8,32,512]{2,1,0:T(8,128)(2,1)S(1)} %slice.30), channel_id=1, source_target_pairs={{8,0},{16,8},{24,16},{0,24},{9,1},{17,9},{25,17},{1,25},{10,2},{18... | collective-permute-start | bytes 786440 | tf_op jit(solution)/shard_map/ppermute | solution.py:237
  75.5 8.3 %collective-permute-done.20.b.rows = bf16[128,1024]{1,0:T(8,128)(2,1)S(1)} collective-permute-done((bf16[128,1024]{1,0:T(8,128)(2,1)S(1)}, bf16[128,1024]{1,0:T(8,128)(2,1)S(1)}, u32[]{:S(2)}, u32[]{:S(2)}) %collective-permute-start.20) | collective-permute-done | bytes 262176 | tf_op jit(solution)/shard_map/ppermute | solution.py:237
  83.8 4.7 %collective-permute-done.22.d.rows = bf16[128,1024]{1,0:T(8,128)(2,1)S(1)} collective-permute-done((bf16[128,1024]{1,0:T(8,128)(2,1)S(1)}, bf16[128,1024]{1,0:T(8,128)(2,1)S(1)}, u32[]{:S(2)}, u32[]{:S(2)}) %collective-permute-start.22) | collective-permute-done | bytes 262176 | tf_op jit(solution)/shard_map/ppermute | solution.py:237
  89.7 1.4 %mlp_first.1.part = f32[512,1024]{1,0:T(8,128)S(1)} custom-call(bf16[128,1024]{1,0:T(8,128)(2,1)S(1)} %get-tuple-element.44.a.rows, bf16[128,1024]{1,0:T(8,128)(2,1)S(1)} %collective-permute-done.20.b.rows, bf16[128,1024]{1,0:T(8,128)(2,1)S(1)} %collective-permute-done.21.c.rows, bf16[128,1024]{1,0:T(8,128)(2,1)S(1)} %collective-permute-done.22.d.rows, ...), custom_call_target="tpu_custom_call" | custom-call | flops 1048576 | bytes 2097152 | tf_op jit(solution)/shard_map/mlp_first/pallas_call | solution.py:342
  91.1 2.4 %collective-permute-done.23.weight = bf16[1024,1024]{1,0:T(8,128)(2,1)S(1)} collective-permute-done((bf16[1024,1024]{1,0:T(8,128)(2,1)S(1)}, bf16[1024,1024]{1,0:T(8,128)(2,1)S(1)}, u32[]{:S(2)}, u32[]{:S(2)}) %collective-permute-start.23) | collective-permute-done | bytes 2097184 | tf_op jit(solution)/shard_map/ppermute | solution.py:237
  97.1 2.2 %collective-permute-start.26 = (bf16[128,1024]{1,0:T(8,128)(2,1)S(1)}, bf16[128,1024]{1,0:T(8,128)(2,1)S(1)}, u32[]{:S(2)}, u32[]{:S(2)}) collective-permute-start(bf16[128,1024]{1,0:T(8,128)(2,1)S(1)} %mlp_second.7), channel_id=1, source_target_pairs={{2,0},{4,2},{6,4},{0,6},{3,1},{5,3},{7,5},{1,7},{10,8},{12,10},{14... | collective-permute-start | bytes 786440 | tf_op jit(solution)/shard_map/ppermute | solution.py:237
  100.0 3.6 %collective-permute-done.24.a = bf16[128,1024]{1,0:T(8,128)(2,1)S(1)} collective-permute-done((bf16[128,1024]{1,0:T(8,128)(2,1)S(1)}, bf16[128,1024]{1,0:T(8,128)(2,1)S(1)}, u32[]{:S(2)}, u32[]{:S(2)}) %collective-permute-start.24) | collective-permute-done | bytes 262176 | tf_op jit(solution)/shard_map/ppermute | solution.py:237
  103.6 6.3 %collective-permute-done.25.b = bf16[128,1024]{1,0:T(8,128)(2,1)S(1)} collective-permute-done((bf16[128,1024]{1,0:T(8,128)(2,1)S(1)}, bf16[128,1024]{1,0:T(8,128)(2,1)S(1)}, u32[]{:S(2)}, u32[]{:S(2)}) %collective-permute-start.25) | collective-permute-done | bytes 262176 | tf_op jit(solution)/shard_map/ppermute | solution.py:237
  (62 shorter events, 16.0 us)
Async XLA Ops:
  2.2 19.4 %all-to-all-start = ((bf16[8,32,512]{2,1,0:T(8,128)(2,1)}), bf16[8,32,512]{2,1,0:T(8,128)(2,1)S(1)}, u32[]{:S(2)}, u32[]{:S(2)}) async-start(bf16[8,32,512]{2,1,0:T(8,128)(2,1)} %get-tuple-element.31), calls=%async_computation | async-start | bytes 524288 | tf_op jit(solution)/shard_map/all_to_all | solution.py:280
  11.2 16.4 %collective-permute-start = (bf16[128,1024]{1,0:T(8,128)(2,1)S(1)}, bf16[128,1024]{1,0:T(8,128)(2,1)S(1)}, u32[]{:S(2)}, u32[]{:S(2)}) collective-permute-start(bf16[128,1024]{1,0:T(8,128)(2,1)S(1)} %get-tuple-element.30.refs_0_), channel_id=1, source_target_pairs={{2,0},{4,2},{6,4},{0,6},{3,1},{5,3},{7,5},{1,7},{10,8},{12,10},{14... | collective-permute-start | bytes 786440 | tf_op jit(solution)/shard_map/ppermute | solution.py:237
  14.0 13.7 %collective-permute-start.1 = (bf16[128,1024]{1,0:T(8,128)(2,1)S(1)}, bf16[128,1024]{1,0:T(8,128)(2,1)S(1)}, u32[]{:S(2)}, u32[]{:S(2)}) collective-permute-start(bf16[128,1024]{1,0:T(8,128)(2,1)S(1)} %get-tuple-element.30.refs_0_), channel_id=1, source_target_pairs={{4,0},{6,2},{0,4},{2,6},{5,1},{7,3},{1,5},{3,7},{12,8},{14,10},{8,... | collective-permute-start | bytes 786440 | tf_op jit(solution)/shard_map/ppermute | solution.py:237
  14.3 15.0 %collective-permute-start.2 = (bf16[128,1024]{1,0:T(8,128)(2,1)S(1)}, bf16[128,1024]{1,0:T(8,128)(2,1)S(1)}, u32[]{:S(2)}, u32[]{:S(2)}) collective-permute-start(bf16[128,1024]{1,0:T(8,128)(2,1)S(1)} %get-tuple-element.30.refs_0_), channel_id=1, source_target_pairs={{6,0},{0,2},{2,4},{4,6},{7,1},{1,3},{3,5},{5,7},{14,8},{8,10},{10,... | collective-permute-start | bytes 786440 | tf_op jit(solution)/shard_map/ppermute | solution.py:237
  21.6 7.7 %collective-permute-start.3 = (bf16[8,32,512]{2,1,0:T(8,128)(2,1)S(1)}, bf16[8,32,512]{2,1,0:T(8,128)(2,1)S(1)}, u32[]{:S(2)}, u32[]{:S(2)}) collective-permute-start(bf16[8,32,512]{2,1,0:T(8,128)(2,1)S(1)} %all-to-all-done.here), channel_id=1, source_target_pairs={{8,0},{16,8},{24,16},{0,24},{9,1},{17,9},{25,17},{1,25},{10,2},{18... | collective-permute-start | bytes 786440 | tf_op jit(solution)/shard_map/ppermute | solution.py:237
  24.1 27.7 %all-to-all-start.1 = ((bf16[8,32,1024]{2,1,0:T(8,128)(2,1)}), bf16[8,32,1024]{2,1,0:T(8,128)(2,1)S(1)}, u32[]{:S(2)}, u32[]{:S(2)}) async-start(bf16[8,32,1024]{2,1,0:T(8,128)(2,1)} %get-tuple-element.46), calls=%async_computation.1 | async-start | bytes 1048576 | tf_op jit(solution)/shard_map/all_to_all | solution.py:284
  31.2 15.4 %collective-permute-start.5 = (bf16[2,128,1024]{2,1,0:T(8,128)(2,1)S(1)}, bf16[2,128,1024]{2,1,0:T(8,128)(2,1)S(1)}, u32[]{:S(2)}, u32[]{:S(2)}) collective-permute-start(bf16[2,128,1024]{2,1,0:T(8,128)(2,1)S(1)} %get-tuple-element.35.own_low), channel_id=1, source_target_pairs={{1,0},{0,1},{3,2},{2,3},{5,4},{4,5},{7,6},{6,7},{9,8},{8,9},{11,10... | collective-permute-start | bytes 1572872 | tf_op jit(solution)/shard_map/ppermute | solution.py:237
  35.2 11.4 %collective-permute-start.6 = (bf16[2,128,1024]{2,1,0:T(8,128)(2,1)S(1)}, bf16[2,128,1024]{2,1,0:T(8,128)(2,1)S(1)}, u32[]{:S(2)}, u32[]{:S(2)}) collective-permute-start(bf16[2,128,1024]{2,1,0:T(8,128)(2,1)S(1)} %get-tuple-element.36.own_high), channel_id=1, source_target_pairs={{1,0},{0,1},{3,2},{2,3},{5,4},{4,5},{7,6},{6,7},{9,8},{8,9},{11,10... | collective-permute-start | bytes 1572872 | tf_op jit(solution)/shard_map/ppermute | solution.py:237
  35.3 9.9 %collective-permute-start.9 = (bf16[64,1024]{1,0:T(8,128)(2,1)S(1)}, bf16[64,1024]{1,0:T(8,128)(2,1)S(1)}, u32[]{:S(2)}, u32[]{:S(2)}) collective-permute-start(bf16[64,1024]{1,0:T(8,128)(2,1)S(1)} %get-tuple-element.37), channel_id=1, source_target_pairs={{0,248},{1,9},{2,250},{3,11},{4,252},{5,13},{6,254},{7,15},{8,0},{... | collective-permute-start | bytes 393224 | tf_op jit(solution)/shard_map/ppermute | solution.py:295
  35.3 9.9 %collective-permute-start.7 = (bf16[8,32,256]{2,1,0:T(8,128)(2,1)S(1)}, bf16[8,32,256]{2,1,0:T(8,128)(2,1)S(1)}, u32[]{:S(2)}, u32[]{:S(2)}) collective-permute-start(bf16[8,32,256]{2,1,0:T(8,128)(2,1)S(1)} %slice.28), channel_id=1, source_target_pairs={{8,0},{16,8},{24,16},{0,24},{9,1},{17,9},{25,17},{1,25},{10,2},{18... | collective-permute-start | bytes 393224 | tf_op jit(solution)/shard_map/ppermute | solution.py:237
  38.1 8.1 %collective-permute-start.8 = (bf16[8,32,256]{2,1,0:T(8,128)(2,1)S(1)}, bf16[8,32,256]{2,1,0:T(8,128)(2,1)S(1)}, u32[]{:S(2)}, u32[]{:S(2)}) collective-permute-start(bf16[8,32,256]{2,1,0:T(8,128)(2,1)S(1)} %slice.29), channel_id=1, source_target_pairs={{24,0},{0,8},{8,16},{16,24},{25,1},{1,9},{9,17},{17,25},{26,2},{2,... | collective-permute-start | bytes 393224 | tf_op jit(solution)/shard_map/ppermute | solution.py:237
  51.8 22.0 %collective-permute-start.16 = (bf16[8,32,1024]{2,1,0:T(8,128)(2,1)S(1)}, bf16[8,32,1024]{2,1,0:T(8,128)(2,1)S(1)}, u32[]{:S(2)}, u32[]{:S(2)}) collective-permute-start(bf16[8,32,1024]{2,1,0:T(8,128)(2,1)S(1)} %all-to-all-done.1.refs_0_), channel_id=1, source_target_pairs={{8,0},{16,8},{24,16},{0,24},{9,1},{17,9},{25,17},{1,25},{10,2},{18... | collective-permute-start | bytes 1572872 | tf_op jit(solution)/shard_map/ppermute | solution.py:237
  52.1 23.2 %collective-permute-start.18 = (bf16[8,32,1024]{2,1,0:T(8,128)(2,1)S(1)}, bf16[8,32,1024]{2,1,0:T(8,128)(2,1)S(1)}, u32[]{:S(2)}, u32[]{:S(2)}) collective-permute-start(bf16[8,32,1024]{2,1,0:T(8,128)(2,1)S(1)} %all-to-all-done.1.refs_0_), channel_id=1, source_target_pairs={{24,0},{0,8},{8,16},{16,24},{25,1},{1,9},{9,17},{17,25},{26,2},{2,... | collective-permute-start | bytes 1572872 | tf_op jit(solution)/shard_map/ppermute | solution.py:237
  54.5 8.7 %collective-permute-start.13 = (bf16[128,1024]{1,0:T(8,128)(2,1)S(1)}, bf16[128,1024]{1,0:T(8,128)(2,1)S(1)}, u32[]{:S(2)}, u32[]{:S(2)}) collective-permute-start(bf16[128,1024]{1,0:T(8,128)(2,1)S(1)} %get-tuple-element.57), channel_id=1, source_target_pairs={{4,0},{6,2},{0,4},{2,6},{5,1},{7,3},{1,5},{3,7},{12,8},{14,10},{8,... | collective-permute-start | bytes 786440 | tf_op jit(solution)/shard_map/ppermute | solution.py:237
  57.5 12.4 %collective-permute-start.14 = (bf16[128,1024]{1,0:T(8,128)(2,1)S(1)}, bf16[128,1024]{1,0:T(8,128)(2,1)S(1)}, u32[]{:S(2)}, u32[]{:S(2)}) collective-permute-start(bf16[128,1024]{1,0:T(8,128)(2,1)S(1)} %get-tuple-element.56), channel_id=1, source_target_pairs={{6,0},{0,2},{2,4},{4,6},{7,1},{1,3},{3,5},{5,7},{14,8},{8,10},{10,... | collective-permute-start | bytes 786440 | tf_op jit(solution)/shard_map/ppermute | solution.py:237
  57.9 12.0 %collective-permute-start.15 = (bf16[128,1024]{1,0:T(8,128)(2,1)S(1)}, bf16[128,1024]{1,0:T(8,128)(2,1)S(1)}, u32[]{:S(2)}, u32[]{:S(2)}) collective-permute-start(bf16[128,1024]{1,0:T(8,128)(2,1)S(1)} %get-tuple-element.55), channel_id=1, source_target_pairs={{2,0},{4,2},{6,4},{0,6},{3,1},{5,3},{7,5},{1,7},{10,8},{12,10},{14... | collective-permute-start | bytes 786440 | tf_op jit(solution)/shard_map/ppermute | solution.py:237
  70.3 13.5 %collective-permute-start.20 = (bf16[128,1024]{1,0:T(8,128)(2,1)S(1)}, bf16[128,1024]{1,0:T(8,128)(2,1)S(1)}, u32[]{:S(2)}, u32[]{:S(2)}) collective-permute-start(bf16[128,1024]{1,0:T(8,128)(2,1)S(1)} %get-tuple-element.44.a.rows), channel_id=1, source_target_pairs={{2,0},{4,2},{6,4},{0,6},{3,1},{5,3},{7,5},{1,7},{10,8},{12,10},{14... | collective-permute-start | bytes 786440 | tf_op jit(solution)/shard_map/ppermute | solution.py:237
  73.1 10.7 %collective-permute-start.21 = (bf16[128,1024]{1,0:T(8,128)(2,1)S(1)}, bf16[128,1024]{1,0:T(8,128)(2,1)S(1)}, u32[]{:S(2)}, u32[]{:S(2)}) collective-permute-start(bf16[128,1024]{1,0:T(8,128)(2,1)S(1)} %get-tuple-element.44.a.rows), channel_id=1, source_target_pairs={{4,0},{6,2},{0,4},{2,6},{5,1},{7,3},{1,5},{3,7},{12,8},{14,10},{8,... | collective-permute-start | bytes 786440 | tf_op jit(solution)/shard_map/ppermute | solution.py:237
  73.5 15.0 %collective-permute-start.22 = (bf16[128,1024]{1,0:T(8,128)(2,1)S(1)}, bf16[128,1024]{1,0:T(8,128)(2,1)S(1)}, u32[]{:S(2)}, u32[]{:S(2)}) collective-permute-start(bf16[128,1024]{1,0:T(8,128)(2,1)S(1)} %get-tuple-element.44.a.rows), channel_id=1, source_target_pairs={{6,0},{0,2},{2,4},{4,6},{7,1},{1,3},{3,5},{5,7},{14,8},{8,10},{10,... | collective-permute-start | bytes 786440 | tf_op jit(solution)/shard_map/ppermute | solution.py:237
  73.8 14.6 %collective-permute-start.17 = (bf16[8,32,512]{2,1,0:T(8,128)(2,1)S(1)}, bf16[8,32,512]{2,1,0:T(8,128)(2,1)S(1)}, u32[]{:S(2)}, u32[]{:S(2)}) collective-permute-start(bf16[8,32,512]{2,1,0:T(8,128)(2,1)S(1)} %slice.30), channel_id=1, source_target_pairs={{8,0},{16,8},{24,16},{0,24},{9,1},{17,9},{25,17},{1,25},{10,2},{18... | collective-permute-start | bytes 786440 | tf_op jit(solution)/shard_map/ppermute | solution.py:237
  75.3 13.1 %collective-permute-start.19 = (bf16[8,32,512]{2,1,0:T(8,128)(2,1)S(1)}, bf16[8,32,512]{2,1,0:T(8,128)(2,1)S(1)}, u32[]{:S(2)}, u32[]{:S(2)}) collective-permute-start(bf16[8,32,512]{2,1,0:T(8,128)(2,1)S(1)} %slice.31), channel_id=1, source_target_pairs={{24,0},{0,8},{8,16},{16,24},{25,1},{1,9},{9,17},{17,25},{26,2},{2,... | collective-permute-start | bytes 786440 | tf_op jit(solution)/shard_map/ppermute | solution.py:237
  94.3 9.4 %collective-permute-start.24 = (bf16[128,1024]{1,0:T(8,128)(2,1)S(1)}, bf16[128,1024]{1,0:T(8,128)(2,1)S(1)}, u32[]{:S(2)}, u32[]{:S(2)}) collective-permute-start(bf16[128,1024]{1,0:T(8,128)(2,1)S(1)} %mlp_second.5), channel_id=1, source_target_pairs={{4,0},{6,2},{0,4},{2,6},{5,1},{7,3},{1,5},{3,7},{12,8},{14,10},{8,... | collective-permute-start | bytes 786440 | tf_op jit(solution)/shard_map/ppermute | solution.py:237
  95.7 14.3 %collective-permute-start.25 = (bf16[128,1024]{1,0:T(8,128)(2,1)S(1)}, bf16[128,1024]{1,0:T(8,128)(2,1)S(1)}, u32[]{:S(2)}, u32[]{:S(2)}) collective-permute-start(bf16[128,1024]{1,0:T(8,128)(2,1)S(1)} %mlp_second.6), channel_id=1, source_target_pairs={{6,0},{0,2},{2,4},{4,6},{7,1},{1,3},{3,5},{5,7},{14,8},{8,10},{10,... | collective-permute-start | bytes 786440 | tf_op jit(solution)/shard_map/ppermute | solution.py:237
  97.1 12.9 %collective-permute-start.26 = (bf16[128,1024]{1,0:T(8,128)(2,1)S(1)}, bf16[128,1024]{1,0:T(8,128)(2,1)S(1)}, u32[]{:S(2)}, u32[]{:S(2)}) collective-permute-start(bf16[128,1024]{1,0:T(8,128)(2,1)S(1)} %mlp_second.7), channel_id=1, source_target_pairs={{2,0},{4,2},{6,4},{0,6},{3,1},{5,3},{7,5},{1,7},{10,8},{12,10},{14... | collective-permute-start | bytes 786440 | tf_op jit(solution)/shard_map/ppermute | solution.py:237
  (10 other events, 202.7 us)

commit v5 on v4

--- a/solution.py
+++ b/solution.py
@@ -37,27 +37,48 @@
     return lax.broadcasted_iota(jnp.int32, (rows, 128), 1) < 64
 
 
-def start_kernel(*refs):
-    held, (normed, front, back), here, sems = refs[:6], refs[6:9], refs[9:15], refs[15]
+def bring(held, here, sems):
     copies = [
         pltpu.make_async_copy(a, b, sems.at[i]) for i, (a, b) in enumerate(zip(held, here))
     ]
     for copy in copies:
         copy.start()
-    qkv, out_t, tok, gain, up, down_t = here
-    copies[0].wait()
-    copies[1].wait()
+    return copies
+
+
+def pack_kernel(*refs):
+    held, front, here, sems = refs[:2], refs[2], refs[3:5], refs[5]
+    for copy in bring(held, here, sems):
+        copy.wait()
+    qkv, out_t = here
     pack = jnp.concatenate([qkv[0], qkv[1], qkv[2], out_t[...]], axis=1)
     for i in range(8):
         front[i] = pack
+
+
+def start_kernel(*refs):
+    held, (normed, back), here, sems = refs[:4], refs[4:6], refs[6:10], refs[10]
+    copies = bring(held, here, sems)
+    tok, gain, up, down_t = here
+    copies[0].wait()
+    copies[1].wait()
+    normed[...] = layer_norm(tok[...].astype(F32), gain[...])
     copies[2].wait()
     copies[3].wait()
-    normed[...] = layer_norm(tok[...].astype(F32), gain[...])
-    copies[4].wait()
-    copies[5].wait()
     pack = jnp.concatenate([up[...], down_t[...]], axis=1)
     for i in range(8):
         back[i] = pack
+
+
+def from_hbm(kernel, outs, given, name):
+    return call(
+        kernel,
+        outs,
+        [HBM] * len(given),
+        name,
+        scratch=[pltpu.VMEM(v.shape, v.dtype) for v in given]
+        + [pltpu.SemaphoreType.DMA((len(given),))],
+    )(*[pltpu.with_memory_space_constraint(v, pltpu.HBM) for v in given])
 
 
 def collect_kernel(at, *refs):
@@ -110,7 +131,7 @@
         score = lax.dot_general(query[:, lanes], kv[:, lanes], NT, preferred_element_type=F32)
         weight = jnp.where(allowed, jnp.exp(score * 0.125), 0.0)
         total = jnp.sum(weight, axis=-1, keepdims=True)
-        prob = (weight / total).astype(BF16)
+        prob = (weight * (1.0 / total)).astype(BF16)
         value = kv[:, 128 + h * 64 : 192 + h * 64]
         outs.append(jnp.dot(prob, value, preferred_element_type=F32))
     return jnp.concatenate(outs, axis=1).astype(BF16)
@@ -134,20 +155,18 @@
     kv_s[pl.ds(pl.multiple_of((1 - core) * end, WIN), WIN)] = kv[:WIN]
     kv_s[pl.ds(pl.multiple_of(core * end, WIN), WIN)] = kv[WIN:]
 
-    half = first_half(256)
-    for t in range(4):
-        other = peer_low[t] if t < 2 else peer_high[t - 2]
-        rows = jnp.concatenate([own_low[t] if t < 2 else own_high[t - 2], other], axis=0)
+    half = first_half(512)
+    for low, (own, peer) in enumerate(((own_low, peer_low), (own_high, peer_high))):
+        rows = jnp.concatenate([own[0], own[1], peer[0], peer[1]], axis=0)
         qkv = jnp.dot(rows, weight[:, :384], preferred_element_type=F32)
         query = head_norm(qkv[:, :128], gain[0:1], half)
         key = head_norm(qkv[:, 128:256], gain[1:2], half)
         kv = jnp.concatenate([key, qkv[:, 256:].astype(BF16)], axis=1)
-        mine = pl.multiple_of(t * 256 + core * 128, 128)
-        theirs = pl.multiple_of(t * 256 + (1 - core) * 128, 128)
-        q_s[pl.ds(mine, 128)] = query[:128]
-        q_s[pl.ds(theirs, 128)] = query[128:]
-        kv_s[pl.ds(pl.multiple_of(mine + WIN, WIN), 128)] = kv[:128]
-        kv_s[pl.ds(pl.multiple_of(theirs + WIN, WIN), 128)] = kv[128:]
+        for i in range(4):
+            place = core if i < 2 else 1 - core
+            row = pl.multiple_of(low * 512 + i % 2 * 256 + place * 128, 128)
+            q_s[pl.ds(row, 128)] = query[i * 128 : i * 128 + 128]
+            kv_s[pl.ds(pl.multiple_of(row + WIN, WIN), 128)] = kv[i * 128 : i * 128 + 128]
     for b in range(8):
         att[lax.rem(core + b, 2), b // 2] = attend(
             q_s[b * 128 : b * 128 + 128],
@@ -261,24 +280,20 @@
     at = jnp.stack([y, core, lax.axis_index("x"), seq * 1024]).astype(jnp.int32)
     first, count = win_first.reshape(8, 128), win_count.reshape(8, 128)
 
-    given = [
-        jnp.transpose(qkv_weight, (1, 0, 2)),
-        out_weight.T,
-        tokens,
-        norm1_gain.reshape(1, 1024),
-        up_weight,
-        down_weight.T,
-    ]
-    normed, front, back = call(
+    (front,) = from_hbm(
+        pack_kernel,
+        [((8, 32, 512), BF16)],
+        [jnp.transpose(qkv_weight, (1, 0, 2)), out_weight.T],
+        "pack",
+    )
+    normed, back = from_hbm(
         start_kernel,
-        [((128, 1024), BF16), ((8, 32, 512), BF16), ((8, 32, 1024), BF16)],
-        [HBM] * 6,
+        [((128, 1024), BF16), ((8, 32, 1024), BF16)],
+        [tokens, norm1_gain.reshape(1, 1024), up_weight, down_weight.T],
         "start",
-        scratch=[pltpu.VMEM(v.shape, v.dtype) for v in given]
-        + [pltpu.SemaphoreType.DMA((6,))],
-    )(*[pltpu.with_memory_space_constraint(v, pltpu.HBM) for v in given])
+    )
     front = lax.all_to_all(front, "z", 0, 0, tiled=True)
-    far = {k: fetch(normed, "y", k) for k in (2, 1, 3)}
+    far = {k: fetch(normed, "y", k) for k in (1, 3, 2)}
     weights = relay(front)
     back, _ = lax.optimization_barrier((back, front))
     back = lax.all_to_all(back, "z", 0, 0, tiled=True)
@@ -325,7 +340,7 @@
         [SMEM] + [VMEM] * 4,
         "project",
     )(at, keep, got, weight, out_peer)
-    parts = [fetch(away[k - 1], "y", 4 - k) for k in (2, 1, 3)]
+    parts = [fetch(away[k - 1], "y", 4 - k) for k in (1, 3, 2)]
     middle, normed_two = call(
         middle_kernel,
         [((128, 1024), BF16)] * 2,
@@ -333,7 +348,7 @@
         "middle",
     )(tokens, mine_attended, *parts, norm2_gain.reshape(1, 1024))
 
-    far = {k: fetch(normed_two, "y", k) for k in (2, 1, 3)}
+    far = {k: fetch(normed_two, "y", k) for k in (1, 3, 2)}
     laid, far = lax.optimization_barrier((mlp_weights, far))
     (mlp_own,) = call(lay_kernel, [((1024, 1024), BF16)], [SMEM] + [VMEM] * 5, "mlp_lay")(
         at, *laid
@@ -342,7 +357,7 @@
     (part,) = call(mlp_first_kernel, [((512, 1024), F32)], [VMEM] * 5, "mlp_first", mib=16)(
         normed_two, far[1], far[2], far[3], mlp_own
     )
-    parts = [fetch(mlp_second(far[k], mlp_peer, part, k), "y", 4 - k) for k in (2, 1, 3)]
+    parts = [fetch(mlp_second(far[k], mlp_peer, part, k), "y", 4 - k) for k in (1, 3, 2)]
     mine = mlp_second(normed_two, mlp_peer, part, 0)
     (out,) = call(end_kernel, [((128, 1024), BF16)], [VMEM] * 5, "end")(middle, mine, *parts)
     return out

time: 111 us -> 108 us (0.973)
  starting transfers between devices: 42.8 us -> 40.1 us
  waiting for transfers between devices: 52.9 us -> 50.6 us
  Pallas kernels: 14.7 us -> 16.2 us
    ppermute x26, starting transfers between devices: 30.3 us -> 27.6 us  [fetch(): return lax.ppermute(value, axis, [((i + step) % n, i) for i in range(n)])]
    all_to_all x1, waiting for transfers between devices: 6.59 us -> 4.46 us  [local(): front = lax.all_to_all(front, 'z', 0, 0, tiled=True)]
    pallas_call x1 -> x2, Pallas kernels: 2.19 us -> 3.56 us  [from_hbm(): call(kernel, outs, [HBM] * len(given), name, scratch=[pltpu.VMEM(v.shape,...]
  transfers between devices with their start and end apart: 29 -> 29, of which waited for: 13 -> 12; matrix products, arithmetic and copies ran while one was open for 0% -> 0% of each run, Pallas kernels for 9% -> 12%
where the time goes in v5:
time: 108 us; the launch traced here: 107 us
  waiting for transfers between devices  50.6 us (47%)
  starting transfers between devices  40.1 us (37%)
  Pallas kernels  16.2 us (15%)
    ppermute x26, waiting for transfers between devices, fetch(): return lax.ppermute(value, axis, [((i + step) % n, i) for i in range(n)])  39.1 us
    ppermute x26, starting transfers between devices, fetch(): return lax.ppermute(value, axis, [((i + step) % n, i) for i in range(n)])  27.6 us
    all_to_all x1, starting transfers between devices, local(): front = lax.all_to_all(front, 'z', 0, 0, tiled=True)  9.03 us
    ppermute x1, waiting for transfers between devices, local(): lax.ppermute(border, ('z', 'x', 'y', 'core'), [(spot(*divmod(s, 4), j, c)...  7.08 us
    pallas_call x1, Pallas kernels, local(): call(attention_kernel, [((4, 128, 128), BF16), ((4, 128, 128), BF16), ((1...  4.49 us
    all_to_all x1, waiting for transfers between devices, local(): front = lax.all_to_all(front, 'z', 0, 0, tiled=True)  4.46 us
    pallas_call x2, Pallas kernels, from_hbm(): call(kernel, outs, [HBM] * len(given), name, scratch=[pltpu.VMEM(v.shape,...  3.56 us
    all_to_all x1, starting transfers between devices, local(): back = lax.all_to_all(back, 'z', 0, 0, tiled=True)  3.49 us
  transfers between devices with their start and end apart: 29, of which 12 were waited for; matrix products, arithmetic and copies ran while one was open for 0% of the time, Pallas kernels for 12%

profile of v5, /device:TPU:1, one launch (start us, length us, event | category | flops | bytes accessed | tf_op | source)
XLA Modules:
  0.0 107.3 jit_solution(15826258313847049221)
XLA Ops:
  0.0 1.5 %pack.1 = bf16[8,32,512]{2,1,0:T(8,128)(2,1)} custom-call(bf16[3,32,128]{2,1,0:T(8,128)(2,1)} %bitcast.21, bf16[32,128]{1,0:T(8,128)(2,1)} %bitcast.22), custom_call_target="tpu_custom_call" | custom-call | flops 1048576 | bytes 2097152 | tf_op jit(solution)/shard_map/pack/pallas_call | solution.py:74
  1.5 9.0 %all-to-all-start = ((bf16[8,32,512]{2,1,0:T(8,128)(2,1)}), bf16[8,32,512]{2,1,0:T(8,128)(2,1)S(1)}, u32[]{:S(2)}, u32[]{:S(2)}) async-start(bf16[8,32,512]{2,1,0:T(8,128)(2,1)} %pack.1), calls=%async_computation | async-start | bytes 524288 | tf_op jit(solution)/shard_map/all_to_all | solution.py:295
  10.6 2.0 %start.1 = (bf16[128,1024]{1,0:T(8,128)(2,1)S(1)}, bf16[8,32,1024]{2,1,0:T(8,128)(2,1)}) custom-call(bf16[128,1024]{1,0:T(8,128)(2,1)} %tok.1, f32[1,1024]{1,0:T(1,128)} %bitcast.23, bf16[32,512]{1,0:T(8,128)(2,1)} %refs_2_.1, bf16[32,512]{1,0:T(8,128)(2,1)} %bitcast.20), custom_call_target="tpu_custom_call" | custom-call | flops 1048576 | bytes 2097152 | tf_op jit(solution)/shard_map/start/pallas_call | solution.py:74
  12.6 2.8 %collective-permute-start = (bf16[128,1024]{1,0:T(8,128)(2,1)S(1)}, bf16[128,1024]{1,0:T(8,128)(2,1)S(1)}, u32[]{:S(2)}, u32[]{:S(2)}) collective-permute-start(bf16[128,1024]{1,0:T(8,128)(2,1)S(1)} %get-tuple-element.29.refs_0_), channel_id=1, source_target_pairs={{2,0},{4,2},{6,4},{0,6},{3,1},{5,3},{7,5},{1,7},{10,8},{12,10},{14... | collective-permute-start | bytes 786440 | tf_op jit(solution)/shard_map/ppermute | solution.py:256
  16.5 4.5 %all-to-all-done.here = bf16[8,32,512]{2,1,0:T(8,128)(2,1)S(1)} async-done(((bf16[8,32,512]{2,1,0:T(8,128)(2,1)}), bf16[8,32,512]{2,1,0:T(8,128)(2,1)S(1)}, u32[]{:S(2)}, u32[]{:S(2)}) %all-to-all-start) | async-done | bytes 262176 | tf_op jit(solution)/shard_map/all_to_all | solution.py:295
  20.9 2.5 %collective-permute-start.3 = (bf16[8,32,512]{2,1,0:T(8,128)(2,1)S(1)}, bf16[8,32,512]{2,1,0:T(8,128)(2,1)S(1)}, u32[]{:S(2)}, u32[]{:S(2)}) collective-permute-start(bf16[8,32,512]{2,1,0:T(8,128)(2,1)S(1)} %all-to-all-done.here), channel_id=1, source_target_pairs={{8,0},{16,8},{24,16},{0,24},{9,1},{17,9},{25,17},{1,25},{10,2},{18... | collective-permute-start | bytes 786440 | tf_op jit(solution)/shard_map/ppermute | solution.py:256
  23.4 3.5 %all-to-all-start.1 = ((bf16[8,32,1024]{2,1,0:T(8,128)(2,1)}), bf16[8,32,1024]{2,1,0:T(8,128)(2,1)S(1)}, u32[]{:S(2)}, u32[]{:S(2)}) async-start(bf16[8,32,1024]{2,1,0:T(8,128)(2,1)} %get-tuple-element.44), calls=%async_computation.1 | async-start | bytes 1048576 | tf_op jit(solution)/shard_map/all_to_all | solution.py:299
  27.0 3.8 %collective-permute-done.2.refs_3_ = bf16[128,1024]{1,0:T(8,128)(2,1)S(1)} collective-permute-done((bf16[128,1024]{1,0:T(8,128)(2,1)S(1)}, bf16[128,1024]{1,0:T(8,128)(2,1)S(1)}, u32[]{:S(2)}, u32[]{:S(2)}) %collective-permute-start.2) | collective-permute-done | bytes 262176 | tf_op jit(solution)/shard_map/ppermute | solution.py:256
  31.5 3.0 %collective-permute-start.5 = (bf16[2,128,1024]{2,1,0:T(8,128)(2,1)S(1)}, bf16[2,128,1024]{2,1,0:T(8,128)(2,1)S(1)}, u32[]{:S(2)}, u32[]{:S(2)}) collective-permute-start(bf16[2,128,1024]{2,1,0:T(8,128)(2,1)S(1)} %get-tuple-element.33.own_low), channel_id=1, source_target_pairs={{1,0},{0,1},{3,2},{2,3},{5,4},{4,5},{7,6},{6,7},{9,8},{8,9},{11,10... | collective-permute-start | bytes 1572872 | tf_op jit(solution)/shard_map/ppermute | solution.py:256
  34.7 2.8 %collective-permute-start.7 = (bf16[8,32,256]{2,1,0:T(8,128)(2,1)S(1)}, bf16[8,32,256]{2,1,0:T(8,128)(2,1)S(1)}, u32[]{:S(2)}, u32[]{:S(2)}) collective-permute-start(bf16[8,32,256]{2,1,0:T(8,128)(2,1)S(1)} %slice.28), channel_id=1, source_target_pairs={{8,0},{16,8},{24,16},{0,24},{9,1},{17,9},{25,17},{1,25},{10,2},{18... | collective-permute-start | bytes 393224 | tf_op jit(solution)/shard_map/ppermute | solution.py:256
  37.5 7.1 %collective-permute-done.9.near_own = bf16[64,1024]{1,0:T(8,128)(2,1)S(1)} collective-permute-done((bf16[64,1024]{1,0:T(8,128)(2,1)S(1)}, bf16[64,1024]{1,0:T(8,128)(2,1)S(1)}, u32[]{:S(2)}, u32[]{:S(2)}) %collective-permute-start.9) | collective-permute-done | bytes 131104 | tf_op jit(solution)/shard_map/ppermute | solution.py:310
  46.0 4.5 %attention.1 = (bf16[4,128,128]{2,1,0:T(8,128)(2,1)S(1)}, bf16[4,128,128]{2,1,0:T(8,128)(2,1)S(1)}, bf16[1024,128]{1,0:T(8,128)(2,1)S(1)}) custom-call(s32[4]{0:T(128)S(1)} %pad_add_fusion.at, bf16[2,128,1024]{2,1,0:T(8,128)(2,1)S(1)} %get-tuple-element.33.own_low, bf16[2,128,1024]{2,1,0:T(8,128)(2,1)S(1)} %get-tuple-element.34.own_high, ...), custom_call_target="tpu_custom_call" | custom-call | flops 1048576 | bytes 2097152 | tf_op jit(solution)/shard_map/attention/pallas_call | solution.py:321
  55.3 1.5 %collective-permute-start.14 = (bf16[128,1024]{1,0:T(8,128)(2,1)S(1)}, bf16[128,1024]{1,0:T(8,128)(2,1)S(1)}, u32[]{:S(2)}, u32[]{:S(2)}) collective-permute-start(bf16[128,1024]{1,0:T(8,128)(2,1)S(1)} %get-tuple-element.54), channel_id=1, source_target_pairs={{2,0},{4,2},{6,4},{0,6},{3,1},{5,3},{7,5},{1,7},{10,8},{12,10},{14... | collective-permute-start | bytes 786440 | tf_op jit(solution)/shard_map/ppermute | solution.py:256
  56.9 1.6 %collective-permute-start.15 = (bf16[128,1024]{1,0:T(8,128)(2,1)S(1)}, bf16[128,1024]{1,0:T(8,128)(2,1)S(1)}, u32[]{:S(2)}, u32[]{:S(2)}) collective-permute-start(bf16[128,1024]{1,0:T(8,128)(2,1)S(1)} %get-tuple-element.53), channel_id=1, source_target_pairs={{4,0},{6,2},{0,4},{2,6},{5,1},{7,3},{1,5},{3,7},{12,8},{14,10},{8,... | collective-permute-start | bytes 786440 | tf_op jit(solution)/shard_map/ppermute | solution.py:256
  58.4 4.1 %collective-permute-done.13.a = bf16[128,1024]{1,0:T(8,128)(2,1)S(1)} collective-permute-done((bf16[128,1024]{1,0:T(8,128)(2,1)S(1)}, bf16[128,1024]{1,0:T(8,128)(2,1)S(1)}, u32[]{:S(2)}, u32[]{:S(2)}) %collective-permute-start.13) | collective-permute-done | bytes 262176 | tf_op jit(solution)/shard_map/ppermute | solution.py:256
  62.5 6.7 %collective-permute-done.15.c = bf16[128,1024]{1,0:T(8,128)(2,1)S(1)} collective-permute-done((bf16[128,1024]{1,0:T(8,128)(2,1)S(1)}, bf16[128,1024]{1,0:T(8,128)(2,1)S(1)}, u32[]{:S(2)}, u32[]{:S(2)}) %collective-permute-start.15) | collective-permute-done | bytes 262176 | tf_op jit(solution)/shard_map/ppermute | solution.py:256
  72.0 1.4 %collective-permute-start.17 = (bf16[8,32,512]{2,1,0:T(8,128)(2,1)S(1)}, bf16[8,32,512]{2,1,0:T(8,128)(2,1)S(1)}, u32[]{:S(2)}, u32[]{:S(2)}) collective-permute-start(bf16[8,32,512]{2,1,0:T(8,128)(2,1)S(1)} %slice.30), channel_id=1, source_target_pairs={{8,0},{16,8},{24,16},{0,24},{9,1},{17,9},{25,17},{1,25},{10,2},{18... | collective-permute-start | bytes 786440 | tf_op jit(solution)/shard_map/ppermute | solution.py:256
  73.7 2.2 %collective-permute-done.20.b.rows = bf16[128,1024]{1,0:T(8,128)(2,1)S(1)} collective-permute-done((bf16[128,1024]{1,0:T(8,128)(2,1)S(1)}, bf16[128,1024]{1,0:T(8,128)(2,1)S(1)}, u32[]{:S(2)}, u32[]{:S(2)}) %collective-permute-start.20) | collective-permute-done | bytes 262176 | tf_op jit(solution)/shard_map/ppermute | solution.py:256
  75.9 1.6 %collective-permute-done.21.c.rows = bf16[128,1024]{1,0:T(8,128)(2,1)S(1)} collective-permute-done((bf16[128,1024]{1,0:T(8,128)(2,1)S(1)}, bf16[128,1024]{1,0:T(8,128)(2,1)S(1)}, u32[]{:S(2)}, u32[]{:S(2)}) %collective-permute-start.21) | collective-permute-done | bytes 262176 | tf_op jit(solution)/shard_map/ppermute | solution.py:256
  77.5 7.8 %collective-permute-done.22.d.rows = bf16[128,1024]{1,0:T(8,128)(2,1)S(1)} collective-permute-done((bf16[128,1024]{1,0:T(8,128)(2,1)S(1)}, bf16[128,1024]{1,0:T(8,128)(2,1)S(1)}, u32[]{:S(2)}, u32[]{:S(2)}) %collective-permute-start.22) | collective-permute-done | bytes 262176 | tf_op jit(solution)/shard_map/ppermute | solution.py:256
  87.3 1.4 %mlp_first.1.part = f32[512,1024]{1,0:T(8,128)S(1)} custom-call(bf16[128,1024]{1,0:T(8,128)(2,1)S(1)} %get-tuple-element.42.a.rows, bf16[128,1024]{1,0:T(8,128)(2,1)S(1)} %collective-permute-done.20.b.rows, bf16[128,1024]{1,0:T(8,128)(2,1)S(1)} %collective-permute-done.21.c.rows, bf16[128,1024]{1,0:T(8,128)(2,1)S(1)} %collective-permute-done.22.d.rows, ...), custom_call_target="tpu_custom_call" | custom-call | flops 1048576 | bytes 2097152 | tf_op jit(solution)/shard_map/mlp_first/pallas_call | solution.py:357
  88.7 2.4 %collective-permute-done.23.weight = bf16[1024,1024]{1,0:T(8,128)(2,1)S(1)} collective-permute-done((bf16[1024,1024]{1,0:T(8,128)(2,1)S(1)}, bf16[1024,1024]{1,0:T(8,128)(2,1)S(1)}, u32[]{:S(2)}, u32[]{:S(2)}) %collective-permute-start.23) | collective-permute-done | bytes 2097184 | tf_op jit(solution)/shard_map/ppermute | solution.py:256
  92.9 2.7 %collective-permute-start.25 = (bf16[128,1024]{1,0:T(8,128)(2,1)S(1)}, bf16[128,1024]{1,0:T(8,128)(2,1)S(1)}, u32[]{:S(2)}, u32[]{:S(2)}) collective-permute-start(bf16[128,1024]{1,0:T(8,128)(2,1)S(1)} %mlp_second.6), channel_id=1, source_target_pairs={{2,0},{4,2},{6,4},{0,6},{3,1},{5,3},{7,5},{1,7},{10,8},{12,10},{14... | collective-permute-start | bytes 786440 | tf_op jit(solution)/shard_map/ppermute | solution.py:256
  97.4 9.1 %collective-permute-done.24.a = bf16[128,1024]{1,0:T(8,128)(2,1)S(1)} collective-permute-done((bf16[128,1024]{1,0:T(8,128)(2,1)S(1)}, bf16[128,1024]{1,0:T(8,128)(2,1)S(1)}, u32[]{:S(2)}, u32[]{:S(2)}) %collective-permute-start.24) | collective-permute-done | bytes 262176 | tf_op jit(solution)/shard_map/ppermute | solution.py:256
  (63 shorter events, 17.6 us)
Async XLA Ops:
  1.5 19.4 %all-to-all-start = ((bf16[8,32,512]{2,1,0:T(8,128)(2,1)}), bf16[8,32,512]{2,1,0:T(8,128)(2,1)S(1)}, u32[]{:S(2)}, u32[]{:S(2)}) async-start(bf16[8,32,512]{2,1,0:T(8,128)(2,1)} %pack.1), calls=%async_computation | async-start | bytes 524288 | tf_op jit(solution)/shard_map/all_to_all | solution.py:295
  12.6 14.4 %collective-permute-start = (bf16[128,1024]{1,0:T(8,128)(2,1)S(1)}, bf16[128,1024]{1,0:T(8,128)(2,1)S(1)}, u32[]{:S(2)}, u32[]{:S(2)}) collective-permute-start(bf16[128,1024]{1,0:T(8,128)(2,1)S(1)} %get-tuple-element.29.refs_0_), channel_id=1, source_target_pairs={{2,0},{4,2},{6,4},{0,6},{3,1},{5,3},{7,5},{1,7},{10,8},{12,10},{14... | collective-permute-start | bytes 786440 | tf_op jit(solution)/shard_map/ppermute | solution.py:256
  15.4 11.6 %collective-permute-start.1 = (bf16[128,1024]{1,0:T(8,128)(2,1)S(1)}, bf16[128,1024]{1,0:T(8,128)(2,1)S(1)}, u32[]{:S(2)}, u32[]{:S(2)}) collective-permute-start(bf16[128,1024]{1,0:T(8,128)(2,1)S(1)} %get-tuple-element.29.refs_0_), channel_id=1, source_target_pairs={{4,0},{6,2},{0,4},{2,6},{5,1},{7,3},{1,5},{3,7},{12,8},{14,10},{8,... | collective-permute-start | bytes 786440 | tf_op jit(solution)/shard_map/ppermute | solution.py:256
  15.8 15.0 %collective-permute-start.2 = (bf16[128,1024]{1,0:T(8,128)(2,1)S(1)}, bf16[128,1024]{1,0:T(8,128)(2,1)S(1)}, u32[]{:S(2)}, u32[]{:S(2)}) collective-permute-start(bf16[128,1024]{1,0:T(8,128)(2,1)S(1)} %get-tuple-element.29.refs_0_), channel_id=1, source_target_pairs={{6,0},{0,2},{2,4},{4,6},{7,1},{1,3},{3,5},{5,7},{14,8},{8,10},{10,... | collective-permute-start | bytes 786440 | tf_op jit(solution)/shard_map/ppermute | solution.py:256
  20.9 9.8 %collective-permute-start.3 = (bf16[8,32,512]{2,1,0:T(8,128)(2,1)S(1)}, bf16[8,32,512]{2,1,0:T(8,128)(2,1)S(1)}, u32[]{:S(2)}, u32[]{:S(2)}) collective-permute-start(bf16[8,32,512]{2,1,0:T(8,128)(2,1)S(1)} %all-to-all-done.here), channel_id=1, source_target_pairs={{8,0},{16,8},{24,16},{0,24},{9,1},{17,9},{25,17},{1,25},{10,2},{18... | collective-permute-start | bytes 786440 | tf_op jit(solution)/shard_map/ppermute | solution.py:256
  23.4 7.4 %collective-permute-start.4 = (bf16[8,32,512]{2,1,0:T(8,128)(2,1)S(1)}, bf16[8,32,512]{2,1,0:T(8,128)(2,1)S(1)}, u32[]{:S(2)}, u32[]{:S(2)}) collective-permute-start(bf16[8,32,512]{2,1,0:T(8,128)(2,1)S(1)} %all-to-all-done.here), channel_id=1, source_target_pairs={{24,0},{0,8},{8,16},{16,24},{25,1},{1,9},{9,17},{17,25},{26,2},{2,... | collective-permute-start | bytes 786440 | tf_op jit(solution)/shard_map/ppermute | solution.py:256
  23.4 27.9 %all-to-all-start.1 = ((bf16[8,32,1024]{2,1,0:T(8,128)(2,1)}), bf16[8,32,1024]{2,1,0:T(8,128)(2,1)S(1)}, u32[]{:S(2)}, u32[]{:S(2)}) async-start(bf16[8,32,1024]{2,1,0:T(8,128)(2,1)} %get-tuple-element.44), calls=%async_computation.1 | async-start | bytes 1048576 | tf_op jit(solution)/shard_map/all_to_all | solution.py:299
  31.5 14.4 %collective-permute-start.5 = (bf16[2,128,1024]{2,1,0:T(8,128)(2,1)S(1)}, bf16[2,128,1024]{2,1,0:T(8,128)(2,1)S(1)}, u32[]{:S(2)}, u32[]{:S(2)}) collective-permute-start(bf16[2,128,1024]{2,1,0:T(8,128)(2,1)S(1)} %get-tuple-element.33.own_low), channel_id=1, source_target_pairs={{1,0},{0,1},{3,2},{2,3},{5,4},{4,5},{7,6},{6,7},{9,8},{8,9},{11,10... | collective-permute-start | bytes 1572872 | tf_op jit(solution)/shard_map/ppermute | solution.py:256
  34.5 11.4 %collective-permute-start.6 = (bf16[2,128,1024]{2,1,0:T(8,128)(2,1)S(1)}, bf16[2,128,1024]{2,1,0:T(8,128)(2,1)S(1)}, u32[]{:S(2)}, u32[]{:S(2)}) collective-permute-start(bf16[2,128,1024]{2,1,0:T(8,128)(2,1)S(1)} %get-tuple-element.34.own_high), channel_id=1, source_target_pairs={{1,0},{0,1},{3,2},{2,3},{5,4},{4,5},{7,6},{6,7},{9,8},{8,9},{11,10... | collective-permute-start | bytes 1572872 | tf_op jit(solution)/shard_map/ppermute | solution.py:256
  34.6 9.9 %collective-permute-start.9 = (bf16[64,1024]{1,0:T(8,128)(2,1)S(1)}, bf16[64,1024]{1,0:T(8,128)(2,1)S(1)}, u32[]{:S(2)}, u32[]{:S(2)}) collective-permute-start(bf16[64,1024]{1,0:T(8,128)(2,1)S(1)} %get-tuple-element.35), channel_id=1, source_target_pairs={{0,248},{1,9},{2,250},{3,11},{4,252},{5,13},{6,254},{7,15},{8,0},{... | collective-permute-start | bytes 393224 | tf_op jit(solution)/shard_map/ppermute | solution.py:310
  34.7 9.9 %collective-permute-start.7 = (bf16[8,32,256]{2,1,0:T(8,128)(2,1)S(1)}, bf16[8,32,256]{2,1,0:T(8,128)(2,1)S(1)}, u32[]{:S(2)}, u32[]{:S(2)}) collective-permute-start(bf16[8,32,256]{2,1,0:T(8,128)(2,1)S(1)} %slice.28), channel_id=1, source_target_pairs={{8,0},{16,8},{24,16},{0,24},{9,1},{17,9},{25,17},{1,25},{10,2},{18... | collective-permute-start | bytes 393224 | tf_op jit(solution)/shard_map/ppermute | solution.py:256
  37.4 7.4 %collective-permute-start.8 = (bf16[8,32,256]{2,1,0:T(8,128)(2,1)S(1)}, bf16[8,32,256]{2,1,0:T(8,128)(2,1)S(1)}, u32[]{:S(2)}, u32[]{:S(2)}) collective-permute-start(bf16[8,32,256]{2,1,0:T(8,128)(2,1)S(1)} %slice.29), channel_id=1, source_target_pairs={{24,0},{0,8},{8,16},{16,24},{25,1},{1,9},{9,17},{17,25},{26,2},{2,... | collective-permute-start | bytes 393224 | tf_op jit(solution)/shard_map/ppermute | solution.py:256
  51.3 20.7 %collective-permute-start.16 = (bf16[8,32,1024]{2,1,0:T(8,128)(2,1)S(1)}, bf16[8,32,1024]{2,1,0:T(8,128)(2,1)S(1)}, u32[]{:S(2)}, u32[]{:S(2)}) collective-permute-start(bf16[8,32,1024]{2,1,0:T(8,128)(2,1)S(1)} %all-to-all-done.1.refs_0_), channel_id=1, source_target_pairs={{8,0},{16,8},{24,16},{0,24},{9,1},{17,9},{25,17},{1,25},{10,2},{18... | collective-permute-start | bytes 1572872 | tf_op jit(solution)/shard_map/ppermute | solution.py:256
  51.6 21.9 %collective-permute-start.18 = (bf16[8,32,1024]{2,1,0:T(8,128)(2,1)S(1)}, bf16[8,32,1024]{2,1,0:T(8,128)(2,1)S(1)}, u32[]{:S(2)}, u32[]{:S(2)}) collective-permute-start(bf16[8,32,1024]{2,1,0:T(8,128)(2,1)S(1)} %all-to-all-done.1.refs_0_), channel_id=1, source_target_pairs={{24,0},{0,8},{8,16},{16,24},{25,1},{1,9},{9,17},{17,25},{26,2},{2,... | collective-permute-start | bytes 1572872 | tf_op jit(solution)/shard_map/ppermute | solution.py:256
  54.0 8.6 %collective-permute-start.13 = (bf16[128,1024]{1,0:T(8,128)(2,1)S(1)}, bf16[128,1024]{1,0:T(8,128)(2,1)S(1)}, u32[]{:S(2)}, u32[]{:S(2)}) collective-permute-start(bf16[128,1024]{1,0:T(8,128)(2,1)S(1)} %get-tuple-element.55), channel_id=1, source_target_pairs={{6,0},{0,2},{2,4},{4,6},{7,1},{1,3},{3,5},{5,7},{14,8},{8,10},{10,... | collective-permute-start | bytes 786440 | tf_op jit(solution)/shard_map/ppermute | solution.py:256
  55.3 7.2 %collective-permute-start.14 = (bf16[128,1024]{1,0:T(8,128)(2,1)S(1)}, bf16[128,1024]{1,0:T(8,128)(2,1)S(1)}, u32[]{:S(2)}, u32[]{:S(2)}) collective-permute-start(bf16[128,1024]{1,0:T(8,128)(2,1)S(1)} %get-tuple-element.54), channel_id=1, source_target_pairs={{2,0},{4,2},{6,4},{0,6},{3,1},{5,3},{7,5},{1,7},{10,8},{12,10},{14... | collective-permute-start | bytes 786440 | tf_op jit(solution)/shard_map/ppermute | solution.py:256
  56.9 12.4 %collective-permute-start.15 = (bf16[128,1024]{1,0:T(8,128)(2,1)S(1)}, bf16[128,1024]{1,0:T(8,128)(2,1)S(1)}, u32[]{:S(2)}, u32[]{:S(2)}) collective-permute-start(bf16[128,1024]{1,0:T(8,128)(2,1)S(1)} %get-tuple-element.53), channel_id=1, source_target_pairs={{4,0},{6,2},{0,4},{2,6},{5,1},{7,3},{1,5},{3,7},{12,8},{14,10},{8,... | collective-permute-start | bytes 786440 | tf_op jit(solution)/shard_map/ppermute | solution.py:256
  70.6 6.8 %collective-permute-start.21 = (bf16[128,1024]{1,0:T(8,128)(2,1)S(1)}, bf16[128,1024]{1,0:T(8,128)(2,1)S(1)}, u32[]{:S(2)}, u32[]{:S(2)}) collective-permute-start(bf16[128,1024]{1,0:T(8,128)(2,1)S(1)} %get-tuple-element.42.a.rows), channel_id=1, source_target_pairs={{4,0},{6,2},{0,4},{2,6},{5,1},{7,3},{1,5},{3,7},{12,8},{14,10},{8,... | collective-permute-start | bytes 786440 | tf_op jit(solution)/shard_map/ppermute | solution.py:256
  72.0 13.3 %collective-permute-start.22 = (bf16[128,1024]{1,0:T(8,128)(2,1)S(1)}, bf16[128,1024]{1,0:T(8,128)(2,1)S(1)}, u32[]{:S(2)}, u32[]{:S(2)}) collective-permute-start(bf16[128,1024]{1,0:T(8,128)(2,1)S(1)} %get-tuple-element.42.a.rows), channel_id=1, source_target_pairs={{6,0},{0,2},{2,4},{4,6},{7,1},{1,3},{3,5},{5,7},{14,8},{8,10},{10,... | collective-permute-start | bytes 786440 | tf_op jit(solution)/shard_map/ppermute | solution.py:256
  72.0 13.3 %collective-permute-start.17 = (bf16[8,32,512]{2,1,0:T(8,128)(2,1)S(1)}, bf16[8,32,512]{2,1,0:T(8,128)(2,1)S(1)}, u32[]{:S(2)}, u32[]{:S(2)}) collective-permute-start(bf16[8,32,512]{2,1,0:T(8,128)(2,1)S(1)} %slice.30), channel_id=1, source_target_pairs={{8,0},{16,8},{24,16},{0,24},{9,1},{17,9},{25,17},{1,25},{10,2},{18... | collective-permute-start | bytes 786440 | tf_op jit(solution)/shard_map/ppermute | solution.py:256
  73.5 11.9 %collective-permute-start.19 = (bf16[8,32,512]{2,1,0:T(8,128)(2,1)S(1)}, bf16[8,32,512]{2,1,0:T(8,128)(2,1)S(1)}, u32[]{:S(2)}, u32[]{:S(2)}) collective-permute-start(bf16[8,32,512]{2,1,0:T(8,128)(2,1)S(1)} %slice.31), channel_id=1, source_target_pairs={{24,0},{0,8},{8,16},{16,24},{25,1},{1,9},{9,17},{17,25},{26,2},{2,... | collective-permute-start | bytes 786440 | tf_op jit(solution)/shard_map/ppermute | solution.py:256
  91.8 14.6 %collective-permute-start.24 = (bf16[128,1024]{1,0:T(8,128)(2,1)S(1)}, bf16[128,1024]{1,0:T(8,128)(2,1)S(1)}, u32[]{:S(2)}, u32[]{:S(2)}) collective-permute-start(bf16[128,1024]{1,0:T(8,128)(2,1)S(1)} %mlp_second.5), channel_id=1, source_target_pairs={{6,0},{0,2},{2,4},{4,6},{7,1},{1,3},{3,5},{5,7},{14,8},{8,10},{10,... | collective-permute-start | bytes 786440 | tf_op jit(solution)/shard_map/ppermute | solution.py:256
  92.9 13.6 %collective-permute-start.25 = (bf16[128,1024]{1,0:T(8,128)(2,1)S(1)}, bf16[128,1024]{1,0:T(8,128)(2,1)S(1)}, u32[]{:S(2)}, u32[]{:S(2)}) collective-permute-start(bf16[128,1024]{1,0:T(8,128)(2,1)S(1)} %mlp_second.6), channel_id=1, source_target_pairs={{2,0},{4,2},{6,4},{0,6},{3,1},{5,3},{7,5},{1,7},{10,8},{12,10},{14... | collective-permute-start | bytes 786440 | tf_op jit(solution)/shard_map/ppermute | solution.py:256
  96.4 10.1 %collective-permute-start.26 = (bf16[128,1024]{1,0:T(8,128)(2,1)S(1)}, bf16[128,1024]{1,0:T(8,128)(2,1)S(1)}, u32[]{:S(2)}, u32[]{:S(2)}) collective-permute-start(bf16[128,1024]{1,0:T(8,128)(2,1)S(1)} %mlp_second.7), channel_id=1, source_target_pairs={{4,0},{6,2},{0,4},{2,6},{5,1},{7,3},{1,5},{3,7},{12,8},{14,10},{8,... | collective-permute-start | bytes 786440 | tf_op jit(solution)/shard_map/ppermute | solution.py:256
  (10 other events, 201.1 us)

commit v6 on v5

--- a/solution.py
+++ b/solution.py
@@ -56,15 +56,19 @@
         front[i] = pack
 
 
-def start_kernel(*refs):
-    held, (normed, back), here, sems = refs[:4], refs[4:6], refs[6:10], refs[10]
-    copies = bring(held, here, sems)
-    tok, gain, up, down_t = here
-    copies[0].wait()
-    copies[1].wait()
+def norm_kernel(*refs):
+    held, normed, here, sems = refs[:2], refs[2], refs[3:5], refs[5]
+    for copy in bring(held, here, sems):
+        copy.wait()
+    tok, gain = here
     normed[...] = layer_norm(tok[...].astype(F32), gain[...])
-    copies[2].wait()
-    copies[3].wait()
+
+
+def mlp_pack_kernel(*refs):
+    held, back, here, sems = refs[:2], refs[2], refs[3:5], refs[5]
+    for copy in bring(held, here, sems):
+        copy.wait()
+    up, down_t = here
     pack = jnp.concatenate([up[...], down_t[...]], axis=1)
     for i in range(8):
         back[i] = pack
@@ -125,16 +129,22 @@
     lower = jnp.concatenate([lower, lower], axis=1)
     upper = jnp.concatenate([upper, upper], axis=1)
     allowed = (index >= lower) & (index < upper)
-    outs = []
+    low = first_half(128)
+    values = kv[:, 128:]
+    one, none = jnp.ones_like(values), jnp.zeros_like(query)
+    pick = first_half(256)
+    sums = []
     for h in range(2):
-        lanes = slice(h * 64, h * 64 + 64)
-        score = lax.dot_general(query[:, lanes], kv[:, lanes], NT, preferred_element_type=F32)
-        weight = jnp.where(allowed, jnp.exp(score * 0.125), 0.0)
-        total = jnp.sum(weight, axis=-1, keepdims=True)
-        prob = (weight * (1.0 / total)).astype(BF16)
-        value = kv[:, 128 + h * 64 : 192 + h * 64]
-        outs.append(jnp.dot(prob, value, preferred_element_type=F32))
-    return jnp.concatenate(outs, axis=1).astype(BF16)
+        own = low if h == 0 else ~low
+        score = lax.dot_general(
+            jnp.where(own, query, none), kv[:, :128], NT, preferred_element_type=F32
+        )
+        weight = jnp.where(allowed, jnp.exp(score * 0.125), 0.0).astype(BF16)
+        held = jnp.where(pick if h == 0 else ~pick, values, one)
+        sums.append(jnp.dot(weight, held, preferred_element_type=F32))
+    mixed = jnp.where(low, sums[0], sums[1])
+    total = pltpu.roll(jnp.where(low, sums[1], sums[0]), 64, 1)
+    return (mixed / total).astype(BF16)
 
 
 def attention_kernel(
@@ -286,16 +296,22 @@
         [jnp.transpose(qkv_weight, (1, 0, 2)), out_weight.T],
         "pack",
     )
-    normed, back = from_hbm(
-        start_kernel,
-        [((128, 1024), BF16), ((8, 32, 1024), BF16)],
-        [tokens, norm1_gain.reshape(1, 1024), up_weight, down_weight.T],
-        "start",
+    (normed,) = from_hbm(
+        norm_kernel,
+        [((128, 1024), BF16)],
+        [tokens, norm1_gain.reshape(1, 1024)],
+        "norm",
+    )
+    (back,) = from_hbm(
+        mlp_pack_kernel,
+        [((8, 32, 1024), BF16)],
+        [up_weight, down_weight.T],
+        "mlp_pack",
     )
     front = lax.all_to_all(front, "z", 0, 0, tiled=True)
     far = {k: fetch(normed, "y", k) for k in (1, 3, 2)}
+    back, front = lax.optimization_barrier((back, front))
     weights = relay(front)
-    back, _ = lax.optimization_barrier((back, front))
     back = lax.all_to_all(back, "z", 0, 0, tiled=True)
     far, _ = lax.optimization_barrier((far, (weights[1], weights[4])))
     own_low, own_high, border = call(

time: 108 us -> 107 us (level); the launches traced: 107 us -> 105 us
  waiting for transfers between devices: 50.6 us -> 47.5 us
    ppermute x26, waiting for transfers between devices: 39.1 us -> 36.8 us  [fetch(): return lax.ppermute(value, axis, [((i + step) % n, i) for i in range(n)])]
    pallas_call x1, Pallas kernels: 4.49 us -> 3.34 us  [local(): call(attention_kernel, [((4, 128, 128), BF16), ((4, 128, 128), BF16), ((1...]
    pallas_call x2 -> x3, Pallas kernels: 3.56 us -> 4.31 us  [from_hbm(): call(kernel, outs, [HBM] * len(given), name, scratch=[pltpu.VMEM(v.shape,...]
  transfers between devices with their start and end apart: 29 -> 29, of which waited for: 12 -> 15; matrix products, arithmetic and copies ran while one was open for 0% -> 0% of each run, Pallas kernels for 12% -> 11%
where the time goes in v6:
time: 107 us; the launch traced here: 105 us
  waiting for transfers between devices  47.5 us (44%)
  starting transfers between devices  40.9 us (38%)
  Pallas kernels  15.8 us (15%)
    ppermute x26, waiting for transfers between devices, fetch(): return lax.ppermute(value, axis, [((i + step) % n, i) for i in range(n)])  36.8 us
    ppermute x26, starting transfers between devices, fetch(): return lax.ppermute(value, axis, [((i + step) % n, i) for i in range(n)])  28.3 us
    all_to_all x1, starting transfers between devices, local(): front = lax.all_to_all(front, 'z', 0, 0, tiled=True)  9.16 us
    ppermute x1, waiting for transfers between devices, local(): lax.ppermute(border, ('z', 'x', 'y', 'core'), [(spot(*divmod(s, 4), j, c)...  7.08 us
    pallas_call x3, Pallas kernels, from_hbm(): call(kernel, outs, [HBM] * len(given), name, scratch=[pltpu.VMEM(v.shape,...  4.31 us
    all_to_all x1, waiting for transfers between devices, local(): front = lax.all_to_all(front, 'z', 0, 0, tiled=True)  3.67 us
    all_to_all x1, starting transfers between devices, local(): back = lax.all_to_all(back, 'z', 0, 0, tiled=True)  3.49 us
    pallas_call x1, Pallas kernels, local(): call(attention_kernel, [((4, 128, 128), BF16), ((4, 128, 128), BF16), ((1...  3.34 us
  transfers between devices with their start and end apart: 29, of which 15 were waited for; matrix products, arithmetic and copies ran while one was open for 0% of the time, Pallas kernels for 11%

profile of v6, /device:TPU:1, one launch (start us, length us, event | category | flops | bytes accessed | tf_op | source)
XLA Modules:
  0.0 104.7 jit_solution(5036307023483367105)
XLA Ops:
  0.0 1.5 %pack.1 = bf16[8,32,512]{2,1,0:T(8,128)(2,1)} custom-call(bf16[3,32,128]{2,1,0:T(8,128)(2,1)} %bitcast.21, bf16[32,128]{1,0:T(8,128)(2,1)} %bitcast.22), custom_call_target="tpu_custom_call" | custom-call | flops 1048576 | bytes 2097152 | tf_op jit(solution)/shard_map/pack/pallas_call | solution.py:78
  1.5 9.2 %all-to-all-start = ((bf16[8,32,512]{2,1,0:T(8,128)(2,1)}), bf16[8,32,512]{2,1,0:T(8,128)(2,1)S(1)}, u32[]{:S(2)}, u32[]{:S(2)}) async-start(bf16[8,32,512]{2,1,0:T(8,128)(2,1)} %pack.1), calls=%async_computation | async-start | bytes 524288 | tf_op jit(solution)/shard_map/all_to_all | solution.py:311
  11.9 2.8 %collective-permute-start = (bf16[128,1024]{1,0:T(8,128)(2,1)S(1)}, bf16[128,1024]{1,0:T(8,128)(2,1)S(1)}, u32[]{:S(2)}, u32[]{:S(2)}) collective-permute-start(bf16[128,1024]{1,0:T(8,128)(2,1)S(1)} %norm.1.refs_0_), channel_id=1, source_target_pairs={{2,0},{4,2},{6,4},{0,6},{3,1},{5,3},{7,5},{1,7},{10,8},{12,10},{14... | collective-permute-start | bytes 786440 | tf_op jit(solution)/shard_map/ppermute | solution.py:266
  15.7 1.6 %mlp_pack.1 = bf16[8,32,1024]{2,1,0:T(8,128)(2,1)} custom-call(bf16[32,512]{1,0:T(8,128)(2,1)} %refs_0_.3, bf16[32,512]{1,0:T(8,128)(2,1)} %bitcast.20), custom_call_target="tpu_custom_call" | custom-call | flops 1048576 | bytes 2097152 | tf_op jit(solution)/shard_map/mlp_pack/pallas_call | solution.py:78
  17.4 3.7 %all-to-all-done.here = bf16[8,32,512]{2,1,0:T(8,128)(2,1)S(1)} async-done(((bf16[8,32,512]{2,1,0:T(8,128)(2,1)}), bf16[8,32,512]{2,1,0:T(8,128)(2,1)S(1)}, u32[]{:S(2)}, u32[]{:S(2)}) %all-to-all-start) | async-done | bytes 262176 | tf_op jit(solution)/shard_map/all_to_all | solution.py:311
  21.0 2.5 %collective-permute-start.3 = (bf16[8,32,512]{2,1,0:T(8,128)(2,1)S(1)}, bf16[8,32,512]{2,1,0:T(8,128)(2,1)S(1)}, u32[]{:S(2)}, u32[]{:S(2)}) collective-permute-start(bf16[8,32,512]{2,1,0:T(8,128)(2,1)S(1)} %all-to-all-done.here), channel_id=1, source_target_pairs={{8,0},{16,8},{24,16},{0,24},{9,1},{17,9},{25,17},{1,25},{10,2},{18... | collective-permute-start | bytes 786440 | tf_op jit(solution)/shard_map/ppermute | solution.py:266
  23.5 3.5 %all-to-all-start.1 = ((bf16[8,32,1024]{2,1,0:T(8,128)(2,1)}), bf16[8,32,1024]{2,1,0:T(8,128)(2,1)S(1)}, u32[]{:S(2)}, u32[]{:S(2)}) async-start(bf16[8,32,1024]{2,1,0:T(8,128)(2,1)} %mlp_pack.1), calls=%async_computation.1 | async-start | bytes 1048576 | tf_op jit(solution)/shard_map/all_to_all | solution.py:315
  27.1 2.9 %collective-permute-done.2.refs_3_ = bf16[128,1024]{1,0:T(8,128)(2,1)S(1)} collective-permute-done((bf16[128,1024]{1,0:T(8,128)(2,1)S(1)}, bf16[128,1024]{1,0:T(8,128)(2,1)S(1)}, u32[]{:S(2)}, u32[]{:S(2)}) %collective-permute-start.2) | collective-permute-done | bytes 262176 | tf_op jit(solution)/shard_map/ppermute | solution.py:266
  30.9 3.8 %collective-permute-start.5 = (bf16[2,128,1024]{2,1,0:T(8,128)(2,1)S(1)}, bf16[2,128,1024]{2,1,0:T(8,128)(2,1)S(1)}, u32[]{:S(2)}, u32[]{:S(2)}) collective-permute-start(bf16[2,128,1024]{2,1,0:T(8,128)(2,1)S(1)} %get-tuple-element.32.own_low), channel_id=1, source_target_pairs={{1,0},{0,1},{3,2},{2,3},{5,4},{4,5},{7,6},{6,7},{9,8},{8,9},{11,10... | collective-permute-start | bytes 1572872 | tf_op jit(solution)/shard_map/ppermute | solution.py:266
  34.8 2.8 %collective-permute-start.7 = (bf16[8,32,256]{2,1,0:T(8,128)(2,1)S(1)}, bf16[8,32,256]{2,1,0:T(8,128)(2,1)S(1)}, u32[]{:S(2)}, u32[]{:S(2)}) collective-permute-start(bf16[8,32,256]{2,1,0:T(8,128)(2,1)S(1)} %slice.28), channel_id=1, source_target_pairs={{8,0},{16,8},{24,16},{0,24},{9,1},{17,9},{25,17},{1,25},{10,2},{18... | collective-permute-start | bytes 393224 | tf_op jit(solution)/shard_map/ppermute | solution.py:266
  37.6 7.1 %collective-permute-done.9.near_own = bf16[64,1024]{1,0:T(8,128)(2,1)S(1)} collective-permute-done((bf16[64,1024]{1,0:T(8,128)(2,1)S(1)}, bf16[64,1024]{1,0:T(8,128)(2,1)S(1)}, u32[]{:S(2)}, u32[]{:S(2)}) %collective-permute-start.9) | collective-permute-done | bytes 131104 | tf_op jit(solution)/shard_map/ppermute | solution.py:326
  46.1 3.3 %attention.1 = (bf16[4,128,128]{2,1,0:T(8,128)(2,1)S(1)}, bf16[4,128,128]{2,1,0:T(8,128)(2,1)S(1)}, bf16[1024,128]{1,0:T(8,128)(2,1)S(1)}) custom-call(s32[4]{0:T(128)S(1)} %pad_add_fusion.at, bf16[2,128,1024]{2,1,0:T(8,128)(2,1)S(1)} %get-tuple-element.32.own_low, bf16[2,128,1024]{2,1,0:T(8,128)(2,1)S(1)} %get-tuple-element.33.own_high, ...), custom_call_target="tpu_custom_call" | custom-call | flops 1048576 | bytes 2097152 | tf_op jit(solution)/shard_map/attention/pallas_call | solution.py:337
  54.1 1.5 %collective-permute-start.14 = (bf16[128,1024]{1,0:T(8,128)(2,1)S(1)}, bf16[128,1024]{1,0:T(8,128)(2,1)S(1)}, u32[]{:S(2)}, u32[]{:S(2)}) collective-permute-start(bf16[128,1024]{1,0:T(8,128)(2,1)S(1)} %get-tuple-element.52), channel_id=1, source_target_pairs={{2,0},{4,2},{6,4},{0,6},{3,1},{5,3},{7,5},{1,7},{10,8},{12,10},{14... | collective-permute-start | bytes 786440 | tf_op jit(solution)/shard_map/ppermute | solution.py:266
  55.6 1.6 %collective-permute-start.15 = (bf16[128,1024]{1,0:T(8,128)(2,1)S(1)}, bf16[128,1024]{1,0:T(8,128)(2,1)S(1)}, u32[]{:S(2)}, u32[]{:S(2)}) collective-permute-start(bf16[128,1024]{1,0:T(8,128)(2,1)S(1)} %get-tuple-element.51), channel_id=1, source_target_pairs={{4,0},{6,2},{0,4},{2,6},{5,1},{7,3},{1,5},{3,7},{12,8},{14,10},{8,... | collective-permute-start | bytes 786440 | tf_op jit(solution)/shard_map/ppermute | solution.py:266
  57.2 4.0 %collective-permute-done.13.a = bf16[128,1024]{1,0:T(8,128)(2,1)S(1)} collective-permute-done((bf16[128,1024]{1,0:T(8,128)(2,1)S(1)}, bf16[128,1024]{1,0:T(8,128)(2,1)S(1)}, u32[]{:S(2)}, u32[]{:S(2)}) %collective-permute-start.13) | collective-permute-done | bytes 262176 | tf_op jit(solution)/shard_map/ppermute | solution.py:266
  61.2 6.7 %collective-permute-done.15.c = bf16[128,1024]{1,0:T(8,128)(2,1)S(1)} collective-permute-done((bf16[128,1024]{1,0:T(8,128)(2,1)S(1)}, bf16[128,1024]{1,0:T(8,128)(2,1)S(1)}, u32[]{:S(2)}, u32[]{:S(2)}) %collective-permute-start.15) | collective-permute-done | bytes 262176 | tf_op jit(solution)/shard_map/ppermute | solution.py:266
  70.7 1.8 %collective-permute-start.17 = (bf16[8,32,512]{2,1,0:T(8,128)(2,1)S(1)}, bf16[8,32,512]{2,1,0:T(8,128)(2,1)S(1)}, u32[]{:S(2)}, u32[]{:S(2)}) collective-permute-start(bf16[8,32,512]{2,1,0:T(8,128)(2,1)S(1)} %slice.30), channel_id=1, source_target_pairs={{8,0},{16,8},{24,16},{0,24},{9,1},{17,9},{25,17},{1,25},{10,2},{18... | collective-permute-start | bytes 786440 | tf_op jit(solution)/shard_map/ppermute | solution.py:266
  72.6 1.8 %collective-permute-done.20.b.rows = bf16[128,1024]{1,0:T(8,128)(2,1)S(1)} collective-permute-done((bf16[128,1024]{1,0:T(8,128)(2,1)S(1)}, bf16[128,1024]{1,0:T(8,128)(2,1)S(1)}, u32[]{:S(2)}, u32[]{:S(2)}) %collective-permute-start.20) | collective-permute-done | bytes 262176 | tf_op jit(solution)/shard_map/ppermute | solution.py:266
  74.4 1.7 %collective-permute-done.21.c.rows = bf16[128,1024]{1,0:T(8,128)(2,1)S(1)} collective-permute-done((bf16[128,1024]{1,0:T(8,128)(2,1)S(1)}, bf16[128,1024]{1,0:T(8,128)(2,1)S(1)}, u32[]{:S(2)}, u32[]{:S(2)}) %collective-permute-start.21) | collective-permute-done | bytes 262176 | tf_op jit(solution)/shard_map/ppermute | solution.py:266
  76.1 7.7 %collective-permute-done.22.d.rows = bf16[128,1024]{1,0:T(8,128)(2,1)S(1)} collective-permute-done((bf16[128,1024]{1,0:T(8,128)(2,1)S(1)}, bf16[128,1024]{1,0:T(8,128)(2,1)S(1)}, u32[]{:S(2)}, u32[]{:S(2)}) %collective-permute-start.22) | collective-permute-done | bytes 262176 | tf_op jit(solution)/shard_map/ppermute | solution.py:266
  87.3 2.4 %collective-permute-done.23.weight = bf16[1024,1024]{1,0:T(8,128)(2,1)S(1)} collective-permute-done((bf16[1024,1024]{1,0:T(8,128)(2,1)S(1)}, bf16[1024,1024]{1,0:T(8,128)(2,1)S(1)}, u32[]{:S(2)}, u32[]{:S(2)}) %collective-permute-start.23) | collective-permute-done | bytes 2097184 | tf_op jit(solution)/shard_map/ppermute | solution.py:266
  91.3 2.7 %collective-permute-start.25 = (bf16[128,1024]{1,0:T(8,128)(2,1)S(1)}, bf16[128,1024]{1,0:T(8,128)(2,1)S(1)}, u32[]{:S(2)}, u32[]{:S(2)}) collective-permute-start(bf16[128,1024]{1,0:T(8,128)(2,1)S(1)} %mlp_second.6), channel_id=1, source_target_pairs={{2,0},{4,2},{6,4},{0,6},{3,1},{5,3},{7,5},{1,7},{10,8},{12,10},{14... | collective-permute-start | bytes 786440 | tf_op jit(solution)/shard_map/ppermute | solution.py:266
  95.8 3.6 %collective-permute-done.24.a = bf16[128,1024]{1,0:T(8,128)(2,1)S(1)} collective-permute-done((bf16[128,1024]{1,0:T(8,128)(2,1)S(1)}, bf16[128,1024]{1,0:T(8,128)(2,1)S(1)}, u32[]{:S(2)}, u32[]{:S(2)}) %collective-permute-start.24) | collective-permute-done | bytes 262176 | tf_op jit(solution)/shard_map/ppermute | solution.py:266
  99.9 3.9 %collective-permute-done.26.c = bf16[128,1024]{1,0:T(8,128)(2,1)S(1)} collective-permute-done((bf16[128,1024]{1,0:T(8,128)(2,1)S(1)}, bf16[128,1024]{1,0:T(8,128)(2,1)S(1)}, u32[]{:S(2)}, u32[]{:S(2)}) %collective-permute-start.26) | collective-permute-done | bytes 262176 | tf_op jit(solution)/shard_map/ppermute | solution.py:266
  (64 shorter events, 20.4 us)
Async XLA Ops:
  1.5 19.5 %all-to-all-start = ((bf16[8,32,512]{2,1,0:T(8,128)(2,1)}), bf16[8,32,512]{2,1,0:T(8,128)(2,1)S(1)}, u32[]{:S(2)}, u32[]{:S(2)}) async-start(bf16[8,32,512]{2,1,0:T(8,128)(2,1)} %pack.1), calls=%async_computation | async-start | bytes 524288 | tf_op jit(solution)/shard_map/all_to_all | solution.py:311
  11.9 15.2 %collective-permute-start = (bf16[128,1024]{1,0:T(8,128)(2,1)S(1)}, bf16[128,1024]{1,0:T(8,128)(2,1)S(1)}, u32[]{:S(2)}, u32[]{:S(2)}) collective-permute-start(bf16[128,1024]{1,0:T(8,128)(2,1)S(1)} %norm.1.refs_0_), channel_id=1, source_target_pairs={{2,0},{4,2},{6,4},{0,6},{3,1},{5,3},{7,5},{1,7},{10,8},{12,10},{14... | collective-permute-start | bytes 786440 | tf_op jit(solution)/shard_map/ppermute | solution.py:266
  14.7 12.4 %collective-permute-start.1 = (bf16[128,1024]{1,0:T(8,128)(2,1)S(1)}, bf16[128,1024]{1,0:T(8,128)(2,1)S(1)}, u32[]{:S(2)}, u32[]{:S(2)}) collective-permute-start(bf16[128,1024]{1,0:T(8,128)(2,1)S(1)} %norm.1.refs_0_), channel_id=1, source_target_pairs={{4,0},{6,2},{0,4},{2,6},{5,1},{7,3},{1,5},{3,7},{12,8},{14,10},{8,... | collective-permute-start | bytes 786440 | tf_op jit(solution)/shard_map/ppermute | solution.py:266
  15.1 15.0 %collective-permute-start.2 = (bf16[128,1024]{1,0:T(8,128)(2,1)S(1)}, bf16[128,1024]{1,0:T(8,128)(2,1)S(1)}, u32[]{:S(2)}, u32[]{:S(2)}) collective-permute-start(bf16[128,1024]{1,0:T(8,128)(2,1)S(1)} %norm.1.refs_0_), channel_id=1, source_target_pairs={{6,0},{0,2},{2,4},{4,6},{7,1},{1,3},{3,5},{5,7},{14,8},{8,10},{10,... | collective-permute-start | bytes 786440 | tf_op jit(solution)/shard_map/ppermute | solution.py:266
  21.0 9.0 %collective-permute-start.3 = (bf16[8,32,512]{2,1,0:T(8,128)(2,1)S(1)}, bf16[8,32,512]{2,1,0:T(8,128)(2,1)S(1)}, u32[]{:S(2)}, u32[]{:S(2)}) collective-permute-start(bf16[8,32,512]{2,1,0:T(8,128)(2,1)S(1)} %all-to-all-done.here), channel_id=1, source_target_pairs={{8,0},{16,8},{24,16},{0,24},{9,1},{17,9},{25,17},{1,25},{10,2},{18... | collective-permute-start | bytes 786440 | tf_op jit(solution)/shard_map/ppermute | solution.py:266
  23.5 6.6 %collective-permute-start.4 = (bf16[8,32,512]{2,1,0:T(8,128)(2,1)S(1)}, bf16[8,32,512]{2,1,0:T(8,128)(2,1)S(1)}, u32[]{:S(2)}, u32[]{:S(2)}) collective-permute-start(bf16[8,32,512]{2,1,0:T(8,128)(2,1)S(1)} %all-to-all-done.here), channel_id=1, source_target_pairs={{24,0},{0,8},{8,16},{16,24},{25,1},{1,9},{9,17},{17,25},{26,2},{2,... | collective-permute-start | bytes 786440 | tf_op jit(solution)/shard_map/ppermute | solution.py:266
  23.5 26.5 %all-to-all-start.1 = ((bf16[8,32,1024]{2,1,0:T(8,128)(2,1)}), bf16[8,32,1024]{2,1,0:T(8,128)(2,1)S(1)}, u32[]{:S(2)}, u32[]{:S(2)}) async-start(bf16[8,32,1024]{2,1,0:T(8,128)(2,1)} %mlp_pack.1), calls=%async_computation.1 | async-start | bytes 1048576 | tf_op jit(solution)/shard_map/all_to_all | solution.py:315
  30.9 15.2 %collective-permute-start.5 = (bf16[2,128,1024]{2,1,0:T(8,128)(2,1)S(1)}, bf16[2,128,1024]{2,1,0:T(8,128)(2,1)S(1)}, u32[]{:S(2)}, u32[]{:S(2)}) collective-permute-start(bf16[2,128,1024]{2,1,0:T(8,128)(2,1)S(1)} %get-tuple-element.32.own_low), channel_id=1, source_target_pairs={{1,0},{0,1},{3,2},{2,3},{5,4},{4,5},{7,6},{6,7},{9,8},{8,9},{11,10... | collective-permute-start | bytes 1572872 | tf_op jit(solution)/shard_map/ppermute | solution.py:266
  34.7 11.4 %collective-permute-start.6 = (bf16[2,128,1024]{2,1,0:T(8,128)(2,1)S(1)}, bf16[2,128,1024]{2,1,0:T(8,128)(2,1)S(1)}, u32[]{:S(2)}, u32[]{:S(2)}) collective-permute-start(bf16[2,128,1024]{2,1,0:T(8,128)(2,1)S(1)} %get-tuple-element.33.own_high), channel_id=1, source_target_pairs={{1,0},{0,1},{3,2},{2,3},{5,4},{4,5},{7,6},{6,7},{9,8},{8,9},{11,10... | collective-permute-start | bytes 1572872 | tf_op jit(solution)/shard_map/ppermute | solution.py:266
  34.8 9.9 %collective-permute-start.9 = (bf16[64,1024]{1,0:T(8,128)(2,1)S(1)}, bf16[64,1024]{1,0:T(8,128)(2,1)S(1)}, u32[]{:S(2)}, u32[]{:S(2)}) collective-permute-start(bf16[64,1024]{1,0:T(8,128)(2,1)S(1)} %get-tuple-element.34), channel_id=1, source_target_pairs={{0,248},{1,9},{2,250},{3,11},{4,252},{5,13},{6,254},{7,15},{8,0},{... | collective-permute-start | bytes 393224 | tf_op jit(solution)/shard_map/ppermute | solution.py:326
  34.8 9.9 %collective-permute-start.7 = (bf16[8,32,256]{2,1,0:T(8,128)(2,1)S(1)}, bf16[8,32,256]{2,1,0:T(8,128)(2,1)S(1)}, u32[]{:S(2)}, u32[]{:S(2)}) collective-permute-start(bf16[8,32,256]{2,1,0:T(8,128)(2,1)S(1)} %slice.28), channel_id=1, source_target_pairs={{8,0},{16,8},{24,16},{0,24},{9,1},{17,9},{25,17},{1,25},{10,2},{18... | collective-permute-start | bytes 393224 | tf_op jit(solution)/shard_map/ppermute | solution.py:266
  37.6 8.1 %collective-permute-start.8 = (bf16[8,32,256]{2,1,0:T(8,128)(2,1)S(1)}, bf16[8,32,256]{2,1,0:T(8,128)(2,1)S(1)}, u32[]{:S(2)}, u32[]{:S(2)}) collective-permute-start(bf16[8,32,256]{2,1,0:T(8,128)(2,1)S(1)} %slice.29), channel_id=1, source_target_pairs={{24,0},{0,8},{8,16},{16,24},{25,1},{1,9},{9,17},{17,25},{26,2},{2,... | collective-permute-start | bytes 393224 | tf_op jit(solution)/shard_map/ppermute | solution.py:266
  50.1 20.6 %collective-permute-start.16 = (bf16[8,32,1024]{2,1,0:T(8,128)(2,1)S(1)}, bf16[8,32,1024]{2,1,0:T(8,128)(2,1)S(1)}, u32[]{:S(2)}, u32[]{:S(2)}) collective-permute-start(bf16[8,32,1024]{2,1,0:T(8,128)(2,1)S(1)} %all-to-all-done.1.refs_0_), channel_id=1, source_target_pairs={{8,0},{16,8},{24,16},{0,24},{9,1},{17,9},{25,17},{1,25},{10,2},{18... | collective-permute-start | bytes 1572872 | tf_op jit(solution)/shard_map/ppermute | solution.py:266
  50.5 22.0 %collective-permute-start.18 = (bf16[8,32,1024]{2,1,0:T(8,128)(2,1)S(1)}, bf16[8,32,1024]{2,1,0:T(8,128)(2,1)S(1)}, u32[]{:S(2)}, u32[]{:S(2)}) collective-permute-start(bf16[8,32,1024]{2,1,0:T(8,128)(2,1)S(1)} %all-to-all-done.1.refs_0_), channel_id=1, source_target_pairs={{24,0},{0,8},{8,16},{16,24},{25,1},{1,9},{9,17},{17,25},{26,2},{2,... | collective-permute-start | bytes 1572872 | tf_op jit(solution)/shard_map/ppermute | solution.py:266
  52.7 8.4 %collective-permute-start.13 = (bf16[128,1024]{1,0:T(8,128)(2,1)S(1)}, bf16[128,1024]{1,0:T(8,128)(2,1)S(1)}, u32[]{:S(2)}, u32[]{:S(2)}) collective-permute-start(bf16[128,1024]{1,0:T(8,128)(2,1)S(1)} %get-tuple-element.53), channel_id=1, source_target_pairs={{6,0},{0,2},{2,4},{4,6},{7,1},{1,3},{3,5},{5,7},{14,8},{8,10},{10,... | collective-permute-start | bytes 786440 | tf_op jit(solution)/shard_map/ppermute | solution.py:266
  54.1 7.0 %collective-permute-start.14 = (bf16[128,1024]{1,0:T(8,128)(2,1)S(1)}, bf16[128,1024]{1,0:T(8,128)(2,1)S(1)}, u32[]{:S(2)}, u32[]{:S(2)}) collective-permute-start(bf16[128,1024]{1,0:T(8,128)(2,1)S(1)} %get-tuple-element.52), channel_id=1, source_target_pairs={{2,0},{4,2},{6,4},{0,6},{3,1},{5,3},{7,5},{1,7},{10,8},{12,10},{14... | collective-permute-start | bytes 786440 | tf_op jit(solution)/shard_map/ppermute | solution.py:266
  55.6 12.2 %collective-permute-start.15 = (bf16[128,1024]{1,0:T(8,128)(2,1)S(1)}, bf16[128,1024]{1,0:T(8,128)(2,1)S(1)}, u32[]{:S(2)}, u32[]{:S(2)}) collective-permute-start(bf16[128,1024]{1,0:T(8,128)(2,1)S(1)} %get-tuple-element.51), channel_id=1, source_target_pairs={{4,0},{6,2},{0,4},{2,6},{5,1},{7,3},{1,5},{3,7},{12,8},{14,10},{8,... | collective-permute-start | bytes 786440 | tf_op jit(solution)/shard_map/ppermute | solution.py:266
  69.3 6.8 %collective-permute-start.21 = (bf16[128,1024]{1,0:T(8,128)(2,1)S(1)}, bf16[128,1024]{1,0:T(8,128)(2,1)S(1)}, u32[]{:S(2)}, u32[]{:S(2)}) collective-permute-start(bf16[128,1024]{1,0:T(8,128)(2,1)S(1)} %get-tuple-element.41.a.rows), channel_id=1, source_target_pairs={{4,0},{6,2},{0,4},{2,6},{5,1},{7,3},{1,5},{3,7},{12,8},{14,10},{8,... | collective-permute-start | bytes 786440 | tf_op jit(solution)/shard_map/ppermute | solution.py:266
  70.7 13.2 %collective-permute-start.22 = (bf16[128,1024]{1,0:T(8,128)(2,1)S(1)}, bf16[128,1024]{1,0:T(8,128)(2,1)S(1)}, u32[]{:S(2)}, u32[]{:S(2)}) collective-permute-start(bf16[128,1024]{1,0:T(8,128)(2,1)S(1)} %get-tuple-element.41.a.rows), channel_id=1, source_target_pairs={{6,0},{0,2},{2,4},{4,6},{7,1},{1,3},{3,5},{5,7},{14,8},{8,10},{10,... | collective-permute-start | bytes 786440 | tf_op jit(solution)/shard_map/ppermute | solution.py:266
  70.7 13.1 %collective-permute-start.17 = (bf16[8,32,512]{2,1,0:T(8,128)(2,1)S(1)}, bf16[8,32,512]{2,1,0:T(8,128)(2,1)S(1)}, u32[]{:S(2)}, u32[]{:S(2)}) collective-permute-start(bf16[8,32,512]{2,1,0:T(8,128)(2,1)S(1)} %slice.30), channel_id=1, source_target_pairs={{8,0},{16,8},{24,16},{0,24},{9,1},{17,9},{25,17},{1,25},{10,2},{18... | collective-permute-start | bytes 786440 | tf_op jit(solution)/shard_map/ppermute | solution.py:266
  72.5 11.4 %collective-permute-start.19 = (bf16[8,32,512]{2,1,0:T(8,128)(2,1)S(1)}, bf16[8,32,512]{2,1,0:T(8,128)(2,1)S(1)}, u32[]{:S(2)}, u32[]{:S(2)}) collective-permute-start(bf16[8,32,512]{2,1,0:T(8,128)(2,1)S(1)} %slice.31), channel_id=1, source_target_pairs={{24,0},{0,8},{8,16},{16,24},{25,1},{1,9},{9,17},{17,25},{26,2},{2,... | collective-permute-start | bytes 786440 | tf_op jit(solution)/shard_map/ppermute | solution.py:266
  90.5 8.9 %collective-permute-start.24 = (bf16[128,1024]{1,0:T(8,128)(2,1)S(1)}, bf16[128,1024]{1,0:T(8,128)(2,1)S(1)}, u32[]{:S(2)}, u32[]{:S(2)}) collective-permute-start(bf16[128,1024]{1,0:T(8,128)(2,1)S(1)} %mlp_second.5), channel_id=1, source_target_pairs={{6,0},{0,2},{2,4},{4,6},{7,1},{1,3},{3,5},{5,7},{14,8},{8,10},{10,... | collective-permute-start | bytes 786440 | tf_op jit(solution)/shard_map/ppermute | solution.py:266
  91.3 8.6 %collective-permute-start.25 = (bf16[128,1024]{1,0:T(8,128)(2,1)S(1)}, bf16[128,1024]{1,0:T(8,128)(2,1)S(1)}, u32[]{:S(2)}, u32[]{:S(2)}) collective-permute-start(bf16[128,1024]{1,0:T(8,128)(2,1)S(1)} %mlp_second.6), channel_id=1, source_target_pairs={{2,0},{4,2},{6,4},{0,6},{3,1},{5,3},{7,5},{1,7},{10,8},{12,10},{14... | collective-permute-start | bytes 786440 | tf_op jit(solution)/shard_map/ppermute | solution.py:266
  94.8 9.0 %collective-permute-start.26 = (bf16[128,1024]{1,0:T(8,128)(2,1)S(1)}, bf16[128,1024]{1,0:T(8,128)(2,1)S(1)}, u32[]{:S(2)}, u32[]{:S(2)}) collective-permute-start(bf16[128,1024]{1,0:T(8,128)(2,1)S(1)} %mlp_second.7), channel_id=1, source_target_pairs={{4,0},{6,2},{0,4},{2,6},{5,1},{7,3},{1,5},{3,7},{12,8},{14,10},{8,... | collective-permute-start | bytes 786440 | tf_op jit(solution)/shard_map/ppermute | solution.py:266
  (10 other events, 193.9 us)

commit v7 on v6

--- a/solution.py
+++ b/solution.py
@@ -1,5 +1,3 @@
-import functools
-
 import jax
 import jax.numpy as jnp
 from jax import lax
@@ -149,13 +147,12 @@
 
 def attention_kernel(
     at, own_low, own_high, peer_low, peer_high, here, right, far_low, far_high, left,
-    near_own, near_peer, gains, first, count, keep, give, out_w, weight, q_s, kv_s, att,
+    near_own, near_peer, gains, first, count, keep, both, weight, q_s, kv_s, att,
 ):
     lay(at[2], here, right, far_low, far_high, left, weight)
     core, anchor = at[1], at[3]
     gain = gains[...]
     gain = jnp.concatenate([gain[:, 0], gain[:, 1]], axis=1)
-    out_w[...] = weight[:, 384:]
 
     rows = jnp.concatenate([near_own[...], near_peer[...]], axis=0)
     part = jnp.dot(rows, weight[:, 128:384], preferred_element_type=F32)
@@ -185,17 +182,16 @@
             count[b : b + 1],
             anchor + (b * 128 - WIN),
         )
-    keep[...] = att[0]
-    give[...] = att[1]
-
-
-def project_kernel(at, keep, got, weight, other, mine, away):
+    keep[...] = att[0].reshape(512, 128)
+    both[:512] = att[1].reshape(512, 128)
+    both[512:] = weight[:, 384:]
+
+
+def project_kernel(at, keep, sent, got, mine, away):
     y = at[0]
-    rows = jnp.concatenate(
-        [keep[...].reshape(512, 128), got[...].reshape(512, 128)], axis=1
-    )
-    both = jnp.concatenate([weight[...], other[...]], axis=1)
-    part = lax.dot_general(rows, both, NT, preferred_element_type=F32)
+    rows = jnp.concatenate([keep[...], got[:512]], axis=1)
+    weight = jnp.concatenate([sent[512:], got[512:]], axis=1)
+    part = lax.dot_general(rows, weight, NT, preferred_element_type=F32)
     for t in range(4):
         block = part[t * 128 : t * 128 + 128]
 
@@ -227,18 +223,12 @@
     out[...] = hidden_share(rows, weight)
 
 
-def mlp_second_kernel(rows, weight, part, out, *, at):
-    total = part[at * 128 : at * 128 + 128] + hidden_share(rows[...], weight)
-    out[...] = total.astype(out.dtype)
-
-
-def mlp_second(rows, weight, part, at):
-    return call(
-        functools.partial(mlp_second_kernel, at=at),
-        [((128, 1024), F32 if at == 0 else BF16)],
-        [VMEM] * 3,
-        "mlp_second",
-    )(rows, weight, part)[0]
+def mlp_second_kernel(a, b, c, d, weight, part, mine, to_b, to_c, to_d):
+    rows = jnp.concatenate([a[...], b[...], c[...], d[...]], axis=0)
+    total = part[...] + hidden_share(rows, weight)
+    mine[...] = total[:128]
+    for i, out in enumerate((to_b, to_c, to_d)):
+        out[...] = total[i * 128 + 128 : i * 128 + 256].astype(BF16)
 
 
 def end_kernel(middle, mine, a, b, c, out):
@@ -334,9 +324,9 @@
         ],
     )
     near_peer = fetch(near_own, "core", 1)
-    keep, give, weight = call(
+    keep, both = call(
         attention_kernel,
-        [((4, 128, 128), BF16), ((4, 128, 128), BF16), ((1024, 128), BF16)],
+        [((512, 128), BF16), ((1536, 128), BF16)],
         [SMEM] + [VMEM] * 14,
         "attention",
         scratch=[
@@ -348,14 +338,13 @@
     )(at, own_low, own_high, peer_low, peer_high, *weights, near_own, near_peer, qk_gain, first, count)
 
     mlp_weights = relay(back)
-    out_peer = fetch(weight, "core", 1)
-    got = fetch(give, "core", 1)
+    got = fetch(both, "core", 1)
     mine_attended, away = call(
         project_kernel,
         [((128, 1024), F32), ((3, 128, 1024), BF16)],
-        [SMEM] + [VMEM] * 4,
+        [SMEM] + [VMEM] * 3,
         "project",
-    )(at, keep, got, weight, out_peer)
+    )(at, keep, both, got)
     parts = [fetch(away[k - 1], "y", 4 - k) for k in (1, 3, 2)]
     middle, normed_two = call(
         middle_kernel,
@@ -373,8 +362,14 @@
     (part,) = call(mlp_first_kernel, [((512, 1024), F32)], [VMEM] * 5, "mlp_first", mib=16)(
         normed_two, far[1], far[2], far[3], mlp_own
     )
-    parts = [fetch(mlp_second(far[k], mlp_peer, part, k), "y", 4 - k) for k in (1, 3, 2)]
-    mine = mlp_second(normed_two, mlp_peer, part, 0)
+    mine, *away = call(
+        mlp_second_kernel,
+        [((128, 1024), F32)] + [((128, 1024), BF16)] * 3,
+        [VMEM] * 6,
+        "mlp_second",
+        mib=16,
+    )(normed_two, far[1], far[2], far[3], mlp_peer, part)
+    parts = [fetch(away[k - 1], "y", 4 - k) for k in (1, 3, 2)]
     (out,) = call(end_kernel, [((128, 1024), BF16)], [VMEM] * 5, "end")(middle, mine, *parts)
     return out
 

time: 107 us -> 106 us (level); the launches traced: 105 us -> 105 us
  waiting for transfers between devices: 47.5 us -> 50.5 us
  Pallas kernels: 15.8 us -> 14.1 us
    ppermute x26 -> x25, waiting for transfers between devices: 36.8 us -> 39.7 us  [fetch(): return lax.ppermute(value, axis, [((i + step) % n, i) for i in range(n)])]
    pallas_call x5 -> x2, Pallas kernels: 6.32 us -> 4.71 us  [the longest x1 3.32 us: local(): call(attention_kernel, [((512, 128), BF16), ((1536, 128), BF16)], [SMEM]...]
    ppermute x26 -> x25, starting transfers between devices: 28.3 us -> 27.7 us  [fetch(): return lax.ppermute(value, axis, [((i + step) % n, i) for i in range(n)])]
  transfers between devices with their start and end apart: 29 -> 28, of which waited for: 15 -> 14; matrix products, arithmetic and copies ran while one was open for 0% -> 0% of each run, Pallas kernels for 11% -> 9%
where the time goes in v7:
time: 106 us; the launch traced here: 105 us
  waiting for transfers between devices  50.5 us (48%)
  starting transfers between devices  40.4 us (38%)
  Pallas kernels  14.1 us (13%)
    ppermute x25, waiting for transfers between devices, fetch(): return lax.ppermute(value, axis, [((i + step) % n, i) for i in range(n)])  39.7 us
    ppermute x25, starting transfers between devices, fetch(): return lax.ppermute(value, axis, [((i + step) % n, i) for i in range(n)])  27.7 us
    all_to_all x1, starting transfers between devices, local(): front = lax.all_to_all(front, 'z', 0, 0, tiled=True)  9.16 us
    ppermute x1, waiting for transfers between devices, local(): lax.ppermute(border, ('z', 'x', 'y', 'core'), [(spot(*divmod(s, 4), j, c)...  7.08 us
    pallas_call x3, Pallas kernels, from_hbm(): call(kernel, outs, [HBM] * len(given), name, scratch=[pltpu.VMEM(v.shape,...  4.31 us
    all_to_all x1, waiting for transfers between devices, local(): front = lax.all_to_all(front, 'z', 0, 0, tiled=True)  3.67 us
    all_to_all x1, starting transfers between devices, local(): back = lax.all_to_all(back, 'z', 0, 0, tiled=True)  3.49 us
    pallas_call x1, Pallas kernels, local(): call(attention_kernel, [((512, 128), BF16), ((1536, 128), BF16)], [SMEM]...  3.32 us
  transfers between devices with their start and end apart: 28, of which 14 were waited for; matrix products, arithmetic and copies ran while one was open for 0% of the time, Pallas kernels for 9%

profile of v7, /device:TPU:1, one launch (start us, length us, event | category | flops | bytes accessed | tf_op | source)
XLA Modules:
  0.0 105.4 jit_solution(9988508017922837392)
XLA Ops:
  0.0 1.5 %pack.1 = bf16[8,32,512]{2,1,0:T(8,128)(2,1)} custom-call(bf16[3,32,128]{2,1,0:T(8,128)(2,1)} %bitcast.21, bf16[32,128]{1,0:T(8,128)(2,1)} %bitcast.22), custom_call_target="tpu_custom_call" | custom-call | flops 1048576 | bytes 2097152 | tf_op jit(solution)/shard_map/pack/pallas_call | solution.py:76
  1.5 9.2 %all-to-all-start = ((bf16[8,32,512]{2,1,0:T(8,128)(2,1)}), bf16[8,32,512]{2,1,0:T(8,128)(2,1)S(1)}, u32[]{:S(2)}, u32[]{:S(2)}) async-start(bf16[8,32,512]{2,1,0:T(8,128)(2,1)} %pack.1), calls=%async_computation | async-start | bytes 524288 | tf_op jit(solution)/shard_map/all_to_all | solution.py:301
  11.9 2.8 %collective-permute-start = (bf16[128,1024]{1,0:T(8,128)(2,1)S(1)}, bf16[128,1024]{1,0:T(8,128)(2,1)S(1)}, u32[]{:S(2)}, u32[]{:S(2)}) collective-permute-start(bf16[128,1024]{1,0:T(8,128)(2,1)S(1)} %norm.1.refs_0_), channel_id=1, source_target_pairs={{2,0},{4,2},{6,4},{0,6},{3,1},{5,3},{7,5},{1,7},{10,8},{12,10},{14... | collective-permute-start | bytes 786440 | tf_op jit(solution)/shard_map/ppermute | solution.py:256
  15.7 1.6 %mlp_pack.1 = bf16[8,32,1024]{2,1,0:T(8,128)(2,1)} custom-call(bf16[32,512]{1,0:T(8,128)(2,1)} %refs_0_.3, bf16[32,512]{1,0:T(8,128)(2,1)} %bitcast.20), custom_call_target="tpu_custom_call" | custom-call | flops 1048576 | bytes 2097152 | tf_op jit(solution)/shard_map/mlp_pack/pallas_call | solution.py:76
  17.4 3.7 %all-to-all-done.here = bf16[8,32,512]{2,1,0:T(8,128)(2,1)S(1)} async-done(((bf16[8,32,512]{2,1,0:T(8,128)(2,1)}), bf16[8,32,512]{2,1,0:T(8,128)(2,1)S(1)}, u32[]{:S(2)}, u32[]{:S(2)}) %all-to-all-start) | async-done | bytes 262176 | tf_op jit(solution)/shard_map/all_to_all | solution.py:301
  21.0 2.5 %collective-permute-start.3 = (bf16[8,32,512]{2,1,0:T(8,128)(2,1)S(1)}, bf16[8,32,512]{2,1,0:T(8,128)(2,1)S(1)}, u32[]{:S(2)}, u32[]{:S(2)}) collective-permute-start(bf16[8,32,512]{2,1,0:T(8,128)(2,1)S(1)} %all-to-all-done.here), channel_id=1, source_target_pairs={{8,0},{16,8},{24,16},{0,24},{9,1},{17,9},{25,17},{1,25},{10,2},{18... | collective-permute-start | bytes 786440 | tf_op jit(solution)/shard_map/ppermute | solution.py:256
  23.5 3.5 %all-to-all-start.1 = ((bf16[8,32,1024]{2,1,0:T(8,128)(2,1)}), bf16[8,32,1024]{2,1,0:T(8,128)(2,1)S(1)}, u32[]{:S(2)}, u32[]{:S(2)}) async-start(bf16[8,32,1024]{2,1,0:T(8,128)(2,1)} %mlp_pack.1), calls=%async_computation.1 | async-start | bytes 1048576 | tf_op jit(solution)/shard_map/all_to_all | solution.py:305
  27.1 2.9 %collective-permute-done.2.refs_3_ = bf16[128,1024]{1,0:T(8,128)(2,1)S(1)} collective-permute-done((bf16[128,1024]{1,0:T(8,128)(2,1)S(1)}, bf16[128,1024]{1,0:T(8,128)(2,1)S(1)}, u32[]{:S(2)}, u32[]{:S(2)}) %collective-permute-start.2) | collective-permute-done | bytes 262176 | tf_op jit(solution)/shard_map/ppermute | solution.py:256
  30.9 3.8 %collective-permute-start.5 = (bf16[2,128,1024]{2,1,0:T(8,128)(2,1)S(1)}, bf16[2,128,1024]{2,1,0:T(8,128)(2,1)S(1)}, u32[]{:S(2)}, u32[]{:S(2)}) collective-permute-start(bf16[2,128,1024]{2,1,0:T(8,128)(2,1)S(1)} %get-tuple-element.35.own_low), channel_id=1, source_target_pairs={{1,0},{0,1},{3,2},{2,3},{5,4},{4,5},{7,6},{6,7},{9,8},{8,9},{11,10... | collective-permute-start | bytes 1572872 | tf_op jit(solution)/shard_map/ppermute | solution.py:256
  34.8 2.8 %collective-permute-start.7 = (bf16[8,32,256]{2,1,0:T(8,128)(2,1)S(1)}, bf16[8,32,256]{2,1,0:T(8,128)(2,1)S(1)}, u32[]{:S(2)}, u32[]{:S(2)}) collective-permute-start(bf16[8,32,256]{2,1,0:T(8,128)(2,1)S(1)} %slice.28), channel_id=1, source_target_pairs={{8,0},{16,8},{24,16},{0,24},{9,1},{17,9},{25,17},{1,25},{10,2},{18... | collective-permute-start | bytes 393224 | tf_op jit(solution)/shard_map/ppermute | solution.py:256
  37.6 7.1 %collective-permute-done.9.near_own = bf16[64,1024]{1,0:T(8,128)(2,1)S(1)} collective-permute-done((bf16[64,1024]{1,0:T(8,128)(2,1)S(1)}, bf16[64,1024]{1,0:T(8,128)(2,1)S(1)}, u32[]{:S(2)}, u32[]{:S(2)}) %collective-permute-start.9) | collective-permute-done | bytes 131104 | tf_op jit(solution)/shard_map/ppermute | solution.py:316
  46.1 3.3 %attention.1 = (bf16[512,128]{1,0:T(8,128)(2,1)S(1)}, bf16[1536,128]{1,0:T(8,128)(2,1)S(1)}) custom-call(s32[4]{0:T(128)S(1)} %pad_add_fusion.at, bf16[2,128,1024]{2,1,0:T(8,128)(2,1)S(1)} %get-tuple-element.35.own_low, bf16[2,128,1024]{2,1,0:T(8,128)(2,1)S(1)} %get-tuple-element.36.own_high, bf16[2,128,1024]{2,1,0:T(8,128)(2,1)S(1)} %collective-permute-done.5.peer_low, ...), custom_call_target="tpu_custom_call" | custom-call | flops 1048576 | bytes 2097152 | tf_op jit(solution)/shard_map/attention/pallas_call | solution.py:327
  53.9 1.5 %collective-permute-start.13 = (bf16[128,1024]{1,0:T(8,128)(2,1)S(1)}, bf16[128,1024]{1,0:T(8,128)(2,1)S(1)}, u32[]{:S(2)}, u32[]{:S(2)}) collective-permute-start(bf16[128,1024]{1,0:T(8,128)(2,1)S(1)} %get-tuple-element.58), channel_id=1, source_target_pairs={{2,0},{4,2},{6,4},{0,6},{3,1},{5,3},{7,5},{1,7},{10,8},{12,10},{14... | collective-permute-start | bytes 786440 | tf_op jit(solution)/shard_map/ppermute | solution.py:256
  55.4 1.6 %collective-permute-start.14 = (bf16[128,1024]{1,0:T(8,128)(2,1)S(1)}, bf16[128,1024]{1,0:T(8,128)(2,1)S(1)}, u32[]{:S(2)}, u32[]{:S(2)}) collective-permute-start(bf16[128,1024]{1,0:T(8,128)(2,1)S(1)} %get-tuple-element.57), channel_id=1, source_target_pairs={{4,0},{6,2},{0,4},{2,6},{5,1},{7,3},{1,5},{3,7},{12,8},{14,10},{8,... | collective-permute-start | bytes 786440 | tf_op jit(solution)/shard_map/ppermute | solution.py:256
  56.9 4.0 %collective-permute-done.12.a = bf16[128,1024]{1,0:T(8,128)(2,1)S(1)} collective-permute-done((bf16[128,1024]{1,0:T(8,128)(2,1)S(1)}, bf16[128,1024]{1,0:T(8,128)(2,1)S(1)}, u32[]{:S(2)}, u32[]{:S(2)}) %collective-permute-start.12) | collective-permute-done | bytes 262176 | tf_op jit(solution)/shard_map/ppermute | solution.py:256
  61.0 6.7 %collective-permute-done.14.c = bf16[128,1024]{1,0:T(8,128)(2,1)S(1)} collective-permute-done((bf16[128,1024]{1,0:T(8,128)(2,1)S(1)}, bf16[128,1024]{1,0:T(8,128)(2,1)S(1)}, u32[]{:S(2)}, u32[]{:S(2)}) %collective-permute-start.14) | collective-permute-done | bytes 262176 | tf_op jit(solution)/shard_map/ppermute | solution.py:256
  70.5 1.6 %collective-permute-start.16 = (bf16[8,32,512]{2,1,0:T(8,128)(2,1)S(1)}, bf16[8,32,512]{2,1,0:T(8,128)(2,1)S(1)}, u32[]{:S(2)}, u32[]{:S(2)}) collective-permute-start(bf16[8,32,512]{2,1,0:T(8,128)(2,1)S(1)} %slice.30), channel_id=1, source_target_pairs={{8,0},{16,8},{24,16},{0,24},{9,1},{17,9},{25,17},{1,25},{10,2},{18... | collective-permute-start | bytes 786440 | tf_op jit(solution)/shard_map/ppermute | solution.py:256
  72.2 2.0 %collective-permute-done.19.b = bf16[128,1024]{1,0:T(8,128)(2,1)S(1)} collective-permute-done((bf16[128,1024]{1,0:T(8,128)(2,1)S(1)}, bf16[128,1024]{1,0:T(8,128)(2,1)S(1)}, u32[]{:S(2)}, u32[]{:S(2)}) %collective-permute-start.19) | collective-permute-done | bytes 262176 | tf_op jit(solution)/shard_map/ppermute | solution.py:256
  74.2 1.7 %collective-permute-done.20.c = bf16[128,1024]{1,0:T(8,128)(2,1)S(1)} collective-permute-done((bf16[128,1024]{1,0:T(8,128)(2,1)S(1)}, bf16[128,1024]{1,0:T(8,128)(2,1)S(1)}, u32[]{:S(2)}, u32[]{:S(2)}) %collective-permute-start.20) | collective-permute-done | bytes 262176 | tf_op jit(solution)/shard_map/ppermute | solution.py:256
  75.9 7.8 %collective-permute-done.21.d = bf16[128,1024]{1,0:T(8,128)(2,1)S(1)} collective-permute-done((bf16[128,1024]{1,0:T(8,128)(2,1)S(1)}, bf16[128,1024]{1,0:T(8,128)(2,1)S(1)}, u32[]{:S(2)}, u32[]{:S(2)}) %collective-permute-start.21) | collective-permute-done | bytes 262176 | tf_op jit(solution)/shard_map/ppermute | solution.py:256
  87.1 2.4 %collective-permute-done.22.weight = bf16[1024,1024]{1,0:T(8,128)(2,1)S(1)} collective-permute-done((bf16[1024,1024]{1,0:T(8,128)(2,1)S(1)}, bf16[1024,1024]{1,0:T(8,128)(2,1)S(1)}, u32[]{:S(2)}, u32[]{:S(2)}) %collective-permute-start.22) | collective-permute-done | bytes 2097184 | tf_op jit(solution)/shard_map/ppermute | solution.py:256
  91.0 2.7 %collective-permute-start.24 = (bf16[128,1024]{1,0:T(8,128)(2,1)S(1)}, bf16[128,1024]{1,0:T(8,128)(2,1)S(1)}, u32[]{:S(2)}, u32[]{:S(2)}) collective-permute-start(bf16[128,1024]{1,0:T(8,128)(2,1)S(1)} %get-tuple-element.55), channel_id=1, source_target_pairs={{2,0},{4,2},{6,4},{0,6},{3,1},{5,3},{7,5},{1,7},{10,8},{12,10},{14... | collective-permute-start | bytes 786440 | tf_op jit(solution)/shard_map/ppermute | solution.py:256
  93.8 6.7 %collective-permute-done.23.a = bf16[128,1024]{1,0:T(8,128)(2,1)S(1)} collective-permute-done((bf16[128,1024]{1,0:T(8,128)(2,1)S(1)}, bf16[128,1024]{1,0:T(8,128)(2,1)S(1)}, u32[]{:S(2)}, u32[]{:S(2)}) %collective-permute-start.23) | collective-permute-done | bytes 262176 | tf_op jit(solution)/shard_map/ppermute | solution.py:256
  100.5 4.0 %collective-permute-done.25.c = bf16[128,1024]{1,0:T(8,128)(2,1)S(1)} collective-permute-done((bf16[128,1024]{1,0:T(8,128)(2,1)S(1)}, bf16[128,1024]{1,0:T(8,128)(2,1)S(1)}, u32[]{:S(2)}, u32[]{:S(2)}) %collective-permute-start.25) | collective-permute-done | bytes 262176 | tf_op jit(solution)/shard_map/ppermute | solution.py:256
  (59 shorter events, 17.9 us)
Async XLA Ops:
  1.5 19.5 %all-to-all-start = ((bf16[8,32,512]{2,1,0:T(8,128)(2,1)}), bf16[8,32,512]{2,1,0:T(8,128)(2,1)S(1)}, u32[]{:S(2)}, u32[]{:S(2)}) async-start(bf16[8,32,512]{2,1,0:T(8,128)(2,1)} %pack.1), calls=%async_computation | async-start | bytes 524288 | tf_op jit(solution)/shard_map/all_to_all | solution.py:301
  11.9 15.2 %collective-permute-start = (bf16[128,1024]{1,0:T(8,128)(2,1)S(1)}, bf16[128,1024]{1,0:T(8,128)(2,1)S(1)}, u32[]{:S(2)}, u32[]{:S(2)}) collective-permute-start(bf16[128,1024]{1,0:T(8,128)(2,1)S(1)} %norm.1.refs_0_), channel_id=1, source_target_pairs={{2,0},{4,2},{6,4},{0,6},{3,1},{5,3},{7,5},{1,7},{10,8},{12,10},{14... | collective-permute-start | bytes 786440 | tf_op jit(solution)/shard_map/ppermute | solution.py:256
  14.7 12.4 %collective-permute-start.1 = (bf16[128,1024]{1,0:T(8,128)(2,1)S(1)}, bf16[128,1024]{1,0:T(8,128)(2,1)S(1)}, u32[]{:S(2)}, u32[]{:S(2)}) collective-permute-start(bf16[128,1024]{1,0:T(8,128)(2,1)S(1)} %norm.1.refs_0_), channel_id=1, source_target_pairs={{4,0},{6,2},{0,4},{2,6},{5,1},{7,3},{1,5},{3,7},{12,8},{14,10},{8,... | collective-permute-start | bytes 786440 | tf_op jit(solution)/shard_map/ppermute | solution.py:256
  15.1 15.0 %collective-permute-start.2 = (bf16[128,1024]{1,0:T(8,128)(2,1)S(1)}, bf16[128,1024]{1,0:T(8,128)(2,1)S(1)}, u32[]{:S(2)}, u32[]{:S(2)}) collective-permute-start(bf16[128,1024]{1,0:T(8,128)(2,1)S(1)} %norm.1.refs_0_), channel_id=1, source_target_pairs={{6,0},{0,2},{2,4},{4,6},{7,1},{1,3},{3,5},{5,7},{14,8},{8,10},{10,... | collective-permute-start | bytes 786440 | tf_op jit(solution)/shard_map/ppermute | solution.py:256
  21.0 9.0 %collective-permute-start.3 = (bf16[8,32,512]{2,1,0:T(8,128)(2,1)S(1)}, bf16[8,32,512]{2,1,0:T(8,128)(2,1)S(1)}, u32[]{:S(2)}, u32[]{:S(2)}) collective-permute-start(bf16[8,32,512]{2,1,0:T(8,128)(2,1)S(1)} %all-to-all-done.here), channel_id=1, source_target_pairs={{8,0},{16,8},{24,16},{0,24},{9,1},{17,9},{25,17},{1,25},{10,2},{18... | collective-permute-start | bytes 786440 | tf_op jit(solution)/shard_map/ppermute | solution.py:256
  23.5 6.6 %collective-permute-start.4 = (bf16[8,32,512]{2,1,0:T(8,128)(2,1)S(1)}, bf16[8,32,512]{2,1,0:T(8,128)(2,1)S(1)}, u32[]{:S(2)}, u32[]{:S(2)}) collective-permute-start(bf16[8,32,512]{2,1,0:T(8,128)(2,1)S(1)} %all-to-all-done.here), channel_id=1, source_target_pairs={{24,0},{0,8},{8,16},{16,24},{25,1},{1,9},{9,17},{17,25},{26,2},{2,... | collective-permute-start | bytes 786440 | tf_op jit(solution)/shard_map/ppermute | solution.py:256
  23.5 26.1 %all-to-all-start.1 = ((bf16[8,32,1024]{2,1,0:T(8,128)(2,1)}), bf16[8,32,1024]{2,1,0:T(8,128)(2,1)S(1)}, u32[]{:S(2)}, u32[]{:S(2)}) async-start(bf16[8,32,1024]{2,1,0:T(8,128)(2,1)} %mlp_pack.1), calls=%async_computation.1 | async-start | bytes 1048576 | tf_op jit(solution)/shard_map/all_to_all | solution.py:305
  30.9 15.2 %collective-permute-start.5 = (bf16[2,128,1024]{2,1,0:T(8,128)(2,1)S(1)}, bf16[2,128,1024]{2,1,0:T(8,128)(2,1)S(1)}, u32[]{:S(2)}, u32[]{:S(2)}) collective-permute-start(bf16[2,128,1024]{2,1,0:T(8,128)(2,1)S(1)} %get-tuple-element.35.own_low), channel_id=1, source_target_pairs={{1,0},{0,1},{3,2},{2,3},{5,4},{4,5},{7,6},{6,7},{9,8},{8,9},{11,10... | collective-permute-start | bytes 1572872 | tf_op jit(solution)/shard_map/ppermute | solution.py:256
  34.7 11.4 %collective-permute-start.6 = (bf16[2,128,1024]{2,1,0:T(8,128)(2,1)S(1)}, bf16[2,128,1024]{2,1,0:T(8,128)(2,1)S(1)}, u32[]{:S(2)}, u32[]{:S(2)}) collective-permute-start(bf16[2,128,1024]{2,1,0:T(8,128)(2,1)S(1)} %get-tuple-element.36.own_high), channel_id=1, source_target_pairs={{1,0},{0,1},{3,2},{2,3},{5,4},{4,5},{7,6},{6,7},{9,8},{8,9},{11,10... | collective-permute-start | bytes 1572872 | tf_op jit(solution)/shard_map/ppermute | solution.py:256
  34.8 9.9 %collective-permute-start.9 = (bf16[64,1024]{1,0:T(8,128)(2,1)S(1)}, bf16[64,1024]{1,0:T(8,128)(2,1)S(1)}, u32[]{:S(2)}, u32[]{:S(2)}) collective-permute-start(bf16[64,1024]{1,0:T(8,128)(2,1)S(1)} %get-tuple-element.37), channel_id=1, source_target_pairs={{0,248},{1,9},{2,250},{3,11},{4,252},{5,13},{6,254},{7,15},{8,0},{... | collective-permute-start | bytes 393224 | tf_op jit(solution)/shard_map/ppermute | solution.py:316
  34.8 9.9 %collective-permute-start.7 = (bf16[8,32,256]{2,1,0:T(8,128)(2,1)S(1)}, bf16[8,32,256]{2,1,0:T(8,128)(2,1)S(1)}, u32[]{:S(2)}, u32[]{:S(2)}) collective-permute-start(bf16[8,32,256]{2,1,0:T(8,128)(2,1)S(1)} %slice.28), channel_id=1, source_target_pairs={{8,0},{16,8},{24,16},{0,24},{9,1},{17,9},{25,17},{1,25},{10,2},{18... | collective-permute-start | bytes 393224 | tf_op jit(solution)/shard_map/ppermute | solution.py:256
  37.6 8.1 %collective-permute-start.8 = (bf16[8,32,256]{2,1,0:T(8,128)(2,1)S(1)}, bf16[8,32,256]{2,1,0:T(8,128)(2,1)S(1)}, u32[]{:S(2)}, u32[]{:S(2)}) collective-permute-start(bf16[8,32,256]{2,1,0:T(8,128)(2,1)S(1)} %slice.29), channel_id=1, source_target_pairs={{24,0},{0,8},{8,16},{16,24},{25,1},{1,9},{9,17},{17,25},{26,2},{2,... | collective-permute-start | bytes 393224 | tf_op jit(solution)/shard_map/ppermute | solution.py:256
  49.7 20.8 %collective-permute-start.15 = (bf16[8,32,1024]{2,1,0:T(8,128)(2,1)S(1)}, bf16[8,32,1024]{2,1,0:T(8,128)(2,1)S(1)}, u32[]{:S(2)}, u32[]{:S(2)}) collective-permute-start(bf16[8,32,1024]{2,1,0:T(8,128)(2,1)S(1)} %all-to-all-done.1.refs_0_), channel_id=1, source_target_pairs={{8,0},{16,8},{24,16},{0,24},{9,1},{17,9},{25,17},{1,25},{10,2},{18... | collective-permute-start | bytes 1572872 | tf_op jit(solution)/shard_map/ppermute | solution.py:256
  50.2 21.9 %collective-permute-start.17 = (bf16[8,32,1024]{2,1,0:T(8,128)(2,1)S(1)}, bf16[8,32,1024]{2,1,0:T(8,128)(2,1)S(1)}, u32[]{:S(2)}, u32[]{:S(2)}) collective-permute-start(bf16[8,32,1024]{2,1,0:T(8,128)(2,1)S(1)} %all-to-all-done.1.refs_0_), channel_id=1, source_target_pairs={{24,0},{0,8},{8,16},{16,24},{25,1},{1,9},{9,17},{17,25},{26,2},{2,... | collective-permute-start | bytes 1572872 | tf_op jit(solution)/shard_map/ppermute | solution.py:256
  52.5 8.5 %collective-permute-start.12 = (bf16[128,1024]{1,0:T(8,128)(2,1)S(1)}, bf16[128,1024]{1,0:T(8,128)(2,1)S(1)}, u32[]{:S(2)}, u32[]{:S(2)}) collective-permute-start(bf16[128,1024]{1,0:T(8,128)(2,1)S(1)} %get-tuple-element.59), channel_id=1, source_target_pairs={{6,0},{0,2},{2,4},{4,6},{7,1},{1,3},{3,5},{5,7},{14,8},{8,10},{10,... | collective-permute-start | bytes 786440 | tf_op jit(solution)/shard_map/ppermute | solution.py:256
  53.9 7.1 %collective-permute-start.13 = (bf16[128,1024]{1,0:T(8,128)(2,1)S(1)}, bf16[128,1024]{1,0:T(8,128)(2,1)S(1)}, u32[]{:S(2)}, u32[]{:S(2)}) collective-permute-start(bf16[128,1024]{1,0:T(8,128)(2,1)S(1)} %get-tuple-element.58), channel_id=1, source_target_pairs={{2,0},{4,2},{6,4},{0,6},{3,1},{5,3},{7,5},{1,7},{10,8},{12,10},{14... | collective-permute-start | bytes 786440 | tf_op jit(solution)/shard_map/ppermute | solution.py:256
  55.4 12.3 %collective-permute-start.14 = (bf16[128,1024]{1,0:T(8,128)(2,1)S(1)}, bf16[128,1024]{1,0:T(8,128)(2,1)S(1)}, u32[]{:S(2)}, u32[]{:S(2)}) collective-permute-start(bf16[128,1024]{1,0:T(8,128)(2,1)S(1)} %get-tuple-element.57), channel_id=1, source_target_pairs={{4,0},{6,2},{0,4},{2,6},{5,1},{7,3},{1,5},{3,7},{12,8},{14,10},{8,... | collective-permute-start | bytes 786440 | tf_op jit(solution)/shard_map/ppermute | solution.py:256
  69.1 6.8 %collective-permute-start.20 = (bf16[128,1024]{1,0:T(8,128)(2,1)S(1)}, bf16[128,1024]{1,0:T(8,128)(2,1)S(1)}, u32[]{:S(2)}, u32[]{:S(2)}) collective-permute-start(bf16[128,1024]{1,0:T(8,128)(2,1)S(1)} %get-tuple-element.43.a), channel_id=1, source_target_pairs={{4,0},{6,2},{0,4},{2,6},{5,1},{7,3},{1,5},{3,7},{12,8},{14,10},{8,... | collective-permute-start | bytes 786440 | tf_op jit(solution)/shard_map/ppermute | solution.py:256
  70.5 13.2 %collective-permute-start.21 = (bf16[128,1024]{1,0:T(8,128)(2,1)S(1)}, bf16[128,1024]{1,0:T(8,128)(2,1)S(1)}, u32[]{:S(2)}, u32[]{:S(2)}) collective-permute-start(bf16[128,1024]{1,0:T(8,128)(2,1)S(1)} %get-tuple-element.43.a), channel_id=1, source_target_pairs={{6,0},{0,2},{2,4},{4,6},{7,1},{1,3},{3,5},{5,7},{14,8},{8,10},{10,... | collective-permute-start | bytes 786440 | tf_op jit(solution)/shard_map/ppermute | solution.py:256
  70.5 13.2 %collective-permute-start.16 = (bf16[8,32,512]{2,1,0:T(8,128)(2,1)S(1)}, bf16[8,32,512]{2,1,0:T(8,128)(2,1)S(1)}, u32[]{:S(2)}, u32[]{:S(2)}) collective-permute-start(bf16[8,32,512]{2,1,0:T(8,128)(2,1)S(1)} %slice.30), channel_id=1, source_target_pairs={{8,0},{16,8},{24,16},{0,24},{9,1},{17,9},{25,17},{1,25},{10,2},{18... | collective-permute-start | bytes 786440 | tf_op jit(solution)/shard_map/ppermute | solution.py:256
  72.1 11.6 %collective-permute-start.18 = (bf16[8,32,512]{2,1,0:T(8,128)(2,1)S(1)}, bf16[8,32,512]{2,1,0:T(8,128)(2,1)S(1)}, u32[]{:S(2)}, u32[]{:S(2)}) collective-permute-start(bf16[8,32,512]{2,1,0:T(8,128)(2,1)S(1)} %slice.31), channel_id=1, source_target_pairs={{24,0},{0,8},{8,16},{16,24},{25,1},{1,9},{9,17},{17,25},{26,2},{2,... | collective-permute-start | bytes 786440 | tf_op jit(solution)/shard_map/ppermute | solution.py:256
  90.9 9.6 %collective-permute-start.23 = (bf16[128,1024]{1,0:T(8,128)(2,1)S(1)}, bf16[128,1024]{1,0:T(8,128)(2,1)S(1)}, u32[]{:S(2)}, u32[]{:S(2)}) collective-permute-start(bf16[128,1024]{1,0:T(8,128)(2,1)S(1)} %get-tuple-element.54), channel_id=1, source_target_pairs={{6,0},{0,2},{2,4},{4,6},{7,1},{1,3},{3,5},{5,7},{14,8},{8,10},{10,... | collective-permute-start | bytes 786440 | tf_op jit(solution)/shard_map/ppermute | solution.py:256
  91.0 9.5 %collective-permute-start.24 = (bf16[128,1024]{1,0:T(8,128)(2,1)S(1)}, bf16[128,1024]{1,0:T(8,128)(2,1)S(1)}, u32[]{:S(2)}, u32[]{:S(2)}) collective-permute-start(bf16[128,1024]{1,0:T(8,128)(2,1)S(1)} %get-tuple-element.55), channel_id=1, source_target_pairs={{2,0},{4,2},{6,4},{0,6},{3,1},{5,3},{7,5},{1,7},{10,8},{12,10},{14... | collective-permute-start | bytes 786440 | tf_op jit(solution)/shard_map/ppermute | solution.py:256
  93.7 10.9 %collective-permute-start.25 = (bf16[128,1024]{1,0:T(8,128)(2,1)S(1)}, bf16[128,1024]{1,0:T(8,128)(2,1)S(1)}, u32[]{:S(2)}, u32[]{:S(2)}) collective-permute-start(bf16[128,1024]{1,0:T(8,128)(2,1)S(1)} %get-tuple-element.56), channel_id=1, source_target_pairs={{4,0},{6,2},{0,4},{2,6},{5,1},{7,3},{1,5},{3,7},{12,8},{14,10},{8,... | collective-permute-start | bytes 786440 | tf_op jit(solution)/shard_map/ppermute | solution.py:256
  (9 other events, 184.8 us)

commit v8 on v7

--- a/solution.py
+++ b/solution.py
@@ -354,10 +354,10 @@
     )(tokens, mine_attended, *parts, norm2_gain.reshape(1, 1024))
 
     far = {k: fetch(normed_two, "y", k) for k in (1, 3, 2)}
-    laid, far = lax.optimization_barrier((mlp_weights, far))
     (mlp_own,) = call(lay_kernel, [((1024, 1024), BF16)], [SMEM] + [VMEM] * 5, "mlp_lay")(
-        at, *laid
-    )
+        at, *mlp_weights
+    )
+    mlp_own, far = lax.optimization_barrier((mlp_own, far))
     mlp_peer = fetch(mlp_own, "core", 1)
     (part,) = call(mlp_first_kernel, [((512, 1024), F32)], [VMEM] * 5, "mlp_first", mib=16)(
         normed_two, far[1], far[2], far[3], mlp_own

time: 106 us -> 106 us (level)
  transfers between devices with their start and end apart: 28 -> 28, of which waited for: 14 -> 14; matrix products, arithmetic and copies ran while one was open for 0% -> 0% of each run, Pallas kernels for 9% -> 10%
where the time goes in v8:
time: 106 us; the launch traced here: 105 us
  waiting for transfers between devices  50.5 us (48%)
  starting transfers between devices  40.3 us (38%)
  Pallas kernels  14.1 us (13%)
    ppermute x25, waiting for transfers between devices, fetch(): return lax.ppermute(value, axis, [((i + step) % n, i) for i in range(n)])  39.8 us
    ppermute x25, starting transfers between devices, fetch(): return lax.ppermute(value, axis, [((i + step) % n, i) for i in range(n)])  27.6 us
    all_to_all x1, starting transfers between devices, local(): front = lax.all_to_all(front, 'z', 0, 0, tiled=True)  9.16 us
    ppermute x1, waiting for transfers between devices, local(): lax.ppermute(border, ('z', 'x', 'y', 'core'), [(spot(*divmod(s, 4), j, c)...  7.08 us
    pallas_call x3, Pallas kernels, from_hbm(): call(kernel, outs, [HBM] * len(given), name, scratch=[pltpu.VMEM(v.shape,...  4.31 us
    all_to_all x1, waiting for transfers between devices, local(): front = lax.all_to_all(front, 'z', 0, 0, tiled=True)  3.67 us
    all_to_all x1, starting transfers between devices, local(): back = lax.all_to_all(back, 'z', 0, 0, tiled=True)  3.49 us
    pallas_call x1, Pallas kernels, local(): call(attention_kernel, [((512, 128), BF16), ((1536, 128), BF16)], [SMEM]...  3.32 us
  transfers between devices with their start and end apart: 28, of which 14 were waited for; matrix products, arithmetic and copies ran while one was open for 0% of the time, Pallas kernels for 10%

profile of v8, /device:TPU:1, one launch (start us, length us, event | category | flops | bytes accessed | tf_op | source)
XLA Modules:
  0.0 105.4 jit_solution(6067610860923547661)
XLA Ops:
  0.0 1.5 %pack.1 = bf16[8,32,512]{2,1,0:T(8,128)(2,1)} custom-call(bf16[3,32,128]{2,1,0:T(8,128)(2,1)} %bitcast.21, bf16[32,128]{1,0:T(8,128)(2,1)} %bitcast.22), custom_call_target="tpu_custom_call" | custom-call | flops 1048576 | bytes 2097152 | tf_op jit(solution)/shard_map/pack/pallas_call | solution.py:76
  1.5 9.2 %all-to-all-start = ((bf16[8,32,512]{2,1,0:T(8,128)(2,1)}), bf16[8,32,512]{2,1,0:T(8,128)(2,1)S(1)}, u32[]{:S(2)}, u32[]{:S(2)}) async-start(bf16[8,32,512]{2,1,0:T(8,128)(2,1)} %pack.1), calls=%async_computation | async-start | bytes 524288 | tf_op jit(solution)/shard_map/all_to_all | solution.py:301
  11.9 2.8 %collective-permute-start = (bf16[128,1024]{1,0:T(8,128)(2,1)S(1)}, bf16[128,1024]{1,0:T(8,128)(2,1)S(1)}, u32[]{:S(2)}, u32[]{:S(2)}) collective-permute-start(bf16[128,1024]{1,0:T(8,128)(2,1)S(1)} %norm.1.refs_0_), channel_id=1, source_target_pairs={{2,0},{4,2},{6,4},{0,6},{3,1},{5,3},{7,5},{1,7},{10,8},{12,10},{14... | collective-permute-start | bytes 786440 | tf_op jit(solution)/shard_map/ppermute | solution.py:256
  15.7 1.6 %mlp_pack.1 = bf16[8,32,1024]{2,1,0:T(8,128)(2,1)} custom-call(bf16[32,512]{1,0:T(8,128)(2,1)} %refs_0_.3, bf16[32,512]{1,0:T(8,128)(2,1)} %bitcast.20), custom_call_target="tpu_custom_call" | custom-call | flops 1048576 | bytes 2097152 | tf_op jit(solution)/shard_map/mlp_pack/pallas_call | solution.py:76
  17.4 3.7 %all-to-all-done.here = bf16[8,32,512]{2,1,0:T(8,128)(2,1)S(1)} async-done(((bf16[8,32,512]{2,1,0:T(8,128)(2,1)}), bf16[8,32,512]{2,1,0:T(8,128)(2,1)S(1)}, u32[]{:S(2)}, u32[]{:S(2)}) %all-to-all-start) | async-done | bytes 262176 | tf_op jit(solution)/shard_map/all_to_all | solution.py:301
  21.0 2.5 %collective-permute-start.3 = (bf16[8,32,512]{2,1,0:T(8,128)(2,1)S(1)}, bf16[8,32,512]{2,1,0:T(8,128)(2,1)S(1)}, u32[]{:S(2)}, u32[]{:S(2)}) collective-permute-start(bf16[8,32,512]{2,1,0:T(8,128)(2,1)S(1)} %all-to-all-done.here), channel_id=1, source_target_pairs={{8,0},{16,8},{24,16},{0,24},{9,1},{17,9},{25,17},{1,25},{10,2},{18... | collective-permute-start | bytes 786440 | tf_op jit(solution)/shard_map/ppermute | solution.py:256
  23.5 3.5 %all-to-all-start.1 = ((bf16[8,32,1024]{2,1,0:T(8,128)(2,1)}), bf16[8,32,1024]{2,1,0:T(8,128)(2,1)S(1)}, u32[]{:S(2)}, u32[]{:S(2)}) async-start(bf16[8,32,1024]{2,1,0:T(8,128)(2,1)} %mlp_pack.1), calls=%async_computation.1 | async-start | bytes 1048576 | tf_op jit(solution)/shard_map/all_to_all | solution.py:305
  27.1 2.9 %collective-permute-done.2.refs_3_ = bf16[128,1024]{1,0:T(8,128)(2,1)S(1)} collective-permute-done((bf16[128,1024]{1,0:T(8,128)(2,1)S(1)}, bf16[128,1024]{1,0:T(8,128)(2,1)S(1)}, u32[]{:S(2)}, u32[]{:S(2)}) %collective-permute-start.2) | collective-permute-done | bytes 262176 | tf_op jit(solution)/shard_map/ppermute | solution.py:256
  30.9 3.8 %collective-permute-start.5 = (bf16[2,128,1024]{2,1,0:T(8,128)(2,1)S(1)}, bf16[2,128,1024]{2,1,0:T(8,128)(2,1)S(1)}, u32[]{:S(2)}, u32[]{:S(2)}) collective-permute-start(bf16[2,128,1024]{2,1,0:T(8,128)(2,1)S(1)} %get-tuple-element.31.own_low), channel_id=1, source_target_pairs={{1,0},{0,1},{3,2},{2,3},{5,4},{4,5},{7,6},{6,7},{9,8},{8,9},{11,10... | collective-permute-start | bytes 1572872 | tf_op jit(solution)/shard_map/ppermute | solution.py:256
  34.8 2.8 %collective-permute-start.7 = (bf16[8,32,256]{2,1,0:T(8,128)(2,1)S(1)}, bf16[8,32,256]{2,1,0:T(8,128)(2,1)S(1)}, u32[]{:S(2)}, u32[]{:S(2)}) collective-permute-start(bf16[8,32,256]{2,1,0:T(8,128)(2,1)S(1)} %slice.28), channel_id=1, source_target_pairs={{8,0},{16,8},{24,16},{0,24},{9,1},{17,9},{25,17},{1,25},{10,2},{18... | collective-permute-start | bytes 393224 | tf_op jit(solution)/shard_map/ppermute | solution.py:256
  37.6 7.1 %collective-permute-done.9.near_own = bf16[64,1024]{1,0:T(8,128)(2,1)S(1)} collective-permute-done((bf16[64,1024]{1,0:T(8,128)(2,1)S(1)}, bf16[64,1024]{1,0:T(8,128)(2,1)S(1)}, u32[]{:S(2)}, u32[]{:S(2)}) %collective-permute-start.9) | collective-permute-done | bytes 131104 | tf_op jit(solution)/shard_map/ppermute | solution.py:316
  46.1 3.3 %attention.1 = (bf16[512,128]{1,0:T(8,128)(2,1)S(1)}, bf16[1536,128]{1,0:T(8,128)(2,1)S(1)}) custom-call(s32[4]{0:T(128)S(1)} %pad_add_fusion.at, bf16[2,128,1024]{2,1,0:T(8,128)(2,1)S(1)} %get-tuple-element.31.own_low, bf16[2,128,1024]{2,1,0:T(8,128)(2,1)S(1)} %get-tuple-element.32.own_high, bf16[2,128,1024]{2,1,0:T(8,128)(2,1)S(1)} %collective-permute-done.5.peer_low, ...), custom_call_target="tpu_custom_call" | custom-call | flops 1048576 | bytes 2097152 | tf_op jit(solution)/shard_map/attention/pallas_call | solution.py:327
  53.9 1.5 %collective-permute-start.13 = (bf16[128,1024]{1,0:T(8,128)(2,1)S(1)}, bf16[128,1024]{1,0:T(8,128)(2,1)S(1)}, u32[]{:S(2)}, u32[]{:S(2)}) collective-permute-start(bf16[128,1024]{1,0:T(8,128)(2,1)S(1)} %get-tuple-element.50), channel_id=1, source_target_pairs={{2,0},{4,2},{6,4},{0,6},{3,1},{5,3},{7,5},{1,7},{10,8},{12,10},{14... | collective-permute-start | bytes 786440 | tf_op jit(solution)/shard_map/ppermute | solution.py:256
  55.4 1.6 %collective-permute-start.14 = (bf16[128,1024]{1,0:T(8,128)(2,1)S(1)}, bf16[128,1024]{1,0:T(8,128)(2,1)S(1)}, u32[]{:S(2)}, u32[]{:S(2)}) collective-permute-start(bf16[128,1024]{1,0:T(8,128)(2,1)S(1)} %get-tuple-element.49), channel_id=1, source_target_pairs={{4,0},{6,2},{0,4},{2,6},{5,1},{7,3},{1,5},{3,7},{12,8},{14,10},{8,... | collective-permute-start | bytes 786440 | tf_op jit(solution)/shard_map/ppermute | solution.py:256
  56.9 6.2 %collective-permute-done.15.refs_1_ = bf16[8,32,1024]{2,1,0:T(8,128)(2,1)S(1)} collective-permute-done((bf16[8,32,1024]{2,1,0:T(8,128)(2,1)S(1)}, bf16[8,32,1024]{2,1,0:T(8,128)(2,1)S(1)}, u32[]{:S(2)}, u32[]{:S(2)}) %collective-permute-start.15) | collective-permute-done | bytes 524320 | tf_op jit(solution)/shard_map/ppermute | solution.py:256
  63.1 1.6 %collective-permute-start.16 = (bf16[8,32,512]{2,1,0:T(8,128)(2,1)S(1)}, bf16[8,32,512]{2,1,0:T(8,128)(2,1)S(1)}, u32[]{:S(2)}, u32[]{:S(2)}) collective-permute-start(bf16[8,32,512]{2,1,0:T(8,128)(2,1)S(1)} %slice.30), channel_id=1, source_target_pairs={{8,0},{16,8},{24,16},{0,24},{9,1},{17,9},{25,17},{1,25},{10,2},{18... | collective-permute-start | bytes 786440 | tf_op jit(solution)/shard_map/ppermute | solution.py:256
  64.9 2.8 %collective-permute-done.14.c = bf16[128,1024]{1,0:T(8,128)(2,1)S(1)} collective-permute-done((bf16[128,1024]{1,0:T(8,128)(2,1)S(1)}, bf16[128,1024]{1,0:T(8,128)(2,1)S(1)}, u32[]{:S(2)}, u32[]{:S(2)}) %collective-permute-start.14) | collective-permute-done | bytes 262176 | tf_op jit(solution)/shard_map/ppermute | solution.py:256
  70.5 2.0 %collective-permute-done.18.refs_3_ = bf16[8,32,512]{2,1,0:T(8,128)(2,1)S(1)} collective-permute-done((bf16[8,32,512]{2,1,0:T(8,128)(2,1)S(1)}, bf16[8,32,512]{2,1,0:T(8,128)(2,1)S(1)}, u32[]{:S(2)}, u32[]{:S(2)}) %collective-permute-start.18) | collective-permute-done | bytes 262176 | tf_op jit(solution)/shard_map/ppermute | solution.py:256
  74.2 1.7 %collective-permute-done.20.c = bf16[128,1024]{1,0:T(8,128)(2,1)S(1)} collective-permute-done((bf16[128,1024]{1,0:T(8,128)(2,1)S(1)}, bf16[128,1024]{1,0:T(8,128)(2,1)S(1)}, u32[]{:S(2)}, u32[]{:S(2)}) %collective-permute-start.20) | collective-permute-done | bytes 262176 | tf_op jit(solution)/shard_map/ppermute | solution.py:256
  75.9 7.8 %collective-permute-done.21.d = bf16[128,1024]{1,0:T(8,128)(2,1)S(1)} collective-permute-done((bf16[128,1024]{1,0:T(8,128)(2,1)S(1)}, bf16[128,1024]{1,0:T(8,128)(2,1)S(1)}, u32[]{:S(2)}, u32[]{:S(2)}) %collective-permute-start.21) | collective-permute-done | bytes 262176 | tf_op jit(solution)/shard_map/ppermute | solution.py:256
  84.9 1.4 %mlp_first.1.part = f32[512,1024]{1,0:T(8,128)S(1)} custom-call(bf16[128,1024]{1,0:T(8,128)(2,1)S(1)} %get-tuple-element.39.a, bf16[128,1024]{1,0:T(8,128)(2,1)S(1)} %collective-permute-done.19.b, bf16[128,1024]{1,0:T(8,128)(2,1)S(1)} %collective-permute-done.20.c, bf16[128,1024]{1,0:T(8,128)(2,1)S(1)} %collective-permute-done.21.d, ...), custom_call_target="tpu_custom_call" | custom-call | flops 1048576 | bytes 2097152 | tf_op jit(solution)/shard_map/mlp_first/pallas_call | solution.py:362
  86.3 2.4 %collective-permute-done.22.weight = bf16[1024,1024]{1,0:T(8,128)(2,1)S(1)} collective-permute-done((bf16[1024,1024]{1,0:T(8,128)(2,1)S(1)}, bf16[1024,1024]{1,0:T(8,128)(2,1)S(1)}, u32[]{:S(2)}, u32[]{:S(2)}) %collective-permute-start.22) | collective-permute-done | bytes 2097184 | tf_op jit(solution)/shard_map/ppermute | solution.py:256
  90.2 2.7 %collective-permute-start.24 = (bf16[128,1024]{1,0:T(8,128)(2,1)S(1)}, bf16[128,1024]{1,0:T(8,128)(2,1)S(1)}, u32[]{:S(2)}, u32[]{:S(2)}) collective-permute-start(bf16[128,1024]{1,0:T(8,128)(2,1)S(1)} %get-tuple-element.47), channel_id=1, source_target_pairs={{2,0},{4,2},{6,4},{0,6},{3,1},{5,3},{7,5},{1,7},{10,8},{12,10},{14... | collective-permute-start | bytes 786440 | tf_op jit(solution)/shard_map/ppermute | solution.py:256
  93.0 11.5 %collective-permute-done.23.a = bf16[128,1024]{1,0:T(8,128)(2,1)S(1)} collective-permute-done((bf16[128,1024]{1,0:T(8,128)(2,1)S(1)}, bf16[128,1024]{1,0:T(8,128)(2,1)S(1)}, u32[]{:S(2)}, u32[]{:S(2)}) %collective-permute-start.23) | collective-permute-done | bytes 262176 | tf_op jit(solution)/shard_map/ppermute | solution.py:256
  (59 shorter events, 17.5 us)
Async XLA Ops:
  1.5 19.5 %all-to-all-start = ((bf16[8,32,512]{2,1,0:T(8,128)(2,1)}), bf16[8,32,512]{2,1,0:T(8,128)(2,1)S(1)}, u32[]{:S(2)}, u32[]{:S(2)}) async-start(bf16[8,32,512]{2,1,0:T(8,128)(2,1)} %pack.1), calls=%async_computation | async-start | bytes 524288 | tf_op jit(solution)/shard_map/all_to_all | solution.py:301
  11.9 15.2 %collective-permute-start = (bf16[128,1024]{1,0:T(8,128)(2,1)S(1)}, bf16[128,1024]{1,0:T(8,128)(2,1)S(1)}, u32[]{:S(2)}, u32[]{:S(2)}) collective-permute-start(bf16[128,1024]{1,0:T(8,128)(2,1)S(1)} %norm.1.refs_0_), channel_id=1, source_target_pairs={{2,0},{4,2},{6,4},{0,6},{3,1},{5,3},{7,5},{1,7},{10,8},{12,10},{14... | collective-permute-start | bytes 786440 | tf_op jit(solution)/shard_map/ppermute | solution.py:256
  14.7 12.4 %collective-permute-start.1 = (bf16[128,1024]{1,0:T(8,128)(2,1)S(1)}, bf16[128,1024]{1,0:T(8,128)(2,1)S(1)}, u32[]{:S(2)}, u32[]{:S(2)}) collective-permute-start(bf16[128,1024]{1,0:T(8,128)(2,1)S(1)} %norm.1.refs_0_), channel_id=1, source_target_pairs={{4,0},{6,2},{0,4},{2,6},{5,1},{7,3},{1,5},{3,7},{12,8},{14,10},{8,... | collective-permute-start | bytes 786440 | tf_op jit(solution)/shard_map/ppermute | solution.py:256
  15.1 15.0 %collective-permute-start.2 = (bf16[128,1024]{1,0:T(8,128)(2,1)S(1)}, bf16[128,1024]{1,0:T(8,128)(2,1)S(1)}, u32[]{:S(2)}, u32[]{:S(2)}) collective-permute-start(bf16[128,1024]{1,0:T(8,128)(2,1)S(1)} %norm.1.refs_0_), channel_id=1, source_target_pairs={{6,0},{0,2},{2,4},{4,6},{7,1},{1,3},{3,5},{5,7},{14,8},{8,10},{10,... | collective-permute-start | bytes 786440 | tf_op jit(solution)/shard_map/ppermute | solution.py:256
  21.0 9.0 %collective-permute-start.3 = (bf16[8,32,512]{2,1,0:T(8,128)(2,1)S(1)}, bf16[8,32,512]{2,1,0:T(8,128)(2,1)S(1)}, u32[]{:S(2)}, u32[]{:S(2)}) collective-permute-start(bf16[8,32,512]{2,1,0:T(8,128)(2,1)S(1)} %all-to-all-done.here), channel_id=1, source_target_pairs={{8,0},{16,8},{24,16},{0,24},{9,1},{17,9},{25,17},{1,25},{10,2},{18... | collective-permute-start | bytes 786440 | tf_op jit(solution)/shard_map/ppermute | solution.py:256
  23.5 6.6 %collective-permute-start.4 = (bf16[8,32,512]{2,1,0:T(8,128)(2,1)S(1)}, bf16[8,32,512]{2,1,0:T(8,128)(2,1)S(1)}, u32[]{:S(2)}, u32[]{:S(2)}) collective-permute-start(bf16[8,32,512]{2,1,0:T(8,128)(2,1)S(1)} %all-to-all-done.here), channel_id=1, source_target_pairs={{24,0},{0,8},{8,16},{16,24},{25,1},{1,9},{9,17},{17,25},{26,2},{2,... | collective-permute-start | bytes 786440 | tf_op jit(solution)/shard_map/ppermute | solution.py:256
  23.5 26.1 %all-to-all-start.1 = ((bf16[8,32,1024]{2,1,0:T(8,128)(2,1)}), bf16[8,32,1024]{2,1,0:T(8,128)(2,1)S(1)}, u32[]{:S(2)}, u32[]{:S(2)}) async-start(bf16[8,32,1024]{2,1,0:T(8,128)(2,1)} %mlp_pack.1), calls=%async_computation.1 | async-start | bytes 1048576 | tf_op jit(solution)/shard_map/all_to_all | solution.py:305
  30.9 15.2 %collective-permute-start.5 = (bf16[2,128,1024]{2,1,0:T(8,128)(2,1)S(1)}, bf16[2,128,1024]{2,1,0:T(8,128)(2,1)S(1)}, u32[]{:S(2)}, u32[]{:S(2)}) collective-permute-start(bf16[2,128,1024]{2,1,0:T(8,128)(2,1)S(1)} %get-tuple-element.31.own_low), channel_id=1, source_target_pairs={{1,0},{0,1},{3,2},{2,3},{5,4},{4,5},{7,6},{6,7},{9,8},{8,9},{11,10... | collective-permute-start | bytes 1572872 | tf_op jit(solution)/shard_map/ppermute | solution.py:256
  34.7 11.4 %collective-permute-start.6 = (bf16[2,128,1024]{2,1,0:T(8,128)(2,1)S(1)}, bf16[2,128,1024]{2,1,0:T(8,128)(2,1)S(1)}, u32[]{:S(2)}, u32[]{:S(2)}) collective-permute-start(bf16[2,128,1024]{2,1,0:T(8,128)(2,1)S(1)} %get-tuple-element.32.own_high), channel_id=1, source_target_pairs={{1,0},{0,1},{3,2},{2,3},{5,4},{4,5},{7,6},{6,7},{9,8},{8,9},{11,10... | collective-permute-start | bytes 1572872 | tf_op jit(solution)/shard_map/ppermute | solution.py:256
  34.8 9.9 %collective-permute-start.9 = (bf16[64,1024]{1,0:T(8,128)(2,1)S(1)}, bf16[64,1024]{1,0:T(8,128)(2,1)S(1)}, u32[]{:S(2)}, u32[]{:S(2)}) collective-permute-start(bf16[64,1024]{1,0:T(8,128)(2,1)S(1)} %get-tuple-element.33), channel_id=1, source_target_pairs={{0,248},{1,9},{2,250},{3,11},{4,252},{5,13},{6,254},{7,15},{8,0},{... | collective-permute-start | bytes 393224 | tf_op jit(solution)/shard_map/ppermute | solution.py:316
  34.8 9.9 %collective-permute-start.7 = (bf16[8,32,256]{2,1,0:T(8,128)(2,1)S(1)}, bf16[8,32,256]{2,1,0:T(8,128)(2,1)S(1)}, u32[]{:S(2)}, u32[]{:S(2)}) collective-permute-start(bf16[8,32,256]{2,1,0:T(8,128)(2,1)S(1)} %slice.28), channel_id=1, source_target_pairs={{8,0},{16,8},{24,16},{0,24},{9,1},{17,9},{25,17},{1,25},{10,2},{18... | collective-permute-start | bytes 393224 | tf_op jit(solution)/shard_map/ppermute | solution.py:256
  37.6 8.1 %collective-permute-start.8 = (bf16[8,32,256]{2,1,0:T(8,128)(2,1)S(1)}, bf16[8,32,256]{2,1,0:T(8,128)(2,1)S(1)}, u32[]{:S(2)}, u32[]{:S(2)}) collective-permute-start(bf16[8,32,256]{2,1,0:T(8,128)(2,1)S(1)} %slice.29), channel_id=1, source_target_pairs={{24,0},{0,8},{8,16},{16,24},{25,1},{1,9},{9,17},{17,25},{26,2},{2,... | collective-permute-start | bytes 393224 | tf_op jit(solution)/shard_map/ppermute | solution.py:256
  49.7 13.4 %collective-permute-start.15 = (bf16[8,32,1024]{2,1,0:T(8,128)(2,1)S(1)}, bf16[8,32,1024]{2,1,0:T(8,128)(2,1)S(1)}, u32[]{:S(2)}, u32[]{:S(2)}) collective-permute-start(bf16[8,32,1024]{2,1,0:T(8,128)(2,1)S(1)} %all-to-all-done.1.refs_0_), channel_id=1, source_target_pairs={{8,0},{16,8},{24,16},{0,24},{9,1},{17,9},{25,17},{1,25},{10,2},{18... | collective-permute-start | bytes 1572872 | tf_op jit(solution)/shard_map/ppermute | solution.py:256
  50.2 14.6 %collective-permute-start.17 = (bf16[8,32,1024]{2,1,0:T(8,128)(2,1)S(1)}, bf16[8,32,1024]{2,1,0:T(8,128)(2,1)S(1)}, u32[]{:S(2)}, u32[]{:S(2)}) collective-permute-start(bf16[8,32,1024]{2,1,0:T(8,128)(2,1)S(1)} %all-to-all-done.1.refs_0_), channel_id=1, source_target_pairs={{24,0},{0,8},{8,16},{16,24},{25,1},{1,9},{9,17},{17,25},{26,2},{2,... | collective-permute-start | bytes 1572872 | tf_op jit(solution)/shard_map/ppermute | solution.py:256
  52.5 12.4 %collective-permute-start.12 = (bf16[128,1024]{1,0:T(8,128)(2,1)S(1)}, bf16[128,1024]{1,0:T(8,128)(2,1)S(1)}, u32[]{:S(2)}, u32[]{:S(2)}) collective-permute-start(bf16[128,1024]{1,0:T(8,128)(2,1)S(1)} %get-tuple-element.51), channel_id=1, source_target_pairs={{6,0},{0,2},{2,4},{4,6},{7,1},{1,3},{3,5},{5,7},{14,8},{8,10},{10,... | collective-permute-start | bytes 786440 | tf_op jit(solution)/shard_map/ppermute | solution.py:256
  53.9 11.0 %collective-permute-start.13 = (bf16[128,1024]{1,0:T(8,128)(2,1)S(1)}, bf16[128,1024]{1,0:T(8,128)(2,1)S(1)}, u32[]{:S(2)}, u32[]{:S(2)}) collective-permute-start(bf16[128,1024]{1,0:T(8,128)(2,1)S(1)} %get-tuple-element.50), channel_id=1, source_target_pairs={{2,0},{4,2},{6,4},{0,6},{3,1},{5,3},{7,5},{1,7},{10,8},{12,10},{14... | collective-permute-start | bytes 786440 | tf_op jit(solution)/shard_map/ppermute | solution.py:256
  55.4 12.3 %collective-permute-start.14 = (bf16[128,1024]{1,0:T(8,128)(2,1)S(1)}, bf16[128,1024]{1,0:T(8,128)(2,1)S(1)}, u32[]{:S(2)}, u32[]{:S(2)}) collective-permute-start(bf16[128,1024]{1,0:T(8,128)(2,1)S(1)} %get-tuple-element.49), channel_id=1, source_target_pairs={{4,0},{6,2},{0,4},{2,6},{5,1},{7,3},{1,5},{3,7},{12,8},{14,10},{8,... | collective-permute-start | bytes 786440 | tf_op jit(solution)/shard_map/ppermute | solution.py:256
  63.1 7.3 %collective-permute-start.16 = (bf16[8,32,512]{2,1,0:T(8,128)(2,1)S(1)}, bf16[8,32,512]{2,1,0:T(8,128)(2,1)S(1)}, u32[]{:S(2)}, u32[]{:S(2)}) collective-permute-start(bf16[8,32,512]{2,1,0:T(8,128)(2,1)S(1)} %slice.30), channel_id=1, source_target_pairs={{8,0},{16,8},{24,16},{0,24},{9,1},{17,9},{25,17},{1,25},{10,2},{18... | collective-permute-start | bytes 786440 | tf_op jit(solution)/shard_map/ppermute | solution.py:256
  64.8 7.7 %collective-permute-start.18 = (bf16[8,32,512]{2,1,0:T(8,128)(2,1)S(1)}, bf16[8,32,512]{2,1,0:T(8,128)(2,1)S(1)}, u32[]{:S(2)}, u32[]{:S(2)}) collective-permute-start(bf16[8,32,512]{2,1,0:T(8,128)(2,1)S(1)} %slice.31), channel_id=1, source_target_pairs={{24,0},{0,8},{8,16},{16,24},{25,1},{1,9},{9,17},{17,25},{26,2},{2,... | collective-permute-start | bytes 786440 | tf_op jit(solution)/shard_map/ppermute | solution.py:256
  69.1 6.8 %collective-permute-start.20 = (bf16[128,1024]{1,0:T(8,128)(2,1)S(1)}, bf16[128,1024]{1,0:T(8,128)(2,1)S(1)}, u32[]{:S(2)}, u32[]{:S(2)}) collective-permute-start(bf16[128,1024]{1,0:T(8,128)(2,1)S(1)} %get-tuple-element.39.a), channel_id=1, source_target_pairs={{4,0},{6,2},{0,4},{2,6},{5,1},{7,3},{1,5},{3,7},{12,8},{14,10},{8,... | collective-permute-start | bytes 786440 | tf_op jit(solution)/shard_map/ppermute | solution.py:256
  70.5 13.2 %collective-permute-start.21 = (bf16[128,1024]{1,0:T(8,128)(2,1)S(1)}, bf16[128,1024]{1,0:T(8,128)(2,1)S(1)}, u32[]{:S(2)}, u32[]{:S(2)}) collective-permute-start(bf16[128,1024]{1,0:T(8,128)(2,1)S(1)} %get-tuple-element.39.a), channel_id=1, source_target_pairs={{6,0},{0,2},{2,4},{4,6},{7,1},{1,3},{3,5},{5,7},{14,8},{8,10},{10,... | collective-permute-start | bytes 786440 | tf_op jit(solution)/shard_map/ppermute | solution.py:256
  90.1 14.4 %collective-permute-start.23 = (bf16[128,1024]{1,0:T(8,128)(2,1)S(1)}, bf16[128,1024]{1,0:T(8,128)(2,1)S(1)}, u32[]{:S(2)}, u32[]{:S(2)}) collective-permute-start(bf16[128,1024]{1,0:T(8,128)(2,1)S(1)} %get-tuple-element.46), channel_id=1, source_target_pairs={{6,0},{0,2},{2,4},{4,6},{7,1},{1,3},{3,5},{5,7},{14,8},{8,10},{10,... | collective-permute-start | bytes 786440 | tf_op jit(solution)/shard_map/ppermute | solution.py:256
  90.2 14.3 %collective-permute-start.24 = (bf16[128,1024]{1,0:T(8,128)(2,1)S(1)}, bf16[128,1024]{1,0:T(8,128)(2,1)S(1)}, u32[]{:S(2)}, u32[]{:S(2)}) collective-permute-start(bf16[128,1024]{1,0:T(8,128)(2,1)S(1)} %get-tuple-element.47), channel_id=1, source_target_pairs={{2,0},{4,2},{6,4},{0,6},{3,1},{5,3},{7,5},{1,7},{10,8},{12,10},{14... | collective-permute-start | bytes 786440 | tf_op jit(solution)/shard_map/ppermute | solution.py:256
  92.9 11.7 %collective-permute-start.25 = (bf16[128,1024]{1,0:T(8,128)(2,1)S(1)}, bf16[128,1024]{1,0:T(8,128)(2,1)S(1)}, u32[]{:S(2)}, u32[]{:S(2)}) collective-permute-start(bf16[128,1024]{1,0:T(8,128)(2,1)S(1)} %get-tuple-element.48), channel_id=1, source_target_pairs={{4,0},{6,2},{0,4},{2,6},{5,1},{7,3},{1,5},{3,7},{12,8},{14,10},{8,... | collective-permute-start | bytes 786440 | tf_op jit(solution)/shard_map/ppermute | solution.py:256
  (9 other events, 184.7 us)

commit v9 on v8

--- a/solution.py
+++ b/solution.py
@@ -218,17 +218,22 @@
     return lax.dot_general(hidden, weight[:, 512:], NT, preferred_element_type=F32)
 
 
-def mlp_first_kernel(a, b, c, d, weight, out):
-    rows = jnp.concatenate([a[...], b[...], c[...], d[...]], axis=0)
+def mlp_first_kernel(a, b, c, weight, out):
+    rows = jnp.concatenate([a[...], b[...], c[...]], axis=0)
     out[...] = hidden_share(rows, weight)
 
 
-def mlp_second_kernel(a, b, c, d, weight, part, mine, to_b, to_c, to_d):
-    rows = jnp.concatenate([a[...], b[...], c[...], d[...]], axis=0)
+def mlp_second_kernel(a, b, c, weight, part, mine, to_b, to_c):
+    rows = jnp.concatenate([a[...], b[...], c[...]], axis=0)
     total = part[...] + hidden_share(rows, weight)
     mine[...] = total[:128]
-    for i, out in enumerate((to_b, to_c, to_d)):
-        out[...] = total[i * 128 + 128 : i * 128 + 256].astype(BF16)
+    to_b[...] = total[128:256].astype(BF16)
+    to_c[...] = total[256:].astype(BF16)
+
+
+def mlp_far_kernel(low, high, weight, other, out):
+    rows = jnp.concatenate([low[...], high[...]], axis=0)
+    out[...] = (hidden_share(rows, weight) + hidden_share(rows, other)).astype(BF16)
 
 
 def end_kernel(middle, mine, a, b, c, out):
@@ -353,23 +358,29 @@
         "middle",
     )(tokens, mine_attended, *parts, norm2_gain.reshape(1, 1024))
 
-    far = {k: fetch(normed_two, "y", k) for k in (1, 3, 2)}
+    near = {k: fetch(normed_two, "y", k) for k in (1, 3)}
     (mlp_own,) = call(lay_kernel, [((1024, 1024), BF16)], [SMEM] + [VMEM] * 5, "mlp_lay")(
         at, *mlp_weights
     )
-    mlp_own, far = lax.optimization_barrier((mlp_own, far))
+    mlp_own, near = lax.optimization_barrier((mlp_own, near))
+    low, high = fetch(near[1][:64], "y", 1), fetch(near[3][64:], "y", 3)
     mlp_peer = fetch(mlp_own, "core", 1)
-    (part,) = call(mlp_first_kernel, [((512, 1024), F32)], [VMEM] * 5, "mlp_first", mib=16)(
-        normed_two, far[1], far[2], far[3], mlp_own
-    )
-    mine, *away = call(
+    (part,) = call(mlp_first_kernel, [((384, 1024), F32)], [VMEM] * 4, "mlp_first", mib=16)(
+        normed_two, near[1], near[3], mlp_own
+    )
+    mine, to_right, to_left = call(
         mlp_second_kernel,
-        [((128, 1024), F32)] + [((128, 1024), BF16)] * 3,
-        [VMEM] * 6,
+        [((128, 1024), F32)] + [((128, 1024), BF16)] * 2,
+        [VMEM] * 5,
         "mlp_second",
         mib=16,
-    )(normed_two, far[1], far[2], far[3], mlp_peer, part)
-    parts = [fetch(away[k - 1], "y", 4 - k) for k in (1, 3, 2)]
+    )(normed_two, near[1], near[3], mlp_peer, part)
+    parts = [fetch(to_right, "y", 3), fetch(to_left, "y", 1)]
+    (low, high), mine = lax.optimization_barrier(((low, high), mine))
+    (to_far,) = call(mlp_far_kernel, [((128, 1024), BF16)], [VMEM] * 4, "mlp_far", mib=16)(
+        low, high, mlp_own, mlp_peer
+    )
+    parts.append(fetch(to_far, "y", 2))
     (out,) = call(end_kernel, [((128, 1024), BF16)], [VMEM] * 5, "end")(middle, mine, *parts)
     return out
 

time: 106 us -> 104 us (0.981)
  waiting for transfers between devices: 50.5 us -> 44 us
  starting transfers between devices: 40.3 us -> 44 us
    ppermute x25 -> x26, waiting for transfers between devices: 39.8 us -> 33.2 us  [fetch(): return lax.ppermute(value, axis, [((i + step) % n, i) for i in range(n)])]
    ppermute x25 -> x26, starting transfers between devices: 27.6 us -> 31.3 us  [fetch(): return lax.ppermute(value, axis, [((i + step) % n, i) for i in range(n)])]
    pallas_call x2 -> x3, Pallas kernels: 2.76 us -> 3.52 us  [the longest x1 1.21 us: local(): call(mlp_far_kernel, [((128, 1024), BF16)], [VMEM] * 4, 'mlp_far', mib=16)]
  transfers between devices with their start and end apart: 28 -> 29, of which waited for: 14 -> 17; matrix products, arithmetic and copies ran while one was open for 0% -> 0% of each run, Pallas kernels for 10% -> 11%
where the time goes in v9:
time: 104 us; the launch traced here: 103 us
  starting transfers between devices  44 us (42%)
  waiting for transfers between devices  44 us (42%)
  Pallas kernels  14.9 us (14%)
    ppermute x26, waiting for transfers between devices, fetch(): return lax.ppermute(value, axis, [((i + step) % n, i) for i in range(n)])  33.2 us
    ppermute x26, starting transfers between devices, fetch(): return lax.ppermute(value, axis, [((i + step) % n, i) for i in range(n)])  31.3 us
    all_to_all x1, starting transfers between devices, local(): front = lax.all_to_all(front, 'z', 0, 0, tiled=True)  9.16 us
    ppermute x1, waiting for transfers between devices, local(): lax.ppermute(border, ('z', 'x', 'y', 'core'), [(spot(*divmod(s, 4), j, c)...  7.08 us
    pallas_call x3, Pallas kernels, from_hbm(): call(kernel, outs, [HBM] * len(given), name, scratch=[pltpu.VMEM(v.shape,...  4.29 us
    all_to_all x1, waiting for transfers between devices, local(): front = lax.all_to_all(front, 'z', 0, 0, tiled=True)  3.69 us
    all_to_all x1, starting transfers between devices, local(): back = lax.all_to_all(back, 'z', 0, 0, tiled=True)  3.49 us
    pallas_call x1, Pallas kernels, local(): call(attention_kernel, [((512, 128), BF16), ((1536, 128), BF16)], [SMEM]...  3.32 us
  transfers between devices with their start and end apart: 29, of which 17 were waited for; matrix products, arithmetic and copies ran while one was open for 0% of the time, Pallas kernels for 11%

profile of v9, /device:TPU:1, one launch (start us, length us, event | category | flops | bytes accessed | tf_op | source)
XLA Modules:
  0.0 103.3 jit_solution(3913962892598736415)
XLA Ops:
  0.0 1.5 %pack.1 = bf16[8,32,512]{2,1,0:T(8,128)(2,1)} custom-call(bf16[3,32,128]{2,1,0:T(8,128)(2,1)} %bitcast.21, bf16[32,128]{1,0:T(8,128)(2,1)} %bitcast.22), custom_call_target="tpu_custom_call" | custom-call | flops 1048576 | bytes 2097152 | tf_op jit(solution)/shard_map/pack/pallas_call | solution.py:76
  1.5 9.2 %all-to-all-start = ((bf16[8,32,512]{2,1,0:T(8,128)(2,1)}), bf16[8,32,512]{2,1,0:T(8,128)(2,1)S(1)}, u32[]{:S(2)}, u32[]{:S(2)}) async-start(bf16[8,32,512]{2,1,0:T(8,128)(2,1)} %pack.1), calls=%async_computation | async-start | bytes 524288 | tf_op jit(solution)/shard_map/all_to_all | solution.py:306
  11.9 2.8 %collective-permute-start = (bf16[128,1024]{1,0:T(8,128)(2,1)S(1)}, bf16[128,1024]{1,0:T(8,128)(2,1)S(1)}, u32[]{:S(2)}, u32[]{:S(2)}) collective-permute-start(bf16[128,1024]{1,0:T(8,128)(2,1)S(1)} %norm.1.refs_0_), channel_id=1, source_target_pairs={{2,0},{4,2},{6,4},{0,6},{3,1},{5,3},{7,5},{1,7},{10,8},{12,10},{14... | collective-permute-start | bytes 786440 | tf_op jit(solution)/shard_map/ppermute | solution.py:261
  15.7 1.6 %mlp_pack.1 = bf16[8,32,1024]{2,1,0:T(8,128)(2,1)} custom-call(bf16[32,512]{1,0:T(8,128)(2,1)} %refs_0_.3, bf16[32,512]{1,0:T(8,128)(2,1)} %bitcast.20), custom_call_target="tpu_custom_call" | custom-call | flops 1048576 | bytes 2097152 | tf_op jit(solution)/shard_map/mlp_pack/pallas_call | solution.py:76
  17.4 3.7 %all-to-all-done.here = bf16[8,32,512]{2,1,0:T(8,128)(2,1)S(1)} async-done(((bf16[8,32,512]{2,1,0:T(8,128)(2,1)}), bf16[8,32,512]{2,1,0:T(8,128)(2,1)S(1)}, u32[]{:S(2)}, u32[]{:S(2)}) %all-to-all-start) | async-done | bytes 262176 | tf_op jit(solution)/shard_map/all_to_all | solution.py:306
  21.0 2.5 %collective-permute-start.3 = (bf16[8,32,512]{2,1,0:T(8,128)(2,1)S(1)}, bf16[8,32,512]{2,1,0:T(8,128)(2,1)S(1)}, u32[]{:S(2)}, u32[]{:S(2)}) collective-permute-start(bf16[8,32,512]{2,1,0:T(8,128)(2,1)S(1)} %all-to-all-done.here), channel_id=1, source_target_pairs={{8,0},{16,8},{24,16},{0,24},{9,1},{17,9},{25,17},{1,25},{10,2},{18... | collective-permute-start | bytes 786440 | tf_op jit(solution)/shard_map/ppermute | solution.py:261
  23.5 3.5 %all-to-all-start.1 = ((bf16[8,32,1024]{2,1,0:T(8,128)(2,1)}), bf16[8,32,1024]{2,1,0:T(8,128)(2,1)S(1)}, u32[]{:S(2)}, u32[]{:S(2)}) async-start(bf16[8,32,1024]{2,1,0:T(8,128)(2,1)} %mlp_pack.1), calls=%async_computation.1 | async-start | bytes 1048576 | tf_op jit(solution)/shard_map/all_to_all | solution.py:310
  27.1 2.9 %collective-permute-done.2.refs_3_ = bf16[128,1024]{1,0:T(8,128)(2,1)S(1)} collective-permute-done((bf16[128,1024]{1,0:T(8,128)(2,1)S(1)}, bf16[128,1024]{1,0:T(8,128)(2,1)S(1)}, u32[]{:S(2)}, u32[]{:S(2)}) %collective-permute-start.2) | collective-permute-done | bytes 262176 | tf_op jit(solution)/shard_map/ppermute | solution.py:261
  30.9 3.8 %collective-permute-start.5 = (bf16[2,128,1024]{2,1,0:T(8,128)(2,1)S(1)}, bf16[2,128,1024]{2,1,0:T(8,128)(2,1)S(1)}, u32[]{:S(2)}, u32[]{:S(2)}) collective-permute-start(bf16[2,128,1024]{2,1,0:T(8,128)(2,1)S(1)} %get-tuple-element.32.own_low), channel_id=1, source_target_pairs={{1,0},{0,1},{3,2},{2,3},{5,4},{4,5},{7,6},{6,7},{9,8},{8,9},{11,10... | collective-permute-start | bytes 1572872 | tf_op jit(solution)/shard_map/ppermute | solution.py:261
  34.8 2.8 %collective-permute-start.7 = (bf16[8,32,256]{2,1,0:T(8,128)(2,1)S(1)}, bf16[8,32,256]{2,1,0:T(8,128)(2,1)S(1)}, u32[]{:S(2)}, u32[]{:S(2)}) collective-permute-start(bf16[8,32,256]{2,1,0:T(8,128)(2,1)S(1)} %slice.36), channel_id=1, source_target_pairs={{8,0},{16,8},{24,16},{0,24},{9,1},{17,9},{25,17},{1,25},{10,2},{18... | collective-permute-start | bytes 393224 | tf_op jit(solution)/shard_map/ppermute | solution.py:261
  37.6 7.1 %collective-permute-done.9.near_own = bf16[64,1024]{1,0:T(8,128)(2,1)S(1)} collective-permute-done((bf16[64,1024]{1,0:T(8,128)(2,1)S(1)}, bf16[64,1024]{1,0:T(8,128)(2,1)S(1)}, u32[]{:S(2)}, u32[]{:S(2)}) %collective-permute-start.9) | collective-permute-done | bytes 131104 | tf_op jit(solution)/shard_map/ppermute | solution.py:321
  46.1 3.3 %attention.1 = (bf16[512,128]{1,0:T(8,128)(2,1)S(1)}, bf16[1536,128]{1,0:T(8,128)(2,1)S(1)}) custom-call(s32[4]{0:T(128)S(1)} %pad_add_fusion.at, bf16[2,128,1024]{2,1,0:T(8,128)(2,1)S(1)} %get-tuple-element.32.own_low, bf16[2,128,1024]{2,1,0:T(8,128)(2,1)S(1)} %get-tuple-element.33.own_high, bf16[2,128,1024]{2,1,0:T(8,128)(2,1)S(1)} %collective-permute-done.5.peer_low, ...), custom_call_target="tpu_custom_call" | custom-call | flops 1048576 | bytes 2097152 | tf_op jit(solution)/shard_map/attention/pallas_call | solution.py:332
  52.5 1.4 %collective-permute-start.12 = (bf16[128,1024]{1,0:T(8,128)(2,1)S(1)}, bf16[128,1024]{1,0:T(8,128)(2,1)S(1)}, u32[]{:S(2)}, u32[]{:S(2)}) collective-permute-start(bf16[128,1024]{1,0:T(8,128)(2,1)S(1)} %get-tuple-element.53), channel_id=1, source_target_pairs={{6,0},{0,2},{2,4},{4,6},{7,1},{1,3},{3,5},{5,7},{14,8},{8,10},{10,... | collective-permute-start | bytes 786440 | tf_op jit(solution)/shard_map/ppermute | solution.py:261
  53.9 1.5 %collective-permute-start.13 = (bf16[128,1024]{1,0:T(8,128)(2,1)S(1)}, bf16[128,1024]{1,0:T(8,128)(2,1)S(1)}, u32[]{:S(2)}, u32[]{:S(2)}) collective-permute-start(bf16[128,1024]{1,0:T(8,128)(2,1)S(1)} %get-tuple-element.52), channel_id=1, source_target_pairs={{2,0},{4,2},{6,4},{0,6},{3,1},{5,3},{7,5},{1,7},{10,8},{12,10},{14... | collective-permute-start | bytes 786440 | tf_op jit(solution)/shard_map/ppermute | solution.py:261
  55.4 1.6 %collective-permute-start.14 = (bf16[128,1024]{1,0:T(8,128)(2,1)S(1)}, bf16[128,1024]{1,0:T(8,128)(2,1)S(1)}, u32[]{:S(2)}, u32[]{:S(2)}) collective-permute-start(bf16[128,1024]{1,0:T(8,128)(2,1)S(1)} %get-tuple-element.51), channel_id=1, source_target_pairs={{4,0},{6,2},{0,4},{2,6},{5,1},{7,3},{1,5},{3,7},{12,8},{14,10},{8,... | collective-permute-start | bytes 786440 | tf_op jit(solution)/shard_map/ppermute | solution.py:261
  56.9 6.2 %collective-permute-done.15.refs_1_ = bf16[8,32,1024]{2,1,0:T(8,128)(2,1)S(1)} collective-permute-done((bf16[8,32,1024]{2,1,0:T(8,128)(2,1)S(1)}, bf16[8,32,1024]{2,1,0:T(8,128)(2,1)S(1)}, u32[]{:S(2)}, u32[]{:S(2)}) %collective-permute-start.15) | collective-permute-done | bytes 524320 | tf_op jit(solution)/shard_map/ppermute | solution.py:261
  63.1 1.6 %collective-permute-start.16 = (bf16[8,32,512]{2,1,0:T(8,128)(2,1)S(1)}, bf16[8,32,512]{2,1,0:T(8,128)(2,1)S(1)}, u32[]{:S(2)}, u32[]{:S(2)}) collective-permute-start(bf16[8,32,512]{2,1,0:T(8,128)(2,1)S(1)} %slice.38), channel_id=1, source_target_pairs={{8,0},{16,8},{24,16},{0,24},{9,1},{17,9},{25,17},{1,25},{10,2},{18... | collective-permute-start | bytes 786440 | tf_op jit(solution)/shard_map/ppermute | solution.py:261
  64.9 2.8 %collective-permute-done.14.c = bf16[128,1024]{1,0:T(8,128)(2,1)S(1)} collective-permute-done((bf16[128,1024]{1,0:T(8,128)(2,1)S(1)}, bf16[128,1024]{1,0:T(8,128)(2,1)S(1)}, u32[]{:S(2)}, u32[]{:S(2)}) %collective-permute-start.14) | collective-permute-done | bytes 262176 | tf_op jit(solution)/shard_map/ppermute | solution.py:261
  70.0 2.5 %collective-permute-done.18.refs_3_ = bf16[8,32,512]{2,1,0:T(8,128)(2,1)S(1)} collective-permute-done((bf16[8,32,512]{2,1,0:T(8,128)(2,1)S(1)}, bf16[8,32,512]{2,1,0:T(8,128)(2,1)S(1)}, u32[]{:S(2)}, u32[]{:S(2)}) %collective-permute-start.18) | collective-permute-done | bytes 262176 | tf_op jit(solution)/shard_map/ppermute | solution.py:261
  75.5 3.7 %collective-permute-start.23 = (bf16[1024,1024]{1,0:T(8,128)(2,1)S(1)}, bf16[1024,1024]{1,0:T(8,128)(2,1)S(1)}, u32[]{:S(2)}, u32[]{:S(2)}) collective-permute-start(bf16[1024,1024]{1,0:T(8,128)(2,1)S(1)} %mlp_lay.1.weight), channel_id=1, source_target_pairs={{1,0},{0,1},{3,2},{2,3},{5,4},{4,5},{7,6},{6,7},{9,8},{8,9},{11,10... | collective-permute-start | bytes 6291464 | tf_op jit(solution)/shard_map/ppermute | solution.py:261
  79.4 1.5 %collective-permute-start.22 = (bf16[64,1024]{1,0:T(8,128)(2,1)S(1)}, bf16[64,1024]{1,0:T(8,128)(2,1)S(1)}, u32[]{:S(2)}, u32[]{:S(2)}) collective-permute-start(bf16[64,1024]{1,0:T(8,128)(2,1)S(1)} %slice.35), channel_id=1, source_target_pairs={{6,0},{0,2},{2,4},{4,6},{7,1},{1,3},{3,5},{5,7},{14,8},{8,10},{10,... | collective-permute-start | bytes 393224 | tf_op jit(solution)/shard_map/ppermute | solution.py:261
  87.8 2.6 %collective-permute-start.25 = (bf16[128,1024]{1,0:T(8,128)(2,1)S(1)}, bf16[128,1024]{1,0:T(8,128)(2,1)S(1)}, u32[]{:S(2)}, u32[]{:S(2)}) collective-permute-start(bf16[128,1024]{1,0:T(8,128)(2,1)S(1)} %get-tuple-element.48), channel_id=1, source_target_pairs={{2,0},{4,2},{6,4},{0,6},{3,1},{5,3},{7,5},{1,7},{10,8},{12,10},{14... | collective-permute-start | bytes 786440 | tf_op jit(solution)/shard_map/ppermute | solution.py:261
  90.4 5.3 %collective-permute-done.26.c = bf16[128,1024]{1,0:T(8,128)(2,1)S(1)} collective-permute-done((bf16[128,1024]{1,0:T(8,128)(2,1)S(1)}, bf16[128,1024]{1,0:T(8,128)(2,1)S(1)}, u32[]{:S(2)}, u32[]{:S(2)}) %collective-permute-start.26) | collective-permute-done | bytes 262176 | tf_op jit(solution)/shard_map/ppermute | solution.py:261
  95.6 6.8 %collective-permute-done.24.a = bf16[128,1024]{1,0:T(8,128)(2,1)S(1)} collective-permute-done((bf16[128,1024]{1,0:T(8,128)(2,1)S(1)}, bf16[128,1024]{1,0:T(8,128)(2,1)S(1)}, u32[]{:S(2)}, u32[]{:S(2)}) %collective-permute-start.24) | collective-permute-done | bytes 262176 | tf_op jit(solution)/shard_map/ppermute | solution.py:261
  (64 shorter events, 21.0 us)
Async XLA Ops:
  1.5 19.5 %all-to-all-start = ((bf16[8,32,512]{2,1,0:T(8,128)(2,1)}), bf16[8,32,512]{2,1,0:T(8,128)(2,1)S(1)}, u32[]{:S(2)}, u32[]{:S(2)}) async-start(bf16[8,32,512]{2,1,0:T(8,128)(2,1)} %pack.1), calls=%async_computation | async-start | bytes 524288 | tf_op jit(solution)/shard_map/all_to_all | solution.py:306
  11.9 15.2 %collective-permute-start = (bf16[128,1024]{1,0:T(8,128)(2,1)S(1)}, bf16[128,1024]{1,0:T(8,128)(2,1)S(1)}, u32[]{:S(2)}, u32[]{:S(2)}) collective-permute-start(bf16[128,1024]{1,0:T(8,128)(2,1)S(1)} %norm.1.refs_0_), channel_id=1, source_target_pairs={{2,0},{4,2},{6,4},{0,6},{3,1},{5,3},{7,5},{1,7},{10,8},{12,10},{14... | collective-permute-start | bytes 786440 | tf_op jit(solution)/shard_map/ppermute | solution.py:261
  14.7 12.4 %collective-permute-start.1 = (bf16[128,1024]{1,0:T(8,128)(2,1)S(1)}, bf16[128,1024]{1,0:T(8,128)(2,1)S(1)}, u32[]{:S(2)}, u32[]{:S(2)}) collective-permute-start(bf16[128,1024]{1,0:T(8,128)(2,1)S(1)} %norm.1.refs_0_), channel_id=1, source_target_pairs={{4,0},{6,2},{0,4},{2,6},{5,1},{7,3},{1,5},{3,7},{12,8},{14,10},{8,... | collective-permute-start | bytes 786440 | tf_op jit(solution)/shard_map/ppermute | solution.py:261
  15.1 15.0 %collective-permute-start.2 = (bf16[128,1024]{1,0:T(8,128)(2,1)S(1)}, bf16[128,1024]{1,0:T(8,128)(2,1)S(1)}, u32[]{:S(2)}, u32[]{:S(2)}) collective-permute-start(bf16[128,1024]{1,0:T(8,128)(2,1)S(1)} %norm.1.refs_0_), channel_id=1, source_target_pairs={{6,0},{0,2},{2,4},{4,6},{7,1},{1,3},{3,5},{5,7},{14,8},{8,10},{10,... | collective-permute-start | bytes 786440 | tf_op jit(solution)/shard_map/ppermute | solution.py:261
  21.0 9.0 %collective-permute-start.3 = (bf16[8,32,512]{2,1,0:T(8,128)(2,1)S(1)}, bf16[8,32,512]{2,1,0:T(8,128)(2,1)S(1)}, u32[]{:S(2)}, u32[]{:S(2)}) collective-permute-start(bf16[8,32,512]{2,1,0:T(8,128)(2,1)S(1)} %all-to-all-done.here), channel_id=1, source_target_pairs={{8,0},{16,8},{24,16},{0,24},{9,1},{17,9},{25,17},{1,25},{10,2},{18... | collective-permute-start | bytes 786440 | tf_op jit(solution)/shard_map/ppermute | solution.py:261
  23.5 6.6 %collective-permute-start.4 = (bf16[8,32,512]{2,1,0:T(8,128)(2,1)S(1)}, bf16[8,32,512]{2,1,0:T(8,128)(2,1)S(1)}, u32[]{:S(2)}, u32[]{:S(2)}) collective-permute-start(bf16[8,32,512]{2,1,0:T(8,128)(2,1)S(1)} %all-to-all-done.here), channel_id=1, source_target_pairs={{24,0},{0,8},{8,16},{16,24},{25,1},{1,9},{9,17},{17,25},{26,2},{2,... | collective-permute-start | bytes 786440 | tf_op jit(solution)/shard_map/ppermute | solution.py:261
  23.5 26.1 %all-to-all-start.1 = ((bf16[8,32,1024]{2,1,0:T(8,128)(2,1)}), bf16[8,32,1024]{2,1,0:T(8,128)(2,1)S(1)}, u32[]{:S(2)}, u32[]{:S(2)}) async-start(bf16[8,32,1024]{2,1,0:T(8,128)(2,1)} %mlp_pack.1), calls=%async_computation.1 | async-start | bytes 1048576 | tf_op jit(solution)/shard_map/all_to_all | solution.py:310
  30.9 15.2 %collective-permute-start.5 = (bf16[2,128,1024]{2,1,0:T(8,128)(2,1)S(1)}, bf16[2,128,1024]{2,1,0:T(8,128)(2,1)S(1)}, u32[]{:S(2)}, u32[]{:S(2)}) collective-permute-start(bf16[2,128,1024]{2,1,0:T(8,128)(2,1)S(1)} %get-tuple-element.32.own_low), channel_id=1, source_target_pairs={{1,0},{0,1},{3,2},{2,3},{5,4},{4,5},{7,6},{6,7},{9,8},{8,9},{11,10... | collective-permute-start | bytes 1572872 | tf_op jit(solution)/shard_map/ppermute | solution.py:261
  34.7 11.4 %collective-permute-start.6 = (bf16[2,128,1024]{2,1,0:T(8,128)(2,1)S(1)}, bf16[2,128,1024]{2,1,0:T(8,128)(2,1)S(1)}, u32[]{:S(2)}, u32[]{:S(2)}) collective-permute-start(bf16[2,128,1024]{2,1,0:T(8,128)(2,1)S(1)} %get-tuple-element.33.own_high), channel_id=1, source_target_pairs={{1,0},{0,1},{3,2},{2,3},{5,4},{4,5},{7,6},{6,7},{9,8},{8,9},{11,10... | collective-permute-start | bytes 1572872 | tf_op jit(solution)/shard_map/ppermute | solution.py:261
  34.8 9.9 %collective-permute-start.9 = (bf16[64,1024]{1,0:T(8,128)(2,1)S(1)}, bf16[64,1024]{1,0:T(8,128)(2,1)S(1)}, u32[]{:S(2)}, u32[]{:S(2)}) collective-permute-start(bf16[64,1024]{1,0:T(8,128)(2,1)S(1)} %get-tuple-element.34), channel_id=1, source_target_pairs={{0,248},{1,9},{2,250},{3,11},{4,252},{5,13},{6,254},{7,15},{8,0},{... | collective-permute-start | bytes 393224 | tf_op jit(solution)/shard_map/ppermute | solution.py:321
  34.8 9.9 %collective-permute-start.7 = (bf16[8,32,256]{2,1,0:T(8,128)(2,1)S(1)}, bf16[8,32,256]{2,1,0:T(8,128)(2,1)S(1)}, u32[]{:S(2)}, u32[]{:S(2)}) collective-permute-start(bf16[8,32,256]{2,1,0:T(8,128)(2,1)S(1)} %slice.36), channel_id=1, source_target_pairs={{8,0},{16,8},{24,16},{0,24},{9,1},{17,9},{25,17},{1,25},{10,2},{18... | collective-permute-start | bytes 393224 | tf_op jit(solution)/shard_map/ppermute | solution.py:261
  37.6 8.1 %collective-permute-start.8 = (bf16[8,32,256]{2,1,0:T(8,128)(2,1)S(1)}, bf16[8,32,256]{2,1,0:T(8,128)(2,1)S(1)}, u32[]{:S(2)}, u32[]{:S(2)}) collective-permute-start(bf16[8,32,256]{2,1,0:T(8,128)(2,1)S(1)} %slice.37), channel_id=1, source_target_pairs={{24,0},{0,8},{8,16},{16,24},{25,1},{1,9},{9,17},{17,25},{26,2},{2,... | collective-permute-start | bytes 393224 | tf_op jit(solution)/shard_map/ppermute | solution.py:261
  49.7 13.4 %collective-permute-start.15 = (bf16[8,32,1024]{2,1,0:T(8,128)(2,1)S(1)}, bf16[8,32,1024]{2,1,0:T(8,128)(2,1)S(1)}, u32[]{:S(2)}, u32[]{:S(2)}) collective-permute-start(bf16[8,32,1024]{2,1,0:T(8,128)(2,1)S(1)} %all-to-all-done.1.refs_0_), channel_id=1, source_target_pairs={{8,0},{16,8},{24,16},{0,24},{9,1},{17,9},{25,17},{1,25},{10,2},{18... | collective-permute-start | bytes 1572872 | tf_op jit(solution)/shard_map/ppermute | solution.py:261
  50.2 14.6 %collective-permute-start.17 = (bf16[8,32,1024]{2,1,0:T(8,128)(2,1)S(1)}, bf16[8,32,1024]{2,1,0:T(8,128)(2,1)S(1)}, u32[]{:S(2)}, u32[]{:S(2)}) collective-permute-start(bf16[8,32,1024]{2,1,0:T(8,128)(2,1)S(1)} %all-to-all-done.1.refs_0_), channel_id=1, source_target_pairs={{24,0},{0,8},{8,16},{16,24},{25,1},{1,9},{9,17},{17,25},{26,2},{2,... | collective-permute-start | bytes 1572872 | tf_op jit(solution)/shard_map/ppermute | solution.py:261
  52.5 12.4 %collective-permute-start.12 = (bf16[128,1024]{1,0:T(8,128)(2,1)S(1)}, bf16[128,1024]{1,0:T(8,128)(2,1)S(1)}, u32[]{:S(2)}, u32[]{:S(2)}) collective-permute-start(bf16[128,1024]{1,0:T(8,128)(2,1)S(1)} %get-tuple-element.53), channel_id=1, source_target_pairs={{6,0},{0,2},{2,4},{4,6},{7,1},{1,3},{3,5},{5,7},{14,8},{8,10},{10,... | collective-permute-start | bytes 786440 | tf_op jit(solution)/shard_map/ppermute | solution.py:261
  53.9 11.0 %collective-permute-start.13 = (bf16[128,1024]{1,0:T(8,128)(2,1)S(1)}, bf16[128,1024]{1,0:T(8,128)(2,1)S(1)}, u32[]{:S(2)}, u32[]{:S(2)}) collective-permute-start(bf16[128,1024]{1,0:T(8,128)(2,1)S(1)} %get-tuple-element.52), channel_id=1, source_target_pairs={{2,0},{4,2},{6,4},{0,6},{3,1},{5,3},{7,5},{1,7},{10,8},{12,10},{14... | collective-permute-start | bytes 786440 | tf_op jit(solution)/shard_map/ppermute | solution.py:261
  55.4 12.3 %collective-permute-start.14 = (bf16[128,1024]{1,0:T(8,128)(2,1)S(1)}, bf16[128,1024]{1,0:T(8,128)(2,1)S(1)}, u32[]{:S(2)}, u32[]{:S(2)}) collective-permute-start(bf16[128,1024]{1,0:T(8,128)(2,1)S(1)} %get-tuple-element.51), channel_id=1, source_target_pairs={{4,0},{6,2},{0,4},{2,6},{5,1},{7,3},{1,5},{3,7},{12,8},{14,10},{8,... | collective-permute-start | bytes 786440 | tf_op jit(solution)/shard_map/ppermute | solution.py:261
  63.1 6.8 %collective-permute-start.16 = (bf16[8,32,512]{2,1,0:T(8,128)(2,1)S(1)}, bf16[8,32,512]{2,1,0:T(8,128)(2,1)S(1)}, u32[]{:S(2)}, u32[]{:S(2)}) collective-permute-start(bf16[8,32,512]{2,1,0:T(8,128)(2,1)S(1)} %slice.38), channel_id=1, source_target_pairs={{8,0},{16,8},{24,16},{0,24},{9,1},{17,9},{25,17},{1,25},{10,2},{18... | collective-permute-start | bytes 786440 | tf_op jit(solution)/shard_map/ppermute | solution.py:261
  64.8 7.7 %collective-permute-start.18 = (bf16[8,32,512]{2,1,0:T(8,128)(2,1)S(1)}, bf16[8,32,512]{2,1,0:T(8,128)(2,1)S(1)}, u32[]{:S(2)}, u32[]{:S(2)}) collective-permute-start(bf16[8,32,512]{2,1,0:T(8,128)(2,1)S(1)} %slice.39), channel_id=1, source_target_pairs={{24,0},{0,8},{8,16},{16,24},{25,1},{1,9},{9,17},{17,25},{26,2},{2,... | collective-permute-start | bytes 786440 | tf_op jit(solution)/shard_map/ppermute | solution.py:261
  69.1 6.4 %collective-permute-start.20 = (bf16[128,1024]{1,0:T(8,128)(2,1)S(1)}, bf16[128,1024]{1,0:T(8,128)(2,1)S(1)}, u32[]{:S(2)}, u32[]{:S(2)}) collective-permute-start(bf16[128,1024]{1,0:T(8,128)(2,1)S(1)} %get-tuple-element.41.a), channel_id=1, source_target_pairs={{6,0},{0,2},{2,4},{4,6},{7,1},{1,3},{3,5},{5,7},{14,8},{8,10},{10,... | collective-permute-start | bytes 786440 | tf_op jit(solution)/shard_map/ppermute | solution.py:261
  75.5 7.5 %collective-permute-start.23 = (bf16[1024,1024]{1,0:T(8,128)(2,1)S(1)}, bf16[1024,1024]{1,0:T(8,128)(2,1)S(1)}, u32[]{:S(2)}, u32[]{:S(2)}) collective-permute-start(bf16[1024,1024]{1,0:T(8,128)(2,1)S(1)} %mlp_lay.1.weight), channel_id=1, source_target_pairs={{1,0},{0,1},{3,2},{2,3},{5,4},{4,5},{7,6},{6,7},{9,8},{8,9},{11,10... | collective-permute-start | bytes 6291464 | tf_op jit(solution)/shard_map/ppermute | solution.py:261
  87.0 8.6 %collective-permute-start.26 = (bf16[128,1024]{1,0:T(8,128)(2,1)S(1)}, bf16[128,1024]{1,0:T(8,128)(2,1)S(1)}, u32[]{:S(2)}, u32[]{:S(2)}) collective-permute-start(bf16[128,1024]{1,0:T(8,128)(2,1)S(1)} %mlp_far.1), channel_id=1, source_target_pairs={{4,0},{6,2},{0,4},{2,6},{5,1},{7,3},{1,5},{3,7},{12,8},{14,10},{8,... | collective-permute-start | bytes 786440 | tf_op jit(solution)/shard_map/ppermute | solution.py:261
  87.7 14.7 %collective-permute-start.24 = (bf16[128,1024]{1,0:T(8,128)(2,1)S(1)}, bf16[128,1024]{1,0:T(8,128)(2,1)S(1)}, u32[]{:S(2)}, u32[]{:S(2)}) collective-permute-start(bf16[128,1024]{1,0:T(8,128)(2,1)S(1)} %get-tuple-element.47), channel_id=1, source_target_pairs={{6,0},{0,2},{2,4},{4,6},{7,1},{1,3},{3,5},{5,7},{14,8},{8,10},{10,... | collective-permute-start | bytes 786440 | tf_op jit(solution)/shard_map/ppermute | solution.py:261
  87.8 14.7 %collective-permute-start.25 = (bf16[128,1024]{1,0:T(8,128)(2,1)S(1)}, bf16[128,1024]{1,0:T(8,128)(2,1)S(1)}, u32[]{:S(2)}, u32[]{:S(2)}) collective-permute-start(bf16[128,1024]{1,0:T(8,128)(2,1)S(1)} %get-tuple-element.48), channel_id=1, source_target_pairs={{2,0},{4,2},{6,4},{0,6},{3,1},{5,3},{7,5},{1,7},{10,8},{12,10},{14... | collective-permute-start | bytes 786440 | tf_op jit(solution)/shard_map/ppermute | solution.py:261
  (10 other events, 191.2 us)

commit v10 on v9

--- a/solution.py
+++ b/solution.py
@@ -231,15 +231,18 @@
     to_c[...] = total[256:].astype(BF16)
 
 
-def mlp_far_kernel(low, high, weight, other, out):
+def mlp_far_kernel(low, high, weight, other, to_low, to_high):
     rows = jnp.concatenate([low[...], high[...]], axis=0)
-    out[...] = (hidden_share(rows, weight) + hidden_share(rows, other)).astype(BF16)
-
-
-def end_kernel(middle, mine, a, b, c, out):
+    total = (hidden_share(rows, weight) + hidden_share(rows, other)).astype(BF16)
+    to_low[...] = total[:64]
+    to_high[...] = total[64:]
+
+
+def end_kernel(middle, mine, a, b, low, high, out):
     total = middle[...].astype(F32) + mine[...]
-    total += a[...].astype(F32) + b[...].astype(F32) + c[...].astype(F32)
-    out[...] = total.astype(BF16)
+    total += a[...].astype(F32) + b[...].astype(F32)
+    out[:64] = (total[:64] + low[...].astype(F32)).astype(BF16)
+    out[64:] = (total[64:] + high[...].astype(F32)).astype(BF16)
 
 
 def call(kernel, outs, specs, name, mib=8, scratch=(), flops=2**20, **more):
@@ -377,11 +380,11 @@
     )(normed_two, near[1], near[3], mlp_peer, part)
     parts = [fetch(to_right, "y", 3), fetch(to_left, "y", 1)]
     (low, high), mine = lax.optimization_barrier(((low, high), mine))
-    (to_far,) = call(mlp_far_kernel, [((128, 1024), BF16)], [VMEM] * 4, "mlp_far", mib=16)(
+    to_far = call(mlp_far_kernel, [((64, 1024), BF16)] * 2, [VMEM] * 4, "mlp_far", mib=16)(
         low, high, mlp_own, mlp_peer
     )
-    parts.append(fetch(to_far, "y", 2))
-    (out,) = call(end_kernel, [((128, 1024), BF16)], [VMEM] * 5, "end")(middle, mine, *parts)
+    parts += [fetch(half, "y", 2) for half in to_far]
+    (out,) = call(end_kernel, [((128, 1024), BF16)], [VMEM] * 6, "end")(middle, mine, *parts)
     return out
 
 

time: 104 us -> 99.9 us (0.961)
  waiting for transfers between devices: 44 us -> 37.7 us
  starting transfers between devices: 44 us -> 46.4 us
    ppermute x26 -> x27, waiting for transfers between devices: 33.2 us -> 27 us  [fetch(): return lax.ppermute(value, axis, [((i + step) % n, i) for i in range(n)])]
    ppermute x26 -> x27, starting transfers between devices: 31.3 us -> 33.7 us  [fetch(): return lax.ppermute(value, axis, [((i + step) % n, i) for i in range(n)])]
  transfers between devices with their start and end apart: 29 -> 30, of which waited for: 17 -> 16; matrix products, arithmetic and copies ran while one was open for 0% -> 0% of each run, Pallas kernels for 11% -> 13%
where the time goes in v10:
time: 99.9 us; the launch traced here: 99.5 us
  starting transfers between devices  46.4 us (46%)
  waiting for transfers between devices  37.7 us (38%)
  Pallas kernels  14.9 us (15%)
    ppermute x27, starting transfers between devices, fetch(): return lax.ppermute(value, axis, [((i + step) % n, i) for i in range(n)])  33.7 us
    ppermute x27, waiting for transfers between devices, fetch(): return lax.ppermute(value, axis, [((i + step) % n, i) for i in range(n)])  27 us
    all_to_all x1, starting transfers between devices, local(): front = lax.all_to_all(front, 'z', 0, 0, tiled=True)  9.16 us
    ppermute x1, waiting for transfers between devices, local(): lax.ppermute(border, ('z', 'x', 'y', 'core'), [(spot(*divmod(s, 4), j, c)...  7.08 us
    pallas_call x3, Pallas kernels, from_hbm(): call(kernel, outs, [HBM] * len(given), name, scratch=[pltpu.VMEM(v.shape,...  4.29 us
    all_to_all x1, waiting for transfers between devices, local(): front = lax.all_to_all(front, 'z', 0, 0, tiled=True)  3.69 us
    all_to_all x1, starting transfers between devices, local(): back = lax.all_to_all(back, 'z', 0, 0, tiled=True)  3.49 us
    pallas_call x1, Pallas kernels, local(): call(attention_kernel, [((512, 128), BF16), ((1536, 128), BF16)], [SMEM]...  3.32 us
  transfers between devices with their start and end apart: 30, of which 16 were waited for; matrix products, arithmetic and copies ran while one was open for 0% of the time, Pallas kernels for 13%

profile of v10, /device:TPU:1, one launch (start us, length us, event | category | flops | bytes accessed | tf_op | source)
XLA Modules:
  0.0 99.5 jit_solution(8264175050750269710)
XLA Ops:
  1.5 9.2 %all-to-all-start = ((bf16[8,32,512]{2,1,0:T(8,128)(2,1)}), bf16[8,32,512]{2,1,0:T(8,128)(2,1)S(1)}, u32[]{:S(2)}, u32[]{:S(2)}) async-start(bf16[8,32,512]{2,1,0:T(8,128)(2,1)} %pack.1), calls=%async_computation | async-start | bytes 524288 | tf_op jit(solution)/shard_map/all_to_all | solution.py:309
  11.9 2.8 %collective-permute-start = (bf16[128,1024]{1,0:T(8,128)(2,1)S(1)}, bf16[128,1024]{1,0:T(8,128)(2,1)S(1)}, u32[]{:S(2)}, u32[]{:S(2)}) collective-permute-start(bf16[128,1024]{1,0:T(8,128)(2,1)S(1)} %norm.1.refs_0_), channel_id=1, source_target_pairs={{2,0},{4,2},{6,4},{0,6},{3,1},{5,3},{7,5},{1,7},{10,8},{12,10},{14... | collective-permute-start | bytes 786440 | tf_op jit(solution)/shard_map/ppermute | solution.py:264
  15.7 1.6 %mlp_pack.1 = bf16[8,32,1024]{2,1,0:T(8,128)(2,1)} custom-call(bf16[32,512]{1,0:T(8,128)(2,1)} %refs_0_.3, bf16[32,512]{1,0:T(8,128)(2,1)} %bitcast.20), custom_call_target="tpu_custom_call" | custom-call | flops 1048576 | bytes 2097152 | tf_op jit(solution)/shard_map/mlp_pack/pallas_call | solution.py:76
  17.4 3.7 %all-to-all-done.here = bf16[8,32,512]{2,1,0:T(8,128)(2,1)S(1)} async-done(((bf16[8,32,512]{2,1,0:T(8,128)(2,1)}), bf16[8,32,512]{2,1,0:T(8,128)(2,1)S(1)}, u32[]{:S(2)}, u32[]{:S(2)}) %all-to-all-start) | async-done | bytes 262176 | tf_op jit(solution)/shard_map/all_to_all | solution.py:309
  21.0 2.5 %collective-permute-start.3 = (bf16[8,32,512]{2,1,0:T(8,128)(2,1)S(1)}, bf16[8,32,512]{2,1,0:T(8,128)(2,1)S(1)}, u32[]{:S(2)}, u32[]{:S(2)}) collective-permute-start(bf16[8,32,512]{2,1,0:T(8,128)(2,1)S(1)} %all-to-all-done.here), channel_id=1, source_target_pairs={{8,0},{16,8},{24,16},{0,24},{9,1},{17,9},{25,17},{1,25},{10,2},{18... | collective-permute-start | bytes 786440 | tf_op jit(solution)/shard_map/ppermute | solution.py:264
  23.5 3.5 %all-to-all-start.1 = ((bf16[8,32,1024]{2,1,0:T(8,128)(2,1)}), bf16[8,32,1024]{2,1,0:T(8,128)(2,1)S(1)}, u32[]{:S(2)}, u32[]{:S(2)}) async-start(bf16[8,32,1024]{2,1,0:T(8,128)(2,1)} %mlp_pack.1), calls=%async_computation.1 | async-start | bytes 1048576 | tf_op jit(solution)/shard_map/all_to_all | solution.py:313
  27.1 2.9 %collective-permute-done.2.refs_3_ = bf16[128,1024]{1,0:T(8,128)(2,1)S(1)} collective-permute-done((bf16[128,1024]{1,0:T(8,128)(2,1)S(1)}, bf16[128,1024]{1,0:T(8,128)(2,1)S(1)}, u32[]{:S(2)}, u32[]{:S(2)}) %collective-permute-start.2) | collective-permute-done | bytes 262176 | tf_op jit(solution)/shard_map/ppermute | solution.py:264
  30.9 3.8 %collective-permute-start.5 = (bf16[2,128,1024]{2,1,0:T(8,128)(2,1)S(1)}, bf16[2,128,1024]{2,1,0:T(8,128)(2,1)S(1)}, u32[]{:S(2)}, u32[]{:S(2)}) collective-permute-start(bf16[2,128,1024]{2,1,0:T(8,128)(2,1)S(1)} %get-tuple-element.34.own_low), channel_id=1, source_target_pairs={{1,0},{0,1},{3,2},{2,3},{5,4},{4,5},{7,6},{6,7},{9,8},{8,9},{11,10... | collective-permute-start | bytes 1572872 | tf_op jit(solution)/shard_map/ppermute | solution.py:264
  34.8 2.8 %collective-permute-start.7 = (bf16[8,32,256]{2,1,0:T(8,128)(2,1)S(1)}, bf16[8,32,256]{2,1,0:T(8,128)(2,1)S(1)}, u32[]{:S(2)}, u32[]{:S(2)}) collective-permute-start(bf16[8,32,256]{2,1,0:T(8,128)(2,1)S(1)} %slice.36), channel_id=1, source_target_pairs={{8,0},{16,8},{24,16},{0,24},{9,1},{17,9},{25,17},{1,25},{10,2},{18... | collective-permute-start | bytes 393224 | tf_op jit(solution)/shard_map/ppermute | solution.py:264
  37.6 7.1 %collective-permute-done.9.near_own = bf16[64,1024]{1,0:T(8,128)(2,1)S(1)} collective-permute-done((bf16[64,1024]{1,0:T(8,128)(2,1)S(1)}, bf16[64,1024]{1,0:T(8,128)(2,1)S(1)}, u32[]{:S(2)}, u32[]{:S(2)}) %collective-permute-start.9) | collective-permute-done | bytes 131104 | tf_op jit(solution)/shard_map/ppermute | solution.py:324
  46.1 3.3 %attention.1 = (bf16[512,128]{1,0:T(8,128)(2,1)S(1)}, bf16[1536,128]{1,0:T(8,128)(2,1)S(1)}) custom-call(s32[4]{0:T(128)S(1)} %pad_add_fusion.at, bf16[2,128,1024]{2,1,0:T(8,128)(2,1)S(1)} %get-tuple-element.34.own_low, bf16[2,128,1024]{2,1,0:T(8,128)(2,1)S(1)} %get-tuple-element.35.own_high, bf16[2,128,1024]{2,1,0:T(8,128)(2,1)S(1)} %collective-permute-done.5.peer_low, ...), custom_call_target="tpu_custom_call" | custom-call | flops 1048576 | bytes 2097152 | tf_op jit(solution)/shard_map/attention/pallas_call | solution.py:335
  53.9 1.5 %collective-permute-start.13 = (bf16[128,1024]{1,0:T(8,128)(2,1)S(1)}, bf16[128,1024]{1,0:T(8,128)(2,1)S(1)}, u32[]{:S(2)}, u32[]{:S(2)}) collective-permute-start(bf16[128,1024]{1,0:T(8,128)(2,1)S(1)} %get-tuple-element.56), channel_id=1, source_target_pairs={{2,0},{4,2},{6,4},{0,6},{3,1},{5,3},{7,5},{1,7},{10,8},{12,10},{14... | collective-permute-start | bytes 786440 | tf_op jit(solution)/shard_map/ppermute | solution.py:264
  55.4 1.6 %collective-permute-start.14 = (bf16[128,1024]{1,0:T(8,128)(2,1)S(1)}, bf16[128,1024]{1,0:T(8,128)(2,1)S(1)}, u32[]{:S(2)}, u32[]{:S(2)}) collective-permute-start(bf16[128,1024]{1,0:T(8,128)(2,1)S(1)} %get-tuple-element.55), channel_id=1, source_target_pairs={{4,0},{6,2},{0,4},{2,6},{5,1},{7,3},{1,5},{3,7},{12,8},{14,10},{8,... | collective-permute-start | bytes 786440 | tf_op jit(solution)/shard_map/ppermute | solution.py:264
  56.9 6.2 %collective-permute-done.15.refs_1_ = bf16[8,32,1024]{2,1,0:T(8,128)(2,1)S(1)} collective-permute-done((bf16[8,32,1024]{2,1,0:T(8,128)(2,1)S(1)}, bf16[8,32,1024]{2,1,0:T(8,128)(2,1)S(1)}, u32[]{:S(2)}, u32[]{:S(2)}) %collective-permute-start.15) | collective-permute-done | bytes 524320 | tf_op jit(solution)/shard_map/ppermute | solution.py:264
  63.1 1.6 %collective-permute-start.16 = (bf16[8,32,512]{2,1,0:T(8,128)(2,1)S(1)}, bf16[8,32,512]{2,1,0:T(8,128)(2,1)S(1)}, u32[]{:S(2)}, u32[]{:S(2)}) collective-permute-start(bf16[8,32,512]{2,1,0:T(8,128)(2,1)S(1)} %slice.38), channel_id=1, source_target_pairs={{8,0},{16,8},{24,16},{0,24},{9,1},{17,9},{25,17},{1,25},{10,2},{18... | collective-permute-start | bytes 786440 | tf_op jit(solution)/shard_map/ppermute | solution.py:264
  64.9 2.8 %collective-permute-done.14.c = bf16[128,1024]{1,0:T(8,128)(2,1)S(1)} collective-permute-done((bf16[128,1024]{1,0:T(8,128)(2,1)S(1)}, bf16[128,1024]{1,0:T(8,128)(2,1)S(1)}, u32[]{:S(2)}, u32[]{:S(2)}) %collective-permute-start.14) | collective-permute-done | bytes 262176 | tf_op jit(solution)/shard_map/ppermute | solution.py:264
  70.0 2.5 %collective-permute-done.18.refs_3_ = bf16[8,32,512]{2,1,0:T(8,128)(2,1)S(1)} collective-permute-done((bf16[8,32,512]{2,1,0:T(8,128)(2,1)S(1)}, bf16[8,32,512]{2,1,0:T(8,128)(2,1)S(1)}, u32[]{:S(2)}, u32[]{:S(2)}) %collective-permute-start.18) | collective-permute-done | bytes 262176 | tf_op jit(solution)/shard_map/ppermute | solution.py:264
  75.5 3.7 %collective-permute-start.23 = (bf16[1024,1024]{1,0:T(8,128)(2,1)S(1)}, bf16[1024,1024]{1,0:T(8,128)(2,1)S(1)}, u32[]{:S(2)}, u32[]{:S(2)}) collective-permute-start(bf16[1024,1024]{1,0:T(8,128)(2,1)S(1)} %mlp_lay.1.weight), channel_id=1, source_target_pairs={{1,0},{0,1},{3,2},{2,3},{5,4},{4,5},{7,6},{6,7},{9,8},{8,9},{11,10... | collective-permute-start | bytes 6291464 | tf_op jit(solution)/shard_map/ppermute | solution.py:264
  79.4 1.5 %collective-permute-start.22 = (bf16[64,1024]{1,0:T(8,128)(2,1)S(1)}, bf16[64,1024]{1,0:T(8,128)(2,1)S(1)}, u32[]{:S(2)}, u32[]{:S(2)}) collective-permute-start(bf16[64,1024]{1,0:T(8,128)(2,1)S(1)} %slice.35), channel_id=1, source_target_pairs={{6,0},{0,2},{2,4},{4,6},{7,1},{1,3},{3,5},{5,7},{14,8},{8,10},{10,... | collective-permute-start | bytes 393224 | tf_op jit(solution)/shard_map/ppermute | solution.py:264
  84.3 2.7 %collective-permute-start.25 = (bf16[128,1024]{1,0:T(8,128)(2,1)S(1)}, bf16[128,1024]{1,0:T(8,128)(2,1)S(1)}, u32[]{:S(2)}, u32[]{:S(2)}) collective-permute-start(bf16[128,1024]{1,0:T(8,128)(2,1)S(1)} %get-tuple-element.50), channel_id=1, source_target_pairs={{2,0},{4,2},{6,4},{0,6},{3,1},{5,3},{7,5},{1,7},{10,8},{12,10},{14... | collective-permute-start | bytes 786440 | tf_op jit(solution)/shard_map/ppermute | solution.py:264
  88.3 3.0 %collective-permute-start.27 = (bf16[64,1024]{1,0:T(8,128)(2,1)S(1)}, bf16[64,1024]{1,0:T(8,128)(2,1)S(1)}, u32[]{:S(2)}, u32[]{:S(2)}) collective-permute-start(bf16[64,1024]{1,0:T(8,128)(2,1)S(1)} %get-tuple-element.54), channel_id=1, source_target_pairs={{4,0},{6,2},{0,4},{2,6},{5,1},{7,3},{1,5},{3,7},{12,8},{14,10},{8,... | collective-permute-start | bytes 393224 | tf_op jit(solution)/shard_map/ppermute | solution.py:264
  91.2 2.9 %collective-permute-done.26.low = bf16[64,1024]{1,0:T(8,128)(2,1)S(1)} collective-permute-done((bf16[64,1024]{1,0:T(8,128)(2,1)S(1)}, bf16[64,1024]{1,0:T(8,128)(2,1)S(1)}, u32[]{:S(2)}, u32[]{:S(2)}) %collective-permute-start.26) | collective-permute-done | bytes 131104 | tf_op jit(solution)/shard_map/ppermute | solution.py:264
  94.1 2.8 %collective-permute-done.27.high = bf16[64,1024]{1,0:T(8,128)(2,1)S(1)} collective-permute-done((bf16[64,1024]{1,0:T(8,128)(2,1)S(1)}, bf16[64,1024]{1,0:T(8,128)(2,1)S(1)}, u32[]{:S(2)}, u32[]{:S(2)}) %collective-permute-start.27) | collective-permute-done | bytes 131104 | tf_op jit(solution)/shard_map/ppermute | solution.py:264
  96.9 1.7 %collective-permute-done.24.a = bf16[128,1024]{1,0:T(8,128)(2,1)S(1)} collective-permute-done((bf16[128,1024]{1,0:T(8,128)(2,1)S(1)}, bf16[128,1024]{1,0:T(8,128)(2,1)S(1)}, u32[]{:S(2)}, u32[]{:S(2)}) %collective-permute-start.24) | collective-permute-done | bytes 262176 | tf_op jit(solution)/shard_map/ppermute | solution.py:264
  (66 shorter events, 21.7 us)
Async XLA Ops:
  1.5 19.5 %all-to-all-start = ((bf16[8,32,512]{2,1,0:T(8,128)(2,1)}), bf16[8,32,512]{2,1,0:T(8,128)(2,1)S(1)}, u32[]{:S(2)}, u32[]{:S(2)}) async-start(bf16[8,32,512]{2,1,0:T(8,128)(2,1)} %pack.1), calls=%async_computation | async-start | bytes 524288 | tf_op jit(solution)/shard_map/all_to_all | solution.py:309
  11.9 15.2 %collective-permute-start = (bf16[128,1024]{1,0:T(8,128)(2,1)S(1)}, bf16[128,1024]{1,0:T(8,128)(2,1)S(1)}, u32[]{:S(2)}, u32[]{:S(2)}) collective-permute-start(bf16[128,1024]{1,0:T(8,128)(2,1)S(1)} %norm.1.refs_0_), channel_id=1, source_target_pairs={{2,0},{4,2},{6,4},{0,6},{3,1},{5,3},{7,5},{1,7},{10,8},{12,10},{14... | collective-permute-start | bytes 786440 | tf_op jit(solution)/shard_map/ppermute | solution.py:264
  14.7 12.4 %collective-permute-start.1 = (bf16[128,1024]{1,0:T(8,128)(2,1)S(1)}, bf16[128,1024]{1,0:T(8,128)(2,1)S(1)}, u32[]{:S(2)}, u32[]{:S(2)}) collective-permute-start(bf16[128,1024]{1,0:T(8,128)(2,1)S(1)} %norm.1.refs_0_), channel_id=1, source_target_pairs={{4,0},{6,2},{0,4},{2,6},{5,1},{7,3},{1,5},{3,7},{12,8},{14,10},{8,... | collective-permute-start | bytes 786440 | tf_op jit(solution)/shard_map/ppermute | solution.py:264
  15.1 15.0 %collective-permute-start.2 = (bf16[128,1024]{1,0:T(8,128)(2,1)S(1)}, bf16[128,1024]{1,0:T(8,128)(2,1)S(1)}, u32[]{:S(2)}, u32[]{:S(2)}) collective-permute-start(bf16[128,1024]{1,0:T(8,128)(2,1)S(1)} %norm.1.refs_0_), channel_id=1, source_target_pairs={{6,0},{0,2},{2,4},{4,6},{7,1},{1,3},{3,5},{5,7},{14,8},{8,10},{10,... | collective-permute-start | bytes 786440 | tf_op jit(solution)/shard_map/ppermute | solution.py:264
  21.0 9.0 %collective-permute-start.3 = (bf16[8,32,512]{2,1,0:T(8,128)(2,1)S(1)}, bf16[8,32,512]{2,1,0:T(8,128)(2,1)S(1)}, u32[]{:S(2)}, u32[]{:S(2)}) collective-permute-start(bf16[8,32,512]{2,1,0:T(8,128)(2,1)S(1)} %all-to-all-done.here), channel_id=1, source_target_pairs={{8,0},{16,8},{24,16},{0,24},{9,1},{17,9},{25,17},{1,25},{10,2},{18... | collective-permute-start | bytes 786440 | tf_op jit(solution)/shard_map/ppermute | solution.py:264
  23.5 26.1 %all-to-all-start.1 = ((bf16[8,32,1024]{2,1,0:T(8,128)(2,1)}), bf16[8,32,1024]{2,1,0:T(8,128)(2,1)S(1)}, u32[]{:S(2)}, u32[]{:S(2)}) async-start(bf16[8,32,1024]{2,1,0:T(8,128)(2,1)} %mlp_pack.1), calls=%async_computation.1 | async-start | bytes 1048576 | tf_op jit(solution)/shard_map/all_to_all | solution.py:313
  30.9 15.2 %collective-permute-start.5 = (bf16[2,128,1024]{2,1,0:T(8,128)(2,1)S(1)}, bf16[2,128,1024]{2,1,0:T(8,128)(2,1)S(1)}, u32[]{:S(2)}, u32[]{:S(2)}) collective-permute-start(bf16[2,128,1024]{2,1,0:T(8,128)(2,1)S(1)} %get-tuple-element.34.own_low), channel_id=1, source_target_pairs={{1,0},{0,1},{3,2},{2,3},{5,4},{4,5},{7,6},{6,7},{9,8},{8,9},{11,10... | collective-permute-start | bytes 1572872 | tf_op jit(solution)/shard_map/ppermute | solution.py:264
  34.7 11.4 %collective-permute-start.6 = (bf16[2,128,1024]{2,1,0:T(8,128)(2,1)S(1)}, bf16[2,128,1024]{2,1,0:T(8,128)(2,1)S(1)}, u32[]{:S(2)}, u32[]{:S(2)}) collective-permute-start(bf16[2,128,1024]{2,1,0:T(8,128)(2,1)S(1)} %get-tuple-element.35.own_high), channel_id=1, source_target_pairs={{1,0},{0,1},{3,2},{2,3},{5,4},{4,5},{7,6},{6,7},{9,8},{8,9},{11,10... | collective-permute-start | bytes 1572872 | tf_op jit(solution)/shard_map/ppermute | solution.py:264
  34.8 9.9 %collective-permute-start.9 = (bf16[64,1024]{1,0:T(8,128)(2,1)S(1)}, bf16[64,1024]{1,0:T(8,128)(2,1)S(1)}, u32[]{:S(2)}, u32[]{:S(2)}) collective-permute-start(bf16[64,1024]{1,0:T(8,128)(2,1)S(1)} %get-tuple-element.36), channel_id=1, source_target_pairs={{0,248},{1,9},{2,250},{3,11},{4,252},{5,13},{6,254},{7,15},{8,0},{... | collective-permute-start | bytes 393224 | tf_op jit(solution)/shard_map/ppermute | solution.py:324
  34.8 9.9 %collective-permute-start.7 = (bf16[8,32,256]{2,1,0:T(8,128)(2,1)S(1)}, bf16[8,32,256]{2,1,0:T(8,128)(2,1)S(1)}, u32[]{:S(2)}, u32[]{:S(2)}) collective-permute-start(bf16[8,32,256]{2,1,0:T(8,128)(2,1)S(1)} %slice.36), channel_id=1, source_target_pairs={{8,0},{16,8},{24,16},{0,24},{9,1},{17,9},{25,17},{1,25},{10,2},{18... | collective-permute-start | bytes 393224 | tf_op jit(solution)/shard_map/ppermute | solution.py:264
  37.6 8.1 %collective-permute-start.8 = (bf16[8,32,256]{2,1,0:T(8,128)(2,1)S(1)}, bf16[8,32,256]{2,1,0:T(8,128)(2,1)S(1)}, u32[]{:S(2)}, u32[]{:S(2)}) collective-permute-start(bf16[8,32,256]{2,1,0:T(8,128)(2,1)S(1)} %slice.37), channel_id=1, source_target_pairs={{24,0},{0,8},{8,16},{16,24},{25,1},{1,9},{9,17},{17,25},{26,2},{2,... | collective-permute-start | bytes 393224 | tf_op jit(solution)/shard_map/ppermute | solution.py:264
  49.7 13.4 %collective-permute-start.15 = (bf16[8,32,1024]{2,1,0:T(8,128)(2,1)S(1)}, bf16[8,32,1024]{2,1,0:T(8,128)(2,1)S(1)}, u32[]{:S(2)}, u32[]{:S(2)}) collective-permute-start(bf16[8,32,1024]{2,1,0:T(8,128)(2,1)S(1)} %all-to-all-done.1.refs_0_), channel_id=1, source_target_pairs={{8,0},{16,8},{24,16},{0,24},{9,1},{17,9},{25,17},{1,25},{10,2},{18... | collective-permute-start | bytes 1572872 | tf_op jit(solution)/shard_map/ppermute | solution.py:264
  50.2 14.6 %collective-permute-start.17 = (bf16[8,32,1024]{2,1,0:T(8,128)(2,1)S(1)}, bf16[8,32,1024]{2,1,0:T(8,128)(2,1)S(1)}, u32[]{:S(2)}, u32[]{:S(2)}) collective-permute-start(bf16[8,32,1024]{2,1,0:T(8,128)(2,1)S(1)} %all-to-all-done.1.refs_0_), channel_id=1, source_target_pairs={{24,0},{0,8},{8,16},{16,24},{25,1},{1,9},{9,17},{17,25},{26,2},{2,... | collective-permute-start | bytes 1572872 | tf_op jit(solution)/shard_map/ppermute | solution.py:264
  52.5 12.4 %collective-permute-start.12 = (bf16[128,1024]{1,0:T(8,128)(2,1)S(1)}, bf16[128,1024]{1,0:T(8,128)(2,1)S(1)}, u32[]{:S(2)}, u32[]{:S(2)}) collective-permute-start(bf16[128,1024]{1,0:T(8,128)(2,1)S(1)} %get-tuple-element.57), channel_id=1, source_target_pairs={{6,0},{0,2},{2,4},{4,6},{7,1},{1,3},{3,5},{5,7},{14,8},{8,10},{10,... | collective-permute-start | bytes 786440 | tf_op jit(solution)/shard_map/ppermute | solution.py:264
  53.9 11.0 %collective-permute-start.13 = (bf16[128,1024]{1,0:T(8,128)(2,1)S(1)}, bf16[128,1024]{1,0:T(8,128)(2,1)S(1)}, u32[]{:S(2)}, u32[]{:S(2)}) collective-permute-start(bf16[128,1024]{1,0:T(8,128)(2,1)S(1)} %get-tuple-element.56), channel_id=1, source_target_pairs={{2,0},{4,2},{6,4},{0,6},{3,1},{5,3},{7,5},{1,7},{10,8},{12,10},{14... | collective-permute-start | bytes 786440 | tf_op jit(solution)/shard_map/ppermute | solution.py:264
  55.4 12.3 %collective-permute-start.14 = (bf16[128,1024]{1,0:T(8,128)(2,1)S(1)}, bf16[128,1024]{1,0:T(8,128)(2,1)S(1)}, u32[]{:S(2)}, u32[]{:S(2)}) collective-permute-start(bf16[128,1024]{1,0:T(8,128)(2,1)S(1)} %get-tuple-element.55), channel_id=1, source_target_pairs={{4,0},{6,2},{0,4},{2,6},{5,1},{7,3},{1,5},{3,7},{12,8},{14,10},{8,... | collective-permute-start | bytes 786440 | tf_op jit(solution)/shard_map/ppermute | solution.py:264
  63.1 6.8 %collective-permute-start.16 = (bf16[8,32,512]{2,1,0:T(8,128)(2,1)S(1)}, bf16[8,32,512]{2,1,0:T(8,128)(2,1)S(1)}, u32[]{:S(2)}, u32[]{:S(2)}) collective-permute-start(bf16[8,32,512]{2,1,0:T(8,128)(2,1)S(1)} %slice.38), channel_id=1, source_target_pairs={{8,0},{16,8},{24,16},{0,24},{9,1},{17,9},{25,17},{1,25},{10,2},{18... | collective-permute-start | bytes 786440 | tf_op jit(solution)/shard_map/ppermute | solution.py:264
  64.8 7.7 %collective-permute-start.18 = (bf16[8,32,512]{2,1,0:T(8,128)(2,1)S(1)}, bf16[8,32,512]{2,1,0:T(8,128)(2,1)S(1)}, u32[]{:S(2)}, u32[]{:S(2)}) collective-permute-start(bf16[8,32,512]{2,1,0:T(8,128)(2,1)S(1)} %slice.39), channel_id=1, source_target_pairs={{24,0},{0,8},{8,16},{16,24},{25,1},{1,9},{9,17},{17,25},{26,2},{2,... | collective-permute-start | bytes 786440 | tf_op jit(solution)/shard_map/ppermute | solution.py:264
  75.5 7.5 %collective-permute-start.23 = (bf16[1024,1024]{1,0:T(8,128)(2,1)S(1)}, bf16[1024,1024]{1,0:T(8,128)(2,1)S(1)}, u32[]{:S(2)}, u32[]{:S(2)}) collective-permute-start(bf16[1024,1024]{1,0:T(8,128)(2,1)S(1)} %mlp_lay.1.weight), channel_id=1, source_target_pairs={{1,0},{0,1},{3,2},{2,3},{5,4},{4,5},{7,6},{6,7},{9,8},{8,9},{11,10... | collective-permute-start | bytes 6291464 | tf_op jit(solution)/shard_map/ppermute | solution.py:264
  79.3 7.7 %collective-permute-start.21 = (bf16[64,1024]{1,0:T(8,128)(2,1)S(1)}, bf16[64,1024]{1,0:T(8,128)(2,1)S(1)}, u32[]{:S(2)}, u32[]{:S(2)}) collective-permute-start(bf16[64,1024]{1,0:T(8,128)(2,1)S(1)} %slice.34), channel_id=1, source_target_pairs={{2,0},{4,2},{6,4},{0,6},{3,1},{5,3},{7,5},{1,7},{10,8},{12,10},{14... | collective-permute-start | bytes 393224 | tf_op jit(solution)/shard_map/ppermute | solution.py:264
  79.4 7.6 %collective-permute-start.22 = (bf16[64,1024]{1,0:T(8,128)(2,1)S(1)}, bf16[64,1024]{1,0:T(8,128)(2,1)S(1)}, u32[]{:S(2)}, u32[]{:S(2)}) collective-permute-start(bf16[64,1024]{1,0:T(8,128)(2,1)S(1)} %slice.35), channel_id=1, source_target_pairs={{6,0},{0,2},{2,4},{4,6},{7,1},{1,3},{3,5},{5,7},{14,8},{8,10},{10,... | collective-permute-start | bytes 393224 | tf_op jit(solution)/shard_map/ppermute | solution.py:264
  84.2 14.4 %collective-permute-start.24 = (bf16[128,1024]{1,0:T(8,128)(2,1)S(1)}, bf16[128,1024]{1,0:T(8,128)(2,1)S(1)}, u32[]{:S(2)}, u32[]{:S(2)}) collective-permute-start(bf16[128,1024]{1,0:T(8,128)(2,1)S(1)} %get-tuple-element.49), channel_id=1, source_target_pairs={{6,0},{0,2},{2,4},{4,6},{7,1},{1,3},{3,5},{5,7},{14,8},{8,10},{10,... | collective-permute-start | bytes 786440 | tf_op jit(solution)/shard_map/ppermute | solution.py:264
  84.3 14.3 %collective-permute-start.25 = (bf16[128,1024]{1,0:T(8,128)(2,1)S(1)}, bf16[128,1024]{1,0:T(8,128)(2,1)S(1)}, u32[]{:S(2)}, u32[]{:S(2)}) collective-permute-start(bf16[128,1024]{1,0:T(8,128)(2,1)S(1)} %get-tuple-element.50), channel_id=1, source_target_pairs={{2,0},{4,2},{6,4},{0,6},{3,1},{5,3},{7,5},{1,7},{10,8},{12,10},{14... | collective-permute-start | bytes 786440 | tf_op jit(solution)/shard_map/ppermute | solution.py:264
  88.3 8.7 %collective-permute-start.27 = (bf16[64,1024]{1,0:T(8,128)(2,1)S(1)}, bf16[64,1024]{1,0:T(8,128)(2,1)S(1)}, u32[]{:S(2)}, u32[]{:S(2)}) collective-permute-start(bf16[64,1024]{1,0:T(8,128)(2,1)S(1)} %get-tuple-element.54), channel_id=1, source_target_pairs={{4,0},{6,2},{0,4},{2,6},{5,1},{7,3},{1,5},{3,7},{12,8},{14,10},{8,... | collective-permute-start | bytes 393224 | tf_op jit(solution)/shard_map/ppermute | solution.py:264
  (11 other events, 198.7 us)
